TPU v7x, 32 devices: a whole 2x2x4 slice. The times are simulated.
32 devices in a mesh: dp: 4 (over y, core), ctx: 2 (over x), tp: 4 (over z).
Axes of the slice: x: 2, y: 2, z: 4, core: 2. Of those that a mesh axis runs over, the one named last changes fastest.
Arguments:
- tokens: bfloat16 [8, 256, 2048], P('dp', 'ctx'), may hold values from -6 to 6
- mixgain: bfloat16 [2048], replicated, may hold values from 0.5 to 1.5
- inproj: bfloat16 [2, 2048, 4096], P(None, ('dp', 'ctx'), 'tp'), may hold values from -0.125 to 0.125
- convkern: bfloat16 [4, 4096], P(None, 'tp'), may hold values from -3 to 3
- convbias: bfloat16 [4096], P('tp'), may hold values from -0.5 to 0.5
- selproj: bfloat16 [4096, 160], P('tp'), may hold values from -0.09375 to 0.09375
- stepproj: bfloat16 [128, 4096], P(None, 'tp'), may hold values from -0.5 to 0.5
- stepbias: bfloat16 [4096], P('tp'), may hold values from -6.875 to -2.296875
- decaylog: bfloat16 [4096, 16], P('tp'), may hold values from -4 to 2.6875
- skipgain: bfloat16 [4096], P('tp'), may hold values from 0.5 to 1.5
- outproj: bfloat16 [4096, 2048], P('tp', ('dp', 'ctx')), may hold values from -0.375 to 0.375
- ffngain: bfloat16 [2048], replicated, may hold values from 0.5 to 1.5
- gateup: bfloat16 [2, 2048, 8192], P(None, ('dp', 'ctx'), 'tp'), may hold values from -0.125 to 0.125
- downproj: bfloat16 [8192, 2048], P('tp', ('dp', 'ctx')), may hold values from -0.0625 to 0.0625
- cotangent: bfloat16 [8, 256, 2048], P('dp', 'ctx'), may hold values from -6 to 6
Outputs:
- layer_out: bfloat16 [8, 256, 2048], P('dp', 'ctx')
- tokens_grad: bfloat16 [8, 256, 2048], P('dp', 'ctx')
- mixgain_grad: float32 [2048], replicated
- inproj_grad: float32 [2, 2048, 4096], P(None, ('dp', 'ctx'), 'tp')
- convkern_grad: float32 [4, 4096], P(None, 'tp')
- convbias_grad: float32 [4096], P('tp')
- selproj_grad: float32 [4096, 160], P('tp')
- stepproj_grad: float32 [128, 4096], P(None, 'tp')
- stepbias_grad: float32 [4096], P('tp')
- decaylog_grad: float32 [4096, 16], P('tp')
- skipgain_grad: float32 [4096], P('tp')
- outproj_grad: float32 [4096, 2048], P('tp', ('dp', 'ctx'))
- ffngain_grad: float32 [2048], replicated
- gateup_grad: float32 [2, 2048, 8192], P(None, ('dp', 'ctx'), 'tp')
- downproj_grad: float32 [8192, 2048], P('tp', ('dp', 'ctx'))
All inputs are finite; a program needn't handle non-finite values.
Results may differ from a plain program's by a relative error of at most 0.012.
The roundings to bfloat16 on the way count: a program that leaves them out, or rounds other values in their place, can miss the bound.
Values may be sent and summed in bfloat16 or wider, within the bound.
A program may use at most 320 MiB of HBM per device.

v0:
```python
import jax
import jax.numpy as jnp
from jax import lax
from jax.sharding import PartitionSpec as P

EPSILON = 1e-05


def passed_along(value, axis, steps):
    count = lax.axis_size(axis)
    first, last = (max(0, -steps), min(count, count - steps))
    return lax.ppermute(value, axis, [(source, source + steps) for source in range(first, last)])


def carried_in(part, axis, combine, identity):
    place = lax.axis_index(axis)
    gathered = jax.tree.map(lambda a: lax.all_gather(a, axis), part)
    state = jax.tree.map(lambda a, e: jnp.zeros_like(a) + jnp.asarray(e, a.dtype), part, identity)

    def one(turn, state):
        return combine(
            state, jax.tree.map(lambda a: lax.dynamic_index_in_dim(a, turn, 0, False), gathered)
        )

    return lax.fori_loop(0, place, one, state)


def entering(shard, axis, combine, identity):
    devices, index = (lax.axis_size(axis), lax.axis_index(axis))
    everything = jax.tree.map(
        lambda part, kind: lax.all_gather(part.astype(kind), axis),
        shard,
        (jnp.bfloat16, jnp.bfloat16),
    )
    start = jax.tree.map(
        lambda part, zero: jnp.broadcast_to(jnp.asarray(zero, part.dtype), part.shape),
        shard,
        identity,
    )

    def turn(k, before):
        at = devices - 1 - k
        reached = at > index
        new = combine(
            before, jax.tree.map(lambda part, own: part[at].astype(own.dtype), everything, shard)
        )
        return jax.tree.map(lambda a, b: jnp.where(reached, a, b), new, before)

    return lax.fori_loop(0, devices, turn, start)


def matmul(left, right):
    return jnp.dot(left, right, preferred_element_type=jnp.float32)


def matmul_nt(left, right):
    return lax.dot_general(
        left, right, (((1,), (1,)), ((), ())), preferred_element_type=jnp.float32
    )


def matmul_tn(left, right):
    return lax.dot_general(
        left, right, (((0,), (0,)), ((), ())), preferred_element_type=jnp.float32
    )


def affine(earlier, latter):
    return (earlier[0] * latter[0], latter[0] * earlier[1] + latter[1])


def inverse_rms(values):
    return lax.rsqrt(jnp.mean(values * values, -1, keepdims=True) + EPSILON)


def silu_slope(values):
    logistic = jax.nn.sigmoid(values)
    return logistic * (1.0 + values * (1.0 - logistic))


def norm_back(grad_norm, values, scale, gain):
    scaled_grad = grad_norm * gain
    unit_rows = values * scale
    return scale * (scaled_grad - unit_rows * jnp.mean(scaled_grad * unit_rows, -1, keepdims=True))


def decayed_sum(offsets, linear, vectors, decay_rate, block_len):
    blocks = offsets.shape[0] // block_len

    def accumulate(running, pieces):
        offset_blk, linear_blk, vector_blk = pieces
        factor = jnp.exp(offset_blk[:, None, :] * decay_rate[None])
        return (
            running + jnp.sum(factor * linear_blk[:, None, :] * vector_blk[:, :, None], 0),
            None,
        )

    shaped = (
        offsets.reshape(blocks, block_len, -1),
        linear.reshape(blocks, block_len, -1),
        vectors.reshape(blocks, block_len, -1),
    )
    running, _ = lax.scan(accumulate, jnp.zeros(decay_rate.shape, jnp.float32), shaped)
    return running


def forward_states(start_state, step_size, inputs, b_rows, c_rows, decay_rate, block_len):
    blocks = step_size.shape[0] // block_len

    def advance(carried, pieces):
        step_blk, input_blk, brow_blk, crow_blk = pieces
        decays = jnp.exp(step_blk[:, None, :] * decay_rate[None])
        driven = (step_blk * input_blk)[:, None, :] * brow_blk[:, :, None]
        products, partial_sum = lax.associative_scan(affine, (decays, driven), axis=0)
        states = products * carried[None] + partial_sum
        mixed = jnp.sum(states * crow_blk[:, :, None], 1)
        return (states[-1], (states, mixed))

    shaped = (
        step_size.reshape(blocks, block_len, -1),
        inputs.reshape(blocks, block_len, -1),
        b_rows.reshape(blocks, block_len, -1),
        c_rows.reshape(blocks, block_len, -1),
    )
    _, (states, mixed) = lax.scan(advance, start_state, shaped)
    return (states, mixed.reshape(step_size.shape))


def backward_states(
    end_grad,
    start_state,
    states,
    step_size,
    inputs,
    b_rows,
    c_rows,
    out_grad,
    decay_rate,
    block_len,
):
    blocks = step_size.shape[0] // block_len
    starts = jnp.concatenate([start_state[None], states[:-1, -1]], 0)

    def retreat(carried, pieces):
        step_blk, input_blk, brow_blk, crow_blk, ograd_blk, state_blk, first_state = pieces
        decays = jnp.exp(step_blk[:, None, :] * decay_rate[None])
        coefs = jnp.concatenate([decays[1:], jnp.ones_like(decays[:1])], 0)
        driven = ograd_blk[:, None, :] * crow_blk[:, :, None]
        products, partial_sum = lax.associative_scan(affine, (coefs, driven), reverse=True, axis=0)
        state_grad = partial_sum + products * carried[None]
        previous = jnp.concatenate([first_state[None], state_blk[:-1]], 0)
        decay_term = state_grad * previous * decays
        along_b = jnp.sum(state_grad * brow_blk[:, :, None], 1)
        step_grad = jnp.sum(decay_term * decay_rate[None], 1) + along_b * input_blk
        rate_grad = jnp.sum(decay_term * step_blk[:, None, :], 0)
        brow_grad = jnp.sum(state_grad * (step_blk * input_blk)[:, None, :], 2)
        crow_grad = jnp.sum(ograd_blk[:, None, :] * state_blk, 2)
        input_grad = step_blk * along_b
        return (decays[0] * state_grad[0], (step_grad, rate_grad, brow_grad, crow_grad, input_grad))

    shaped = (
        step_size.reshape(blocks, block_len, -1),
        inputs.reshape(blocks, block_len, -1),
        b_rows.reshape(blocks, block_len, -1),
        c_rows.reshape(blocks, block_len, -1),
        out_grad.reshape(blocks, block_len, -1),
        states,
        starts,
    )
    _, results = lax.scan(retreat, end_grad, shaped, reverse=True)
    step_grad, rate_grad, brow_grad, crow_grad, input_grad = results
    return (
        step_grad.reshape(step_size.shape),
        jnp.sum(rate_grad, 0),
        brow_grad.reshape(b_rows.shape),
        crow_grad.reshape(c_rows.shape),
        input_grad.reshape(inputs.shape),
    )


def per_device(
    tokens,
    mixgain,
    inproj,
    convkern,
    convbias,
    selproj,
    stepproj,
    stepbias,
    decaylog,
    skipgain,
    outproj,
    ffngain,
    gateup,
    downproj,
    cotangent,
):
    span_len = tokens.shape[1]
    model_width = tokens.shape[2]
    block_len = min(64, span_len)
    kernel_len = convkern.shape[0]
    rank_len = stepproj.shape[0]
    state_len = decaylog.shape[1]
    gain_mix = mixgain.astype(jnp.float32)
    gain_ffn = ffngain.astype(jnp.float32)
    kernel = convkern.astype(jnp.float32)
    kernel_bias = convbias.astype(jnp.float32)
    step_bias = stepbias.astype(jnp.float32)
    skip_weight = skipgain.astype(jnp.float32)
    decay_rate = -jnp.exp(jnp.transpose(decaylog.astype(jnp.float32)))

    def gather_weights():
        return (
            lax.all_gather(inproj, ("dp", "ctx"), axis=1, tiled=True),
            lax.all_gather(outproj, ("dp", "ctx"), axis=1, tiled=True),
            lax.all_gather(gateup, ("dp", "ctx"), axis=1, tiled=True),
            lax.all_gather(downproj, ("dp", "ctx"), axis=1, tiled=True),
        )

    inner_width = inproj.shape[2]
    hidden_width = gateup.shape[2]
    grad_inproj = jnp.zeros((2, model_width, inner_width), jnp.float32)
    grad_outproj = jnp.zeros((inner_width, model_width), jnp.float32)
    grad_gateup = jnp.zeros((2, model_width, hidden_width), jnp.float32)
    grad_downproj = jnp.zeros((hidden_width, model_width), jnp.float32)
    grad_convkern = jnp.zeros(kernel.shape, jnp.float32)
    grad_convbias = jnp.zeros(kernel_bias.shape, jnp.float32)
    grad_selproj = jnp.zeros(selproj.shape, jnp.float32)
    grad_stepproj = jnp.zeros(stepproj.shape, jnp.float32)
    grad_stepbias = jnp.zeros(step_bias.shape, jnp.float32)
    grad_decaylog = jnp.zeros(decay_rate.shape, jnp.float32)
    grad_skipgain = jnp.zeros(skip_weight.shape, jnp.float32)
    grad_mixgain = jnp.zeros((model_width,), jnp.float32)
    grad_ffngain = jnp.zeros((model_width,), jnp.float32)
    layer_rows = []
    tokens_rows = []
    for micro_batch in range(tokens.shape[0]):
        weights = gather_weights()
        in_full, out_full, gu_full, down_full = weights
        hidden_in = tokens[micro_batch].astype(jnp.float32)
        scale_one = inverse_rms(hidden_in)
        normed_one = (hidden_in * scale_one * gain_mix).astype(jnp.bfloat16)
        conv_in = matmul(normed_one, in_full[0]).astype(jnp.bfloat16)
        gate_mix = matmul(normed_one, in_full[1])
        rim_rows = passed_along(conv_in[span_len - (kernel_len - 1) :], "ctx", 1)
        padded_in = jnp.concatenate([rim_rows, conv_in], 0).astype(jnp.float32)
        conv_out = kernel_bias[None]
        for offset in range(kernel_len):
            conv_out = conv_out + kernel[offset][None] * padded_in[offset : offset + span_len]
        scan_in = jax.nn.silu(conv_out).astype(jnp.bfloat16)
        scan_float = scan_in.astype(jnp.float32)
        select_cols = lax.psum(matmul(scan_in, selproj), "tp")
        step_low = select_cols[:, :rank_len].astype(jnp.bfloat16)
        b_rows = select_cols[:, rank_len : rank_len + state_len]
        c_rows = select_cols[:, rank_len + state_len :]
        step_pre = matmul(step_low, stepproj) + step_bias[None]
        step_size = jax.nn.softplus(step_pre)
        elapsed = jnp.cumsum(step_size, 0)
        span_end = decayed_sum(
            elapsed[-1:] - elapsed, step_size * scan_float, b_rows, decay_rate, block_len
        )
        span_decay = jnp.exp(decay_rate * elapsed[-1][None, :])
        prefix = carried_in(
            (span_decay, span_end),
            "ctx",
            affine,
            (jnp.ones_like(span_decay), jnp.zeros_like(span_end)),
        )
        start_state = prefix[1]
        states, scan_out = forward_states(
            start_state, step_size, scan_float, b_rows, c_rows, decay_rate, block_len
        )
        mixer_core = scan_out + skip_weight[None] * scan_float
        gate_sig = jax.nn.silu(gate_mix)
        gated = (mixer_core * gate_sig).astype(jnp.bfloat16)
        mixed = lax.psum(matmul(gated, out_full), "tp")
        middle = hidden_in + mixed
        scale_two = inverse_rms(middle)
        normed_two = (middle * scale_two * gain_ffn).astype(jnp.bfloat16)
        gate_ffn = matmul(normed_two, gu_full[0])
        up_ffn = matmul(normed_two, gu_full[1])
        activated = (jax.nn.silu(gate_ffn) * up_ffn).astype(jnp.bfloat16)
        ffn_out = lax.psum(matmul(activated, down_full).astype(jnp.bfloat16), "tp").astype(
            jnp.float32
        )
        layer_rows.append((middle + ffn_out).astype(jnp.bfloat16))
        weights = gather_weights()
        in_full, out_full, gu_full, down_full = weights
        ct_low = cotangent[micro_batch]
        ct_float = ct_low.astype(jnp.float32)
        act_grad = matmul_nt(ct_low, down_full)
        grad_downproj = grad_downproj + matmul_tn(activated, ct_low)
        gate_grad = (act_grad * up_ffn * silu_slope(gate_ffn)).astype(jnp.bfloat16)
        up_grad = (act_grad * jax.nn.silu(gate_ffn)).astype(jnp.bfloat16)
        grad_gateup = grad_gateup + jnp.stack(
            [matmul_tn(normed_two, gate_grad), matmul_tn(normed_two, up_grad)]
        )
        normed_two_grad = lax.psum(
            matmul_nt(gate_grad, gu_full[0]) + matmul_nt(up_grad, gu_full[1]), "tp"
        )
        grad_ffngain = grad_ffngain + jnp.sum(normed_two_grad * middle * scale_two, 0)
        middle_grad = ct_float + norm_back(normed_two_grad, middle, scale_two, gain_ffn)
        middle_low = middle_grad.astype(jnp.bfloat16)
        grad_outproj = grad_outproj + matmul_tn(gated, middle_low)
        gated_grad = matmul_nt(middle_low, out_full)
        core_grad = gated_grad * gate_sig
        gate_mix_grad = (gated_grad * mixer_core * silu_slope(gate_mix)).astype(jnp.bfloat16)
        grad_skipgain = grad_skipgain + jnp.sum(core_grad * scan_float, 0)
        local_start = decayed_sum(elapsed, core_grad, c_rows, decay_rate, block_len)
        suffix = entering(
            (span_decay, local_start),
            "ctx",
            affine,
            (jnp.ones_like(span_decay), jnp.zeros_like(local_start)),
        )
        end_grad = suffix[1]
        step_grad, rate_grad, brow_grad, crow_grad, input_grad = backward_states(
            end_grad,
            start_state,
            states,
            step_size,
            scan_float,
            b_rows,
            c_rows,
            core_grad,
            decay_rate,
            block_len,
        )
        grad_decaylog = grad_decaylog + rate_grad * decay_rate
        pre_grad = step_grad * jax.nn.sigmoid(step_pre)
        grad_stepbias = grad_stepbias + jnp.sum(pre_grad, 0)
        pre_low = pre_grad.astype(jnp.bfloat16)
        grad_stepproj = grad_stepproj + matmul_tn(step_low, pre_low)
        select_grad = lax.psum(
            jnp.concatenate([matmul_nt(pre_low, stepproj), brow_grad, crow_grad], 1), "tp"
        )
        select_low = select_grad.astype(jnp.bfloat16)
        grad_selproj = grad_selproj + matmul_tn(scan_in, select_low)
        scan_in_grad = core_grad * skip_weight[None] + input_grad + matmul_nt(select_low, selproj)
        conv_grad = scan_in_grad * silu_slope(conv_out)
        grad_convbias = grad_convbias + jnp.sum(conv_grad, 0)
        padded_grad = jnp.zeros(padded_in.shape, jnp.float32)
        kernel_rows = []
        for offset in range(kernel_len):
            kernel_rows.append(jnp.sum(conv_grad * padded_in[offset : offset + span_len], 0))
            padded_grad = padded_grad + jnp.pad(
                kernel[offset][None] * conv_grad, ((offset, kernel_len - 1 - offset), (0, 0))
            )
        grad_convkern = grad_convkern + jnp.stack(kernel_rows)
        returned = passed_along(padded_grad[: kernel_len - 1], "ctx", -1)
        conv_in_grad = (
            padded_grad[kernel_len - 1 :]
            + jnp.pad(returned, ((span_len - kernel_len + 1, 0), (0, 0)))
        ).astype(jnp.bfloat16)
        grad_inproj = grad_inproj + jnp.stack(
            [matmul_tn(normed_one, conv_in_grad), matmul_tn(normed_one, gate_mix_grad)]
        )
        normed_one_grad = lax.psum(
            matmul_nt(conv_in_grad, in_full[0]) + matmul_nt(gate_mix_grad, in_full[1]), "tp"
        )
        grad_mixgain = grad_mixgain + jnp.sum(normed_one_grad * hidden_in * scale_one, 0)
        tokens_rows.append(
            (middle_grad + norm_back(normed_one_grad, hidden_in, scale_one, gain_mix)).astype(
                jnp.bfloat16
            )
        )
    grad_decaylog = jnp.transpose(grad_decaylog)
    shards = (
        lax.psum_scatter(grad_inproj, ("dp", "ctx"), scatter_dimension=1, tiled=True),
        lax.psum_scatter(grad_outproj, ("dp", "ctx"), scatter_dimension=1, tiled=True),
        lax.psum_scatter(grad_gateup, ("dp", "ctx"), scatter_dimension=1, tiled=True),
        lax.psum_scatter(grad_downproj, ("dp", "ctx"), scatter_dimension=1, tiled=True),
    )
    smalls = lax.psum(
        (
            grad_mixgain,
            grad_convkern,
            grad_convbias,
            grad_selproj,
            grad_stepproj,
            grad_stepbias,
            grad_decaylog,
            grad_skipgain,
            grad_ffngain,
        ),
        ("dp", "ctx"),
    )
    return (
        jnp.stack(layer_rows),
        jnp.stack(tokens_rows),
        smalls[0],
        shards[0],
        smalls[1],
        smalls[2],
        smalls[3],
        smalls[4],
        smalls[5],
        smalls[6],
        smalls[7],
        shards[1],
        smalls[8],
        shards[2],
        shards[3],
    )


def solution(mesh):
    in_specs = (
        P("dp", "ctx", None),
        P(),
        P(None, ("dp", "ctx"), "tp"),
        P(None, "tp"),
        P("tp"),
        P("tp", None),
        P(None, "tp"),
        P("tp"),
        P("tp", None),
        P("tp"),
        P("tp", ("dp", "ctx")),
        P(),
        P(None, ("dp", "ctx"), "tp"),
        P("tp", ("dp", "ctx")),
        P("dp", "ctx", None),
    )
    out_specs = (
        P("dp", "ctx", None),
        P("dp", "ctx", None),
        P(),
        P(None, ("dp", "ctx"), "tp"),
        P(None, "tp"),
        P("tp"),
        P("tp", None),
        P(None, "tp"),
        P("tp"),
        P("tp", None),
        P("tp"),
        P("tp", ("dp", "ctx")),
        P(),
        P(None, ("dp", "ctx"), "tp"),
        P("tp", ("dp", "ctx")),
    )
    return jax.shard_map(
        per_device, mesh=mesh, in_specs=in_specs, out_specs=out_specs, check_vma=False
    )
```

profile of v0, /device:TPU:0, one launch (start us, length us, event | category | flops | bytes accessed | tf_op | source)
XLA Modules:
  0.0 2973.5 jit_solution(8502804249434229414)
XLA Ops:
  11.9 55.2 %all-gather.13.cloned.1.call-done = bf16[2,2048,1024]{2,1,0:T(8,128)(2,1)} async-done(((bf16[2,256,1024]{2,1,0:T(8,128)(2,1)}), bf16[2,2048,1024]{2,1,0:T(8,128)(2,1)}) %all-gather.13.cloned.1.call-update) | async-done | bytes 8388624 | tf_op jit(solution)/shard_map/all_gather | solution.py:214
  89.7 29.5 all-reduce.134.cloned.1.call-done
  179.9 382.5 %while.177 = (s32[]{:T(128)}, f32[16,1024]{1,0:T(8,128)}, f32[2,64,16,1024]{3,2,1,0:T(8,128)}, f32[2,64,1024]{2,1,0:T(8,128)}, f32[2,64,1024]{2,1,0:T(8,128)S(1)...) while((s32[]{:T(128)}, f32[16,1024]{1,0:T(8,128)}, ...), condition=%wide.region_10.11_spmd, body=%wide.region_8.10_spmd.sunk | while | flops 20217856 | bytes 305185856 | solution.py:125
  299.4 18.6 pad.1245
  330.1 18.7 pad.1246
  490.5 18.6 pad.1245
  521.2 18.7 pad.1246
  567.8 385.2 %while.179 = (s32[]{:T(128)}, f32[16,1024]{1,0:T(8,128)}, f32[2,64,16,1024]{3,2,1,0:T(8,128)}, f32[2,64,1024]{2,1,0:T(8,128)}, f32[2,64,1024]{2,1,0:T(8,128)S(1)...) while((s32[]{:T(128)}, f32[16,1024]{1,0:T(8,128)}, ...), condition=%wide.region_24.25_spmd, body=%wide.region_22.24_spmd.sunk | while | flops 20217856 | bytes 298894304 | solution.py:125
  688.9 18.5 pad.1289
  719.5 18.6 pad.1290
  881.3 18.5 pad.1289
  911.9 18.6 pad.1290
  965.0 86.7 %all-reduce.132.cloned.1.call-done = (f32[128,2048]{1,0:T(8,128)}, f32[128,2048]{1,0:T(8,128)}) async-done(((f32[128,2048]{1,0:T(8,128)}, f32[128,2048]{1,0:T(8,128)}), (f32[128,2048]{1,0:T(8,128)}, f32[128,2048]{1,0:T(8,128)})) %all-reduce.132.cloned.1.call-update) | async-done | bytes 2097168 | tf_op jit(solution)/shard_map/psum | solution.py:276
  1054.5 87.9 %all-gather.17.cloned.1.call-done = bf16[2,2048,2048]{2,1,0:T(8,128)(2,1)} async-done(((bf16[2,256,2048]{2,1,0:T(8,128)(2,1)}), bf16[2,2048,2048]{2,1,0:T(8,128)(2,1)}) %all-gather.17.cloned.1.call-update) | async-done | bytes 16777232 | tf_op jit(solution)/shard_map/all_gather | solution.py:216
  1159.7 40.4 %all-gather.19.cloned.1.call-done = bf16[2048,2048]{1,0:T(8,128)(2,1)} async-done(((bf16[2048,256]{1,0:T(8,128)(2,1)}), bf16[2048,2048]{1,0:T(8,128)(2,1)}) %all-gather.19.cloned.1.call-update) | async-done | bytes 8388624 | tf_op jit(solution)/shard_map/all_gather | solution.py:217
  1264.5 62.5 %all-reduce.130.cloned.1.call-done = (f32[128,2048]{1,0:T(8,128)}, f32[128,2048]{1,0:T(8,128)}) async-done(((f32[128,2048]{1,0:T(8,128)}, f32[128,2048]{1,0:T(8,128)}), (f32[128,2048]{1,0:T(8,128)}, f32[128,2048]{1,0:T(8,128)})) %all-reduce.130.cloned.1.call-update) | async-done | bytes 2097168 | tf_op jit(solution)/shard_map/psum | solution.py:298
  1329.8 52.1 %all-reduce.136.cloned.1.call-done = (bf16[128,2048]{1,0:T(8,128)(2,1)}, bf16[128,2048]{1,0:T(8,128)(2,1)}) async-done(((bf16[128,2048]{1,0:T(8,128)(2,1)}, bf16[128,2048]{1,0:T(8,128)(2,1)}), (bf16[128,2048]{1,0:T(8,128)(2,1)}, bf16[128,2048]{1,0:T(8,128)(2,1)})) %all-reduce.136.cloned.1.call-update) | async-done | bytes 1048592 | tf_op jit(solution)/shard_map/psum | solution.py:283
  1401.8 410.7 %while.180 = (s32[]{:T(128)}, f32[16,1024]{1,0:T(8,128)S(1)}, f32[2,64,1024]{2,1,0:T(8,128)}, f32[2,16,1024]{2,1,0:T(8,128)}, f32[2,64,16]{2,1,0:T(8,128)}, /*in...) while((s32[]{:T(128)}, f32[16,1024]{1,0:T(8,128)S(1)}, ...), condition=%wide.region_41.42_spmd, body=%wide.region_35.41_spmd.sunk | while | flops 32405508 | bytes 430863808 | solution.py:170
  1532.5 12.2 pad.1333
  1544.7 18.7 pad.1331
  1737.8 12.2 pad.1333
  1750.0 18.7 pad.1331
  1831.5 412.0 %while.181 = (s32[]{:T(128)}, f32[16,1024]{1,0:T(8,128)S(1)}, f32[2,64,1024]{2,1,0:T(8,128)}, f32[2,16,1024]{2,1,0:T(8,128)}, f32[2,64,16]{2,1,0:T(8,128)}, /*in...) while((s32[]{:T(128)}, f32[16,1024]{1,0:T(8,128)S(1)}, ...), condition=%wide.region_58.59_spmd, body=%wide.region_52.58_spmd.sunk | while | flops 32405508 | bytes 435320320 | solution.py:170
  1975.0 18.7 pad.1375
  2180.7 18.7 pad.1375
  2252.6 20.1 all-reduce.137
  2375.3 33.4 %maximum_add_fusion = f32[2,2048,2048]{2,1,0:T(8,128)} fusion(f32[1,2048,2048]{2,1,0:T(8,128)} %convolution_bitcast_fusion.2, f32[1,2048,2048]{2,1,0:T(8,128)} %convolution_bitcast_fusion.3, f32[1,2048,2048]{2,1,0:T(8,128)} %convolution_bitcast_fusion, f32[1,2048,2048]{2,1,0:T(8,128)} %convolution_bitcast_fusion.1), kind=kLoop, calls=%fused_computation.292 | loop fusion | flops 25165824 | bytes 100663296 | tf_op jit(solution)/shard_map/add | solution.py:295
  2415.5 25.6 all-reduce.110
  2444.4 66.2 %reduce-scatter.7.cloned.1.call-done = f32[1024,256]{1,0:T(8,128)} async-done(((f32[1024,2048]{1,0:T(8,128)}), f32[1024,256]{1,0:T(8,128)}) %reduce-scatter.7.cloned.1.call-update) | async-done | bytes 1048592 | tf_op jit(solution)/shard_map/reduce_scatter | solution.py:370
  2510.6 120.4 %reduce-scatter.11.cloned.1.call-done = f32[2048,256]{1,0:T(8,128)} async-done(((f32[2048,2048]{1,0:T(8,128)}), f32[2048,256]{1,0:T(8,128)}) %reduce-scatter.11.cloned.1.call-update) | async-done | bytes 2097168 | tf_op jit(solution)/shard_map/reduce_scatter | solution.py:372
  2631.0 120.6 %reduce-scatter.5.cloned.1.call-done = f32[2,256,1024]{2,1,0:T(8,128)} async-done(((f32[2,2048,1024]{2,1,0:T(8,128)}), f32[2,256,1024]{2,1,0:T(8,128)}) %reduce-scatter.5.cloned.1.call-update) | async-done | bytes 2097168 | tf_op jit(solution)/shard_map/reduce_scatter | solution.py:369
  2751.5 209.7 %reduce-scatter.9.cloned.1.call-done = f32[2,256,2048]{2,1,0:T(8,128)} async-done(((f32[2,2048,2048]{2,1,0:T(8,128)}), f32[2,256,2048]{2,1,0:T(8,128)}) %reduce-scatter.9.cloned.1.call-update) | async-done | bytes 4194320 | tf_op jit(solution)/shard_map/reduce_scatter | solution.py:371
  (1657 shorter events, 1717.4 us)
Async XLA Ops:
  7.2 74.6 %copy-start = (bf16[1024,160]{0,1:T(8,128)(2,1)S(1)}, bf16[1024,160]{0,1:T(8,128)(2,1)}, u32[]{:S(2)}) copy-start(bf16[1024,160]{0,1:T(8,128)(2,1)} %param.44) | copy-start | bytes 983044
  7.2 59.9 %all-gather.13.cloned.1.call-start = ((), (), s32[]{:S(2)}) async-start(), calls=%async_computation.4 | async-start | bytes 9437184 | tf_op jit(solution)/shard_map/all_gather | solution.py:214
  7.9 111.3 %all-reduce.134.cloned.1.call-start = ((), (), s32[]{:S(2)}) async-start(), calls=%async_computation.16 | async-start | bytes 327680 | tf_op jit(solution)/shard_map/psum | solution.py:252
  9.4 75.6 %copy-start.182 = (f32[2048]{0:T(1024)}, f32[2048]{0:T(1024)S(1)}, u32[]{:S(2)}) copy-start(f32[2048]{0:T(1024)S(1)} %convert_element_type.260) | copy-start | bytes 24580
  11.0 74.1 %copy-start.237 = (f32[128]{0:T(128)}, f32[128]{0:T(128)S(1)}, u32[]{:S(2)}) copy-start(f32[128]{0:T(128)S(1)} %get-tuple-element.2060) | copy-start | bytes 1540
  11.8 67.5 %copy-start.245 = (f32[1,1024]{1,0:T(1,128)}, f32[1,1024]{1,0:T(1,128)S(1)}, u32[]{:S(2)}) copy-start(f32[1,1024]{1,0:T(1,128)S(1)} %get-tuple-element.2050) | copy-start | bytes 12292
  70.2 7.7 collective-permute-start
  76.6 2.6 collective-permute-start.1
  83.5 874.2 %all-gather.15.cloned.1.call-start = ((), (), s32[]{:S(2)}) async-start(), calls=%async_computation.5 | async-start | bytes 4718592 | tf_op jit(solution)/shard_map/all_gather | solution.py:215
  84.3 967.5 %all-reduce.132.cloned.1.call-start = ((), (), s32[]{:S(2)}) async-start(), calls=%async_computation.15 | async-start | bytes 4194304 | tf_op jit(solution)/shard_map/psum | solution.py:276
  567.7 385.3 %copy-start.183 = (f32[2048]{0:T(1024)S(1)}, f32[2048]{0:T(1024)}, u32[]{:S(2)}) copy-start(f32[2048]{0:T(1024)} %copy-done.182) | copy-start | bytes 24580
  567.7 385.3 %copy-start.231 = (f32[1024]{0:T(1024)S(1)}, f32[1024]{0:T(1024)}, u32[]{:S(2)}) copy-start(f32[1024]{0:T(1024)} %convert_element_type.268) | copy-start | bytes 12292
  567.7 385.3 %copy-start.240 = (f32[128]{0:T(128)S(1)}, f32[128]{0:T(128)}, u32[]{:S(2)}) copy-start(f32[128]{0:T(128)} %copy-done.239) | copy-start | bytes 1540
  961.9 89.9 %copy-start.88 = (bf16[2,128,2048]{2,1,0:T(8,128)(2,1)S(1)}, bf16[2,128,2048]{2,1,0:T(8,128)(2,1)}, u32[]{:S(2)}) copy-start(bf16[2,128,2048]{2,1,0:T(8,128)(2,1)} %param.39) | copy-start | bytes 3145732
  963.6 178.8 %all-gather.17.cloned.1.call-start = ((), (), s32[]{:S(2)}) async-start(), calls=%async_computation.6 | async-start | bytes 18874368 | tf_op jit(solution)/shard_map/all_gather | solution.py:216
  964.2 235.9 %all-gather.19.cloned.1.call-start = ((), (), s32[]{:S(2)}) async-start(), calls=%async_computation.7 | async-start | bytes 9437184 | tf_op jit(solution)/shard_map/all_gather | solution.py:217
  964.8 362.3 %all-reduce.130.cloned.1.call-start = ((), (), s32[]{:S(2)}) async-start(), calls=%async_computation.14 | async-start | bytes 4194304 | tf_op jit(solution)/shard_map/psum | solution.py:298
  965.0 89.5 %copy-start.227 = (f32[2048]{0:T(1024)}, f32[2048]{0:T(1024)S(1)}, u32[]{:S(2)}) copy-start(f32[2048]{0:T(1024)S(1)} %convert_element_type.270) | copy-start | bytes 24580
  1054.5 93.7 %copy-start.148 = (bf16[128,2048]{1,0:T(8,128)(2,1)}, bf16[128,2048]{1,0:T(8,128)(2,1)S(1)}, u32[]{:S(2)}) copy-start(bf16[128,2048]{1,0:T(8,128)(2,1)S(1)} %get-tuple-element.2048) | copy-start | bytes 1572868
  1054.5 103.0 %copy-start.150 = (bf16[128,2048]{1,0:T(8,128)(2,1)}, bf16[128,2048]{1,0:T(8,128)(2,1)S(1)}, u32[]{:S(2)}) copy-start(bf16[128,2048]{1,0:T(8,128)(2,1)S(1)} %get-tuple-element.2049) | copy-start | bytes 1572868
  1239.9 142.1 %all-reduce.136.cloned.1.call-start = ((), (), s32[]{:S(2)}) async-start(), calls=%async_computation.17 | async-start | bytes 2097152 | tf_op jit(solution)/shard_map/psum | solution.py:283
  1248.2 78.9 %copy-start.228 = (f32[2048]{0:T(1024)S(1)}, f32[2048]{0:T(1024)}, u32[]{:S(2)}) copy-start(f32[2048]{0:T(1024)} %copy-done.227) | copy-start | bytes 24580
  1248.2 78.9 %copy-start.254 = (f32[128]{0:T(128)S(1)}, f32[128]{0:T(128)}, u32[]{:S(2)}) copy-start(f32[128]{0:T(128)} %copy-done.253) | copy-start | bytes 1540
  1248.2 78.9 %copy-start.256 = (f32[128]{0:T(128)S(1)}, f32[128]{0:T(128)}, u32[]{:S(2)}) copy-start(f32[128]{0:T(128)} %copy-done.255) | copy-start | bytes 1540
  1253.7 1159.5 %all-reduce.128.cloned.1.call-start = ((), (), s32[]{:S(2)}) async-start(), calls=%async_computation.13 | async-start | bytes 4194304 | tf_op jit(solution)/shard_map/psum | solution.py:358
  2274.4 11.3 collective-permute-start.2
  2277.4 5.8 collective-permute-start.3
  2288.3 156.1 %all-reduce.126.cloned.1.call-start = ((), (), s32[]{:S(2)}) async-start(), calls=%async_computation.12 | async-start | bytes 2490368 | tf_op jit(solution)/shard_map/psum | solution.py:374
  2297.3 213.2 %reduce-scatter.7.cloned.1.call-start = ((), (), s32[]{:S(2)}) async-start(), calls=%async_computation.9 | async-start | bytes 9437184 | tf_op jit(solution)/shard_map/reduce_scatter | solution.py:370
  2305.4 325.5 %reduce-scatter.11.cloned.1.call-start = ((), (), s32[]{:S(2)}) async-start(), calls=%async_computation.11 | async-start | bytes 18874368 | tf_op jit(solution)/shard_map/reduce_scatter | solution.py:372
  2319.1 432.4 %reduce-scatter.5.cloned.1.call-start = ((), (), s32[]{:S(2)}) async-start(), calls=%async_computation.8 | async-start | bytes 18874368 | tf_op jit(solution)/shard_map/reduce_scatter | solution.py:369
  2341.1 620.1 %reduce-scatter.9.cloned.1.call-start = ((), (), s32[]{:S(2)}) async-start(), calls=%async_computation.10 | async-start | bytes 37748736 | tf_op jit(solution)/shard_map/reduce_scatter | solution.py:371
  (398 other events, 2657.9 us)
Sparse Core Ops, SparseCore 0:
  9.9 57.0 all-gather.12
  83.7 35.5 all-reduce.133
  121.3 39.2 all-gather.14
  963.7 88.0 all-reduce.131
  1053.5 88.8 all-gather.16
  1144.1 55.9 all-gather.18
  1240.0 87.0 all-reduce.129
  1330.7 51.1 all-reduce.135
  2288.4 85.5 all-reduce.127
  2378.9 57.0 all-reduce.125
  2440.0 70.5 reduce-scatter.6
  2515.0 115.9 reduce-scatter.10
  2635.5 115.9 reduce-scatter.4
  2755.9 205.2 reduce-scatter.8
where the time goes:
time: 3020 us; the launch traced here: 2970 us
  local copies, waits for them, and re-layouts  1230 us (41%)
  waiting for transfers between devices  936 us (31%)
  other arithmetic  498 us (16%)
  matrix products  190 us (6%)
  blocking collectives  87.7 us (3%)
    pad x80, local copies, waits for them, and re-layouts, advance(): lax.associative_scan(affine, (decays, driven), axis=0)  534 us
    pad x80, local copies, waits for them, and re-layouts, retreat(): lax.associative_scan(affine, (coefs, driven), reverse=True, axis=0)  509 us
    reduce_scatter x1, waiting for transfers between devices, per_device(): lax.psum_scatter(grad_gateup, ('dp', 'ctx'), scatter_dimension=1, tiled=T...  210 us
    reduce_scatter x1, waiting for transfers between devices, per_device(): lax.psum_scatter(grad_inproj, ('dp', 'ctx'), scatter_dimension=1, tiled=T...  121 us
    reduce_scatter x1, waiting for transfers between devices, per_device(): lax.psum_scatter(grad_downproj, ('dp', 'ctx'), scatter_dimension=1, tiled...  120 us
    add x48, other arithmetic, retreat(): lax.associative_scan(affine, (coefs, driven), reverse=True, axis=0)  101 us
    all_gather x1, waiting for transfers between devices, gather_weights(): lax.all_gather(gateup, ('dp', 'ctx'), axis=1, tiled=True)  87.9 us
    psum x1, waiting for transfers between devices, per_device(): mixed = lax.psum(matmul(gated, out_full), 'tp')  86.7 us
  transfers between devices with their start and end apart: 18, of which 13 were waited for; matrix products, arithmetic and copies ran while one was open for 33% of the time, Pallas kernels for 0%

commit v1 on v0

v1 whole, which is shorter than its diff:
```python
import functools
import math

import jax
import jax.numpy as jnp
from jax import lax
from jax.experimental import pallas as pl
from jax.experimental.pallas import tpu as pltpu
from jax.sharding import PartitionSpec as P

EPSILON = 1e-05
LOG2E = math.log2(math.e)
LN2 = math.log(2.0)
SUB = 8
LANE = 128
PLANE = ("dp", "ctx")


def passed_along(value, axis, steps):
    count = lax.axis_size(axis)
    first, last = (max(0, -steps), min(count, count - steps))
    return lax.ppermute(value, axis, [(source, source + steps) for source in range(first, last)])


def matmul(left, right):
    return jnp.dot(left, right, preferred_element_type=jnp.float32)


def matmul_nt(left, right):
    return lax.dot_general(
        left, right, (((1,), (1,)), ((), ())), preferred_element_type=jnp.float32
    )


def matmul_tn(left, right):
    return lax.dot_general(
        left, right, (((0,), (0,)), ((), ())), preferred_element_type=jnp.float32
    )


def inverse_rms(values):
    return lax.rsqrt(jnp.mean(values * values, -1, keepdims=True) + EPSILON)


def silu_slope(values):
    logistic = jax.nn.sigmoid(values)
    return logistic * (1.0 + values * (1.0 - logistic))


def norm_back(grad_norm, values, scale, gain):
    scaled_grad = grad_norm * gain
    unit_rows = values * scale
    return scale * (scaled_grad - unit_rows * jnp.mean(scaled_grad * unit_rows, -1, keepdims=True))


def to_tiles(rows):
    count, width = rows.shape
    tiles = width // LANE
    return (
        rows.reshape(count // SUB, SUB, tiles, LANE)
        .transpose(0, 2, 1, 3)
        .reshape(count // SUB, tiles * SUB, LANE)
    )


def from_tiles(tiled):
    groups, rows, _ = tiled.shape
    tiles = rows // SUB
    return (
        tiled.reshape(groups, tiles, SUB, LANE)
        .transpose(0, 2, 1, 3)
        .reshape(groups * SUB, tiles * LANE)
    )


def token_row(ref, group, at, tiles):
    return ref[group, pl.ds(at, tiles, stride=SUB), :]


def ends_kernel(n_state, tiles, groups, reverse, step_ref, drive_ref, rows_ref, rate_ref, end_ref):
    base = pl.program_id(0) * groups * SUB * n_state
    rates = [rate_ref[n] for n in range(n_state)]

    def one(turn, states):
        group = groups - 1 - turn if reverse else turn
        order = range(SUB - 1, -1, -1) if reverse else range(SUB)
        states = list(states)
        for at in order:
            step = token_row(step_ref, group, at, tiles)
            drive = token_row(drive_ref, group, at, tiles)
            if not reverse:
                drive = drive * step
            for n in range(n_state):
                row = rows_ref[base + (group * SUB + at) * n_state + n]
                decay = jnp.exp2(step * rates[n])
                if reverse:
                    states[n] = decay * (states[n] + drive * row)
                else:
                    states[n] = decay * states[n] + drive * row
        return tuple(states)

    zero = jnp.zeros((tiles, LANE), jnp.float32)
    states = lax.fori_loop(0, groups, one, (zero,) * n_state)
    for n in range(n_state):
        end_ref[0, n] = states[n]


def scan_ends(step, drive, rows, rate, seqs, reverse):
    n_state, tiles, _ = rate.shape
    groups = step.shape[0] // seqs
    tile_spec = pl.BlockSpec((groups, tiles * SUB, LANE), lambda s: (s, 0, 0))
    return pl.pallas_call(
        functools.partial(ends_kernel, n_state, tiles, groups, reverse),
        grid=(seqs,),
        in_specs=[
            tile_spec,
            tile_spec,
            pl.BlockSpec(memory_space=pltpu.SMEM),
            pl.BlockSpec((n_state, tiles, LANE), lambda s: (0, 0, 0)),
        ],
        out_specs=pl.BlockSpec((1, n_state, tiles, LANE), lambda s: (s, 0, 0, 0)),
        out_shape=jax.ShapeDtypeStruct((seqs, n_state, tiles, LANE), jnp.float32),
        compiler_params=pltpu.CompilerParams(vmem_limit_bytes=32 * 2**20),
    )(step, drive, rows, rate)


def forward_kernel(
    n_state,
    tiles,
    groups,
    blocks,
    start_ref,
    step_ref,
    input_ref,
    brow_ref,
    crow_ref,
    rate_ref,
    prior_ref,
    mixed_ref,
    carried,
):
    base = (pl.program_id(0) * blocks + pl.program_id(1)) * groups * SUB * n_state

    @pl.when(pl.program_id(1) == 0)
    def _():
        carried[...] = start_ref[0]

    def one(group, states):
        states = list(states)
        for at in range(SUB):
            step = token_row(step_ref, group, at, tiles)
            drive = step * token_row(input_ref, group, at, tiles)
            mixed = [None] * 2
            for n in range(n_state):
                where = base + (group * SUB + at) * n_state + n
                prior_ref[group * SUB + at, n] = states[n]
                decay = jnp.exp2(step * rate_ref[n])
                states[n] = decay * states[n] + drive * brow_ref[where]
                term = states[n] * crow_ref[where]
                mixed[n % 2] = term if mixed[n % 2] is None else mixed[n % 2] + term
            mixed_ref[group, pl.ds(at, tiles, stride=SUB), :] = mixed[0] + mixed[1]
        return tuple(states)

    states = lax.fori_loop(0, groups, one, tuple(carried[n] for n in range(n_state)))
    for n in range(n_state):
        carried[n] = states[n]


def scan_forward(start, step, inputs, b_rows, c_rows, rate, seqs):
    n_state, tiles, _ = rate.shape
    all_groups = step.shape[0]
    groups = math.gcd(all_groups // seqs, 4)
    blocks = all_groups // seqs // groups
    tile_spec = pl.BlockSpec((groups, tiles * SUB, LANE), lambda s, b: (s * blocks + b, 0, 0))
    smem = pl.BlockSpec(memory_space=pltpu.SMEM)
    tokens = all_groups * SUB
    return pl.pallas_call(
        functools.partial(forward_kernel, n_state, tiles, groups, blocks),
        grid=(seqs, blocks),
        in_specs=[
            pl.BlockSpec((1, n_state, tiles, LANE), lambda s, b: (s, 0, 0, 0)),
            tile_spec,
            tile_spec,
            smem,
            smem,
            pl.BlockSpec((n_state, tiles, LANE), lambda s, b: (0, 0, 0)),
        ],
        out_specs=[
            pl.BlockSpec(
                (groups * SUB, n_state, tiles, LANE), lambda s, b: (s * blocks + b, 0, 0, 0)
            ),
            tile_spec,
        ],
        out_shape=[
            jax.ShapeDtypeStruct((tokens, n_state, tiles, LANE), jnp.float32),
            jax.ShapeDtypeStruct(step.shape, jnp.float32),
        ],
        scratch_shapes=[pltpu.VMEM((n_state, tiles, LANE), jnp.float32)],
        compiler_params=pltpu.CompilerParams(vmem_limit_bytes=32 * 2**20),
    )(start, step, inputs, b_rows, c_rows, rate)


def backward_kernel(
    n_state,
    tiles,
    groups,
    blocks,
    end_ref,
    prior_ref,
    step_ref,
    input_ref,
    ograd_ref,
    brow_ref,
    crow_ref,
    rate_ref,
    picks_ref,
    step_grad_ref,
    input_grad_ref,
    rate_grad_ref,
    part_ref,
    carried,
):
    block = blocks - 1 - pl.program_id(1)
    base = (pl.program_id(0) * blocks + block) * groups * SUB * n_state

    @pl.when(pl.program_id(1) == 0)
    def _():
        carried[...] = end_ref[0]

    @pl.when((pl.program_id(0) == 0) & (pl.program_id(1) == 0))
    def _():
        rate_grad_ref[...] = jnp.zeros_like(rate_grad_ref)

    def one(turn, grads):
        group = groups - 1 - turn
        grads = list(grads)
        for at in range(SUB - 1, -1, -1):
            step = token_row(step_ref, group, at, tiles)
            value = token_row(input_ref, group, at, tiles)
            ograd = token_row(ograd_ref, group, at, tiles)
            drive = step * value
            along_b = None
            along_rate = None
            brow_parts, crow_parts = [], []
            for n in range(n_state):
                where = base + (group * SUB + at) * n_state + n
                brow, crow = brow_ref[where], crow_ref[where]
                rate = rate_ref[n]
                decay = jnp.exp2(step * rate)
                grad = ograd * crow + grads[n]
                kept = decay * prior_ref[group * SUB + at, n]
                state = kept + drive * brow
                decay_term = grad * kept
                grads[n] = decay * grad
                rate_grad_ref[n] += decay_term * step
                by_rate, by_brow = decay_term * rate, grad * brow
                along_rate = by_rate if along_rate is None else along_rate + by_rate
                along_b = by_brow if along_b is None else along_b + by_brow
                brow_parts.append(grad * drive)
                crow_parts.append(ograd * state)
            step_grad_ref[group, pl.ds(at, tiles, stride=SUB), :] = (
                along_rate * LN2 + along_b * value
            )
            input_grad_ref[group, pl.ds(at, tiles, stride=SUB), :] = along_b * step
            parts = jnp.concatenate(brow_parts + crow_parts, 0).astype(jnp.bfloat16)
            part_ref[group * SUB + at] = jnp.dot(
                picks_ref[...], parts, preferred_element_type=jnp.float32
            )
        return tuple(grads)

    grads = lax.fori_loop(0, groups, one, tuple(carried[n] for n in range(n_state)))
    for n in range(n_state):
        carried[n] = grads[n]


def scan_backward(end_grad, prior, step, inputs, ograd, b_rows, c_rows, rate, seqs):
    n_state, tiles, _ = rate.shape
    all_groups = step.shape[0]
    groups = math.gcd(all_groups // seqs, 4)
    blocks = all_groups // seqs // groups

    def at(s, b):
        return s * blocks + blocks - 1 - b

    tile_spec = pl.BlockSpec((groups, tiles * SUB, LANE), lambda s, b: (at(s, b), 0, 0))
    smem = pl.BlockSpec(memory_space=pltpu.SMEM)
    tokens = all_groups * SUB
    picks = jnp.repeat(jnp.eye(2 * n_state, dtype=jnp.bfloat16), tiles, 1)
    return pl.pallas_call(
        functools.partial(backward_kernel, n_state, tiles, groups, blocks),
        grid=(seqs, blocks),
        in_specs=[
            pl.BlockSpec((1, n_state, tiles, LANE), lambda s, b: (s, 0, 0, 0)),
            pl.BlockSpec((groups * SUB, n_state, tiles, LANE), lambda s, b: (at(s, b), 0, 0, 0)),
            tile_spec,
            tile_spec,
            tile_spec,
            smem,
            smem,
            pl.BlockSpec((n_state, tiles, LANE), lambda s, b: (0, 0, 0)),
            pl.BlockSpec(picks.shape, lambda s, b: (0, 0)),
        ],
        out_specs=[
            tile_spec,
            tile_spec,
            pl.BlockSpec((n_state, tiles, LANE), lambda s, b: (0, 0, 0)),
            pl.BlockSpec((groups * SUB, 2 * n_state, LANE), lambda s, b: (at(s, b), 0, 0)),
        ],
        out_shape=[
            jax.ShapeDtypeStruct(step.shape, jnp.float32),
            jax.ShapeDtypeStruct(step.shape, jnp.float32),
            jax.ShapeDtypeStruct(rate.shape, jnp.float32),
            jax.ShapeDtypeStruct((tokens, 2 * n_state, LANE), jnp.float32),
        ],
        scratch_shapes=[pltpu.VMEM((n_state, tiles, LANE), jnp.float32)],
        compiler_params=pltpu.CompilerParams(vmem_limit_bytes=32 * 2**20),
    )(end_grad, prior, step, inputs, ograd, b_rows, c_rows, rate, picks)


def from_earlier(ends, decay, steps):
    count = lax.axis_size("ctx")
    if count == 1:
        return jnp.zeros_like(ends)
    if count == 2:
        return passed_along(ends, "ctx", steps)
    index = lax.axis_index("ctx")
    all_ends = lax.all_gather(ends, "ctx")
    all_decays = lax.all_gather(decay, "ctx")

    def one(turn, state):
        at = turn if steps > 0 else count - 1 - turn
        reached = at < index if steps > 0 else at > index
        return jnp.where(reached, all_decays[at] * state + all_ends[at], state)

    return lax.fori_loop(0, count, one, jnp.zeros_like(ends))


def gathered_rows(rows):
    return lax.all_gather(rows, PLANE, axis=0, tiled=True)


def swapped_columns(rows):
    return lax.all_to_all(rows, PLANE, split_axis=1, concat_axis=0, tiled=True)


def per_device(
    tokens,
    mixgain,
    inproj,
    convkern,
    convbias,
    selproj,
    stepproj,
    stepbias,
    decaylog,
    skipgain,
    outproj,
    ffngain,
    gateup,
    downproj,
    cotangent,
):
    seqs, span, width = tokens.shape
    rows = seqs * span
    taps, inner = convkern.shape
    rank = stepproj.shape[0]
    n_state = decaylog.shape[1]
    tiles = inner // LANE
    gain_mix = mixgain.astype(jnp.float32)
    gain_ffn = ffngain.astype(jnp.float32)
    kernel = convkern.astype(jnp.float32)
    kernel_bias = convbias.astype(jnp.float32)
    step_bias = stepbias.astype(jnp.float32)
    skip_weight = skipgain.astype(jnp.float32)
    decay_rate = -jnp.exp(jnp.transpose(decaylog.astype(jnp.float32)))
    rate = (decay_rate * LOG2E).reshape(n_state, tiles, LANE)

    in_full = lax.all_gather(inproj, PLANE, axis=1, tiled=True)
    out_full = lax.all_gather(outproj, PLANE, axis=1, tiled=True)
    gu_full = lax.all_gather(gateup, PLANE, axis=1, tiled=True)
    down_full = lax.all_gather(downproj, PLANE, axis=1, tiled=True)

    hidden_in = tokens.reshape(rows, width).astype(jnp.float32)
    scale_one = inverse_rms(hidden_in)
    normed_one = (hidden_in * scale_one * gain_mix).astype(jnp.bfloat16)
    normed_one_cols = swapped_columns(normed_one)
    conv_in = matmul(normed_one, in_full[0]).astype(jnp.bfloat16)
    gate_mix = matmul(normed_one, in_full[1])
    conv_seqs = conv_in.reshape(seqs, span, inner)
    rim_rows = passed_along(conv_seqs[:, span - (taps - 1) :], "ctx", 1)
    padded_in = jnp.concatenate([rim_rows, conv_seqs], 1).astype(jnp.float32)
    conv_out = kernel_bias[None, None]
    for offset in range(taps):
        conv_out = conv_out + kernel[offset][None, None] * padded_in[:, offset : offset + span]
    conv_out = conv_out.reshape(rows, inner)
    scan_in = jax.nn.silu(conv_out).astype(jnp.bfloat16)
    scan_float = scan_in.astype(jnp.float32)
    select_cols = lax.psum(matmul(scan_in, selproj), "tp")
    step_low = select_cols[:, :rank].astype(jnp.bfloat16)
    b_rows = select_cols[:, rank : rank + n_state].reshape(-1)
    c_rows = select_cols[:, rank + n_state :].reshape(-1)
    step_pre = matmul(step_low, stepproj) + step_bias[None]
    step_size = jax.nn.softplus(step_pre)
    span_decay = jnp.exp(
        decay_rate[None] * jnp.sum(step_size.reshape(seqs, span, inner), 1)[:, None]
    ).reshape(seqs, n_state, tiles, LANE)
    step_tiles, input_tiles = to_tiles(step_size), to_tiles(scan_float)
    ends = scan_ends(step_tiles, input_tiles, b_rows, rate, seqs, False)
    start = from_earlier(ends, span_decay, 1)
    prior, mixed_tiles = scan_forward(start, step_tiles, input_tiles, b_rows, c_rows, rate, seqs)
    mixer_core = from_tiles(mixed_tiles) + skip_weight[None] * scan_float
    gate_sig = jax.nn.silu(gate_mix)
    gated = (mixer_core * gate_sig).astype(jnp.bfloat16)
    mixed = lax.psum(matmul(gated, out_full).astype(jnp.bfloat16), "tp").astype(jnp.float32)
    middle = hidden_in + mixed
    scale_two = inverse_rms(middle)
    normed_two = (middle * scale_two * gain_ffn).astype(jnp.bfloat16)
    normed_two_cols = swapped_columns(normed_two)
    gate_ffn = matmul(normed_two, gu_full[0])
    up_ffn = matmul(normed_two, gu_full[1])
    activated = (jax.nn.silu(gate_ffn) * up_ffn).astype(jnp.bfloat16)
    ct_low = cotangent.reshape(rows, width)
    ct_cols = swapped_columns(ct_low)
    act_grad = matmul_nt(ct_low, down_full)
    gate_grad = (act_grad * up_ffn * silu_slope(gate_ffn)).astype(jnp.bfloat16)
    up_grad = (act_grad * jax.nn.silu(gate_ffn)).astype(jnp.bfloat16)
    normed_two_part = matmul_nt(gate_grad, gu_full[0]) + matmul_nt(up_grad, gu_full[1])
    normed_two_grad = lax.psum(normed_two_part.astype(jnp.bfloat16), "tp").astype(jnp.float32)
    activated_all = gathered_rows(activated)
    gate_grad_all = gathered_rows(gate_grad)
    up_grad_all = gathered_rows(up_grad)
    gated_all = gathered_rows(gated)
    ffn_out = lax.psum(matmul(activated, down_full).astype(jnp.bfloat16), "tp")
    layer_out = (middle + ffn_out.astype(jnp.float32)).astype(jnp.bfloat16)
    grad_downproj = matmul_tn(activated_all, ct_cols)
    grad_gateup = jnp.stack(
        [matmul_tn(normed_two_cols, gate_grad_all), matmul_tn(normed_two_cols, up_grad_all)]
    )
    grad_ffngain = jnp.sum(normed_two_grad * middle * scale_two, 0)
    middle_grad = ct_low.astype(jnp.float32) + norm_back(
        normed_two_grad, middle, scale_two, gain_ffn
    )
    middle_low = middle_grad.astype(jnp.bfloat16)
    middle_cols = swapped_columns(middle_low)
    grad_outproj = matmul_tn(gated_all, middle_cols)
    gated_grad = matmul_nt(middle_low, out_full)
    core_grad = gated_grad * gate_sig
    gate_mix_grad = (gated_grad * mixer_core * silu_slope(gate_mix)).astype(jnp.bfloat16)
    gate_mix_grad_all = gathered_rows(gate_mix_grad)
    grad_skipgain = jnp.sum(core_grad * scan_float, 0)
    ograd_tiles = to_tiles(core_grad)
    back_ends = scan_ends(step_tiles, ograd_tiles, c_rows, rate, seqs, True)
    end_grad = from_earlier(back_ends, span_decay, -1)
    step_grad_tiles, input_grad_tiles, rate_grad, parts = scan_backward(
        end_grad, prior, step_tiles, input_tiles, ograd_tiles, b_rows, c_rows, rate, seqs
    )
    grad_decaylog = rate_grad.reshape(n_state, inner) * decay_rate
    pre_grad = from_tiles(step_grad_tiles) * jax.nn.sigmoid(step_pre)
    grad_stepbias = jnp.sum(pre_grad, 0)
    pre_low = pre_grad.astype(jnp.bfloat16)
    grad_stepproj = matmul_tn(step_low, pre_low)
    select_grad = lax.psum(
        jnp.concatenate([matmul_nt(pre_low, stepproj), jnp.sum(parts, -1)], 1), "tp"
    )
    select_low = select_grad.astype(jnp.bfloat16)
    grad_selproj = matmul_tn(scan_in, select_low)
    scan_in_grad = (
        core_grad * skip_weight[None] + from_tiles(input_grad_tiles) + matmul_nt(select_low, selproj)
    )
    conv_grad = scan_in_grad * silu_slope(conv_out)
    grad_convbias = jnp.sum(conv_grad, 0)
    conv_grad_seqs = conv_grad.reshape(seqs, span, inner)
    padded_grad = jnp.zeros(padded_in.shape, jnp.float32)
    kernel_rows = []
    for offset in range(taps):
        kernel_rows.append(jnp.sum(conv_grad_seqs * padded_in[:, offset : offset + span], (0, 1)))
        padded_grad = padded_grad + jnp.pad(
            kernel[offset][None, None] * conv_grad_seqs,
            ((0, 0), (offset, taps - 1 - offset), (0, 0)),
        )
    grad_convkern = jnp.stack(kernel_rows)
    returned = passed_along(padded_grad[:, : taps - 1], "ctx", -1)
    conv_in_grad = (
        (padded_grad[:, taps - 1 :] + jnp.pad(returned, ((0, 0), (span - taps + 1, 0), (0, 0))))
        .astype(jnp.bfloat16)
        .reshape(rows, inner)
    )
    conv_in_grad_all = gathered_rows(conv_in_grad)
    normed_one_part = matmul_nt(conv_in_grad, in_full[0]) + matmul_nt(gate_mix_grad, in_full[1])
    normed_one_grad = lax.psum(normed_one_part.astype(jnp.bfloat16), "tp").astype(jnp.float32)
    grad_inproj = jnp.stack(
        [
            matmul_tn(normed_one_cols, conv_in_grad_all),
            matmul_tn(normed_one_cols, gate_mix_grad_all),
        ]
    )
    grad_mixgain = jnp.sum(normed_one_grad * hidden_in * scale_one, 0)
    tokens_grad = (middle_grad + norm_back(normed_one_grad, hidden_in, scale_one, gain_mix)).astype(
        jnp.bfloat16
    )
    smalls = lax.psum(
        (
            grad_mixgain,
            grad_convkern,
            grad_convbias,
            grad_selproj,
            grad_stepproj,
            grad_stepbias,
            grad_decaylog,
            grad_skipgain,
            grad_ffngain,
        ),
        PLANE,
    )
    return (
        layer_out.reshape(tokens.shape),
        tokens_grad.reshape(tokens.shape),
        smalls[0],
        grad_inproj,
        smalls[1],
        smalls[2],
        smalls[3],
        smalls[4],
        smalls[5],
        jnp.transpose(smalls[6]),
        smalls[7],
        grad_outproj,
        smalls[8],
        grad_gateup,
        grad_downproj,
    )


def solution(mesh):
    in_specs = (
        P("dp", "ctx", None),
        P(),
        P(None, ("dp", "ctx"), "tp"),
        P(None, "tp"),
        P("tp"),
        P("tp", None),
        P(None, "tp"),
        P("tp"),
        P("tp", None),
        P("tp"),
        P("tp", ("dp", "ctx")),
        P(),
        P(None, ("dp", "ctx"), "tp"),
        P("tp", ("dp", "ctx")),
        P("dp", "ctx", None),
    )
    out_specs = (
        P("dp", "ctx", None),
        P("dp", "ctx", None),
        P(),
        P(None, ("dp", "ctx"), "tp"),
        P(None, "tp"),
        P("tp"),
        P("tp", None),
        P(None, "tp"),
        P("tp"),
        P("tp", None),
        P("tp"),
        P("tp", ("dp", "ctx")),
        P(),
        P(None, ("dp", "ctx"), "tp"),
        P("tp", ("dp", "ctx")),
    )
    return jax.shard_map(
        per_device, mesh=mesh, in_specs=in_specs, out_specs=out_specs, check_vma=False
    )
```

time: 3020 us -> 946 us (0.31); the launches traced: 2970 us -> 939 us
  local copies, waits for them, and re-layouts: 1230 us -> 29.2 us
  other arithmetic: 498 us -> 34.8 us
  waiting for transfers between devices: 936 us -> 638 us
  matrix products: 190 us -> 114 us
  blocking collectives: 87.7 us -> 46 us
  Pallas kernels: 0 us -> 35.2 us
    pad x160 -> x0, local copies, waits for them, and re-layouts: 1040 us -> none  [the longest x80 534 us: advance(): lax.associative_scan(affine, (decays, driven), axis=0)]
    reduce_scatter x4 -> x0, waiting for transfers between devices: 517 us -> none  [the longest x1 210 us: per_device(): lax.psum_scatter(grad_gateup, ('dp', 'ctx'), scatter_dimension=1, tiled=T...]
    add x145 -> x2, other arithmetic: 265 us -> 1.06 us  [the longest x1 0.57 us: per_device(): padded_grad + jnp.pad(kernel[offset][None, None] * conv_grad_seqs, ((0, 0...]
    all_gather x4 -> x10, waiting for transfers between devices: 184 us -> 383 us  [the longest x6 192 us: gathered_rows(): return lax.all_gather(rows, PLANE, axis=0, tiled=True)]
    slice x91 -> x5, local copies, waits for them, and re-layouts: 83.3 us -> 0.97 us  [the longest x2 0.84 us: per_device(): c_rows = select_cols[:, rank + n_state:].reshape(-1)]
    concatenate x80 -> x1, other arithmetic: 68.3 us -> 0.68 us  [per_device(): jnp.concatenate([matmul_nt(pre_low, stepproj), jnp.sum(parts, -1)], 1)]
    mul x48 -> x1, other arithmetic: 65 us -> 0.55 us  [per_device(): kernel[offset][None, None] * conv_grad_seqs]
    psum x4 -> x3, waiting for transfers between devices: 201 us -> 138 us  [the longest x1 49 us: per_device(): lax.psum(matmul(gated, out_full).astype(jnp.bfloat16), 'tp')]
  transfers between devices with their start and end apart: 18 -> 23, of which waited for: 13 -> 19; matrix products, arithmetic and copies ran while one was open for 33% -> 13% of each run, Pallas kernels for 0% -> 4%
where the time goes in v1:
time: 946 us; the launch traced here: 939 us
  waiting for transfers between devices  638 us (67%)
  matrix products  114 us (12%)
  blocking collectives  46 us (5%)
  Pallas kernels  35.2 us (4%)
  other arithmetic  34.8 us (4%)
  local copies, waits for them, and re-layouts  29.2 us (3%)
  starting transfers between devices  27.3 us (3%)
  between operations  15.4 us (2%)
    all_gather x6, waiting for transfers between devices, gathered_rows(): return lax.all_gather(rows, PLANE, axis=0, tiled=True)  192 us
    all_gather x1, waiting for transfers between devices, per_device(): gu_full = lax.all_gather(gateup, PLANE, axis=1, tiled=True)  87.2 us
    all_gather x1, waiting for transfers between devices, per_device(): in_full = lax.all_gather(inproj, PLANE, axis=1, tiled=True)  55.9 us
    psum x1, waiting for transfers between devices, per_device(): lax.psum((grad_mixgain, grad_convkern, grad_convbias, grad_selproj, grad_...  54.9 us
    psum x1, waiting for transfers between devices, per_device(): lax.psum(matmul(gated, out_full).astype(jnp.bfloat16), 'tp')  49 us
    psum x1, waiting for transfers between devices, per_device(): ffn_out = lax.psum(matmul(activated, down_full).astype(jnp.bfloat16), 'tp')  47.7 us
    all_gather x1, waiting for transfers between devices, per_device(): down_full = lax.all_gather(downproj, PLANE, axis=1, tiled=True)  42.5 us
    psum x1, waiting for transfers between devices, per_device(): lax.psum(normed_two_part.astype(jnp.bfloat16), 'tp').astype(jnp.float32)  41.6 us
  transfers between devices with their start and end apart: 23, of which 19 were waited for; matrix products, arithmetic and copies ran while one was open for 13% of the time, Pallas kernels for 4%

profile of v1, /device:TPU:0, one launch (start us, length us, event | category | flops | bytes accessed | tf_op | source)
XLA Modules:
  0.0 939.4 jit_solution(10051522117957779185)
XLA Ops:
  11.1 55.9 %all-gather.11.cloned.1.call-done = bf16[2,2048,1024]{2,1,0:T(8,128)(2,1)} async-done(((bf16[2,256,1024]{2,1,0:T(8,128)(2,1)}), bf16[2,2048,1024]{2,1,0:T(8,128)(2,1)}) %all-gather.11.cloned.1.call-update) | async-done | bytes 8388624 | tf_op jit(solution)/shard_map/all_gather | solution.py:378
  79.1 34.5 %all-reduce.15.cloned.1.call-done = f32[256,160]{0,1:T(8,128)} async-done(((f32[256,160]{0,1:T(8,128)}), f32[256,160]{0,1:T(8,128)}) %all-reduce.15.cloned.1.call-update) | async-done | bytes 163856 | tf_op jit(solution)/shard_map/psum | solution.py:398
  124.8 5.0 collective-permute-done.1.start_ref
  129.7 6.8 shard_map.263
  136.5 6.2 copy-done.1
  148.4 5.4 all-gather.13.cloned.1.call-done
  161.4 49.0 %all-reduce.17.cloned.1.call-done = bf16[256,2048]{1,0:T(8,128)(2,1)} async-done(((bf16[256,2048]{1,0:T(8,128)(2,1)}), bf16[256,2048]{1,0:T(8,128)(2,1)}) %all-reduce.17.cloned.1.call-update) | async-done | bytes 1048592 | tf_op jit(solution)/shard_map/psum | solution.py:414
  214.2 87.2 %all-gather.15.cloned.1.call-done = bf16[2,2048,2048]{2,1,0:T(8,128)(2,1)} async-done(((bf16[2,256,2048]{2,1,0:T(8,128)(2,1)}), bf16[2,2048,2048]{2,1,0:T(8,128)(2,1)}) %all-gather.15.cloned.1.call-update) | async-done | bytes 16777232 | tf_op jit(solution)/shard_map/all_gather | solution.py:380
  301.4 7.4 fusion.1
  308.9 7.8 fusion.3
  316.7 42.5 %all-gather.17.cloned.1.call-done = bf16[2048,2048]{1,0:T(8,128)(2,1)} async-done(((bf16[2048,256]{1,0:T(8,128)(2,1)}), bf16[2048,2048]{1,0:T(8,128)(2,1)}) %all-gather.17.cloned.1.call-update) | async-done | bytes 8388624 | tf_op jit(solution)/shard_map/all_gather | solution.py:381
  359.2 9.5 %multiply_convert_fusion = (bf16[256,2048]{1,0:T(8,128)(2,1)}, bf16[256,2048]{1,0:T(8,128)(2,1)}, bf16[256,2048]{1,0:T(8,128)(2,1)}) fusion(f32[256,2048]{1,0:T(8,128)} %fusion.1, f32[256,2048]{1,0:T(8,128)} %fusion.3, bf16[256,2048]{1,0:T(8,128)(2,1)} %bitcast.254, bf16[2048,2048]{1,0:T(8,128)(2,1)} %all-gather.17.cloned.1.call-done), kind=kOutput, calls=%fused_computation.53 | convolution fusion | flops 2155347968 | bytes 16777216 | tf_op jit(solution)/shard_map/dot_general | solution.py:30
  368.7 7.4 fusion
  376.1 7.6 fusion.10
  386.9 7.2 convolution_convert_fusion.1
  394.1 41.6 %all-reduce.19.cloned.1.call-done = bf16[256,2048]{1,0:T(8,128)(2,1)} async-done(((bf16[256,2048]{1,0:T(8,128)(2,1)}), bf16[256,2048]{1,0:T(8,128)(2,1)}) %all-reduce.19.cloned.1.call-update) | async-done | bytes 1048592 | tf_op jit(solution)/shard_map/psum | solution.py:428
  440.7 5.3 fusion.36
  446.0 5.1 shard_map.264
  458.7 18.9 %shard_map.265 = (f32[32,64,128]{2,1,0:T(8,128)S(1)}, f32[32,64,128]{2,1,0:T(8,128)S(1)}, f32[16,8,128]{2,1,0:T(8,128)S(1)}, f32[256,32,128]{2,1,0:T(8,128)S(1)}) custom-call(f32[2,16,8,128]{3,2,1,0:T(8,128)} %collective-permute-done.2.end_ref, f32[256,16,8,128]{3,2,1,0:T(8,128)} %copy-done.1, f32[32,64,128]{2,1,0:T(8,128)S(1)} %fusion.37.step_ref, ...), custom_call_target="tpu_custom_call" | custom-call | tf_op jit(solution)/shard_map/pallas_call | solution.py:289
  490.1 19.8 %all-reduce.24 = bf16[256,160]{0,1:T(8,128)(2,1)S(1)} all-reduce(f32[256,160]{0,1:T(8,128)} %pad_maximum_fusion.2), channel_id=1, replica_groups=mesh['dp'=4,'ctx'=2,'tp'=4] {'tp'}, use_global_device_ids=true, to_apply=%region_8.9 | all-reduce | flops 40960 | bytes 245760 | tf_op jit(solution)/shard_map/psum | solution.py:462
  519.0 5.3 fusion.11
  543.1 9.2 all-to-all-done.1
  561.4 47.7 %all-reduce.23.cloned.1.call-done = (bf16[256,2048]{1,0:T(8,128)(2,1)}, bf16[256,2048]{1,0:T(8,128)(2,1)}) async-done(((bf16[256,2048]{1,0:T(8,128)(2,1)}, bf16[256,2048]{1,0:T(8,128)(2,1)}), (bf16[256,2048]{1,0:T(8,128)(2,1)}, bf16[256,2048]{1,0:T(8,128)(2,1)})) %all-reduce.23.cloned.1.call-update) | async-done | bytes 2097168 | tf_op jit(solution)/shard_map/psum | solution.py:433
  611.2 26.3 %all-reduce.5 = (f32[2048]{0:T(1024)}, f32[4,1024]{1,0:T(4,128)}, f32[1024]{0:T(1024)}, f32[1024]{0:T(1024)}, f32[1024]{0:T(1024)}, /*index=5*/f32[2048]{0:T(1024)}) all-reduce(f32[2048]{0:T(1024)S(1)} %get-tuple-element.33, f32[4,1024]{1,0:T(4,128)S(1)} %pad_maximum_fusion.3, ...), channel_id=1, replica_groups=mesh['dp'=4,'ctx'=2,'tp'=4] {'dp','ctx'}, use_global_device_ids=true, to_apply=%region_12.13 | all-reduce | flops 11264 | bytes 90112 | tf_op jit(solution)/shard_map/psum | solution.py:501
  650.7 34.8 %all-gather.19.cloned.1.call-done = bf16[2048,1024]{1,0:T(8,128)(2,1)} async-done(((bf16[256,1024]{1,0:T(8,128)(2,1)}), bf16[2048,1024]{1,0:T(8,128)(2,1)}) %all-gather.19.cloned.1.call-update) | async-done | bytes 4194320 | tf_op jit(solution)/shard_map/all_gather | solution.py:339
  695.4 57.5 %all-gather.27.cloned.1.call-done = bf16[2048,2048]{1,0:T(8,128)(2,1)} async-done(((bf16[256,2048]{1,0:T(8,128)(2,1)}), bf16[2048,2048]{1,0:T(8,128)(2,1)}) %all-gather.27.cloned.1.call-update) | async-done | bytes 8388624 | tf_op jit(solution)/shard_map/all_gather | solution.py:339
  753.0 5.7 convolution_bitcast_fusion
  758.7 50.6 %all-gather.25.cloned.1.call-done = bf16[2048,2048]{1,0:T(8,128)(2,1)} async-done(((bf16[256,2048]{1,0:T(8,128)(2,1)}), bf16[2048,2048]{1,0:T(8,128)(2,1)}) %all-gather.25.cloned.1.call-update) | async-done | bytes 8388624 | tf_op jit(solution)/shard_map/all_gather | solution.py:339
  809.3 5.7 convolution_bitcast_fusion.1
  817.3 48.1 %all-gather.29.cloned.1.call-done = bf16[2048,2048]{1,0:T(8,128)(2,1)} async-done(((bf16[256,2048]{1,0:T(8,128)(2,1)}), bf16[2048,2048]{1,0:T(8,128)(2,1)}) %all-gather.29.cloned.1.call-update) | async-done | bytes 8388624 | tf_op jit(solution)/shard_map/all_gather | solution.py:339
  865.4 7.5 fusion.70
  872.9 54.9 %all-reduce.21.cloned.1.call-done = (f32[1024,160]{0,1:T(8,128)}, f32[128,1024]{1,0:T(8,128)}, f32[1024,16]{0,1:T(8,128)}) async-done(((f32[1024,160]{0,1:T(8,128)}, f32[128,1024]{1,0:T(8,128)}, f32[1024,16]{0,1:T(8,128)}), (f32[1024,160]{0,1:T(8,128)}, f32[128,1024]{1,0:T(8,128)}, f32[1024,16]{0,1:T(8,128)})) %all-reduce.21.cloned.1.call-update) | async-done | bytes 1245200 | tf_op jit(solution)/shard_map/psum | solution.py:501
  (278 shorter events, 140.4 us)
Async XLA Ops:
  7.2 69.7 %copy-start = (bf16[1024,160]{0,1:T(8,128)(2,1)S(1)}, bf16[1024,160]{0,1:T(8,128)(2,1)}, u32[]{:S(2)}) copy-start(bf16[1024,160]{0,1:T(8,128)(2,1)} %param.20) | copy-start | bytes 983044
  7.2 59.9 %all-gather.11.cloned.1.call-start = ((), (), s32[]{:S(2)}) async-start(), calls=%async_computation.4 | async-start | bytes 9437184 | tf_op jit(solution)/shard_map/all_gather | solution.py:378
  7.9 105.6 %all-reduce.15.cloned.1.call-start = ((), (), s32[]{:S(2)}) async-start(), calls=%async_computation.5 | async-start | bytes 327680 | tf_op jit(solution)/shard_map/psum | solution.py:398
  11.1 59.4 %copy-start.43 = (bf16[2,128,2048]{2,1,0:T(8,128)(2,1)}, bf16[2,128,2048]{2,1,0:T(8,128)(2,1)S(1)}, u32[]{:S(2)}) copy-start(bf16[2,128,2048]{2,1,0:T(8,128)(2,1)S(1)} %fusion.32) | copy-start | bytes 3145732
  70.6 4.8 collective-permute-start
  76.9 65.9 %copy-start.33 = (bf16[256,1024]{1,0:T(8,128)(2,1)}, bf16[256,1024]{1,0:T(8,128)(2,1)S(1)}, u32[]{:S(2)}) copy-start(bf16[256,1024]{1,0:T(8,128)(2,1)S(1)} %fusion.44) | copy-start | bytes 1572868
  77.9 76.0 %all-gather.13.cloned.1.call-start = ((), (), s32[]{:S(2)}) async-start(), calls=%async_computation.6 | async-start | bytes 4718592 | tf_op jit(solution)/shard_map/all_gather | solution.py:379
  78.6 131.8 %all-reduce.17.cloned.1.call-start = ((), (), s32[]{:S(2)}) async-start(), calls=%async_computation.7 | async-start | bytes 2097152 | tf_op jit(solution)/shard_map/psum | solution.py:414
  121.1 8.6 collective-permute-start.1
  158.5 143.0 %all-gather.15.cloned.1.call-start = ((), (), s32[]{:S(2)}) async-start(), calls=%async_computation.8 | async-start | bytes 18874368 | tf_op jit(solution)/shard_map/all_gather | solution.py:380
  159.0 200.1 %all-gather.17.cloned.1.call-start = ((), (), s32[]{:S(2)}) async-start(), calls=%async_computation.9 | async-start | bytes 9437184 | tf_op jit(solution)/shard_map/all_gather | solution.py:381
  159.6 276.1 %all-reduce.19.cloned.1.call-start = ((), (), s32[]{:S(2)}) async-start(), calls=%async_computation.10 | async-start | bytes 2097152 | tf_op jit(solution)/shard_map/psum | solution.py:428
  383.7 172.8 %all-gather.23.cloned.1.call-start = ((), (), s32[]{:S(2)}) async-start(), calls=%async_computation.13 | async-start | bytes 4718592 | tf_op jit(solution)/shard_map/all_gather | solution.py:339
  384.5 224.6 %all-reduce.23.cloned.1.call-start = ((), (), s32[]{:S(2)}) async-start(), calls=%async_computation.18 | async-start | bytes 4194304 | tf_op jit(solution)/shard_map/psum | solution.py:433
  451.1 7.6 collective-permute-start.2
  513.1 5.8 collective-permute-start.3
  524.4 122.6 %all-gather.21.cloned.1.call-start = ((), (), s32[]{:S(2)}) async-start(), calls=%async_computation.12 | async-start | bytes 4718592 | tf_op jit(solution)/shard_map/all_gather | solution.py:339
  525.0 160.6 %all-gather.19.cloned.1.call-start = ((), (), s32[]{:S(2)}) async-start(), calls=%async_computation.11 | async-start | bytes 4718592 | tf_op jit(solution)/shard_map/all_gather | solution.py:339
  525.7 227.3 %all-gather.27.cloned.1.call-start = ((), (), s32[]{:S(2)}) async-start(), calls=%async_computation.15 | async-start | bytes 9437184 | tf_op jit(solution)/shard_map/all_gather | solution.py:339
  526.3 283.0 %all-gather.25.cloned.1.call-start = ((), (), s32[]{:S(2)}) async-start(), calls=%async_computation.14 | async-start | bytes 9437184 | tf_op jit(solution)/shard_map/all_gather | solution.py:339
  527.1 338.4 %all-gather.29.cloned.1.call-start = ((), (), s32[]{:S(2)}) async-start(), calls=%async_computation.16 | async-start | bytes 9437184 | tf_op jit(solution)/shard_map/all_gather | solution.py:339
  533.0 19.2 %all-to-all-start.1 = ((bf16[256,8,256]{2,0,1:T(8,128)(2,1)}), bf16[256,8,256]{2,0,1:T(8,128)(2,1)}, u32[]{:S(2)}, u32[]{:S(2)}) async-start(bf16[256,8,256]{2,0,1:T(8,128)(2,1)} %bitcast.259), calls=%async_computation.1 | async-start | bytes 2097152 | tf_op jit(solution)/shard_map/all_to_all | solution.py:343
  537.3 390.5 %all-reduce.21.cloned.1.call-start = ((), (), s32[]{:S(2)}) async-start(), calls=%async_computation.17 | async-start | bytes 2490368 | tf_op jit(solution)/shard_map/psum | solution.py:501
  552.2 90.2 %all-to-all-start = ((bf16[256,8,256]{2,0,1:T(8,128)(2,1)}), bf16[256,8,256]{2,0,1:T(8,128)(2,1)}, u32[]{:S(2)}, u32[]{:S(2)}) async-start(bf16[256,8,256]{2,0,1:T(8,128)(2,1)} %copy.46), calls=%async_computation | async-start | bytes 2097152 | tf_op jit(solution)/shard_map/all_to_all | solution.py:343
  556.5 54.7 %copy-start.75 = (f32[1024]{0:T(1024)S(1)}, f32[1024]{0:T(1024)}, u32[]{:S(2)}) copy-start(f32[1024]{0:T(1024)} %get-tuple-element.46) | copy-start | bytes 12292
  561.3 76.2 %copy-start.22 = (bf16[256,2048]{1,0:T(8,128)(2,1)S(1)}, bf16[256,2048]{1,0:T(8,128)(2,1)}, u32[]{:S(2)}) copy-start(bf16[256,2048]{1,0:T(8,128)(2,1)} %all-reduce.17.cloned.1.call-done) | copy-start | bytes 3145732
  561.3 76.1 %copy-start.31 = (bf16[2,128,2048]{2,1,0:T(8,128)(2,1)S(1)}, bf16[2,128,2048]{2,1,0:T(8,128)(2,1)}, u32[]{:S(2)}) copy-start(bf16[2,128,2048]{2,1,0:T(8,128)(2,1)} %param.29) | copy-start | bytes 3145732
  561.4 76.1 %copy-start.48 = (f32[2048]{0:T(1024)S(1)}, f32[2048]{0:T(1024)}, u32[]{:S(2)}) copy-start(f32[2048]{0:T(1024)} %convert_element_type.160) | copy-start | bytes 24580
  561.4 76.1 %copy-start.66 = (f32[256]{0:T(256)S(1)}, f32[256]{0:T(256)}, u32[]{:S(2)}) copy-start(f32[256]{0:T(256)} %copy-done.64) | copy-start | bytes 3076
  561.4 76.1 %copy-start.74 = (f32[256]{0:T(256)S(1)}, f32[256]{0:T(256)}, u32[]{:S(2)}) copy-start(f32[256]{0:T(256)} %copy-done.73) | copy-start | bytes 3076
  642.4 48.5 %all-to-all-start.2 = ((bf16[256,8,256]{2,0,1:T(8,128)(2,1)}), bf16[256,8,256]{2,0,1:T(8,128)(2,1)S(1)}, u32[]{:S(2)}, u32[]{:S(2)}) async-start(bf16[256,8,256]{2,0,1:T(8,128)(2,1)} %bitcast.258), calls=%async_computation.2 | async-start | bytes 2097152 | tf_op jit(solution)/shard_map/all_to_all | solution.py:343
  690.9 126.4 %all-to-all-start.3 = ((bf16[256,8,256]{2,0,1:T(8,128)(2,1)}), bf16[256,8,256]{2,0,1:T(8,128)(2,1)}, u32[]{:S(2)}, u32[]{:S(2)}) async-start(bf16[256,8,256]{2,0,1:T(8,128)(2,1)} %copy.49), calls=%async_computation.3 | async-start | bytes 2097152 | tf_op jit(solution)/shard_map/all_to_all | solution.py:343
  (71 other events, 584.2 us)
Sparse Core Ops, SparseCore 0:
  9.9 57.0 all-gather.10
  78.0 35.4 all-reduce.14
  115.6 38.2 all-gather.12
  158.6 51.7 all-reduce.16
  212.2 89.2 all-gather.14
  303.2 55.9 all-gather.16
  383.8 51.8 all-reduce.18
  438.3 36.1 all-gather.22
  524.5 84.4 all-reduce.22
  610.8 36.1 all-gather.20
  648.8 36.7 all-gather.18
  687.3 65.6 all-gather.26
  754.9 54.3 all-gather.24
  811.0 54.3 all-gather.28
  869.9 57.8 all-reduce.20

commit v2 on v1

--- a/solution.py
+++ b/solution.py
@@ -343,6 +343,143 @@
     return lax.all_to_all(rows, PLANE, split_axis=1, concat_axis=0, tiled=True)
 
 
+def place_in(axes):
+    index = 0
+    for axis in axes:
+        index = index * lax.axis_size(axis) + lax.axis_index(axis)
+    return index
+
+
+def device_at(axes, index):
+    where = {}
+    for axis in reversed(axes):
+        size = lax.axis_size(axis)
+        where[axis] = lax.rem(index, size)
+        index = lax.div(index, size)
+    return where
+
+
+def exchange_kernel(axes, count, counts, kinds, middle, *refs):
+    n_parts, n_whole, n_own = counts
+    parts, refs = refs[:n_parts], refs[n_parts:]
+    whole, refs = refs[:n_whole], refs[n_whole:]
+    own, refs = refs[:n_own], refs[n_own:]
+    outs, refs = refs[: len(kinds)], refs[len(kinds) :]
+    slots, refs = refs[:n_parts], refs[n_parts:]
+    send_sem, recv_sem = refs
+    me = place_in(axes)
+    peers = [lax.rem(me + hop, count) for hop in range(1, count)]
+
+    barrier = pltpu.get_barrier_semaphore()
+    for peer in peers:
+        pl.semaphore_signal(
+            barrier,
+            inc=1,
+            device_id=device_at(axes, peer),
+            device_id_type=pl.DeviceIdType.MESH,
+        )
+    pl.semaphore_wait(barrier, count - 1)
+
+    def rows_of(ref, index):
+        rows = ref.shape[0] // count
+        return ref.at[pl.ds(pl.multiple_of(index * rows, rows), rows), :]
+
+    def send(source, target, which, hop, peer):
+        copy = pltpu.make_async_remote_copy(
+            src_ref=source,
+            dst_ref=target,
+            send_sem=send_sem.at[which, hop],
+            recv_sem=recv_sem.at[which, hop],
+            device_id=device_at(axes, peer),
+            device_id_type=pl.DeviceIdType.MESH,
+        )
+        copy.start()
+        return copy
+
+    copies = []
+    for which, (part, slot) in enumerate(zip(parts, slots)):
+        for hop, peer in enumerate(peers):
+            copies.append(send(rows_of(part, peer), slot.at[hop], which, hop, peer))
+    for copy in copies:
+        copy.wait()
+    sums = []
+    for part, slot in zip(parts, slots):
+        total = rows_of(part, me)[...].astype(jnp.float32)
+        for hop in range(count - 1):
+            total = total + slot[hop].astype(jnp.float32)
+        sums.append(total)
+    results = middle(sums, [rows_of(ref, me)[...] for ref in whole], [ref[...] for ref in own])
+    copies = []
+    for which, (ref, kind, value) in enumerate(zip(outs, kinds, results)):
+        if kind == "rows":
+            ref[...] = value.astype(ref.dtype)
+        else:
+            rows_of(ref, me)[...] = value.astype(ref.dtype)
+            for hop, peer in enumerate(peers):
+                copies.append(
+                    send(rows_of(ref, me), rows_of(ref, me), n_parts + which, hop, peer)
+                )
+    for copy in copies:
+        copy.wait()
+
+
+def exchange(axes, call_id, parts, whole, own, middle, outs):
+    count = math.prod(lax.axis_size(axis) for axis in axes)
+    vmem = pl.BlockSpec(memory_space=pltpu.VMEM)
+    scratch = [
+        pltpu.VMEM((count - 1, part.shape[0] // count) + part.shape[1:], part.dtype)
+        for part in parts
+    ]
+    sems = (len(parts) + len(outs), count - 1)
+    return pl.pallas_call(
+        functools.partial(
+            exchange_kernel,
+            axes,
+            count,
+            (len(parts), len(whole), len(own)),
+            [kind for kind, _, _ in outs],
+            middle,
+        ),
+        in_specs=[vmem] * (len(parts) + len(whole) + len(own)),
+        out_specs=[vmem] * len(outs),
+        out_shape=[jax.ShapeDtypeStruct(shape, dtype) for _, shape, dtype in outs],
+        scratch_shapes=scratch
+        + [pltpu.SemaphoreType.DMA(sems), pltpu.SemaphoreType.DMA(sems)],
+        compiler_params=pltpu.CompilerParams(
+            collective_id=call_id, has_side_effects=True, vmem_limit_bytes=40 * 2**20
+        ),
+    )(*parts, *whole, *own)
+
+
+def after_mixer(sums, whole, own):
+    (mixed,), (tokens_in,), (gain,) = sums, whole, own
+    middle = tokens_in.astype(jnp.float32) + mixed
+    return middle * inverse_rms(middle) * gain.astype(jnp.float32), middle
+
+
+def after_ffn_back(sums, whole, own):
+    (normed_grad,), (ct,), (middle, gain) = sums, whole, own
+    scale = inverse_rms(middle)
+    gain_grad = jnp.sum(normed_grad * middle * scale, 0, keepdims=True)
+    middle_grad = ct.astype(jnp.float32) + norm_back(
+        normed_grad, middle, scale, gain.astype(jnp.float32)
+    )
+    return middle_grad, middle_grad, gain_grad
+
+
+def after_mixer_back(sums, whole, own):
+    (normed_grad, ffn_out), (tokens_in,), (middle, middle_grad, gain) = sums, whole, own
+    hidden_in = tokens_in.astype(jnp.float32)
+    scale = inverse_rms(hidden_in)
+    gain_grad = jnp.sum(normed_grad * hidden_in * scale, 0, keepdims=True)
+    tokens_grad = middle_grad + norm_back(normed_grad, hidden_in, scale, gain.astype(jnp.float32))
+    return tokens_grad, middle + ffn_out, gain_grad
+
+
+def as_they_are(sums, whole, own):
+    return sums
+
+
 def per_device(
     tokens,
     mixgain,
@@ -367,7 +504,6 @@
     n_state = decaylog.shape[1]
     tiles = inner // LANE
     gain_mix = mixgain.astype(jnp.float32)
-    gain_ffn = ffngain.astype(jnp.float32)
     kernel = convkern.astype(jnp.float32)
     kernel_bias = convbias.astype(jnp.float32)
     step_bias = stepbias.astype(jnp.float32)
@@ -375,17 +511,27 @@
     decay_rate = -jnp.exp(jnp.transpose(decaylog.astype(jnp.float32)))
     rate = (decay_rate * LOG2E).reshape(n_state, tiles, LANE)
 
-    in_full = lax.all_gather(inproj, PLANE, axis=1, tiled=True)
-    out_full = lax.all_gather(outproj, PLANE, axis=1, tiled=True)
-    gu_full = lax.all_gather(gateup, PLANE, axis=1, tiled=True)
-    down_full = lax.all_gather(downproj, PLANE, axis=1, tiled=True)
-
-    hidden_in = tokens.reshape(rows, width).astype(jnp.float32)
+    gain_mix_row, gain_ffn_row = mixgain.reshape(1, width), ffngain.reshape(1, width)
+    own_rows = rows // lax.axis_size("tp")
+    hidden = gateup.shape[2]
+    low = jnp.bfloat16
+
+    mix_pack = gathered_rows(
+        jnp.concatenate([inproj[0], inproj[1], jnp.transpose(outproj)], 1)
+    )
+    ffn_pack = gathered_rows(
+        jnp.concatenate([gateup[0], gateup[1], jnp.transpose(downproj)], 1)
+    )
+
+    tokens_rows = tokens.reshape(rows, width)
+    hidden_in = tokens_rows.astype(jnp.float32)
     scale_one = inverse_rms(hidden_in)
-    normed_one = (hidden_in * scale_one * gain_mix).astype(jnp.bfloat16)
+    normed_one = (hidden_in * scale_one * gain_mix).astype(low)
     normed_one_cols = swapped_columns(normed_one)
-    conv_in = matmul(normed_one, in_full[0]).astype(jnp.bfloat16)
-    gate_mix = matmul(normed_one, in_full[1])
+    ct_low = cotangent.reshape(rows, width)
+    ct_cols = swapped_columns(ct_low)
+    conv_in = matmul(normed_one, mix_pack[:, :inner]).astype(low)
+    gate_mix = matmul(normed_one, mix_pack[:, inner : 2 * inner])
     conv_seqs = conv_in.reshape(seqs, span, inner)
     rim_rows = passed_along(conv_seqs[:, span - (taps - 1) :], "ctx", 1)
     padded_in = jnp.concatenate([rim_rows, conv_seqs], 1).astype(jnp.float32)
@@ -393,12 +539,23 @@
     for offset in range(taps):
         conv_out = conv_out + kernel[offset][None, None] * padded_in[:, offset : offset + span]
     conv_out = conv_out.reshape(rows, inner)
-    scan_in = jax.nn.silu(conv_out).astype(jnp.bfloat16)
+    scan_in = jax.nn.silu(conv_out).astype(low)
     scan_float = scan_in.astype(jnp.float32)
-    select_cols = lax.psum(matmul(scan_in, selproj), "tp")
-    step_low = select_cols[:, :rank].astype(jnp.bfloat16)
+    columns = selproj.shape[1]
+    select_width = -(-columns // LANE) * LANE
+    select_weights = jnp.pad(selproj, ((0, 0), (0, select_width - columns)))
+    (select_cols,) = exchange(
+        ("tp",),
+        0,
+        [matmul(scan_in, select_weights)],
+        [],
+        [],
+        as_they_are,
+        [("all", (rows, select_width), jnp.float32)],
+    )
+    step_low = select_cols[:, :rank].astype(low)
     b_rows = select_cols[:, rank : rank + n_state].reshape(-1)
-    c_rows = select_cols[:, rank + n_state :].reshape(-1)
+    c_rows = select_cols[:, rank + n_state : columns].reshape(-1)
     step_pre = matmul(step_low, stepproj) + step_bias[None]
     step_size = jax.nn.softplus(step_pre)
     span_decay = jnp.exp(
@@ -410,43 +567,47 @@
     prior, mixed_tiles = scan_forward(start, step_tiles, input_tiles, b_rows, c_rows, rate, seqs)
     mixer_core = from_tiles(mixed_tiles) + skip_weight[None] * scan_float
     gate_sig = jax.nn.silu(gate_mix)
-    gated = (mixer_core * gate_sig).astype(jnp.bfloat16)
-    mixed = lax.psum(matmul(gated, out_full).astype(jnp.bfloat16), "tp").astype(jnp.float32)
-    middle = hidden_in + mixed
-    scale_two = inverse_rms(middle)
-    normed_two = (middle * scale_two * gain_ffn).astype(jnp.bfloat16)
+    gated = (mixer_core * gate_sig).astype(low)
+    out_weights = mix_pack[:, 2 * inner :]
+    normed_two, middle = exchange(
+        ("tp",),
+        1,
+        [matmul_nt(gated, out_weights).astype(low)],
+        [tokens_rows],
+        [gain_ffn_row],
+        after_mixer,
+        [("all", (rows, width), low), ("rows", (own_rows, width), jnp.float32)],
+    )
     normed_two_cols = swapped_columns(normed_two)
-    gate_ffn = matmul(normed_two, gu_full[0])
-    up_ffn = matmul(normed_two, gu_full[1])
-    activated = (jax.nn.silu(gate_ffn) * up_ffn).astype(jnp.bfloat16)
-    ct_low = cotangent.reshape(rows, width)
-    ct_cols = swapped_columns(ct_low)
-    act_grad = matmul_nt(ct_low, down_full)
-    gate_grad = (act_grad * up_ffn * silu_slope(gate_ffn)).astype(jnp.bfloat16)
-    up_grad = (act_grad * jax.nn.silu(gate_ffn)).astype(jnp.bfloat16)
-    normed_two_part = matmul_nt(gate_grad, gu_full[0]) + matmul_nt(up_grad, gu_full[1])
-    normed_two_grad = lax.psum(normed_two_part.astype(jnp.bfloat16), "tp").astype(jnp.float32)
-    activated_all = gathered_rows(activated)
-    gate_grad_all = gathered_rows(gate_grad)
-    up_grad_all = gathered_rows(up_grad)
-    gated_all = gathered_rows(gated)
-    ffn_out = lax.psum(matmul(activated, down_full).astype(jnp.bfloat16), "tp")
-    layer_out = (middle + ffn_out.astype(jnp.float32)).astype(jnp.bfloat16)
-    grad_downproj = matmul_tn(activated_all, ct_cols)
-    grad_gateup = jnp.stack(
-        [matmul_tn(normed_two_cols, gate_grad_all), matmul_tn(normed_two_cols, up_grad_all)]
-    )
-    grad_ffngain = jnp.sum(normed_two_grad * middle * scale_two, 0)
-    middle_grad = ct_low.astype(jnp.float32) + norm_back(
-        normed_two_grad, middle, scale_two, gain_ffn
-    )
-    middle_low = middle_grad.astype(jnp.bfloat16)
+    gate_up = ffn_pack[:, : 2 * hidden]
+    down_weights = ffn_pack[:, 2 * hidden :]
+    both_ffn = matmul(normed_two, gate_up)
+    gate_ffn, up_ffn = both_ffn[:, :hidden], both_ffn[:, hidden:]
+    activated = (jax.nn.silu(gate_ffn) * up_ffn).astype(low)
+    act_grad = matmul(ct_low, down_weights)
+    gate_grad = (act_grad * up_ffn * silu_slope(gate_ffn)).astype(low)
+    up_grad = (act_grad * jax.nn.silu(gate_ffn)).astype(low)
+    ffn_grads = jnp.concatenate([gate_grad, up_grad], 1)
+    ffn_all = gathered_rows(jnp.concatenate([activated, ffn_grads, gated], 1))
+    normed_two_part = matmul_nt(ffn_grads, gate_up).astype(low)
+    ffn_part = matmul_nt(activated, down_weights).astype(low)
+    middle_low, middle_grad, ffngain_part = exchange(
+        ("tp",),
+        2,
+        [normed_two_part],
+        [ct_low],
+        [middle, gain_ffn_row],
+        after_ffn_back,
+        [
+            ("all", (rows, width), low),
+            ("rows", (own_rows, width), jnp.float32),
+            ("rows", (1, width), jnp.float32),
+        ],
+    )
     middle_cols = swapped_columns(middle_low)
-    grad_outproj = matmul_tn(gated_all, middle_cols)
-    gated_grad = matmul_nt(middle_low, out_full)
+    gated_grad = matmul(middle_low, out_weights)
     core_grad = gated_grad * gate_sig
-    gate_mix_grad = (gated_grad * mixer_core * silu_slope(gate_mix)).astype(jnp.bfloat16)
-    gate_mix_grad_all = gathered_rows(gate_mix_grad)
+    gate_mix_grad = (gated_grad * mixer_core * silu_slope(gate_mix)).astype(low)
     grad_skipgain = jnp.sum(core_grad * scan_float, 0)
     ograd_tiles = to_tiles(core_grad)
     back_ends = scan_ends(step_tiles, ograd_tiles, c_rows, rate, seqs, True)
@@ -457,15 +618,30 @@
     grad_decaylog = rate_grad.reshape(n_state, inner) * decay_rate
     pre_grad = from_tiles(step_grad_tiles) * jax.nn.sigmoid(step_pre)
     grad_stepbias = jnp.sum(pre_grad, 0)
-    pre_low = pre_grad.astype(jnp.bfloat16)
+    pre_low = pre_grad.astype(low)
     grad_stepproj = matmul_tn(step_low, pre_low)
-    select_grad = lax.psum(
-        jnp.concatenate([matmul_nt(pre_low, stepproj), jnp.sum(parts, -1)], 1), "tp"
-    )
-    select_low = select_grad.astype(jnp.bfloat16)
-    grad_selproj = matmul_tn(scan_in, select_low)
+    select_part = jnp.concatenate(
+        [
+            matmul_nt(pre_low, stepproj),
+            jnp.sum(parts, -1),
+            jnp.zeros((rows, select_width - columns), jnp.float32),
+        ],
+        1,
+    ).astype(low)
+    (select_low,) = exchange(
+        ("tp",),
+        3,
+        [select_part],
+        [],
+        [],
+        as_they_are,
+        [("all", (rows, select_width), low)],
+    )
+    grad_selproj = matmul_tn(select_low, scan_in)
     scan_in_grad = (
-        core_grad * skip_weight[None] + from_tiles(input_grad_tiles) + matmul_nt(select_low, selproj)
+        core_grad * skip_weight[None]
+        + from_tiles(input_grad_tiles)
+        + matmul_nt(select_low, select_weights)
     )
     conv_grad = scan_in_grad * silu_slope(conv_out)
     grad_convbias = jnp.sum(conv_grad, 0)
@@ -482,50 +658,76 @@
     returned = passed_along(padded_grad[:, : taps - 1], "ctx", -1)
     conv_in_grad = (
         (padded_grad[:, taps - 1 :] + jnp.pad(returned, ((0, 0), (span - taps + 1, 0), (0, 0))))
-        .astype(jnp.bfloat16)
+        .astype(low)
         .reshape(rows, inner)
     )
-    conv_in_grad_all = gathered_rows(conv_in_grad)
-    normed_one_part = matmul_nt(conv_in_grad, in_full[0]) + matmul_nt(gate_mix_grad, in_full[1])
-    normed_one_grad = lax.psum(normed_one_part.astype(jnp.bfloat16), "tp").astype(jnp.float32)
+    mix_grads = jnp.concatenate([conv_in_grad, gate_mix_grad], 1)
+    mix_all = gathered_rows(mix_grads)
+    normed_one_part = matmul_nt(mix_grads, mix_pack[:, : 2 * inner]).astype(low)
+    ffn_part, _ = lax.optimization_barrier((ffn_part, normed_one_part))
+    tokens_grad, layer_out, mixgain_part = exchange(
+        ("tp",),
+        4,
+        [normed_one_part, ffn_part],
+        [tokens_rows],
+        [middle, middle_grad, gain_mix_row],
+        after_mixer_back,
+        [
+            ("all", (rows, width), low),
+            ("all", (rows, width), low),
+            ("rows", (1, width), jnp.float32),
+        ],
+    )
+    grad_downproj = matmul_tn(ffn_all[:, :hidden], ct_cols)
+    grad_gateup = jnp.stack(
+        [
+            matmul_tn(normed_two_cols, ffn_all[:, hidden : 2 * hidden]),
+            matmul_tn(normed_two_cols, ffn_all[:, 2 * hidden : 3 * hidden]),
+        ]
+    )
+    grad_outproj = matmul_tn(ffn_all[:, 3 * hidden :], middle_cols)
     grad_inproj = jnp.stack(
         [
-            matmul_tn(normed_one_cols, conv_in_grad_all),
-            matmul_tn(normed_one_cols, gate_mix_grad_all),
+            matmul_tn(normed_one_cols, mix_all[:, :inner]),
+            matmul_tn(normed_one_cols, mix_all[:, inner:]),
         ]
     )
-    grad_mixgain = jnp.sum(normed_one_grad * hidden_in * scale_one, 0)
-    tokens_grad = (middle_grad + norm_back(normed_one_grad, hidden_in, scale_one, gain_mix)).astype(
-        jnp.bfloat16
-    )
-    smalls = lax.psum(
-        (
-            grad_mixgain,
-            grad_convkern,
-            grad_convbias,
-            grad_selproj,
-            grad_stepproj,
-            grad_stepbias,
-            grad_decaylog,
-            grad_skipgain,
-            grad_ffngain,
-        ),
-        PLANE,
-    )
+    small = [
+        grad_convkern,
+        grad_convbias[None],
+        grad_stepbias[None],
+        grad_decaylog,
+        grad_skipgain[None],
+        grad_stepproj,
+        grad_selproj[:columns],
+    ]
+    sizes = [part.shape[0] for part in small]
+    share = 16 * math.prod(lax.axis_size(axis) for axis in PLANE)
+    small.append(jnp.zeros((-sum(sizes) % share, inner), jnp.float32))
+    small = jnp.concatenate(small, 0).astype(low)
+    (small,) = exchange(
+        PLANE, 5, [small], [], [], as_they_are, [("all", small.shape, low)]
+    )
+    small = small.astype(jnp.float32)
+    smalls, at = [], 0
+    for size in sizes:
+        smalls.append(small[at : at + size])
+        at += size
+    gains = lax.psum(jnp.concatenate([mixgain_part, ffngain_part], 0), PLANE + ("tp",))
     return (
         layer_out.reshape(tokens.shape),
         tokens_grad.reshape(tokens.shape),
+        gains[0],
+        grad_inproj,
         smalls[0],
-        grad_inproj,
-        smalls[1],
-        smalls[2],
-        smalls[3],
-        smalls[4],
+        smalls[1][0],
+        jnp.transpose(smalls[6]),
         smalls[5],
-        jnp.transpose(smalls[6]),
-        smalls[7],
+        smalls[2][0],
+        jnp.transpose(smalls[3]),
+        smalls[4][0],
         grad_outproj,
-        smalls[8],
+        gains[1],
         grad_gateup,
         grad_downproj,
     )

time: 946 us -> 679 us (0.72)
  waiting for transfers between devices: 638 us -> 113 us
  Pallas kernels: 35.2 us -> 281 us
  local copies, waits for them, and re-layouts: 29.2 us -> 59.7 us
  other arithmetic: 34.8 us -> 24.6 us
    pallas_call x0 -> x6, Pallas kernels: none -> 245 us  [exchange(): pl.pallas_call(functools.partial(exchange_kernel, axes, count, (len(parts...]
    psum x5 -> x0, waiting for transfers between devices: 228 us -> none  [the longest x1 54.9 us: per_device(): lax.psum((grad_mixgain, grad_convkern, grad_convbias, grad_selproj, grad_...]
    all_gather x4 -> x0, waiting for transfers between devices: 191 us -> none  [the longest x1 87.2 us: per_device(): gu_full = lax.all_gather(gateup, PLANE, axis=1, tiled=True)]
    all_gather x6 -> x4, waiting for transfers between devices: 192 us -> 81.1 us  [gathered_rows(): return lax.all_gather(rows, PLANE, axis=0, tiled=True)]
    all_to_all x4, waiting for transfers between devices: 9.2 us -> 22.1 us  [swapped_columns(): return lax.all_to_all(rows, PLANE, split_axis=1, concat_axis=0, tiled=True)]
    dot_general x8 -> x6, matrix products: 40.7 us -> 31.1 us  [matmul_nt(): lax.dot_general(left, right, (((1,), (1,)), ((), ())), preferred_element_...]
    reshape x1 -> x13, local copies, waits for them, and re-layouts: 0.1 us -> 9.62 us  [the longest x3 4.22 us: from_tiles(): return tiled.reshape(groups, tiles, SUB, LANE).transpose(0, 2, 1, 3).resh...]
    unnamed x166 -> x142, local copies, waits for them, and re-layouts: 20.5 us -> 28.6 us
  transfers between devices with their start and end apart: 23 -> 12, of which waited for: 19 -> 10; matrix products, arithmetic and copies ran while one was open for 13% -> 15% of each run, Pallas kernels for 4% -> 29%
where the time goes in v2:
time: 679 us; the launch traced here: 672 us
  Pallas kernels  281 us (41%)
  waiting for transfers between devices  113 us (17%)
  matrix products  106 us (16%)
  local copies, waits for them, and re-layouts  59.7 us (9%)
  blocking collectives  44.5 us (7%)
  starting transfers between devices  28.6 us (4%)
  other arithmetic  24.6 us (4%)
  between operations  15.4 us (2%)
    pallas_call x6, Pallas kernels, exchange(): pl.pallas_call(functools.partial(exchange_kernel, axes, count, (len(parts...  245 us
    all_gather x4, waiting for transfers between devices, gathered_rows(): return lax.all_gather(rows, PLANE, axis=0, tiled=True)  81.1 us
    psum x1, blocking collectives, per_device(): lax.psum(jnp.concatenate([mixgain_part, ffngain_part], 0), PLANE + ('tp',))  44.5 us
    dot_general x7, matrix products, matmul(): return jnp.dot(left, right, preferred_element_type=jnp.float32)  40.3 us
    dot_general x8, matrix products, matmul_tn(): lax.dot_general(left, right, (((0,), (0,)), ((), ())), preferred_element_...  34.2 us
    dot_general x6, matrix products, matmul_nt(): lax.dot_general(left, right, (((1,), (1,)), ((), ())), preferred_element_...  31.1 us
    unnamed x142, local copies, waits for them, and re-layouts  28.6 us
    all_to_all x4, waiting for transfers between devices, swapped_columns(): return lax.all_to_all(rows, PLANE, split_axis=1, concat_axis=0, tiled=True)  22.1 us
  transfers between devices with their start and end apart: 12, of which 10 were waited for; matrix products, arithmetic and copies ran while one was open for 15% of the time, Pallas kernels for 29%

profile of v2, /device:TPU:0, one launch (start us, length us, event | category | flops | bytes accessed | tf_op | source)
XLA Modules:
  0.0 672.1 jit_solution(13615859885386935840)
XLA Ops:
  17.5 70.3 %all-gather.7.cloned.1.call-done = bf16[2048,3072]{0,1:T(8,128)(2,1)} async-done(((bf16[256,3072]{0,1:T(8,128)(2,1)}), bf16[2048,3072]{0,1:T(8,128)(2,1)}) %all-gather.7.cloned.1.call-update) | async-done | bytes 12582928 | tf_op jit(solution)/shard_map/all_gather | solution.py:339
  100.7 14.6 %shard_map.262 = f32[256,256]{1,0:T(8,128)S(1)} custom-call(f32[256,256]{1,0:T(8,128)S(1)} %fusion.76.refs_0_), custom_call_target="tpu_custom_call" | custom-call | tf_op jit(solution)/shard_map/pallas_call | solution.py:434
  125.2 5.1 shard_map.263
  130.4 4.5 collective-permute-start.1
  137.6 7.4 %shard_map.264 = (f32[256,16,8,128]{3,2,1,0:T(8,128)S(1)}, f32[32,64,128]{2,1,0:T(8,128)S(1)}) custom-call(f32[2,16,8,128]{3,2,1,0:T(8,128)} %collective-permute-done.1.start_ref, f32[32,64,128]{2,1,0:T(8,128)S(1)} %get-tuple-element.83.step_ref, f32[32,64,128]{2,1,0:T(8,128)S(1)} %get-tuple-element.82.drive_ref.input_ref, ...), custom_call_target="tpu_custom_call" | custom-call | tf_op jit(solution)/shard_map/pallas_call | solution.py:177
  145.1 6.3 copy-done.2
  155.3 5.3 multiply_convert_fusion.5
  164.9 45.7 %shard_map.265 = (bf16[256,2048]{1,0:T(8,128)(2,1)S(1)}, f32[64,2048]{1,0:T(8,128)S(1)}) custom-call(bf16[256,2048]{1,0:T(8,128)(2,1)S(1)} %fusion.42.refs_0_, bf16[256,2048]{1,0:T(8,128)(2,1)S(1)} %bitcast.181, bf16[1,2048]{1,0:T(2,128)(2,1)S(1)} %reshape.178.refs_2_.refs_3_), custom_call_target="tpu_custom_call" | custom-call | tf_op jit(solution)/shard_map/pallas_call | solution.py:434
  212.4 8.5 %all-gather.5.cloned.1.call-done = bf16[2048,6144]{0,1:T(8,128)(2,1)} async-done(((bf16[256,6144]{0,1:T(8,128)(2,1)}), bf16[2048,6144]{0,1:T(8,128)(2,1)}) %all-gather.5.cloned.1.call-update) | async-done | bytes 25165840 | tf_op jit(solution)/shard_map/all_gather | solution.py:339
  220.9 12.7 %fusion.2 = f32[256,4096]{0,1:T(8,128)} fusion(bf16[256,2048]{1,0:T(8,128)(2,1)} %copy-done.14, bf16[2048,6144]{0,1:T(8,128)(2,1)} %all-gather.5.cloned.1.call-done), kind=kOutput, calls=%fused_computation.2 | convolution fusion | flops 4294967296 | bytes 22020096 | tf_op jit(solution)/shard_map/dot_general | solution.py:26
  233.6 9.1 %multiply_convert_fusion.2 = (bf16[256,2048]{0,1:T(8,128)(2,1)S(1)}, bf16[256,2048]{0,1:T(8,128)(2,1)S(1)}, bf16[256,2048]{0,1:T(8,128)(2,1)}) fusion(f32[256,4096]{0,1:T(8,128)} %fusion.2, bf16[256,2048]{1,0:T(8,128)(2,1)} %bitcast.186, bf16[2048,6144]{0,1:T(8,128)(2,1)} %all-gather.5.cloned.1.call-done), kind=kOutput, calls=%fused_computation.50 | convolution fusion | flops 2155347968 | bytes 16777216 | tf_op jit(solution)/shard_map/dot_general | solution.py:26
  242.8 11.2 %fusion.39.refs_0_ = bf16[256,2048]{1,0:T(8,128)(2,1)S(1)} fusion(bf16[2048,6144]{0,1:T(8,128)(2,1)} %all-gather.5.cloned.1.call-done, bf16[256,2048]{0,1:T(8,128)(2,1)S(1)} %get-tuple-element.54, bf16[256,2048]{0,1:T(8,128)(2,1)S(1)} %get-tuple-element.53), kind=kOutput, calls=%fused_computation.37 | convolution fusion | flops 4299685888 | bytes 19922944 | tf_op jit(solution)/shard_map/dot_general | solution.py:30
  254.0 45.9 %shard_map.266 = (bf16[256,2048]{1,0:T(8,128)(2,1)S(1)}, f32[64,2048]{1,0:T(8,128)S(1)}, f32[1,2048]{1,0:T(1,128)S(1)}) custom-call(bf16[256,2048]{1,0:T(8,128)(2,1)S(1)} %fusion.39.refs_0_, bf16[256,2048]{1,0:T(8,128)(2,1)S(1)} %bitcast.187, f32[64,2048]{1,0:T(8,128)S(1)} %copy-done.10, bf16[1,2048]{1,0:T(2,128)(2,1)S(1)} %reshape.178.refs_2_.refs_3_), custom_call_target="tpu_custom_call" | custom-call | tf_op jit(solution)/shard_map/pallas_call | solution.py:434
  300.1 6.1 fusion.68
  310.3 5.1 shard_map.267
  324.8 18.5 %shard_map.268 = (f32[32,64,128]{2,1,0:T(8,128)S(1)}, f32[32,64,128]{2,1,0:T(8,128)S(1)}, f32[16,8,128]{2,1,0:T(8,128)S(1)}, f32[256,32,128]{2,1,0:T(8,128)S(1)}) custom-call(f32[2,16,8,128]{3,2,1,0:T(8,128)} %collective-permute-done.2.end_ref, f32[256,16,8,128]{3,2,1,0:T(8,128)} %copy-done.2, f32[32,64,128]{2,1,0:T(8,128)S(1)} %get-tuple-element.83.step_ref, ...), custom_call_target="tpu_custom_call" | custom-call | tf_op jit(solution)/shard_map/pallas_call | solution.py:289
  353.6 18.0 %shard_map.269 = bf16[256,256]{1,0:T(8,128)(2,1)S(1)} custom-call(bf16[256,256]{1,0:T(8,128)(2,1)S(1)} %maximum_maximum_fusion.refs_0_), custom_call_target="tpu_custom_call" | custom-call | tf_op jit(solution)/shard_map/pallas_call | solution.py:434
  392.9 4.4 all-to-all-start
  401.0 6.9 %fusion.45.refs_1_ = bf16[256,2048]{1,0:T(8,128)(2,1)} fusion(bf16[256,2048]{0,1:T(8,128)(2,1)S(1)} %copy-done.40, bf16[2048,6144]{0,1:T(8,128)(2,1)} %all-gather.5.cloned.1.call-done), kind=kOutput, calls=%fused_computation.39 | convolution fusion | flops 2148007936 | bytes 10485760 | tf_op jit(solution)/shard_map/dot_general | solution.py:30
  411.0 28.4 %shard_map.271 = bf16[384,1024]{1,0:T(8,128)(2,1)S(1)} custom-call(bf16[384,1024]{1,0:T(8,128)(2,1)S(1)} %concatenate.37.refs_0_), custom_call_target="tpu_custom_call" | custom-call | tf_op jit(solution)/shard_map/pallas_call | solution.py:434
  443.2 5.9 fusion.48.refs_0_
  449.1 91.9 %shard_map.270 = (bf16[256,2048]{1,0:T(8,128)(2,1)S(1)}, bf16[256,2048]{1,0:T(8,128)(2,1)S(1)}, f32[1,2048]{1,0:T(1,128)S(1)}) custom-call(bf16[256,2048]{1,0:T(8,128)(2,1)S(1)} %fusion.48.refs_0_, bf16[256,2048]{1,0:T(8,128)(2,1)S(1)} %copy-done.20, bf16[256,2048]{1,0:T(8,128)(2,1)S(1)} %bitcast.183, f32[64,2048]{1,0:T(8,128)S(1)} %copy-done.11, ...), custom_call_target="tpu_custom_call" | custom-call | tf_op jit(solution)/shard_map/pallas_call | solution.py:434
  541.1 44.5 %psum.7 = f32[2,2048]{1,0:T(2,128)S(1)} all-reduce(f32[2,2048]{1,0:T(2,128)S(1)} %pad_maximum_fusion.6), channel_id=1, replica_groups=mesh['dp'=4,'ctx'=2,'tp'=4] {'dp','ctx','tp'}, use_global_device_ids=true, to_apply=%region_2.3 | all-reduce | flops 4096 | bytes 32768 | tf_op jit(solution)/shard_map/psum | solution.py:716
  586.2 4.9 all-to-all-start.2
  591.1 4.9 fusion.60
  599.6 17.8 %all-to-all-done.2 = bf16[256,8,256]{2,0,1:T(8,128)(2,1)S(1)} async-done(((bf16[256,8,256]{2,0,1:T(8,128)(2,1)}), bf16[256,8,256]{2,0,1:T(8,128)(2,1)S(1)}, u32[]{:S(2)}, u32[]{:S(2)}) %all-to-all-start.2) | async-done | bytes 1048608 | tf_op jit(solution)/shard_map/all_to_all | solution.py:343
  617.4 4.3 all-to-all-start.1
  627.1 7.1 %fusion.36 = f32[1,256,2048]{2,1,0:T(8,128)} fusion(bf16[2048,256]{1,0:T(8,128)(2,1)S(1)} %bitcast.221, bf16[2048,7168]{0,1:T(8,128)(2,1)} %all-gather.11.cloned.1.call-done), kind=kOutput, calls=%fused_computation.36 | convolution fusion | flops 2147483648 | bytes 11534336 | tf_op jit(solution)/shard_map/dot_general | solution.py:36
  636.7 4.2 all-to-all-start.3
  640.9 5.9 fusion.33
  649.3 4.7 fusion.16
  655.8 7.3 %fusion.4 = f32[2048,256]{1,0:T(8,128)} fusion(bf16[2048,256]{1,0:T(8,128)(2,1)} %bitcast.53, bf16[2048,7168]{0,1:T(8,128)(2,1)} %all-gather.11.cloned.1.call-done), kind=kOutput, calls=%fused_computation.4 | convolution fusion | flops 2147483648 | bytes 11534336 | tf_op jit(solution)/shard_map/dot_general | solution.py:36
  (247 shorter events, 119.2 us)
Async XLA Ops:
  7.2 108.1 %copy-start = (bf16[128,1024]{1,0:T(8,128)(2,1)S(1)}, bf16[128,1024]{1,0:T(8,128)(2,1)}, u32[]{:S(2)}) copy-start(bf16[128,1024]{1,0:T(8,128)(2,1)} %param.21) | copy-start | bytes 786436
  7.2 80.6 %all-gather.7.cloned.1.call-start = ((), (), s32[]{:S(2)}) async-start(), calls=%async_computation.5 | async-start | bytes 14155776 | tf_op jit(solution)/shard_map/all_gather | solution.py:339
  10.3 210.6 %all-gather.5.cloned.1.call-start = ((), (), s32[]{:S(2)}) async-start(), calls=%async_computation.4 | async-start | bytes 28311552 | tf_op jit(solution)/shard_map/all_gather | solution.py:339
  15.9 575.2 %all-gather.9.cloned.1.call-start = ((), (), s32[]{:S(2)}) async-start(), calls=%async_computation.6 | async-start | bytes 9437184 | tf_op jit(solution)/shard_map/all_gather | solution.py:339
  17.2 74.2 %copy-start.52 = (f32[2048]{0:T(1024)}, f32[2048]{0:T(1024)S(1)}, u32[]{:S(2)}) copy-start(f32[2048]{0:T(1024)S(1)} %convert_element_type.110) | copy-start | bytes 24580
  87.8 7.0 %copy-start.57 = (bf16[1024]{0:T(1024)(128)(2,1)S(1)}, bf16[1024]{0:T(1024)(128)(2,1)}, u32[]{:S(2)}) copy-start(bf16[1024]{0:T(1024)(128)(2,1)} %param.19) | copy-start | bytes 6148
  87.8 7.0 %copy-start.58 = (bf16[1024]{0:T(1024)(128)(2,1)S(1)}, bf16[1024]{0:T(1024)(128)(2,1)}, u32[]{:S(2)}) copy-start(bf16[1024]{0:T(1024)(128)(2,1)} %param.22) | copy-start | bytes 6148
  91.3 4.8 collective-permute-start
  99.1 16.2 %copy-start.29 = (bf16[256,1024]{0,1:T(8,128)(2,1)}, bf16[256,1024]{0,1:T(8,128)(2,1)S(1)}, u32[]{:S(2)}) copy-start(bf16[256,1024]{0,1:T(8,128)(2,1)S(1)} %multiply_convert_fusion.6) | copy-start | bytes 1572868
  115.3 7.0 %copy-start.12 = (f32[256,256]{1,0:T(8,128)}, f32[256,256]{1,0:T(8,128)S(1)}, u32[]{:S(2)}) copy-start(f32[256,256]{1,0:T(8,128)S(1)} %shard_map.262) | copy-start | bytes 786436
  123.5 11.4 %copy-start.59 = (bf16[1024]{0:T(1024)(128)(2,1)S(1)}, bf16[1024]{0:T(1024)(128)(2,1)}, u32[]{:S(2)}) copy-start(bf16[1024]{0:T(1024)(128)(2,1)} %param.24) | copy-start | bytes 6148
  123.5 12.0 %copy-start.54 = (bf16[2048]{0:T(1024)(128)(2,1)S(1)}, bf16[2048]{0:T(1024)(128)(2,1)}, u32[]{:S(2)}) copy-start(bf16[2048]{0:T(1024)(128)(2,1)} %param.26) | copy-start | bytes 12292
  130.4 7.3 %collective-permute-start.1 = (f32[2,16,8,128]{3,2,1,0:T(8,128)}, f32[2,16,8,128]{3,2,1,0:T(8,128)}, u32[]{:S(2)}, u32[]{:S(2)}) collective-permute-start(f32[2,16,8,128]{3,2,1,0:T(8,128)} %shard_map.263), channel_id=1, source_target_pairs={{0,4},{1,5},{2,6},{3,7},{8,12},{9,13},{10,14},{11,15},{16,20},{17,... | collective-permute-start | bytes 393224 | tf_op jit(solution)/shard_map/ppermute | solution.py:22
  242.7 11.3 %copy-start.41 = (bf16[256,2048]{0,1:T(8,128)(2,1)}, bf16[256,2048]{0,1:T(8,128)(2,1)S(1)}, u32[]{:S(2)}) copy-start(bf16[256,2048]{0,1:T(8,128)(2,1)S(1)} %get-tuple-element.53) | copy-start | bytes 3145732
  242.7 11.3 %copy-start.42 = (bf16[256,2048]{0,1:T(8,128)(2,1)}, bf16[256,2048]{0,1:T(8,128)(2,1)S(1)}, u32[]{:S(2)}) copy-start(bf16[256,2048]{0,1:T(8,128)(2,1)S(1)} %get-tuple-element.54) | copy-start | bytes 3145732
  242.7 11.3 %copy-start.7 = (bf16[2,128,2048]{2,1,0:T(8,128)(2,1)S(1)}, bf16[2,128,2048]{2,1,0:T(8,128)(2,1)}, u32[]{:S(2)}) copy-start(bf16[2,128,2048]{2,1,0:T(8,128)(2,1)} %param.29) | copy-start | bytes 3145732
  242.7 11.3 %copy-start.10 = (f32[64,2048]{1,0:T(8,128)S(1)}, f32[64,2048]{1,0:T(8,128)}, u32[]{:S(2)}) copy-start(f32[64,2048]{1,0:T(8,128)} %copy-done.9) | copy-start | bytes 1572868
  242.7 57.3 %copy-start.30 = (bf16[256,1024]{0,1:T(8,128)(2,1)S(1)}, bf16[256,1024]{0,1:T(8,128)(2,1)}, u32[]{:S(2)}) copy-start(bf16[256,1024]{0,1:T(8,128)(2,1)} %copy-done.29) | copy-start | bytes 1572868
  242.7 57.3 %copy-start.43 = (f32[256,1024]{0,1:T(8,128)S(1)}, f32[256,1024]{0,1:T(8,128)}, u32[]{:S(2)}) copy-start(f32[256,1024]{0,1:T(8,128)} %copy.139) | copy-start | bytes 3145732
  242.7 57.3 %copy-start.55 = (f32[1024]{0:T(1024)S(1)}, f32[1024]{0:T(1024)}, u32[]{:S(2)}) copy-start(f32[1024]{0:T(1024)} %convert_element_type.118) | copy-start | bytes 12292
  242.7 57.3 %copy-start.63 = (f32[256,1024]{0,1:T(8,128)S(1)}, f32[256,1024]{0,1:T(8,128)}, u32[]{:S(2)}) copy-start(f32[256,1024]{0,1:T(8,128)} %get-tuple-element.79) | copy-start | bytes 3145732
  316.4 7.2 %collective-permute-start.2 = (f32[2,16,8,128]{3,2,1,0:T(8,128)}, f32[2,16,8,128]{3,2,1,0:T(8,128)}, u32[]{:S(2)}, u32[]{:S(2)}) collective-permute-start(f32[2,16,8,128]{3,2,1,0:T(8,128)} %shard_map.267), channel_id=1, source_target_pairs={{4,0},{5,1},{6,2},{7,3},{12,8},{13,9},{14,10},{15,11},{20,16},{21,... | collective-permute-start | bytes 393224 | tf_op jit(solution)/shard_map/ppermute | solution.py:22
  349.1 22.5 %copy-start.19 = (f32[32,64,128]{2,1,0:T(8,128)S(1)}, f32[32,64,128]{2,1,0:T(8,128)}, u32[]{:S(2)}) copy-start(f32[32,64,128]{2,1,0:T(8,128)} %copy-done.18) | copy-start | bytes 3145732
  379.3 5.8 collective-permute-start.3
  387.8 239.3 %all-gather.11.cloned.1.call-start = ((), (), s32[]{:S(2)}) async-start(), calls=%async_computation.7 | async-start | bytes 33030144 | tf_op jit(solution)/shard_map/all_gather | solution.py:339
  392.9 193.3 %all-to-all-start = ((bf16[256,8,256]{2,0,1:T(8,128)(2,1)}), bf16[256,8,256]{2,0,1:T(8,128)(2,1)}, u32[]{:S(2)}, u32[]{:S(2)}) async-start(bf16[256,8,256]{2,0,1:T(8,128)(2,1)} %copy.161), calls=%async_computation | async-start | bytes 2097152 | tf_op jit(solution)/shard_map/all_to_all | solution.py:343
  411.0 32.3 %copy-start.37 = (bf16[256,1024]{0,1:T(8,128)(2,1)S(1)}, bf16[256,1024]{0,1:T(8,128)(2,1)}, u32[]{:S(2)}) copy-start(bf16[256,1024]{0,1:T(8,128)(2,1)} %copy-done.36) | copy-start | bytes 1572868
  411.0 32.2 %copy-start.47 = (bf16[256,1024]{0,1:T(8,128)(2,1)S(1)}, bf16[256,1024]{0,1:T(8,128)(2,1)}, u32[]{:S(2)}) copy-start(bf16[256,1024]{0,1:T(8,128)(2,1)} %get-tuple-element.56) | copy-start | bytes 1572868
  586.2 31.2 %all-to-all-start.2 = ((bf16[256,8,256]{2,0,1:T(8,128)(2,1)}), bf16[256,8,256]{2,0,1:T(8,128)(2,1)S(1)}, u32[]{:S(2)}, u32[]{:S(2)}) async-start(bf16[256,8,256]{2,0,1:T(8,128)(2,1)} %bitcast.204), calls=%async_computation.2 | async-start | bytes 2097152 | tf_op jit(solution)/shard_map/all_to_all | solution.py:343
  617.4 19.2 %all-to-all-start.1 = ((bf16[256,8,256]{2,0,1:T(8,128)(2,1)}), bf16[256,8,256]{2,0,1:T(8,128)(2,1)}, u32[]{:S(2)}, u32[]{:S(2)}) async-start(bf16[256,8,256]{2,0,1:T(8,128)(2,1)} %bitcast.174), calls=%async_computation.1 | async-start | bytes 2097152 | tf_op jit(solution)/shard_map/all_to_all | solution.py:343
  636.7 19.2 %all-to-all-start.3 = ((bf16[256,8,256]{2,0,1:T(8,128)(2,1)}), bf16[256,8,256]{2,0,1:T(8,128)(2,1)}, u32[]{:S(2)}, u32[]{:S(2)}) async-start(bf16[256,8,256]{2,0,1:T(8,128)(2,1)} %copy.168), calls=%async_computation.3 | async-start | bytes 2097152 | tf_op jit(solution)/shard_map/all_to_all | solution.py:343
  655.8 9.3 %copy-start.1 = (bf16[128,1024]{1,0:T(8,128)(2,1)S(1)}, bf16[128,1024]{1,0:T(8,128)(2,1)}, u32[]{:S(2)}) copy-start(bf16[128,1024]{1,0:T(8,128)(2,1)} %param.21) | copy-start | bytes 786436
  (44 other events, 139.2 us)
Sparse Core Ops, SparseCore 0:
  10.5 77.2 all-gather.6
  90.2 130.6 all-gather.4
  387.9 75.3 all-gather.8
  465.6 161.4 all-gather.10

commit v3 on v2

--- a/solution.py
+++ b/solution.py
@@ -53,31 +53,37 @@
     return scale * (scaled_grad - unit_rows * jnp.mean(scaled_grad * unit_rows, -1, keepdims=True))
 
 
-def to_tiles(rows):
-    count, width = rows.shape
-    tiles = width // LANE
-    return (
-        rows.reshape(count // SUB, SUB, tiles, LANE)
-        .transpose(0, 2, 1, 3)
-        .reshape(count // SUB, tiles * SUB, LANE)
-    )
-
-
-def from_tiles(tiled):
-    groups, rows, _ = tiled.shape
-    tiles = rows // SUB
-    return (
-        tiled.reshape(groups, tiles, SUB, LANE)
-        .transpose(0, 2, 1, 3)
-        .reshape(groups * SUB, tiles * LANE)
-    )
-
-
-def token_row(ref, group, at, tiles):
-    return ref[group, pl.ds(at, tiles, stride=SUB), :]
-
-
-def ends_kernel(n_state, tiles, groups, reverse, step_ref, drive_ref, rows_ref, rate_ref, end_ref):
+def stage_in(ref, group, held):
+    for tile in range(held.shape[0] // SUB):
+        held[pl.ds(tile * SUB, SUB), :] = ref[
+            pl.ds(pl.multiple_of(group * SUB, SUB), SUB), pl.ds(tile * LANE, LANE)
+        ]
+
+
+def stage_out(held, ref, group):
+    for tile in range(held.shape[0] // SUB):
+        ref[pl.ds(pl.multiple_of(group * SUB, SUB), SUB), pl.ds(tile * LANE, LANE)] = held[
+            pl.ds(tile * SUB, SUB), :
+        ]
+
+
+def token_row(held, at, tiles):
+    return held[pl.ds(at, tiles, stride=SUB), :]
+
+
+def ends_kernel(
+    n_state,
+    tiles,
+    groups,
+    reverse,
+    step_ref,
+    drive_ref,
+    rows_ref,
+    rate_ref,
+    end_ref,
+    step_held,
+    drive_held,
+):
     base = pl.program_id(0) * groups * SUB * n_state
     rates = [rate_ref[n] for n in range(n_state)]
 
@@ -85,9 +91,11 @@
         group = groups - 1 - turn if reverse else turn
         order = range(SUB - 1, -1, -1) if reverse else range(SUB)
         states = list(states)
+        stage_in(step_ref, group, step_held)
+        stage_in(drive_ref, group, drive_held)
         for at in order:
-            step = token_row(step_ref, group, at, tiles)
-            drive = token_row(drive_ref, group, at, tiles)
+            step = token_row(step_held, at, tiles)
+            drive = token_row(drive_held, at, tiles)
             if not reverse:
                 drive = drive * step
             for n in range(n_state):
@@ -107,19 +115,21 @@
 
 def scan_ends(step, drive, rows, rate, seqs, reverse):
     n_state, tiles, _ = rate.shape
-    groups = step.shape[0] // seqs
-    tile_spec = pl.BlockSpec((groups, tiles * SUB, LANE), lambda s: (s, 0, 0))
+    groups = step.shape[0] // seqs // SUB
+    rows_spec = pl.BlockSpec((groups * SUB, tiles * LANE), lambda s: (s, 0))
+    held = pltpu.VMEM((tiles * SUB, LANE), jnp.float32)
     return pl.pallas_call(
         functools.partial(ends_kernel, n_state, tiles, groups, reverse),
         grid=(seqs,),
         in_specs=[
-            tile_spec,
-            tile_spec,
+            rows_spec,
+            rows_spec,
             pl.BlockSpec(memory_space=pltpu.SMEM),
             pl.BlockSpec((n_state, tiles, LANE), lambda s: (0, 0, 0)),
         ],
         out_specs=pl.BlockSpec((1, n_state, tiles, LANE), lambda s: (s, 0, 0, 0)),
         out_shape=jax.ShapeDtypeStruct((seqs, n_state, tiles, LANE), jnp.float32),
+        scratch_shapes=[held, held],
         compiler_params=pltpu.CompilerParams(vmem_limit_bytes=32 * 2**20),
     )(step, drive, rows, rate)
 
@@ -138,6 +148,9 @@
     prior_ref,
     mixed_ref,
     carried,
+    step_held,
+    input_held,
+    mixed_held,
 ):
     base = (pl.program_id(0) * blocks + pl.program_id(1)) * groups * SUB * n_state
 
@@ -147,9 +160,11 @@
 
     def one(group, states):
         states = list(states)
+        stage_in(step_ref, group, step_held)
+        stage_in(input_ref, group, input_held)
         for at in range(SUB):
-            step = token_row(step_ref, group, at, tiles)
-            drive = step * token_row(input_ref, group, at, tiles)
+            step = token_row(step_held, at, tiles)
+            drive = step * token_row(input_held, at, tiles)
             mixed = [None] * 2
             for n in range(n_state):
                 where = base + (group * SUB + at) * n_state + n
@@ -158,7 +173,8 @@
                 states[n] = decay * states[n] + drive * brow_ref[where]
                 term = states[n] * crow_ref[where]
                 mixed[n % 2] = term if mixed[n % 2] is None else mixed[n % 2] + term
-            mixed_ref[group, pl.ds(at, tiles, stride=SUB), :] = mixed[0] + mixed[1]
+            mixed_held[pl.ds(at, tiles, stride=SUB), :] = mixed[0] + mixed[1]
+        stage_out(mixed_held, mixed_ref, group)
         return tuple(states)
 
     states = lax.fori_loop(0, groups, one, tuple(carried[n] for n in range(n_state)))
@@ -168,10 +184,11 @@
 
 def scan_forward(start, step, inputs, b_rows, c_rows, rate, seqs):
     n_state, tiles, _ = rate.shape
-    all_groups = step.shape[0]
+    all_groups = step.shape[0] // SUB
     groups = math.gcd(all_groups // seqs, 4)
     blocks = all_groups // seqs // groups
-    tile_spec = pl.BlockSpec((groups, tiles * SUB, LANE), lambda s, b: (s * blocks + b, 0, 0))
+    rows_spec = pl.BlockSpec((groups * SUB, tiles * LANE), lambda s, b: (s * blocks + b, 0))
+    held = pltpu.VMEM((tiles * SUB, LANE), jnp.float32)
     smem = pl.BlockSpec(memory_space=pltpu.SMEM)
     tokens = all_groups * SUB
     return pl.pallas_call(
@@ -179,8 +196,8 @@
         grid=(seqs, blocks),
         in_specs=[
             pl.BlockSpec((1, n_state, tiles, LANE), lambda s, b: (s, 0, 0, 0)),
-            tile_spec,
-            tile_spec,
+            rows_spec,
+            rows_spec,
             smem,
             smem,
             pl.BlockSpec((n_state, tiles, LANE), lambda s, b: (0, 0, 0)),
@@ -189,13 +206,13 @@
             pl.BlockSpec(
                 (groups * SUB, n_state, tiles, LANE), lambda s, b: (s * blocks + b, 0, 0, 0)
             ),
-            tile_spec,
+            rows_spec,
         ],
         out_shape=[
             jax.ShapeDtypeStruct((tokens, n_state, tiles, LANE), jnp.float32),
             jax.ShapeDtypeStruct(step.shape, jnp.float32),
         ],
-        scratch_shapes=[pltpu.VMEM((n_state, tiles, LANE), jnp.float32)],
+        scratch_shapes=[pltpu.VMEM((n_state, tiles, LANE), jnp.float32)] + [held] * 3,
         compiler_params=pltpu.CompilerParams(vmem_limit_bytes=32 * 2**20),
     )(start, step, inputs, b_rows, c_rows, rate)
 
@@ -219,6 +236,11 @@
     rate_grad_ref,
     part_ref,
     carried,
+    step_held,
+    input_held,
+    ograd_held,
+    step_grad_held,
+    input_grad_held,
 ):
     block = blocks - 1 - pl.program_id(1)
     base = (pl.program_id(0) * blocks + block) * groups * SUB * n_state
@@ -234,10 +256,13 @@
     def one(turn, grads):
         group = groups - 1 - turn
         grads = list(grads)
+        stage_in(step_ref, group, step_held)
+        stage_in(input_ref, group, input_held)
+        stage_in(ograd_ref, group, ograd_held)
         for at in range(SUB - 1, -1, -1):
-            step = token_row(step_ref, group, at, tiles)
-            value = token_row(input_ref, group, at, tiles)
-            ograd = token_row(ograd_ref, group, at, tiles)
+            step = token_row(step_held, at, tiles)
+            value = token_row(input_held, at, tiles)
+            ograd = token_row(ograd_held, at, tiles)
             drive = step * value
             along_b = None
             along_rate = None
@@ -258,14 +283,14 @@
                 along_b = by_brow if along_b is None else along_b + by_brow
                 brow_parts.append(grad * drive)
                 crow_parts.append(ograd * state)
-            step_grad_ref[group, pl.ds(at, tiles, stride=SUB), :] = (
-                along_rate * LN2 + along_b * value
-            )
-            input_grad_ref[group, pl.ds(at, tiles, stride=SUB), :] = along_b * step
+            step_grad_held[pl.ds(at, tiles, stride=SUB), :] = along_rate * LN2 + along_b * value
+            input_grad_held[pl.ds(at, tiles, stride=SUB), :] = along_b * step
             parts = jnp.concatenate(brow_parts + crow_parts, 0).astype(jnp.bfloat16)
             part_ref[group * SUB + at] = jnp.dot(
                 picks_ref[...], parts, preferred_element_type=jnp.float32
             )
+        stage_out(step_grad_held, step_grad_ref, group)
+        stage_out(input_grad_held, input_grad_ref, group)
         return tuple(grads)
 
     grads = lax.fori_loop(0, groups, one, tuple(carried[n] for n in range(n_state)))
@@ -275,14 +300,15 @@
 
 def scan_backward(end_grad, prior, step, inputs, ograd, b_rows, c_rows, rate, seqs):
     n_state, tiles, _ = rate.shape
-    all_groups = step.shape[0]
+    all_groups = step.shape[0] // SUB
     groups = math.gcd(all_groups // seqs, 4)
     blocks = all_groups // seqs // groups
 
     def at(s, b):
         return s * blocks + blocks - 1 - b
 
-    tile_spec = pl.BlockSpec((groups, tiles * SUB, LANE), lambda s, b: (at(s, b), 0, 0))
+    rows_spec = pl.BlockSpec((groups * SUB, tiles * LANE), lambda s, b: (at(s, b), 0))
+    held = pltpu.VMEM((tiles * SUB, LANE), jnp.float32)
     smem = pl.BlockSpec(memory_space=pltpu.SMEM)
     tokens = all_groups * SUB
     picks = jnp.repeat(jnp.eye(2 * n_state, dtype=jnp.bfloat16), tiles, 1)
@@ -292,17 +318,17 @@
         in_specs=[
             pl.BlockSpec((1, n_state, tiles, LANE), lambda s, b: (s, 0, 0, 0)),
             pl.BlockSpec((groups * SUB, n_state, tiles, LANE), lambda s, b: (at(s, b), 0, 0, 0)),
-            tile_spec,
-            tile_spec,
-            tile_spec,
+            rows_spec,
+            rows_spec,
+            rows_spec,
             smem,
             smem,
             pl.BlockSpec((n_state, tiles, LANE), lambda s, b: (0, 0, 0)),
             pl.BlockSpec(picks.shape, lambda s, b: (0, 0)),
         ],
         out_specs=[
-            tile_spec,
-            tile_spec,
+            rows_spec,
+            rows_spec,
             pl.BlockSpec((n_state, tiles, LANE), lambda s, b: (0, 0, 0)),
             pl.BlockSpec((groups * SUB, 2 * n_state, LANE), lambda s, b: (at(s, b), 0, 0)),
         ],
@@ -312,7 +338,7 @@
             jax.ShapeDtypeStruct(rate.shape, jnp.float32),
             jax.ShapeDtypeStruct((tokens, 2 * n_state, LANE), jnp.float32),
         ],
-        scratch_shapes=[pltpu.VMEM((n_state, tiles, LANE), jnp.float32)],
+        scratch_shapes=[pltpu.VMEM((n_state, tiles, LANE), jnp.float32)] + [held] * 5,
         compiler_params=pltpu.CompilerParams(vmem_limit_bytes=32 * 2**20),
     )(end_grad, prior, step, inputs, ograd, b_rows, c_rows, rate, picks)
 
@@ -468,12 +494,11 @@
 
 
 def after_mixer_back(sums, whole, own):
-    (normed_grad, ffn_out), (tokens_in,), (middle, middle_grad, gain) = sums, whole, own
+    (normed_grad, ffn_out, gains), (tokens_in,), (middle, middle_grad, gain) = sums, whole, own
     hidden_in = tokens_in.astype(jnp.float32)
     scale = inverse_rms(hidden_in)
-    gain_grad = jnp.sum(normed_grad * hidden_in * scale, 0, keepdims=True)
     tokens_grad = middle_grad + norm_back(normed_grad, hidden_in, scale, gain.astype(jnp.float32))
-    return tokens_grad, middle + ffn_out, gain_grad
+    return tokens_grad, middle + ffn_out, gains
 
 
 def as_they_are(sums, whole, own):
@@ -527,9 +552,11 @@
     hidden_in = tokens_rows.astype(jnp.float32)
     scale_one = inverse_rms(hidden_in)
     normed_one = (hidden_in * scale_one * gain_mix).astype(low)
-    normed_one_cols = swapped_columns(normed_one)
     ct_low = cotangent.reshape(rows, width)
-    ct_cols = swapped_columns(ct_low)
+    normed_one_cols, ct_cols = swapped_columns(normed_one), swapped_columns(ct_low)
+    normed_one, normed_one_cols, ct_cols = lax.optimization_barrier(
+        (normed_one, normed_one_cols, ct_cols)
+    )
     conv_in = matmul(normed_one, mix_pack[:, :inner]).astype(low)
     gate_mix = matmul(normed_one, mix_pack[:, inner : 2 * inner])
     conv_seqs = conv_in.reshape(seqs, span, inner)
@@ -561,11 +588,10 @@
     span_decay = jnp.exp(
         decay_rate[None] * jnp.sum(step_size.reshape(seqs, span, inner), 1)[:, None]
     ).reshape(seqs, n_state, tiles, LANE)
-    step_tiles, input_tiles = to_tiles(step_size), to_tiles(scan_float)
-    ends = scan_ends(step_tiles, input_tiles, b_rows, rate, seqs, False)
+    ends = scan_ends(step_size, scan_float, b_rows, rate, seqs, False)
     start = from_earlier(ends, span_decay, 1)
-    prior, mixed_tiles = scan_forward(start, step_tiles, input_tiles, b_rows, c_rows, rate, seqs)
-    mixer_core = from_tiles(mixed_tiles) + skip_weight[None] * scan_float
+    prior, scan_out = scan_forward(start, step_size, scan_float, b_rows, c_rows, rate, seqs)
+    mixer_core = scan_out + skip_weight[None] * scan_float
     gate_sig = jax.nn.silu(gate_mix)
     gated = (mixer_core * gate_sig).astype(low)
     out_weights = mix_pack[:, 2 * inner :]
@@ -588,8 +614,12 @@
     gate_grad = (act_grad * up_ffn * silu_slope(gate_ffn)).astype(low)
     up_grad = (act_grad * jax.nn.silu(gate_ffn)).astype(low)
     ffn_grads = jnp.concatenate([gate_grad, up_grad], 1)
-    ffn_all = gathered_rows(jnp.concatenate([activated, ffn_grads, gated], 1))
+    ffn_sent, ffn_grads = lax.optimization_barrier(
+        (jnp.concatenate([activated, ffn_grads, gated], 1), ffn_grads)
+    )
+    ffn_all = gathered_rows(ffn_sent)
     normed_two_part = matmul_nt(ffn_grads, gate_up).astype(low)
+    normed_two_part, normed_two_cols = lax.optimization_barrier((normed_two_part, normed_two_cols))
     ffn_part = matmul_nt(activated, down_weights).astype(low)
     middle_low, middle_grad, ffngain_part = exchange(
         ("tp",),
@@ -609,14 +639,14 @@
     core_grad = gated_grad * gate_sig
     gate_mix_grad = (gated_grad * mixer_core * silu_slope(gate_mix)).astype(low)
     grad_skipgain = jnp.sum(core_grad * scan_float, 0)
-    ograd_tiles = to_tiles(core_grad)
-    back_ends = scan_ends(step_tiles, ograd_tiles, c_rows, rate, seqs, True)
+    back_ends = scan_ends(step_size, core_grad, c_rows, rate, seqs, True)
     end_grad = from_earlier(back_ends, span_decay, -1)
-    step_grad_tiles, input_grad_tiles, rate_grad, parts = scan_backward(
-        end_grad, prior, step_tiles, input_tiles, ograd_tiles, b_rows, c_rows, rate, seqs
+    end_grad, middle_cols = lax.optimization_barrier((end_grad, middle_cols))
+    step_grad, input_grad, rate_grad, parts = scan_backward(
+        end_grad, prior, step_size, scan_float, core_grad, b_rows, c_rows, rate, seqs
     )
     grad_decaylog = rate_grad.reshape(n_state, inner) * decay_rate
-    pre_grad = from_tiles(step_grad_tiles) * jax.nn.sigmoid(step_pre)
+    pre_grad = step_grad * jax.nn.sigmoid(step_pre)
     grad_stepbias = jnp.sum(pre_grad, 0)
     pre_low = pre_grad.astype(low)
     grad_stepproj = matmul_tn(step_low, pre_low)
@@ -640,7 +670,7 @@
     grad_selproj = matmul_tn(select_low, scan_in)
     scan_in_grad = (
         core_grad * skip_weight[None]
-        + from_tiles(input_grad_tiles)
+        + input_grad
         + matmul_nt(select_low, select_weights)
     )
     conv_grad = scan_in_grad * silu_slope(conv_out)
@@ -662,36 +692,11 @@
         .reshape(rows, inner)
     )
     mix_grads = jnp.concatenate([conv_in_grad, gate_mix_grad], 1)
-    mix_all = gathered_rows(mix_grads)
-    normed_one_part = matmul_nt(mix_grads, mix_pack[:, : 2 * inner]).astype(low)
-    ffn_part, _ = lax.optimization_barrier((ffn_part, normed_one_part))
-    tokens_grad, layer_out, mixgain_part = exchange(
-        ("tp",),
-        4,
-        [normed_one_part, ffn_part],
-        [tokens_rows],
-        [middle, middle_grad, gain_mix_row],
-        after_mixer_back,
-        [
-            ("all", (rows, width), low),
-            ("all", (rows, width), low),
-            ("rows", (1, width), jnp.float32),
-        ],
-    )
-    grad_downproj = matmul_tn(ffn_all[:, :hidden], ct_cols)
-    grad_gateup = jnp.stack(
-        [
-            matmul_tn(normed_two_cols, ffn_all[:, hidden : 2 * hidden]),
-            matmul_tn(normed_two_cols, ffn_all[:, 2 * hidden : 3 * hidden]),
-        ]
-    )
-    grad_outproj = matmul_tn(ffn_all[:, 3 * hidden :], middle_cols)
-    grad_inproj = jnp.stack(
-        [
-            matmul_tn(normed_one_cols, mix_all[:, :inner]),
-            matmul_tn(normed_one_cols, mix_all[:, inner:]),
-        ]
-    )
+    mix_sent, ffn_all = lax.optimization_barrier((mix_grads, ffn_all))
+    mix_all = gathered_rows(mix_sent)
+    normed_one_part = matmul_nt(mix_grads, mix_pack[:, : 2 * inner])
+    mixgain_part = jnp.sum(normed_one_part * hidden_in * scale_one, 0)
+    normed_one_part = normed_one_part.astype(low)
     small = [
         grad_convkern,
         grad_convbias[None],
@@ -700,6 +705,8 @@
         grad_skipgain[None],
         grad_stepproj,
         grad_selproj[:columns],
+        mixgain_part.reshape(-1, inner),
+        ffngain_part.reshape(-1, inner),
     ]
     sizes = [part.shape[0] for part in small]
     share = 16 * math.prod(lax.axis_size(axis) for axis in PLANE)
@@ -713,7 +720,35 @@
     for size in sizes:
         smalls.append(small[at : at + size])
         at += size
-    gains = lax.psum(jnp.concatenate([mixgain_part, ffngain_part], 0), PLANE + ("tp",))
+    gain_rows = jnp.concatenate(smalls[7:9], 0).reshape(-1, LANE)
+    tokens_grad, layer_out, gains = exchange(
+        ("tp",),
+        4,
+        [normed_one_part, ffn_part, gain_rows],
+        [tokens_rows],
+        [middle, middle_grad, gain_mix_row],
+        after_mixer_back,
+        [
+            ("all", (rows, width), low),
+            ("all", (rows, width), low),
+            ("all", gain_rows.shape, jnp.float32),
+        ],
+    )
+    gains = gains.reshape(2, width)
+    grad_downproj = matmul_tn(ffn_all[:, :hidden], ct_cols)
+    grad_gateup = jnp.stack(
+        [
+            matmul_tn(normed_two_cols, ffn_all[:, hidden : 2 * hidden]),
+            matmul_tn(normed_two_cols, ffn_all[:, 2 * hidden : 3 * hidden]),
+        ]
+    )
+    grad_outproj = matmul_tn(ffn_all[:, 3 * hidden :], middle_cols)
+    grad_inproj = jnp.stack(
+        [
+            matmul_tn(normed_one_cols, mix_all[:, :inner]),
+            matmul_tn(normed_one_cols, mix_all[:, inner:]),
+        ]
+    )
     return (
         layer_out.reshape(tokens.shape),
         tokens_grad.reshape(tokens.shape),

time: 679 us -> 648 us (0.954)
  blocking collectives: 44.5 us -> 0 us
  waiting for transfers between devices: 113 us -> 125 us
    psum x1 -> x0, blocking collectives: 44.5 us -> none  [per_device(): lax.psum(jnp.concatenate([mixgain_part, ffngain_part], 0), PLANE + ('tp',))]
    all_gather x4, waiting for transfers between devices: 81.1 us -> 46.2 us  [gathered_rows(): return lax.all_gather(rows, PLANE, axis=0, tiled=True)]
    all_to_all x4, waiting for transfers between devices: 22.1 us -> 54.3 us  [swapped_columns(): return lax.all_to_all(rows, PLANE, split_axis=1, concat_axis=0, tiled=True)]
    ppermute x4, waiting for transfers between devices: 9.92 us -> 24.8 us  [passed_along(): lax.ppermute(value, axis, [(source, source + steps) for source in range(f...]
    reshape x10 -> x3, local copies, waits for them, and re-layouts: 8.6 us -> 0.04 us  [the longest x1 0.01 us: per_device(): ffngain_part.reshape(-1, inner)]
    unnamed x142 -> x149, local copies, waits for them, and re-layouts: 28.6 us -> 33.3 us
  transfers between devices with their start and end apart: 12 -> 12, of which waited for: 10 -> 9; matrix products, arithmetic and copies ran while one was open for 15% -> 19% of each run, Pallas kernels for 29% -> 45%
where the time goes in v3:
time: 648 us; the launch traced here: 640 us
  Pallas kernels  286 us (44%)
  waiting for transfers between devices  125 us (19%)
  matrix products  104 us (16%)
  local copies, waits for them, and re-layouts  54.7 us (8%)
  starting transfers between devices  28.6 us (4%)
  other arithmetic  26 us (4%)
  between operations  15.1 us (2%)
    pallas_call x6, Pallas kernels, exchange(): pl.pallas_call(functools.partial(exchange_kernel, axes, count, (len(parts...  250 us
    all_to_all x4, waiting for transfers between devices, swapped_columns(): return lax.all_to_all(rows, PLANE, split_axis=1, concat_axis=0, tiled=True)  54.3 us
    all_gather x4, waiting for transfers between devices, gathered_rows(): return lax.all_gather(rows, PLANE, axis=0, tiled=True)  46.2 us
    dot_general x7, matrix products, matmul(): return jnp.dot(left, right, preferred_element_type=jnp.float32)  40.6 us
    dot_general x6, matrix products, matmul_nt(): lax.dot_general(left, right, (((1,), (1,)), ((), ())), preferred_element_...  33.3 us
    unnamed x149, local copies, waits for them, and re-layouts  33.3 us
    dot_general x8, matrix products, matmul_tn(): lax.dot_general(left, right, (((0,), (0,)), ((), ())), preferred_element_...  29.7 us
    ppermute x4, waiting for transfers between devices, passed_along(): lax.ppermute(value, axis, [(source, source + steps) for source in range(f...  24.8 us
  transfers between devices with their start and end apart: 12, of which 9 were waited for; matrix products, arithmetic and copies ran while one was open for 19% of the time, Pallas kernels for 45%

profile of v3, /device:TPU:0, one launch (start us, length us, event | category | flops | bytes accessed | tf_op | source)
XLA Modules:
  0.0 639.8 jit_solution(3081275714364386271)
XLA Ops:
  22.5 5.2 all-to-all-start
  29.2 23.9 %all-to-all-done = bf16[256,8,256]{2,0,1:T(8,128)(2,1)S(1)} async-done(((bf16[256,8,256]{2,0,1:T(8,128)(2,1)}), bf16[256,8,256]{2,0,1:T(8,128)(2,1)S(1)}, u32[]{:S(2)}, u32[]{:S(2)}) %all-to-all-start) | async-done | bytes 1048608 | tf_op jit(solution)/shard_map/all_to_all | solution.py:369
  58.1 23.6 %all-to-all-done.1 = bf16[256,8,256]{2,0,1:T(8,128)(2,1)S(1)} async-done(((bf16[256,8,256]{2,0,1:T(8,128)(2,1)}), bf16[256,8,256]{2,0,1:T(8,128)(2,1)S(1)}, u32[]{:S(2)}, u32[]{:S(2)}) %all-to-all-start.1) | async-done | bytes 1048608 | tf_op jit(solution)/shard_map/all_to_all | solution.py:369
  81.7 27.9 %all-gather.5.cloned.1.call-done = bf16[2048,3072]{0,1:T(8,128)(2,1)} async-done(((bf16[256,3072]{0,1:T(8,128)(2,1)}), bf16[2048,3072]{0,1:T(8,128)(2,1)}) %all-gather.5.cloned.1.call-update) | async-done | bytes 12582928 | tf_op jit(solution)/shard_map/all_gather | solution.py:365
  120.5 14.6 %shard_map.262 = f32[256,256]{1,0:T(8,128)S(1)} custom-call(f32[256,256]{1,0:T(8,128)S(1)} %fusion.75.refs_0_), custom_call_target="tpu_custom_call" | custom-call | tf_op jit(solution)/shard_map/pallas_call | solution.py:460
  139.3 5.3 shard_map.263
  144.6 4.7 collective-permute-start.1
  154.2 7.3 %shard_map.264 = (f32[256,16,8,128]{3,2,1,0:T(8,128)S(1)}, f32[256,1024]{1,0:T(8,128)S(1)}) custom-call(f32[2,16,8,128]{3,2,1,0:T(8,128)} %collective-permute-done.1.start_ref, f32[256,1024]{1,0:T(8,128)S(1)} %get-tuple-element.104.step_ref, f32[256,1024]{1,0:T(8,128)S(1)} %get-tuple-element.75.drive_ref.input_ref, f32[4096]{0:T(1024)S(1)} %reshape.144.rows_ref.brow_ref, ...), custom_call_target="tpu_custom_call" | custom-call | tf_op jit(solution)/shard_map/pallas_call | solution.py:194
  161.5 6.4 copy-done.2
  167.9 7.0 %multiply_convert_fusion.4 = (bf16[256,1024]{1,0:T(8,128)(2,1)S(1)}, f32[256,1024]{1,0:T(8,128)}) fusion(f32[256,1024]{1,0:T(8,128)S(1)} %get-tuple-element.41, bf16[256,1024]{1,0:T(8,128)(2,1)} %copy-done.38, f32[1024]{0:T(1024)S(1)} %convert_element_type.117, bf16[256,2048]{1,0:T(8,128)(2,1)} %fusion.49, bf16[2048,3072]{0,1:T(8,128)(2,1)} %all-gather.5.cloned.1.call-done), kind=kOutput, calls=%fused_computation.87 | convolution fusion | flops 1076101120 | bytes 8392704 | tf_op jit(solution)/shard_map/dot_general | solution.py:26
  178.7 45.9 %shard_map.265 = (bf16[256,2048]{1,0:T(8,128)(2,1)S(1)}, f32[64,2048]{1,0:T(8,128)S(1)}) custom-call(bf16[256,2048]{1,0:T(8,128)(2,1)S(1)} %fusion.42.refs_0_, bf16[256,2048]{1,0:T(8,128)(2,1)S(1)} %bitcast.140, bf16[1,2048]{1,0:T(2,128)(2,1)S(1)} %reshape.147.refs_2_.refs_3_), custom_call_target="tpu_custom_call" | custom-call | tf_op jit(solution)/shard_map/pallas_call | solution.py:460
  226.3 18.3 %all-gather.7.cloned.1.call-done = bf16[2048,6144]{0,1:T(8,128)(2,1)} async-done(((bf16[256,6144]{0,1:T(8,128)(2,1)}), bf16[2048,6144]{0,1:T(8,128)(2,1)}) %all-gather.7.cloned.1.call-update) | async-done | bytes 25165840 | tf_op jit(solution)/shard_map/all_gather | solution.py:365
  244.7 12.6 %fusion.2 = f32[256,4096]{1,0:T(8,128)} fusion(bf16[256,2048]{1,0:T(8,128)(2,1)} %copy-done.18, bf16[2048,6144]{0,1:T(8,128)(2,1)} %all-gather.7.cloned.1.call-done), kind=kOutput, calls=%fused_computation.2 | convolution fusion | flops 4294967296 | bytes 22020096 | tf_op jit(solution)/shard_map/dot_general | solution.py:26
  257.3 7.9 %multiply_convert_fusion.1 = (bf16[256,2048]{1,0:T(8,128)(2,1)S(1)}, bf16[256,2048]{1,0:T(8,128)(2,1)S(1)}, bf16[256,2048]{1,0:T(8,128)(2,1)S(1)}) fusion(f32[256,4096]{1,0:T(8,128)} %fusion.2, bf16[256,2048]{1,0:T(8,128)(2,1)} %bitcast.142, bf16[2048,6144]{0,1:T(8,128)(2,1)} %all-gather.7.cloned.1.call-done), kind=kOutput, calls=%fused_computation.52 | convolution fusion | flops 2155347968 | bytes 16777216 | tf_op jit(solution)/shard_map/dot_general | solution.py:26
  271.2 4.7 all-to-all-start.2
  275.8 15.0 %fusion.39.refs_0_ = bf16[256,2048]{1,0:T(8,128)(2,1)} fusion(bf16[256,4096]{1,0:T(8,128)(2,1)} %pad_maximum_fusion.3, bf16[2048,6144]{0,1:T(8,128)(2,1)} %all-gather.7.cloned.1.call-done), kind=kOutput, calls=%fused_computation.39 | convolution fusion | flops 4295491584 | bytes 19922944 | tf_op jit(solution)/shard_map/dot_general | solution.py:30
  290.8 6.8 %all-to-all-done.2 = bf16[256,8,256]{2,0,1:T(8,128)(2,1)} async-done(((bf16[256,8,256]{2,0,1:T(8,128)(2,1)}), bf16[256,8,256]{2,0,1:T(8,128)(2,1)}, u32[]{:S(2)}, u32[]{:S(2)}) %all-to-all-start.2) | async-done | bytes 1048608 | tf_op jit(solution)/shard_map/all_to_all | solution.py:369
  301.1 46.2 %shard_map.266 = (bf16[256,2048]{1,0:T(8,128)(2,1)S(1)}, f32[64,2048]{1,0:T(8,128)S(1)}, f32[1,2048]{1,0:T(1,128)S(1)}) custom-call(bf16[256,2048]{1,0:T(8,128)(2,1)S(1)} %copy-done.22, bf16[256,2048]{1,0:T(8,128)(2,1)S(1)} %bitcast.144, f32[64,2048]{1,0:T(8,128)S(1)} %copy-done.10, bf16[1,2048]{1,0:T(2,128)(2,1)S(1)} %reshape.147.refs_2_.refs_3_), custom_call_target="tpu_custom_call" | custom-call | tf_op jit(solution)/shard_map/pallas_call | solution.py:460
  349.4 4.2 all-to-all-start.3
  353.7 6.4 multiply_reduce_fusion.1
  360.1 5.2 shard_map.267
  369.7 15.5 %collective-permute-done.2.end_ref = f32[2,16,8,128]{3,2,1,0:T(8,128)} collective-permute-done((f32[2,16,8,128]{3,2,1,0:T(8,128)}, f32[2,16,8,128]{3,2,1,0:T(8,128)}, u32[]{:S(2)}, u32[]{:S(2)}) %collective-permute-start.2) | collective-permute-done | bytes 131104 | tf_op jit(solution)/shard_map/ppermute | solution.py:22
  386.5 18.6 %shard_map.268 = (f32[256,1024]{1,0:T(8,128)S(1)}, f32[256,1024]{1,0:T(8,128)S(1)}, f32[16,8,128]{2,1,0:T(8,128)S(1)}, f32[256,32,128]{2,1,0:T(8,128)S(1)}) custom-call(f32[2,16,8,128]{3,2,1,0:T(8,128)} %collective-permute-done.2.end_ref, f32[256,16,8,128]{3,2,1,0:T(8,128)} %copy-done.2, f32[256,1024]{1,0:T(8,128)S(1)} %get-tuple-element.104.step_ref, ...), custom_call_target="tpu_custom_call" | custom-call | tf_op jit(solution)/shard_map/pallas_call | solution.py:315
  415.3 17.1 %shard_map.269 = bf16[256,256]{1,0:T(8,128)(2,1)S(1)} custom-call(bf16[256,256]{1,0:T(8,128)(2,1)S(1)} %maximum_maximum_fusion.refs_0_), custom_call_target="tpu_custom_call" | custom-call | tf_op jit(solution)/shard_map/pallas_call | solution.py:460
  441.6 7.1 %fusion.45.refs_1_ = bf16[256,2048]{1,0:T(8,128)(2,1)} fusion(bf16[256,2048]{1,0:T(8,128)(2,1)} %copy-done.47, bf16[2048,6144]{0,1:T(8,128)(2,1)} %all-gather.7.cloned.1.call-done), kind=kOutput, calls=%fused_computation.41 | convolution fusion | flops 2148007936 | bytes 10485760 | tf_op jit(solution)/shard_map/dot_general | solution.py:30
  451.2 6.8 %fusion.51 = (bf16[2048]{0:T(1024)(128)(2,1)S(1)}, bf16[256,2048]{1,0:T(8,128)(2,1)}) fusion(f32[256]{0:T(256)S(1)} %copy-done.62, bf16[2,128,2048]{2,1,0:T(8,128)(2,1)S(1)} %copy-done.1, bf16[2048,3072]{0,1:T(8,128)(2,1)} %all-gather.5.cloned.1.call-done, bf16[256,1024]{1,0:T(8,128)(2,1)S(1)} %copy-done.56, bf16[256,1024]{1,0:T(8,128)(2,1)S(1)} %bitcast.161), kind=kOutput, calls=%fused_computation.45 | convolution fusion | flops 2152200192 | bytes 11539456 | tf_op jit(solution)/shard_map/dot_general | solution.py:30
  459.7 32.3 %shard_map.270 = bf16[384,1024]{1,0:T(8,128)(2,1)S(1)} custom-call(bf16[384,1024]{1,0:T(8,128)(2,1)S(1)} %concatenate.37.refs_0_), custom_call_target="tpu_custom_call" | custom-call | tf_op jit(solution)/shard_map/pallas_call | solution.py:460
  498.3 94.0 %shard_map.271 = (bf16[256,2048]{1,0:T(8,128)(2,1)S(1)}, bf16[256,2048]{1,0:T(8,128)(2,1)S(1)}, f32[32,128]{1,0:T(8,128)S(1)}) custom-call(bf16[256,2048]{1,0:T(8,128)(2,1)S(1)} %copy-done.24, bf16[256,2048]{1,0:T(8,128)(2,1)S(1)} %copy-done.23, f32[32,128]{1,0:T(8,128)S(1)} %reshape.155.refs_2_, bf16[256,2048]{1,0:T(8,128)(2,1)S(1)} %bitcast.141, ...), custom_call_target="tpu_custom_call" | custom-call | tf_op jit(solution)/shard_map/pallas_call | solution.py:460
  597.1 6.1 fusion.36
  603.2 6.1 fusion.33
  611.6 4.8 fusion.24
  616.4 7.3 %fusion.6 = f32[2048,256]{1,0:T(8,128)} fusion(bf16[2048,256]{1,0:T(8,128)(2,1)S(1)} %bitcast.166, bf16[2048,7168]{1,0:T(8,128)(2,1)} %all-gather.9.cloned.1.call-done), kind=kOutput, calls=%fused_computation.6 | convolution fusion | flops 2147483648 | bytes 11534336 | tf_op jit(solution)/shard_map/dot_general | solution.py:36
  (245 shorter events, 110.0 us)
Async XLA Ops:
  7.2 129.5 %copy-start = (bf16[128,1024]{1,0:T(8,128)(2,1)S(1)}, bf16[128,1024]{1,0:T(8,128)(2,1)}, u32[]{:S(2)}) copy-start(bf16[128,1024]{1,0:T(8,128)(2,1)} %param.21) | copy-start | bytes 786436
  7.2 102.4 %all-gather.5.cloned.1.call-start = ((), (), s32[]{:S(2)}) async-start(), calls=%async_computation.4 | async-start | bytes 14155776 | tf_op jit(solution)/shard_map/all_gather | solution.py:365
  10.3 234.4 %all-gather.7.cloned.1.call-start = ((), (), s32[]{:S(2)}) async-start(), calls=%async_computation.5 | async-start | bytes 28311552 | tf_op jit(solution)/shard_map/all_gather | solution.py:365
  19.0 37.8 %copy-start.61 = (f32[256]{0:T(256)}, f32[256]{0:T(256)S(1)}, u32[]{:S(2)}) copy-start(f32[256]{0:T(256)S(1)} %rsqrt_bitcast_fusion) | copy-start | bytes 3076
  19.0 8.7 %copy-start.7 = (bf16[2,128,2048]{2,1,0:T(8,128)(2,1)S(1)}, bf16[2,128,2048]{2,1,0:T(8,128)(2,1)}, u32[]{:S(2)}) copy-start(bf16[2,128,2048]{2,1,0:T(8,128)(2,1)} %param.29) | copy-start | bytes 3145732
  22.5 30.6 %all-to-all-start = ((bf16[256,8,256]{2,0,1:T(8,128)(2,1)}), bf16[256,8,256]{2,0,1:T(8,128)(2,1)S(1)}, u32[]{:S(2)}, u32[]{:S(2)}) async-start(bf16[256,8,256]{2,0,1:T(8,128)(2,1)} %copy.56), calls=%async_computation | async-start | bytes 2097152 | tf_op jit(solution)/shard_map/all_to_all | solution.py:369
  27.8 29.0 %copy-start.57 = (bf16[1024,16]{0,1:T(8,128)(2,1)S(1)}, bf16[1024,16]{0,1:T(8,128)(2,1)}, u32[]{:S(2)}) copy-start(bf16[1024,16]{0,1:T(8,128)(2,1)} %param.23) | copy-start | bytes 98308
  53.1 60.2 %copy-start.48 = (bf16[256,8,256]{2,0,1:T(8,128)(2,1)}, bf16[256,8,256]{2,0,1:T(8,128)(2,1)S(1)}, u32[]{:S(2)}) copy-start(bf16[256,8,256]{2,0,1:T(8,128)(2,1)S(1)} %all-to-all-done) | copy-start | bytes 3145732
  53.1 28.6 %all-to-all-start.1 = ((bf16[256,8,256]{2,0,1:T(8,128)(2,1)}), bf16[256,8,256]{2,0,1:T(8,128)(2,1)S(1)}, u32[]{:S(2)}, u32[]{:S(2)}) async-start(bf16[256,8,256]{2,0,1:T(8,128)(2,1)} %copy.57), calls=%async_computation.1 | async-start | bytes 2097152 | tf_op jit(solution)/shard_map/all_to_all | solution.py:369
  56.7 384.7 %all-gather.9.cloned.1.call-start = ((), (), s32[]{:S(2)}) async-start(), calls=%async_computation.6 | async-start | bytes 33030144 | tf_op jit(solution)/shard_map/all_gather | solution.py:365
  81.7 31.7 %copy-start.50 = (bf16[256,8,256]{2,0,1:T(8,128)(2,1)}, bf16[256,8,256]{2,0,1:T(8,128)(2,1)S(1)}, u32[]{:S(2)}) copy-start(bf16[256,8,256]{2,0,1:T(8,128)(2,1)S(1)} %all-to-all-done.1) | copy-start | bytes 3145732
  81.7 35.1 %copy-start.60 = (bf16[4,1024]{1,0:T(4,128)(2,1)S(1)}, bf16[4,1024]{1,0:T(4,128)(2,1)}, u32[]{:S(2)}) copy-start(bf16[4,1024]{1,0:T(4,128)(2,1)} %param.18) | copy-start | bytes 24580
  81.7 35.1 %copy-start.64 = (bf16[1024]{0:T(1024)(128)(2,1)S(1)}, bf16[1024]{0:T(1024)(128)(2,1)}, u32[]{:S(2)}) copy-start(bf16[1024]{0:T(1024)(128)(2,1)} %param.19) | copy-start | bytes 6148
  81.7 35.2 %copy-start.65 = (bf16[1024]{0:T(1024)(128)(2,1)S(1)}, bf16[1024]{0:T(1024)(128)(2,1)}, u32[]{:S(2)}) copy-start(bf16[1024]{0:T(1024)(128)(2,1)} %param.22) | copy-start | bytes 6148
  113.4 4.8 collective-permute-start
  120.5 28.8 %copy-start.66 = (bf16[1024]{0:T(1024)(128)(2,1)S(1)}, bf16[1024]{0:T(1024)(128)(2,1)}, u32[]{:S(2)}) copy-start(bf16[1024]{0:T(1024)(128)(2,1)} %param.24) | copy-start | bytes 6148
  120.5 28.8 %copy-start.63 = (bf16[2048]{0:T(1024)(128)(2,1)S(1)}, bf16[2048]{0:T(1024)(128)(2,1)}, u32[]{:S(2)}) copy-start(bf16[2048]{0:T(1024)(128)(2,1)} %param.26) | copy-start | bytes 12292
  144.6 9.6 %collective-permute-start.1 = (f32[2,16,8,128]{3,2,1,0:T(8,128)}, f32[2,16,8,128]{3,2,1,0:T(8,128)}, u32[]{:S(2)}, u32[]{:S(2)}) collective-permute-start(f32[2,16,8,128]{3,2,1,0:T(8,128)} %shard_map.263), channel_id=1, source_target_pairs={{0,4},{1,5},{2,6},{3,7},{8,12},{9,13},{10,14},{11,15},{16,20},{17,... | collective-permute-start | bytes 393224 | tf_op jit(solution)/shard_map/ppermute | solution.py:22
  271.2 26.5 %all-to-all-start.2 = ((bf16[256,8,256]{2,0,1:T(8,128)(2,1)}), bf16[256,8,256]{2,0,1:T(8,128)(2,1)}, u32[]{:S(2)}, u32[]{:S(2)}) async-start(bf16[256,8,256]{2,0,1:T(8,128)(2,1)} %bitcast.156), calls=%async_computation.2 | async-start | bytes 2097152 | tf_op jit(solution)/shard_map/all_to_all | solution.py:369
  349.4 35.9 %all-to-all-start.3 = ((bf16[256,8,256]{2,0,1:T(8,128)(2,1)}), bf16[256,8,256]{2,0,1:T(8,128)(2,1)}, u32[]{:S(2)}, u32[]{:S(2)}) async-start(bf16[256,8,256]{2,0,1:T(8,128)(2,1)} %bitcast.155), calls=%async_computation.3 | async-start | bytes 2097152 | tf_op jit(solution)/shard_map/all_to_all | solution.py:369
  353.6 270.0 %all-gather.11.cloned.1.call-start = ((), (), s32[]{:S(2)}) async-start(), calls=%async_computation.7 | async-start | bytes 9437184 | tf_op jit(solution)/shard_map/all_gather | solution.py:365
  366.3 19.0 %collective-permute-start.2 = (f32[2,16,8,128]{3,2,1,0:T(8,128)}, f32[2,16,8,128]{3,2,1,0:T(8,128)}, u32[]{:S(2)}, u32[]{:S(2)}) collective-permute-start(f32[2,16,8,128]{3,2,1,0:T(8,128)} %shard_map.267), channel_id=1, source_target_pairs={{4,0},{5,1},{6,2},{7,3},{12,8},{13,9},{14,10},{15,11},{20,16},{21,... | collective-permute-start | bytes 393224 | tf_op jit(solution)/shard_map/ppermute | solution.py:22
  409.7 22.7 %copy-start.46 = (bf16[1024,160]{0,1:T(8,128)(2,1)S(1)}, bf16[1024,160]{0,1:T(8,128)(2,1)}, u32[]{:S(2)}) copy-start(bf16[1024,160]{0,1:T(8,128)(2,1)} %param.20) | copy-start | bytes 983044
  413.2 19.5 %copy-start.5 = (f32[256,1024]{1,0:T(8,128)S(1)}, f32[256,1024]{1,0:T(8,128)}, u32[]{:S(2)}) copy-start(f32[256,1024]{1,0:T(8,128)} %copy-done.3) | copy-start | bytes 3145732
  413.2 19.5 %copy-start.26 = (f32[256,1024]{1,0:T(8,128)S(1)}, f32[256,1024]{1,0:T(8,128)}, u32[]{:S(2)}) copy-start(f32[256,1024]{1,0:T(8,128)} %copy-done.25) | copy-start | bytes 3145732
  413.2 19.5 %copy-start.37 = (f32[2,128,1024]{2,1,0:T(8,128)S(1)}, f32[2,128,1024]{2,1,0:T(8,128)}, u32[]{:S(2)}) copy-start(f32[2,128,1024]{2,1,0:T(8,128)} %copy-done.36) | copy-start | bytes 3145732
  414.9 17.8 %copy-start.40 = (bf16[256,1024]{1,0:T(8,128)(2,1)}, bf16[256,1024]{1,0:T(8,128)(2,1)S(1)}, u32[]{:S(2)}) copy-start(bf16[256,1024]{1,0:T(8,128)(2,1)S(1)} %get-tuple-element.72) | copy-start | bytes 1572868
  434.2 5.9 collective-permute-start.3
  458.1 36.6 %copy-start.11 = (f32[64,2048]{1,0:T(8,128)S(1)}, f32[64,2048]{1,0:T(8,128)}, u32[]{:S(2)}) copy-start(f32[64,2048]{1,0:T(8,128)} %copy-done.9) | copy-start | bytes 1572868
  592.3 10.9 %copy-start.14 = (bf16[256,2048]{1,0:T(8,128)(2,1)}, bf16[256,2048]{1,0:T(8,128)(2,1)S(1)}, u32[]{:S(2)}) copy-start(bf16[256,2048]{1,0:T(8,128)(2,1)S(1)} %get-tuple-element.56) | copy-start | bytes 3145732
  592.3 10.9 %copy-start.16 = (bf16[256,2048]{1,0:T(8,128)(2,1)}, bf16[256,2048]{1,0:T(8,128)(2,1)S(1)}, u32[]{:S(2)}) copy-start(bf16[256,2048]{1,0:T(8,128)(2,1)S(1)} %get-tuple-element.55) | copy-start | bytes 3145732
  616.4 7.3 %copy-start.49 = (bf16[256,8,256]{2,0,1:T(8,128)(2,1)S(1)}, bf16[256,8,256]{2,0,1:T(8,128)(2,1)}, u32[]{:S(2)}) copy-start(bf16[256,8,256]{2,0,1:T(8,128)(2,1)} %copy-done.48) | copy-start | bytes 3145732
  (50 other events, 124.6 us)
Sparse Core Ops, SparseCore 0:
  10.5 99.0 all-gather.4
  112.0 132.5 all-gather.6
  269.0 162.9 all-gather.8
  441.6 63.1 all-gather.10

commit v4 on v3

--- a/solution.py
+++ b/solution.py
@@ -385,83 +385,121 @@
     return where
 
 
-def exchange_kernel(axes, count, counts, kinds, middle, *refs):
+def greet(groups):
+    barrier = pltpu.get_barrier_semaphore()
+    total = 0
+    for axes, others in groups:
+        for other in others:
+            pl.semaphore_signal(
+                barrier,
+                inc=1,
+                device_id=device_at(axes, other),
+                device_id_type=pl.DeviceIdType.MESH,
+            )
+            total += 1
+    pl.semaphore_wait(barrier, total)
+
+
+def sent(source, target, send_sem, recv_sem, where):
+    copy = pltpu.make_async_remote_copy(
+        src_ref=source,
+        dst_ref=target,
+        send_sem=send_sem,
+        recv_sem=recv_sem,
+        device_id=where,
+        device_id_type=pl.DeviceIdType.MESH,
+    )
+    copy.start()
+    return copy
+
+
+def finish(copies):
+    for copy in copies:
+        copy.wait()
+
+
+def rows_of(ref, index, count):
+    rows = ref.shape[0] // count
+    return ref.at[pl.ds(pl.multiple_of(index * rows, rows), rows), :]
+
+
+class Group:
+    def __init__(self, axes, send_sem, recv_sem):
+        self.axes = axes
+        self.count = math.prod(lax.axis_size(axis) for axis in axes)
+        self.me = place_in(axes)
+        self.others = [lax.rem(self.me + hop, self.count) for hop in range(1, self.count)]
+        self.send_sem, self.recv_sem = send_sem, recv_sem
+
+    def own(self, ref):
+        return rows_of(ref, self.me, self.count)
+
+    def one(self, source, target, which, hop):
+        return sent(
+            source,
+            target,
+            self.send_sem.at[which, hop],
+            self.recv_sem.at[which, hop],
+            device_at(self.axes, self.others[hop]),
+        )
+
+    def scatter(self, part, slot, which):
+        return [
+            self.one(rows_of(part, other, self.count), slot.at[hop], which, hop)
+            for hop, other in enumerate(self.others)
+        ]
+
+    def total(self, part, slot):
+        total = self.own(part)[...].astype(jnp.float32)
+        for hop in range(self.count - 1):
+            total = total + slot[hop].astype(jnp.float32)
+        return total
+
+    def spread(self, ref, which):
+        return [self.one(self.own(ref), self.own(ref), which, hop) for hop in range(self.count - 1)]
+
+
+def exchange_kernel(axes, counts, kinds, middle, *refs):
     n_parts, n_whole, n_own = counts
     parts, refs = refs[:n_parts], refs[n_parts:]
     whole, refs = refs[:n_whole], refs[n_whole:]
     own, refs = refs[:n_own], refs[n_own:]
     outs, refs = refs[: len(kinds)], refs[len(kinds) :]
     slots, refs = refs[:n_parts], refs[n_parts:]
-    send_sem, recv_sem = refs
-    me = place_in(axes)
-    peers = [lax.rem(me + hop, count) for hop in range(1, count)]
-
-    barrier = pltpu.get_barrier_semaphore()
-    for peer in peers:
-        pl.semaphore_signal(
-            barrier,
-            inc=1,
-            device_id=device_at(axes, peer),
-            device_id_type=pl.DeviceIdType.MESH,
-        )
-    pl.semaphore_wait(barrier, count - 1)
-
-    def rows_of(ref, index):
-        rows = ref.shape[0] // count
-        return ref.at[pl.ds(pl.multiple_of(index * rows, rows), rows), :]
-
-    def send(source, target, which, hop, peer):
-        copy = pltpu.make_async_remote_copy(
-            src_ref=source,
-            dst_ref=target,
-            send_sem=send_sem.at[which, hop],
-            recv_sem=recv_sem.at[which, hop],
-            device_id=device_at(axes, peer),
-            device_id_type=pl.DeviceIdType.MESH,
-        )
-        copy.start()
-        return copy
-
+    group = Group(axes, *refs)
+    greet([(axes, group.others)])
     copies = []
     for which, (part, slot) in enumerate(zip(parts, slots)):
-        for hop, peer in enumerate(peers):
-            copies.append(send(rows_of(part, peer), slot.at[hop], which, hop, peer))
-    for copy in copies:
-        copy.wait()
-    sums = []
-    for part, slot in zip(parts, slots):
-        total = rows_of(part, me)[...].astype(jnp.float32)
-        for hop in range(count - 1):
-            total = total + slot[hop].astype(jnp.float32)
-        sums.append(total)
-    results = middle(sums, [rows_of(ref, me)[...] for ref in whole], [ref[...] for ref in own])
+        copies += group.scatter(part, slot, which)
+    finish(copies)
+    sums = [group.total(part, slot) for part, slot in zip(parts, slots)]
+    results = middle(sums, [group.own(ref)[...] for ref in whole], [ref[...] for ref in own])
     copies = []
     for which, (ref, kind, value) in enumerate(zip(outs, kinds, results)):
         if kind == "rows":
             ref[...] = value.astype(ref.dtype)
         else:
-            rows_of(ref, me)[...] = value.astype(ref.dtype)
-            for hop, peer in enumerate(peers):
-                copies.append(
-                    send(rows_of(ref, me), rows_of(ref, me), n_parts + which, hop, peer)
-                )
-    for copy in copies:
-        copy.wait()
+            group.own(ref)[...] = value.astype(ref.dtype)
+            copies += group.spread(ref, n_parts + which)
+    finish(copies)
+
+
+def slots_for(part, count):
+    return pltpu.VMEM((count - 1, part.shape[0] // count) + part.shape[1:], part.dtype)
+
+
+def group_size(axes):
+    return math.prod(lax.axis_size(axis) for axis in axes)
 
 
 def exchange(axes, call_id, parts, whole, own, middle, outs):
-    count = math.prod(lax.axis_size(axis) for axis in axes)
+    count = group_size(axes)
     vmem = pl.BlockSpec(memory_space=pltpu.VMEM)
-    scratch = [
-        pltpu.VMEM((count - 1, part.shape[0] // count) + part.shape[1:], part.dtype)
-        for part in parts
-    ]
-    sems = (len(parts) + len(outs), count - 1)
+    sems = pltpu.SemaphoreType.DMA((len(parts) + len(outs), count - 1))
     return pl.pallas_call(
         functools.partial(
             exchange_kernel,
             axes,
-            count,
             (len(parts), len(whole), len(own)),
             [kind for kind, _, _ in outs],
             middle,
@@ -469,12 +507,359 @@
         in_specs=[vmem] * (len(parts) + len(whole) + len(own)),
         out_specs=[vmem] * len(outs),
         out_shape=[jax.ShapeDtypeStruct(shape, dtype) for _, shape, dtype in outs],
-        scratch_shapes=scratch
-        + [pltpu.SemaphoreType.DMA(sems), pltpu.SemaphoreType.DMA(sems)],
+        scratch_shapes=[slots_for(part, count) for part in parts] + [sems, sems],
         compiler_params=pltpu.CompilerParams(
             collective_id=call_id, has_side_effects=True, vmem_limit_bytes=40 * 2**20
         ),
     )(*parts, *whole, *own)
+
+
+class PlaneGather:
+    def __init__(self, own, gathered, send_sem, recv_sem):
+        self.own, self.gathered = own, gathered
+        self.send_sem, self.recv_sem = send_sem, recv_sem
+        self.dp, self.ctx = lax.axis_index("dp"), lax.axis_index("ctx")
+        self.n_dp, self.n_ctx = lax.axis_size("dp"), lax.axis_size("ctx")
+        self.hands_on = relayed()
+        self.count = self.n_dp * self.n_ctx
+        self.me = self.dp * self.n_ctx + self.ctx
+        self.others = [lax.rem(self.me + hop, self.count) for hop in range(1, self.count)]
+        self.copies = {}
+        if self.hands_on:
+            core = lax.rem(self.dp, 2)
+            over_core = self.dp + 1 - 2 * core
+            over_y = lax.rem(self.dp + 2, 4)
+            over_x = 1 - self.ctx
+            self.core = {"dp": over_core, "ctx": self.ctx}
+            self.at_x = {"dp": self.dp, "ctx": over_x}
+            self.at_y = {"dp": over_y, "ctx": self.ctx}
+            self.from_x = self.dp * 2 + over_x
+            self.from_y = over_y * 2 + self.ctx
+            self.across = over_y * 2 + over_x
+
+    def part(self, owner, half):
+        rows = self.gathered.shape[0] // self.count
+        start, size = owner * rows, rows
+        if half is not None:
+            size = rows // 2
+            start = start + half * size
+        return self.gathered.at[pl.ds(pl.multiple_of(start, size), size), :]
+
+    def send(self, which, owner, half, where):
+        target = self.part(owner, half)
+        source = target
+        if owner is self.me:
+            rows = self.own.shape[0]
+            source = self.own
+            if half is not None:
+                source = self.own.at[pl.ds(half * (rows // 2), rows // 2), :]
+        self.copies[which] = sent(
+            source, target, self.send_sem.at[which], self.recv_sem.at[which], where
+        )
+
+    def arrived(self, *which):
+        for one in which:
+            self.copies[one].wait_recv()
+
+    def begin(self, local_sem):
+        self.local = pltpu.make_async_copy(self.own, self.part(self.me, None), local_sem)
+        self.local.start()
+        if not self.hands_on:
+            for hop, other in enumerate(self.others):
+                self.send(hop, self.me, None, device_at(PLANE, other))
+            return
+        self.send(0, self.me, 1, self.at_x)
+        self.send(1, self.me, 0, self.at_y)
+        self.send(2, self.me, None, self.core)
+        self.send(3, self.me, 0, self.at_x)
+        self.send(4, self.me, 1, self.at_y)
+
+    def relay(self):
+        if not self.hands_on:
+            return
+        self.arrived(0, 1)
+        self.send(5, self.from_x, 1, self.at_y)
+        self.send(6, self.from_y, 0, self.at_x)
+        self.send(7, self.from_x, 1, self.core)
+        self.send(8, self.from_y, 0, self.core)
+
+    def hand_over(self):
+        if not self.hands_on:
+            return
+        self.arrived(3, 4)
+        self.send(9, self.from_x, 0, self.core)
+        self.send(10, self.from_y, 1, self.core)
+
+    def hand_over_last(self):
+        if not self.hands_on:
+            return
+        self.arrived(5, 6)
+        self.send(11, self.across, 1, self.core)
+        self.send(12, self.across, 0, self.core)
+
+    def end(self):
+        if self.hands_on:
+            self.arrived(2, 7, 8, 9, 10, 11, 12)
+        else:
+            self.arrived(*range(self.count - 1))
+        for copy in self.copies.values():
+            copy.wait_send()
+        self.local.wait()
+
+
+def relayed():
+    return lax.axis_size("dp") == 4 and lax.axis_size("ctx") == 2
+
+
+def gather_sems():
+    count = 13 if relayed() else group_size(PLANE) - 1
+    return pltpu.SemaphoreType.DMA((count,))
+
+
+WIDE = 512
+
+
+def products(source, first, last, dot, target, block_buf, block_sem, out_buf, out_sem):
+    def fetch(j, slot):
+        columns = pl.ds(pl.multiple_of(j * WIDE, WIDE), WIDE)
+        return pltpu.make_async_copy(
+            source.at[:, columns], block_buf.at[slot], block_sem.at[slot]
+        )
+
+    def store(j, slot):
+        return pltpu.make_async_copy(out_buf.at[slot], target(j), out_sem.at[slot])
+
+    fetch(first, first % 2).start()
+
+    @pl.loop(first, last)
+    def _(j):
+        slot = lax.rem(j, 2)
+
+        @pl.when(j + 1 < last)
+        def _():
+            fetch(j + 1, 1 - slot).start()
+
+        fetch(j, slot).wait()
+
+        @pl.when(j >= first + 2)
+        def _():
+            store(j - 2, slot).wait()
+
+        out_buf[slot] = dot(block_buf[slot])
+        store(j, slot).start()
+
+    for j in range(max(first, last - 2), last):
+        store(j, j % 2).wait()
+
+
+def tail_kernel(
+    sizes,
+    mix_grads,
+    normed_part,
+    ffn_part,
+    small,
+    tokens,
+    middle_rows,
+    middle_grad,
+    gain_row,
+    one_cols,
+    two_cols,
+    ct_cols,
+    middle_cols,
+    ffn_all,
+    tokens_grad,
+    layer_out,
+    small_sum,
+    gains,
+    mix_all,
+    grad_inproj,
+    grad_outproj,
+    grad_gateup,
+    grad_downproj,
+    normed_slots,
+    ffn_slots,
+    small_slots,
+    gain_slots,
+    gain_own,
+    block_buf,
+    wide_buf,
+    tall_buf,
+    block_sem,
+    wide_sem,
+    tall_sem,
+    tp_send,
+    tp_recv,
+    plane_send,
+    plane_recv,
+    gather_send,
+    gather_recv,
+    local_sem,
+):
+    inner, hidden, gain_at = sizes
+    tp = Group(("tp",), tp_send, tp_recv)
+    plane = Group(PLANE, plane_send, plane_recv)
+    gather = PlaneGather(mix_grads, mix_all, gather_send, gather_recv)
+    greet([(("tp",), tp.others), (PLANE, plane.others)])
+
+    def flat(lhs):
+        return lambda block: lax.dot_general(
+            lhs[...], block, (((0,), (0,)), ((), ())), preferred_element_type=jnp.float32
+        )
+
+    def tall(rhs):
+        return lambda block: lax.dot_general(
+            block, rhs[...], (((0,), (0,)), ((), ())), preferred_element_type=jnp.float32
+        )
+
+    def side_by_side(ref, first):
+        per = ref.shape[2] // WIDE
+
+        def target(j):
+            at = j - first
+            columns = pl.ds(pl.multiple_of(lax.rem(at, per) * WIDE, WIDE), WIDE)
+            return ref.at[lax.div(at, per), :, columns]
+
+        return target
+
+    def one_above_other(ref, first):
+        return lambda j: ref.at[pl.ds(pl.multiple_of((j - first) * WIDE, WIDE), WIDE), :]
+
+    wide = (block_buf, block_sem, wide_buf, wide_sem)
+    high = (block_buf, block_sem, tall_buf, tall_sem)
+    down_end = hidden // WIDE
+    gu_end = 3 * hidden // WIDE
+    out_end = gu_end + inner // WIDE
+
+    normed_sent = tp.scatter(normed_part, normed_slots, 0)
+    gather.begin(local_sem)
+    ffn_sent = tp.scatter(ffn_part, ffn_slots, 1)
+    small_sent = plane.scatter(small, small_slots, 0)
+    products(
+        ffn_all, down_end, gu_end, flat(two_cols), side_by_side(grad_gateup, down_end), *wide
+    )
+    gather.relay()
+    products(ffn_all, 0, down_end, tall(ct_cols), one_above_other(grad_downproj, 0), *high)
+    gather.hand_over()
+    finish(normed_sent)
+    hidden_in = tp.own(tokens)[...].astype(jnp.float32)
+    tp.own(tokens_grad)[...] = (
+        middle_grad[...]
+        + norm_back(
+            tp.total(normed_part, normed_slots),
+            hidden_in,
+            inverse_rms(hidden_in),
+            gain_row[...].astype(jnp.float32),
+        )
+    ).astype(tokens_grad.dtype)
+    tokens_sent = tp.spread(tokens_grad, 2)
+    finish(small_sent)
+    plane.own(small_sum)[...] = plane.total(small, small_slots).astype(small_sum.dtype)
+    small_sent = plane.spread(small_sum, 1)
+    products(
+        ffn_all, gu_end, out_end, tall(middle_cols), one_above_other(grad_outproj, gu_end), *high
+    )
+    gather.hand_over_last()
+    finish(ffn_sent)
+    tp.own(layer_out)[...] = (middle_rows[...] + tp.total(ffn_part, ffn_slots)).astype(
+        layer_out.dtype
+    )
+    layer_sent = tp.spread(layer_out, 3)
+    finish(small_sent)
+    gain_own[...] = small_sum[pl.ds(gain_at, gain_own.shape[0]), :].astype(jnp.float32)
+    gain_sent = [tp.one(gain_own, gain_slots.at[hop], 4, hop) for hop in range(tp.count - 1)]
+    gather.end()
+    products(
+        mix_all, 0, 2 * inner // WIDE, flat(one_cols), side_by_side(grad_inproj, 0), *wide
+    )
+    finish(gain_sent)
+    total = gain_own[...]
+    for hop in range(tp.count - 1):
+        total = total + gain_slots[hop]
+    gains[...] = total
+    finish(tokens_sent)
+    finish(layer_sent)
+
+
+def run_tail(
+    call_id,
+    gain_at,
+    mix_grads,
+    normed_part,
+    ffn_part,
+    small,
+    tokens,
+    middle_rows,
+    middle_grad,
+    gain_row,
+    one_cols,
+    two_cols,
+    ct_cols,
+    middle_cols,
+    ffn_all,
+):
+    inner = mix_grads.shape[1] // 2
+    hidden = (ffn_all.shape[1] - inner) // 3
+    share = one_cols.shape[1]
+    all_rows = ffn_all.shape[0]
+    tp_count, plane_count = group_size(("tp",)), group_size(PLANE)
+    low, full = jnp.bfloat16, jnp.float32
+    vmem = pl.BlockSpec(memory_space=pltpu.VMEM)
+    hbm = pl.BlockSpec(memory_space=pl.ANY)
+    gain_rows = 16
+    dma = pltpu.SemaphoreType.DMA
+    return pl.pallas_call(
+        functools.partial(tail_kernel, (inner, hidden, gain_at)),
+        in_specs=[vmem] * 12 + [hbm],
+        out_specs=[vmem] * 4 + [hbm] * 5,
+        out_shape=[
+            jax.ShapeDtypeStruct(tokens.shape, low),
+            jax.ShapeDtypeStruct(tokens.shape, low),
+            jax.ShapeDtypeStruct(small.shape, low),
+            jax.ShapeDtypeStruct((gain_rows, inner), full),
+            jax.ShapeDtypeStruct((all_rows, 2 * inner), low),
+            jax.ShapeDtypeStruct((2, share, inner), full),
+            jax.ShapeDtypeStruct((inner, share), full),
+            jax.ShapeDtypeStruct((2, share, hidden), full),
+            jax.ShapeDtypeStruct((hidden, share), full),
+        ],
+        scratch_shapes=[
+            slots_for(normed_part, tp_count),
+            slots_for(ffn_part, tp_count),
+            slots_for(small, plane_count),
+            pltpu.VMEM((tp_count - 1, gain_rows, inner), full),
+            pltpu.VMEM((gain_rows, inner), full),
+            pltpu.VMEM((2, all_rows, WIDE), low),
+            pltpu.VMEM((2, share, WIDE), full),
+            pltpu.VMEM((2, WIDE, share), full),
+            dma((2,)),
+            dma((2,)),
+            dma((2,)),
+            dma((5, tp_count - 1)),
+            dma((5, tp_count - 1)),
+            dma((2, plane_count - 1)),
+            dma((2, plane_count - 1)),
+            gather_sems(),
+            gather_sems(),
+            dma(()),
+        ],
+        compiler_params=pltpu.CompilerParams(
+            collective_id=call_id, has_side_effects=True, vmem_limit_bytes=56 * 2**20
+        ),
+    )(
+        mix_grads,
+        normed_part,
+        ffn_part,
+        small,
+        tokens,
+        middle_rows,
+        middle_grad,
+        gain_row,
+        one_cols,
+        two_cols,
+        ct_cols,
+        middle_cols,
+        ffn_all,
+    )
 
 
 def after_mixer(sums, whole, own):
@@ -491,14 +876,6 @@
         normed_grad, middle, scale, gain.astype(jnp.float32)
     )
     return middle_grad, middle_grad, gain_grad
-
-
-def after_mixer_back(sums, whole, own):
-    (normed_grad, ffn_out, gains), (tokens_in,), (middle, middle_grad, gain) = sums, whole, own
-    hidden_in = tokens_in.astype(jnp.float32)
-    scale = inverse_rms(hidden_in)
-    tokens_grad = middle_grad + norm_back(normed_grad, hidden_in, scale, gain.astype(jnp.float32))
-    return tokens_grad, middle + ffn_out, gains
 
 
 def as_they_are(sums, whole, own):
@@ -692,8 +1069,6 @@
         .reshape(rows, inner)
     )
     mix_grads = jnp.concatenate([conv_in_grad, gate_mix_grad], 1)
-    mix_sent, ffn_all = lax.optimization_barrier((mix_grads, ffn_all))
-    mix_all = gathered_rows(mix_sent)
     normed_one_part = matmul_nt(mix_grads, mix_pack[:, : 2 * inner])
     mixgain_part = jnp.sum(normed_one_part * hidden_in * scale_one, 0)
     normed_one_part = normed_one_part.astype(low)
@@ -709,46 +1084,44 @@
         ffngain_part.reshape(-1, inner),
     ]
     sizes = [part.shape[0] for part in small]
-    share = 16 * math.prod(lax.axis_size(axis) for axis in PLANE)
-    small.append(jnp.zeros((-sum(sizes) % share, inner), jnp.float32))
+    gain_at = sum(sizes[:-2]) + -sum(sizes[:-2]) % 16
+    small.insert(-2, jnp.zeros((gain_at - sum(sizes[:-2]), inner), jnp.float32))
     small = jnp.concatenate(small, 0).astype(low)
-    (small,) = exchange(
-        PLANE, 5, [small], [], [], as_they_are, [("all", small.shape, low)]
+    share = 16 * group_size(PLANE)
+    small = jnp.pad(small, ((0, -(gain_at + 16) % share + 16 - sum(sizes[-2:])), (0, 0)))
+    (
+        tokens_grad,
+        layer_out,
+        small,
+        gains,
+        _,
+        grad_inproj,
+        grad_outproj,
+        grad_gateup,
+        grad_downproj,
+    ) = run_tail(
+        4,
+        gain_at,
+        mix_grads,
+        normed_one_part,
+        ffn_part,
+        small,
+        tokens_rows,
+        middle,
+        middle_grad,
+        gain_mix_row,
+        normed_one_cols,
+        normed_two_cols,
+        ct_cols,
+        middle_cols,
+        ffn_all,
     )
     small = small.astype(jnp.float32)
     smalls, at = [], 0
-    for size in sizes:
+    for size in sizes[:-2]:
         smalls.append(small[at : at + size])
         at += size
-    gain_rows = jnp.concatenate(smalls[7:9], 0).reshape(-1, LANE)
-    tokens_grad, layer_out, gains = exchange(
-        ("tp",),
-        4,
-        [normed_one_part, ffn_part, gain_rows],
-        [tokens_rows],
-        [middle, middle_grad, gain_mix_row],
-        after_mixer_back,
-        [
-            ("all", (rows, width), low),
-            ("all", (rows, width), low),
-            ("all", gain_rows.shape, jnp.float32),
-        ],
-    )
-    gains = gains.reshape(2, width)
-    grad_downproj = matmul_tn(ffn_all[:, :hidden], ct_cols)
-    grad_gateup = jnp.stack(
-        [
-            matmul_tn(normed_two_cols, ffn_all[:, hidden : 2 * hidden]),
-            matmul_tn(normed_two_cols, ffn_all[:, 2 * hidden : 3 * hidden]),
-        ]
-    )
-    grad_outproj = matmul_tn(ffn_all[:, 3 * hidden :], middle_cols)
-    grad_inproj = jnp.stack(
-        [
-            matmul_tn(normed_one_cols, mix_all[:, :inner]),
-            matmul_tn(normed_one_cols, mix_all[:, inner:]),
-        ]
-    )
+    gains = gains[: sum(sizes[-2:])].reshape(2, width)
     return (
         layer_out.reshape(tokens.shape),
         tokens_grad.reshape(tokens.shape),

time: 648 us -> 589 us (0.909)
  matrix products: 104 us -> 71.9 us
  Pallas kernels: 286 us -> 265 us
    dot_general x8 -> x2, matrix products: 29.7 us -> 0.58 us  [matmul_tn(): lax.dot_general(left, right, (((0,), (0,)), ((), ())), preferred_element_...]
    pallas_call x6 -> x5, Pallas kernels: 250 us -> 228 us  [the longest x4 124 us: exchange(): pl.pallas_call(functools.partial(exchange_kernel, axes, (len(parts), len(...]
    unnamed x149 -> x144, local copies, waits for them, and re-layouts: 33.3 us -> 36.5 us
    all_gather x4 -> x3, waiting for transfers between devices: 46.2 us -> 46.2 us  [gathered_rows(): return lax.all_gather(rows, PLANE, axis=0, tiled=True)]
  transfers between devices with their start and end apart: 12 -> 11, of which waited for: 9 -> 9; matrix products, arithmetic and copies ran while one was open for 19% -> 15% of each run, Pallas kernels for 45% -> 28%
where the time goes in v4:
time: 589 us; the launch traced here: 582 us
  Pallas kernels  265 us (45%)
  waiting for transfers between devices  123 us (21%)
  matrix products  71.9 us (12%)
  local copies, waits for them, and re-layouts  55.8 us (9%)
  starting transfers between devices  28.6 us (5%)
  other arithmetic  22.9 us (4%)
  between operations  15.2 us (3%)
    pallas_call x4, Pallas kernels, exchange(): pl.pallas_call(functools.partial(exchange_kernel, axes, (len(parts), len(...  124 us
    pallas_call x1, Pallas kernels, run_tail(): pl.pallas_call(functools.partial(tail_kernel, (inner, hidden, gain_at)),...  105 us
    all_to_all x4, waiting for transfers between devices, swapped_columns(): return lax.all_to_all(rows, PLANE, split_axis=1, concat_axis=0, tiled=True)  58 us
    all_gather x3, waiting for transfers between devices, gathered_rows(): return lax.all_gather(rows, PLANE, axis=0, tiled=True)  46.2 us
    dot_general x7, matrix products, matmul(): return jnp.dot(left, right, preferred_element_type=jnp.float32)  39.6 us
    unnamed x144, local copies, waits for them, and re-layouts  36.5 us
    dot_general x6, matrix products, matmul_nt(): lax.dot_general(left, right, (((1,), (1,)), ((), ())), preferred_element_...  31.7 us
    pallas_call x1, Pallas kernels, scan_backward(): pl.pallas_call(functools.partial(backward_kernel, n_state, tiles, groups,...  18.7 us
  transfers between devices with their start and end apart: 11, of which 9 were waited for; matrix products, arithmetic and copies ran while one was open for 15% of the time, Pallas kernels for 28%

profile of v4, /device:TPU:0, one launch (start us, length us, event | category | flops | bytes accessed | tf_op | source)
XLA Modules:
  0.0 582.1 jit_solution(9004689709936708210)
XLA Ops:
  19.0 3.7 fusion.35
  22.7 5.2 all-to-all-start
  29.4 23.7 %all-to-all-done = bf16[256,8,256]{2,0,1:T(8,128)(2,1)S(1)} async-done(((bf16[256,8,256]{2,0,1:T(8,128)(2,1)}), bf16[256,8,256]{2,0,1:T(8,128)(2,1)S(1)}, u32[]{:S(2)}, u32[]{:S(2)}) %all-to-all-start) | async-done | bytes 1048608 | tf_op jit(solution)/shard_map/all_to_all | solution.py:369
  53.1 3.6 all-to-all-start.1
  58.1 23.6 %all-to-all-done.1 = bf16[256,8,256]{2,0,1:T(8,128)(2,1)S(1)} async-done(((bf16[256,8,256]{2,0,1:T(8,128)(2,1)}), bf16[256,8,256]{2,0,1:T(8,128)(2,1)S(1)}, u32[]{:S(2)}, u32[]{:S(2)}) %all-to-all-start.1) | async-done | bytes 1048608 | tf_op jit(solution)/shard_map/all_to_all | solution.py:369
  81.7 27.9 %all-gather.4.cloned.1.call-done = bf16[2048,3072]{0,1:T(8,128)(2,1)} async-done(((bf16[256,3072]{0,1:T(8,128)(2,1)}), bf16[2048,3072]{0,1:T(8,128)(2,1)}) %all-gather.4.cloned.1.call-update) | async-done | bytes 12582928 | tf_op jit(solution)/shard_map/all_gather | solution.py:365
  109.6 3.8 fusion.37
  121.0 14.6 %shard_map.262 = f32[256,256]{1,0:T(8,128)S(1)} custom-call(f32[256,256]{1,0:T(8,128)S(1)} %fusion.51.refs_0_), custom_call_target="tpu_custom_call" | custom-call | tf_op jit(solution)/shard_map/pallas_call | solution.py:499
  139.8 5.3 shard_map.263
  145.0 4.6 collective-permute-start.1
  150.7 3.9 collective-permute-done.1.start_ref
  154.6 7.3 %shard_map.264 = (f32[256,16,8,128]{3,2,1,0:T(8,128)S(1)}, f32[256,1024]{1,0:T(8,128)S(1)}) custom-call(f32[2,16,8,128]{3,2,1,0:T(8,128)} %collective-permute-done.1.start_ref, f32[256,1024]{1,0:T(8,128)S(1)} %get-tuple-element.108.step_ref, f32[256,1024]{1,0:T(8,128)S(1)} %get-tuple-element.81.drive_ref.input_ref, f32[4096]{0:T(1024)S(1)} %reshape.141.rows_ref.brow_ref, ...), custom_call_target="tpu_custom_call" | custom-call | tf_op jit(solution)/shard_map/pallas_call | solution.py:194
  161.9 6.8 %copy-done.2 = f32[256,16,8,128]{3,2,1,0:T(8,128)} copy-done((f32[256,16,8,128]{3,2,1,0:T(8,128)}, f32[256,16,8,128]{3,2,1,0:T(8,128)S(1)}, u32[]{:S(2)}) %copy-start.2) | copy-done | bytes 16777240
  168.7 6.1 %multiply_convert_fusion.4 = (bf16[256,1024]{1,0:T(8,128)(2,1)S(1)}, f32[256,1024]{1,0:T(8,128)}) fusion(f32[256,1024]{1,0:T(8,128)S(1)} %get-tuple-element.44, bf16[256,1024]{1,0:T(8,128)(2,1)S(1)} %copy-done.29, f32[1024]{0:T(1024)S(1)} %convert_element_type.119, bf16[256,2048]{1,0:T(8,128)(2,1)S(1)} %copy-done.46, ...), kind=kOutput, calls=%fused_computation.69 | convolution fusion | flops 1076101120 | bytes 8392704 | tf_op jit(solution)/shard_map/dot_general | solution.py:26
  174.8 3.8 fusion.24.refs_0_
  178.7 45.9 %shard_map.265 = (bf16[256,2048]{1,0:T(8,128)(2,1)S(1)}, f32[64,2048]{1,0:T(8,128)S(1)}) custom-call(bf16[256,2048]{1,0:T(8,128)(2,1)S(1)} %fusion.24.refs_0_, bf16[256,2048]{1,0:T(8,128)(2,1)S(1)} %bitcast.126, bf16[1,2048]{1,0:T(2,128)(2,1)S(1)} %reshape.144.refs_2_.refs_3_), custom_call_target="tpu_custom_call" | custom-call | tf_op jit(solution)/shard_map/pallas_call | solution.py:499
  226.3 18.3 %all-gather.6.cloned.1.call-done = bf16[2048,6144]{0,1:T(8,128)(2,1)} async-done(((bf16[256,6144]{0,1:T(8,128)(2,1)}), bf16[2048,6144]{0,1:T(8,128)(2,1)}) %all-gather.6.cloned.1.call-update) | async-done | bytes 25165840 | tf_op jit(solution)/shard_map/all_gather | solution.py:365
  244.7 12.6 %fusion.2 = f32[256,4096]{1,0:T(8,128)} fusion(bf16[256,2048]{1,0:T(8,128)(2,1)} %copy-done.13, bf16[2048,6144]{0,1:T(8,128)(2,1)} %all-gather.6.cloned.1.call-done), kind=kOutput, calls=%fused_computation.2 | convolution fusion | flops 4294967296 | bytes 22020096 | tf_op jit(solution)/shard_map/dot_general | solution.py:26
  257.3 7.9 %multiply_convert_fusion.1 = (bf16[256,2048]{1,0:T(8,128)(2,1)S(1)}, bf16[256,2048]{1,0:T(8,128)(2,1)S(1)}, bf16[256,2048]{1,0:T(8,128)(2,1)S(1)}) fusion(f32[256,4096]{1,0:T(8,128)} %fusion.2, bf16[256,2048]{1,0:T(8,128)(2,1)} %bitcast.127, bf16[2048,6144]{0,1:T(8,128)(2,1)} %all-gather.6.cloned.1.call-done), kind=kOutput, calls=%fused_computation.36 | convolution fusion | flops 2155347968 | bytes 16777216 | tf_op jit(solution)/shard_map/dot_general | solution.py:26
  273.9 4.5 all-to-all-start.2
  278.4 13.8 %fusion.21.refs_0_ = bf16[256,2048]{1,0:T(8,128)(2,1)} fusion(bf16[256,4096]{1,0:T(8,128)(2,1)} %pad_maximum_fusion.2, bf16[2048,6144]{0,1:T(8,128)(2,1)} %all-gather.6.cloned.1.call-done), kind=kOutput, calls=%fused_computation.24 | convolution fusion | flops 4295491584 | bytes 19922944 | tf_op jit(solution)/shard_map/dot_general | solution.py:30
  292.3 10.7 %all-to-all-done.2 = bf16[256,8,256]{2,0,1:T(8,128)(2,1)} async-done(((bf16[256,8,256]{2,0,1:T(8,128)(2,1)}), bf16[256,8,256]{2,0,1:T(8,128)(2,1)}, u32[]{:S(2)}, u32[]{:S(2)}) %all-to-all-start.2) | async-done | bytes 1048608 | tf_op jit(solution)/shard_map/all_to_all | solution.py:369
  306.5 46.3 %shard_map.266 = (bf16[256,2048]{1,0:T(8,128)(2,1)S(1)}, f32[64,2048]{1,0:T(8,128)S(1)}, f32[1,2048]{1,0:T(1,128)S(1)}) custom-call(bf16[256,2048]{1,0:T(8,128)(2,1)S(1)} %copy-done.17, bf16[256,2048]{1,0:T(8,128)(2,1)S(1)} %bitcast.129, f32[64,2048]{1,0:T(8,128)S(1)} %copy-done.10, bf16[1,2048]{1,0:T(2,128)(2,1)S(1)} %reshape.144.refs_2_.refs_3_), custom_call_target="tpu_custom_call" | custom-call | tf_op jit(solution)/shard_map/pallas_call | solution.py:499
  354.8 4.2 all-to-all-start.3
  359.0 6.3 %multiply_reduce_fusion.1 = (bf16[1024]{0:T(1024)(128)(2,1)S(1)}, f32[256,1024]{1,0:T(8,128)S(1)}, bf16[256,1024]{1,0:T(8,128)(2,1)}) fusion(bf16[256,1024]{1,0:T(8,128)(2,1)} %copy-done.28, f32[256,1024]{1,0:T(8,128)} %get-tuple-element.111, f32[256,1024]{1,0:T(8,128)} %copy-done.23, f32[1024]{0:T(1024)S(1)} %copy-done.56, ...), kind=kOutput, calls=%fused_computation.62 | convolution fusion | flops 1078197248 | bytes 9443328 | tf_op jit(solution)/shard_map/dot_general | solution.py:26
  365.3 5.2 shard_map.267
  371.8 6.7 %fusion.27.ffn_part = bf16[256,2048]{1,0:T(8,128)(2,1)} fusion(bf16[256,2048]{1,0:T(8,128)(2,1)S(1)} %copy-done.41, bf16[2048,6144]{0,1:T(8,128)(2,1)} %all-gather.6.cloned.1.call-done), kind=kOutput, calls=%fused_computation.26 | convolution fusion | flops 2148007936 | bytes 10485760 | tf_op jit(solution)/shard_map/dot_general | solution.py:30
  379.8 10.8 %collective-permute-done.2.end_ref = f32[2,16,8,128]{3,2,1,0:T(8,128)} collective-permute-done((f32[2,16,8,128]{3,2,1,0:T(8,128)}, f32[2,16,8,128]{3,2,1,0:T(8,128)}, u32[]{:S(2)}, u32[]{:S(2)}) %collective-permute-start.2) | collective-permute-done | bytes 131104 | tf_op jit(solution)/shard_map/ppermute | solution.py:22
  391.9 18.7 %shard_map.268 = (f32[256,1024]{1,0:T(8,128)S(1)}, f32[256,1024]{1,0:T(8,128)S(1)}, f32[16,8,128]{2,1,0:T(8,128)S(1)}, f32[256,32,128]{2,1,0:T(8,128)S(1)}) custom-call(f32[2,16,8,128]{3,2,1,0:T(8,128)} %collective-permute-done.2.end_ref, f32[256,16,8,128]{3,2,1,0:T(8,128)} %copy-done.2, f32[256,1024]{1,0:T(8,128)S(1)} %get-tuple-element.108.step_ref, ...), custom_call_target="tpu_custom_call" | custom-call | tf_op jit(solution)/shard_map/pallas_call | solution.py:315
  419.4 17.1 %shard_map.269 = bf16[256,256]{1,0:T(8,128)(2,1)S(1)} custom-call(bf16[256,256]{1,0:T(8,128)(2,1)S(1)} %maximum_maximum_fusion.refs_0_), custom_call_target="tpu_custom_call" | custom-call | tf_op jit(solution)/shard_map/pallas_call | solution.py:499
  444.2 6.8 %fusion.33 = (bf16[2048]{0:T(1024)(128)(2,1)S(1)}, bf16[256,2048]{1,0:T(8,128)(2,1)}) fusion(f32[256]{0:T(256)S(1)} %copy-done.59, bf16[2,128,2048]{2,1,0:T(8,128)(2,1)S(1)} %copy-done.1, bf16[2048,3072]{0,1:T(8,128)(2,1)} %all-gather.4.cloned.1.call-done, bf16[256,1024]{1,0:T(8,128)(2,1)S(1)} %copy-done.50, bf16[256,1024]{1,0:T(8,128)(2,1)S(1)} %bitcast.146), kind=kOutput, calls=%fused_computation.30 | convolution fusion | flops 2152200192 | bytes 11539456 | tf_op jit(solution)/shard_map/dot_general | solution.py:30
  454.1 104.6 %shard_map.270 = (bf16[256,2048]{1,0:T(8,128)(2,1)}, bf16[256,2048]{1,0:T(8,128)(2,1)}, bf16[384,1024]{1,0:T(8,128)(2,1)}, f32[16,1024]{1,0:T(8,128)}, bf16[2048...) custom-call(bf16[256,2048]{1,0:T(8,128)(2,1)} %pad_maximum_fusion.4., ...), custom_call_target="tpu_custom_call" | custom-call | tf_op jit(solution)/shard_map/pallas_call | solution.py:810
  (228 shorter events, 82.6 us)
Async XLA Ops:
  7.2 130.0 %copy-start = (bf16[128,1024]{1,0:T(8,128)(2,1)S(1)}, bf16[128,1024]{1,0:T(8,128)(2,1)}, u32[]{:S(2)}) copy-start(bf16[128,1024]{1,0:T(8,128)(2,1)} %param.21) | copy-start | bytes 786436
  7.2 102.4 %all-gather.4.cloned.1.call-start = ((), (), s32[]{:S(2)}) async-start(), calls=%async_computation.4 | async-start | bytes 14155776 | tf_op jit(solution)/shard_map/all_gather | solution.py:365
  10.3 234.4 %all-gather.6.cloned.1.call-start = ((), (), s32[]{:S(2)}) async-start(), calls=%async_computation.5 | async-start | bytes 28311552 | tf_op jit(solution)/shard_map/all_gather | solution.py:365
  19.0 37.8 %copy-start.58 = (f32[256]{0:T(256)}, f32[256]{0:T(256)S(1)}, u32[]{:S(2)}) copy-start(f32[256]{0:T(256)S(1)} %rsqrt_bitcast_fusion) | copy-start | bytes 3076
  19.0 8.9 %copy-start.7 = (bf16[2,128,2048]{2,1,0:T(8,128)(2,1)S(1)}, bf16[2,128,2048]{2,1,0:T(8,128)(2,1)}, u32[]{:S(2)}) copy-start(bf16[2,128,2048]{2,1,0:T(8,128)(2,1)} %param.29) | copy-start | bytes 3145732
  22.7 30.4 %all-to-all-start = ((bf16[256,8,256]{2,0,1:T(8,128)(2,1)}), bf16[256,8,256]{2,0,1:T(8,128)(2,1)S(1)}, u32[]{:S(2)}, u32[]{:S(2)}) async-start(bf16[256,8,256]{2,0,1:T(8,128)(2,1)} %fusion.35), calls=%async_computation | async-start | bytes 2097152 | tf_op jit(solution)/shard_map/all_to_all | solution.py:369
  28.3 28.5 %copy-start.51 = (bf16[1024,16]{0,1:T(8,128)(2,1)S(1)}, bf16[1024,16]{0,1:T(8,128)(2,1)}, u32[]{:S(2)}) copy-start(bf16[1024,16]{0,1:T(8,128)(2,1)} %param.23) | copy-start | bytes 98308
  53.1 28.6 %all-to-all-start.1 = ((bf16[256,8,256]{2,0,1:T(8,128)(2,1)}), bf16[256,8,256]{2,0,1:T(8,128)(2,1)S(1)}, u32[]{:S(2)}, u32[]{:S(2)}) async-start(bf16[256,8,256]{2,0,1:T(8,128)(2,1)} %copy.41), calls=%async_computation.1 | async-start | bytes 2097152 | tf_op jit(solution)/shard_map/all_to_all | solution.py:369
  56.7 397.4 %all-gather.8.cloned.1.call-start = ((), (), s32[]{:S(2)}) async-start(), calls=%async_computation.6 | async-start | bytes 33030144 | tf_op jit(solution)/shard_map/all_gather | solution.py:365
  81.7 31.7 %copy-start.32 = (bf16[256,8,256]{2,0,1:T(8,128)(2,1)}, bf16[256,8,256]{2,0,1:T(8,128)(2,1)S(1)}, u32[]{:S(2)}) copy-start(bf16[256,8,256]{2,0,1:T(8,128)(2,1)S(1)} %all-to-all-done.1) | copy-start | bytes 3145732
  81.7 35.1 %copy-start.54 = (bf16[4,1024]{1,0:T(4,128)(2,1)S(1)}, bf16[4,1024]{1,0:T(4,128)(2,1)}, u32[]{:S(2)}) copy-start(bf16[4,1024]{1,0:T(4,128)(2,1)} %param.18) | copy-start | bytes 24580
  81.7 35.1 %copy-start.61 = (bf16[1024]{0:T(1024)(128)(2,1)S(1)}, bf16[1024]{0:T(1024)(128)(2,1)}, u32[]{:S(2)}) copy-start(bf16[1024]{0:T(1024)(128)(2,1)} %param.19) | copy-start | bytes 6148
  81.7 35.1 %copy-start.62 = (bf16[1024]{0:T(1024)(128)(2,1)S(1)}, bf16[1024]{0:T(1024)(128)(2,1)}, u32[]{:S(2)}) copy-start(bf16[1024]{0:T(1024)(128)(2,1)} %param.22) | copy-start | bytes 6148
  113.4 4.8 collective-permute-start
  137.1 12.5 %copy-start.63 = (bf16[1024]{0:T(1024)(128)(2,1)S(1)}, bf16[1024]{0:T(1024)(128)(2,1)}, u32[]{:S(2)}) copy-start(bf16[1024]{0:T(1024)(128)(2,1)} %param.24) | copy-start | bytes 6148
  137.2 12.5 %copy-start.60 = (bf16[2048]{0:T(1024)(128)(2,1)S(1)}, bf16[2048]{0:T(1024)(128)(2,1)}, u32[]{:S(2)}) copy-start(bf16[2048]{0:T(1024)(128)(2,1)} %param.26) | copy-start | bytes 12292
  145.0 9.6 %collective-permute-start.1 = (f32[2,16,8,128]{3,2,1,0:T(8,128)}, f32[2,16,8,128]{3,2,1,0:T(8,128)}, u32[]{:S(2)}, u32[]{:S(2)}) collective-permute-start(f32[2,16,8,128]{3,2,1,0:T(8,128)} %shard_map.263), channel_id=1, source_target_pairs={{0,4},{1,5},{2,6},{3,7},{8,12},{9,13},{10,14},{11,15},{16,20},{17,... | collective-permute-start | bytes 393224 | tf_op jit(solution)/shard_map/ppermute | solution.py:22
  149.7 25.2 %copy-start.55 = (f32[1024]{0:T(1024)}, f32[1024]{0:T(1024)S(1)}, u32[]{:S(2)}) copy-start(f32[1024]{0:T(1024)S(1)} %convert_element_type.119) | copy-start | bytes 12292
  150.7 18.0 %copy-start.29 = (bf16[256,1024]{1,0:T(8,128)(2,1)S(1)}, bf16[256,1024]{1,0:T(8,128)(2,1)}, u32[]{:S(2)}) copy-start(bf16[256,1024]{1,0:T(8,128)(2,1)} %copy-done.28) | copy-start | bytes 1572868
  150.7 18.0 %copy-start.46 = (bf16[256,2048]{1,0:T(8,128)(2,1)S(1)}, bf16[256,2048]{1,0:T(8,128)(2,1)}, u32[]{:S(2)}) copy-start(bf16[256,2048]{1,0:T(8,128)(2,1)} %fusion.31) | copy-start | bytes 3145732
  161.9 6.8 %copy-start.2 = (f32[256,16,8,128]{3,2,1,0:T(8,128)}, f32[256,16,8,128]{3,2,1,0:T(8,128)S(1)}, u32[]{:S(2)}) copy-start(f32[256,16,8,128]{3,2,1,0:T(8,128)S(1)} %get-tuple-element.51.prior_ref) | copy-start | bytes 50331652
  273.9 29.1 %all-to-all-start.2 = ((bf16[256,8,256]{2,0,1:T(8,128)(2,1)}), bf16[256,8,256]{2,0,1:T(8,128)(2,1)}, u32[]{:S(2)}, u32[]{:S(2)}) async-start(bf16[256,8,256]{2,0,1:T(8,128)(2,1)} %bitcast.142), calls=%async_computation.2 | async-start | bytes 2097152 | tf_op jit(solution)/shard_map/all_to_all | solution.py:369
  354.8 35.9 %all-to-all-start.3 = ((bf16[256,8,256]{2,0,1:T(8,128)(2,1)}), bf16[256,8,256]{2,0,1:T(8,128)(2,1)}, u32[]{:S(2)}, u32[]{:S(2)}) async-start(bf16[256,8,256]{2,0,1:T(8,128)(2,1)} %bitcast.141), calls=%async_computation.3 | async-start | bytes 2097152 | tf_op jit(solution)/shard_map/all_to_all | solution.py:369
  365.3 13.2 %copy-start.3 = (f32[256,1024]{1,0:T(8,128)}, f32[256,1024]{1,0:T(8,128)S(1)}, u32[]{:S(2)}) copy-start(f32[256,1024]{1,0:T(8,128)S(1)} %get-tuple-element.76.drive_ref.ograd_ref) | copy-start | bytes 3145732
  370.5 20.1 %collective-permute-start.2 = (f32[2,16,8,128]{3,2,1,0:T(8,128)}, f32[2,16,8,128]{3,2,1,0:T(8,128)}, u32[]{:S(2)}, u32[]{:S(2)}) collective-permute-start(f32[2,16,8,128]{3,2,1,0:T(8,128)} %shard_map.267), channel_id=1, source_target_pairs={{4,0},{5,1},{6,2},{7,3},{12,8},{13,9},{14,10},{15,11},{20,16},{21,... | collective-permute-start | bytes 393224 | tf_op jit(solution)/shard_map/ppermute | solution.py:22
  418.6 17.9 %copy-start.39 = (bf16[1024,160]{0,1:T(8,128)(2,1)S(1)}, bf16[1024,160]{0,1:T(8,128)(2,1)}, u32[]{:S(2)}) copy-start(bf16[1024,160]{0,1:T(8,128)(2,1)} %param.20) | copy-start | bytes 983044
  418.7 18.1 %copy-start.27 = (f32[2,128,1024]{2,1,0:T(8,128)S(1)}, f32[2,128,1024]{2,1,0:T(8,128)}, u32[]{:S(2)}) copy-start(f32[2,128,1024]{2,1,0:T(8,128)} %copy-done.26) | copy-start | bytes 3145732
  419.0 17.8 %copy-start.5 = (f32[256,1024]{1,0:T(8,128)S(1)}, f32[256,1024]{1,0:T(8,128)}, u32[]{:S(2)}) copy-start(f32[256,1024]{1,0:T(8,128)} %copy-done.3) | copy-start | bytes 3145732
  419.0 17.8 %copy-start.19 = (f32[256,1024]{1,0:T(8,128)S(1)}, f32[256,1024]{1,0:T(8,128)}, u32[]{:S(2)}) copy-start(f32[256,1024]{1,0:T(8,128)} %copy-done.18) | copy-start | bytes 3145732
  419.0 17.8 %copy-start.57 = (f32[1024]{0:T(1024)S(1)}, f32[1024]{0:T(1024)}, u32[]{:S(2)}) copy-start(f32[1024]{0:T(1024)} %copy-done.55) | copy-start | bytes 12292
  438.0 5.9 %collective-permute-start.3 = (f32[2,3,1024]{2,1,0:T(4,128)S(1)}, f32[2,3,1024]{2,1,0:T(4,128)S(1)}, u32[]{:S(2)}, u32[]{:S(2)}) collective-permute-start(f32[2,3,1024]{2,1,0:T(4,128)S(1)} %pad_add_fusion.1), channel_id=1, source_target_pairs={{4,0},{5,1},{6,2},{7,3},{12,8},{13,9},{14,10},{15,11},{20,16},{21,... | collective-permute-start | bytes 73736 | tf_op jit(solution)/shard_map/ppermute | solution.py:22
  444.1 6.8 %slice-start = ((bf16[256,1024]{1,0:T(8,128)(2,1)}), bf16[160,1024]{1,0:T(8,128)(2,1)S(1)}, s32[]{:S(2)}) async-start(bf16[256,1024]{1,0:T(8,128)(2,1)} %copy-done.37), calls=%async_computation.7 | async-start | bytes 655360 | tf_op jit(solution)/shard_map/slice | solution.py:1082
  (45 other events, 105.1 us)
Sparse Core Ops, SparseCore 0:
  10.5 99.0 all-gather.3
  112.0 132.5 all-gather.5
  269.0 165.5 all-gather.7

commit v5 on v4

--- a/solution.py
+++ b/solution.py
@@ -459,31 +459,6 @@
         return [self.one(self.own(ref), self.own(ref), which, hop) for hop in range(self.count - 1)]
 
 
-def exchange_kernel(axes, counts, kinds, middle, *refs):
-    n_parts, n_whole, n_own = counts
-    parts, refs = refs[:n_parts], refs[n_parts:]
-    whole, refs = refs[:n_whole], refs[n_whole:]
-    own, refs = refs[:n_own], refs[n_own:]
-    outs, refs = refs[: len(kinds)], refs[len(kinds) :]
-    slots, refs = refs[:n_parts], refs[n_parts:]
-    group = Group(axes, *refs)
-    greet([(axes, group.others)])
-    copies = []
-    for which, (part, slot) in enumerate(zip(parts, slots)):
-        copies += group.scatter(part, slot, which)
-    finish(copies)
-    sums = [group.total(part, slot) for part, slot in zip(parts, slots)]
-    results = middle(sums, [group.own(ref)[...] for ref in whole], [ref[...] for ref in own])
-    copies = []
-    for which, (ref, kind, value) in enumerate(zip(outs, kinds, results)):
-        if kind == "rows":
-            ref[...] = value.astype(ref.dtype)
-        else:
-            group.own(ref)[...] = value.astype(ref.dtype)
-            copies += group.spread(ref, n_parts + which)
-    finish(copies)
-
-
 def slots_for(part, count):
     return pltpu.VMEM((count - 1, part.shape[0] // count) + part.shape[1:], part.dtype)
 
@@ -492,26 +467,183 @@
     return math.prod(lax.axis_size(axis) for axis in axes)
 
 
-def exchange(axes, call_id, parts, whole, own, middle, outs):
-    count = group_size(axes)
+class Swap:
+    def __init__(self, arrays, swapped, send_sem, recv_sem, local_sem):
+        plane = Group(PLANE, send_sem, recv_sem)
+        self.plane, self.arrays, self.swapped, self.local_sem = plane, arrays, swapped, local_sem
+
+    def begin(self):
+        self.copies, plane = [], self.plane
+        for which, (array, swapped) in enumerate(zip(self.arrays, self.swapped)):
+            share = swapped.shape[1]
+
+            def columns(index):
+                return array.at[:, pl.ds(pl.multiple_of(index * share, share), share)]
+
+            for hop, other in enumerate(plane.others):
+                self.copies.append(plane.one(columns(other), plane.own(swapped), which, hop))
+            local = pltpu.make_async_copy(
+                columns(plane.me), plane.own(swapped), self.local_sem.at[which]
+            )
+            local.start()
+            self.copies.append(local)
+
+    def end(self):
+        finish(self.copies)
+
+
+def swap_scratch(arrays):
+    sems = pltpu.SemaphoreType.DMA((len(arrays), group_size(PLANE) - 1))
+    return [sems, sems, pltpu.SemaphoreType.DMA((len(arrays),))] if arrays else []
+
+
+def swap_shapes(arrays):
+    count = group_size(PLANE)
+    return [
+        jax.ShapeDtypeStruct((array.shape[0] * count, array.shape[1] // count), array.dtype)
+        for array in arrays
+    ]
+
+
+def swaps_in_kernels(width):
+    return width // group_size(PLANE) % LANE == 0
+
+
+def sum_kernel(n_swaps, part, *refs):
+    arrays, refs = refs[:n_swaps], refs[n_swaps:]
+    total, refs = refs[0], refs[1:]
+    swapped, refs = refs[:n_swaps], refs[n_swaps:]
+    slots, send_sem, recv_sem, *refs = refs
+    group = Group(("tp",), send_sem, recv_sem)
+    if n_swaps:
+        swap = Swap(arrays, swapped, *refs)
+        greet([(("tp",), group.others), (PLANE, swap.plane.others)])
+    else:
+        greet([(("tp",), group.others)])
+    copies = group.scatter(part, slots, 0)
+    if n_swaps:
+        swap.begin()
+    finish(copies)
+    group.own(total)[...] = group.total(part, slots).astype(total.dtype)
+    finish(group.spread(total, 1))
+    if n_swaps:
+        swap.end()
+
+
+def sum_over_tp(call_id, part, arrays):
+    count = group_size(("tp",))
     vmem = pl.BlockSpec(memory_space=pltpu.VMEM)
-    sems = pltpu.SemaphoreType.DMA((len(parts) + len(outs), count - 1))
+    sems = pltpu.SemaphoreType.DMA((2, count - 1))
     return pl.pallas_call(
-        functools.partial(
-            exchange_kernel,
-            axes,
-            (len(parts), len(whole), len(own)),
-            [kind for kind, _, _ in outs],
-            middle,
-        ),
-        in_specs=[vmem] * (len(parts) + len(whole) + len(own)),
-        out_specs=[vmem] * len(outs),
-        out_shape=[jax.ShapeDtypeStruct(shape, dtype) for _, shape, dtype in outs],
-        scratch_shapes=[slots_for(part, count) for part in parts] + [sems, sems],
+        functools.partial(sum_kernel, len(arrays)),
+        in_specs=[vmem] * (1 + len(arrays)),
+        out_specs=[vmem] * (1 + len(arrays)),
+        out_shape=[jax.ShapeDtypeStruct(part.shape, part.dtype)] + swap_shapes(arrays),
+        scratch_shapes=[slots_for(part, count), sems, sems] + swap_scratch(arrays),
         compiler_params=pltpu.CompilerParams(
             collective_id=call_id, has_side_effects=True, vmem_limit_bytes=40 * 2**20
         ),
-    )(*parts, *whole, *own)
+    )(part, *arrays)
+
+
+def mixer_out_kernel(
+    gated, out_all, tokens, gain, normed, middle, part, slots, send_sem, recv_sem
+):
+    group = Group(("tp",), send_sem, recv_sem)
+    inner = gated.shape[1]
+    share = out_all.shape[1]
+    greet([(("tp",), group.others)])
+    for at in range(out_all.shape[0] // inner):
+        part[:, at * share : (at + 1) * share] = matmul(
+            gated[...], out_all[at * inner : (at + 1) * inner, :]
+        ).astype(part.dtype)
+    finish(group.scatter(part, slots, 0))
+    rows = group.own(tokens)[...].astype(jnp.float32) + group.total(part, slots)
+    middle[...] = rows
+    group.own(normed)[...] = (rows * inverse_rms(rows) * gain[...].astype(jnp.float32)).astype(
+        normed.dtype
+    )
+    finish(group.spread(normed, 1))
+
+
+def mixer_out(call_id, gated, out_all, tokens, gain):
+    count = group_size(("tp",))
+    vmem = pl.BlockSpec(memory_space=pltpu.VMEM)
+    rows, width = tokens.shape
+    part = jax.ShapeDtypeStruct((rows, width), jnp.bfloat16)
+    sems = pltpu.SemaphoreType.DMA((2, count - 1))
+    return pl.pallas_call(
+        mixer_out_kernel,
+        in_specs=[vmem] * 4,
+        out_specs=[vmem] * 2,
+        out_shape=[part, jax.ShapeDtypeStruct((rows // count, width), jnp.float32)],
+        scratch_shapes=[pltpu.VMEM(part.shape, part.dtype), slots_for(part, count), sems, sems],
+        compiler_params=pltpu.CompilerParams(
+            collective_id=call_id, has_side_effects=True, vmem_limit_bytes=40 * 2**20
+        ),
+    )(gated, out_all, tokens, gain)
+
+
+def ffn_back_kernel(n_swaps, part, ct, middle, gain, out_all, *refs):
+    arrays, refs = refs[:n_swaps], refs[n_swaps:]
+    middle_low, middle_grad, gain_grad, gated_grad, *refs = refs
+    swapped, refs = refs[:n_swaps], refs[n_swaps:]
+    slots, send_sem, recv_sem, *refs = refs
+    group = Group(("tp",), send_sem, recv_sem)
+    if n_swaps:
+        swap = Swap(arrays, swapped, *refs)
+        greet([(("tp",), group.others), (PLANE, swap.plane.others)])
+    else:
+        greet([(("tp",), group.others)])
+    copies = group.scatter(part, slots, 0)
+    if n_swaps:
+        swap.begin()
+    finish(copies)
+    normed_grad = group.total(part, slots)
+    rows = middle[...]
+    scale = inverse_rms(rows)
+    gain_grad[...] = jnp.sum(normed_grad * rows * scale, 0, keepdims=True)
+    grad = group.own(ct)[...].astype(jnp.float32) + norm_back(
+        normed_grad, rows, scale, gain[...].astype(jnp.float32)
+    )
+    middle_grad[...] = grad
+    group.own(middle_low)[...] = grad.astype(middle_low.dtype)
+    finish(group.spread(middle_low, 1))
+    inner = gated_grad.shape[1]
+    share = out_all.shape[1]
+    total = None
+    for at in range(out_all.shape[0] // inner):
+        one = matmul_nt(
+            middle_low[:, at * share : (at + 1) * share], out_all[at * inner : (at + 1) * inner, :]
+        )
+        total = one if total is None else total + one
+    gated_grad[...] = total
+    if n_swaps:
+        swap.end()
+
+
+def ffn_back(call_id, part, ct, middle, gain, out_all, arrays):
+    count = group_size(("tp",))
+    vmem = pl.BlockSpec(memory_space=pltpu.VMEM)
+    rows, width = part.shape
+    inner = out_all.shape[0] // group_size(PLANE)
+    sems = pltpu.SemaphoreType.DMA((2, count - 1))
+    return pl.pallas_call(
+        functools.partial(ffn_back_kernel, len(arrays)),
+        in_specs=[vmem] * (5 + len(arrays)),
+        out_specs=[vmem] * (4 + len(arrays)),
+        out_shape=[
+            jax.ShapeDtypeStruct((rows, width), jnp.bfloat16),
+            jax.ShapeDtypeStruct((rows // count, width), jnp.float32),
+            jax.ShapeDtypeStruct((1, width), jnp.float32),
+            jax.ShapeDtypeStruct((rows, inner), jnp.float32),
+        ]
+        + swap_shapes(arrays),
+        scratch_shapes=[slots_for(part, count), sems, sems] + swap_scratch(arrays),
+        compiler_params=pltpu.CompilerParams(
+            collective_id=call_id, has_side_effects=True, vmem_limit_bytes=48 * 2**20
+        ),
+    )(part, ct, middle, gain, out_all, *arrays)
 
 
 class PlaneGather:
@@ -862,24 +994,99 @@
     )
 
 
-def after_mixer(sums, whole, own):
-    (mixed,), (tokens_in,), (gain,) = sums, whole, own
-    middle = tokens_in.astype(jnp.float32) + mixed
-    return middle * inverse_rms(middle) * gain.astype(jnp.float32), middle
-
-
-def after_ffn_back(sums, whole, own):
-    (normed_grad,), (ct,), (middle, gain) = sums, whole, own
-    scale = inverse_rms(middle)
-    gain_grad = jnp.sum(normed_grad * middle * scale, 0, keepdims=True)
-    middle_grad = ct.astype(jnp.float32) + norm_back(
-        normed_grad, middle, scale, gain.astype(jnp.float32)
-    )
-    return middle_grad, middle_grad, gain_grad
-
-
-def as_they_are(sums, whole, own):
-    return sums
+def head_kernel(
+    tokens,
+    gain,
+    in_conv,
+    in_gate,
+    outproj,
+    conv_in,
+    gate_mix,
+    conv_all,
+    gate_all,
+    out_all,
+    normed,
+    block_buf,
+    block_sem,
+    *sems,
+):
+    gathers = [
+        PlaneGather(own, gathered, *sems[3 * at : 3 * at + 2])
+        for at, (own, gathered) in enumerate(
+            [(in_conv, conv_all), (in_gate, gate_all), (outproj, out_all)]
+        )
+    ]
+    local_sems = sems[2::3]
+    conv, gate, out = gathers
+    greet([(PLANE, conv.others)])
+    conv.begin(local_sems[0])
+    gate.begin(local_sems[1])
+    hidden_in = tokens[...].astype(jnp.float32)
+    normed[...] = (
+        hidden_in * inverse_rms(hidden_in) * gain[...].astype(jnp.float32)
+    ).astype(normed.dtype)
+    conv.relay()
+    conv.hand_over()
+    gate.relay()
+    gate.hand_over()
+    out.begin(local_sems[2])
+    conv.hand_over_last()
+    gate.hand_over_last()
+    conv.end()
+    gate.end()
+    jobs = [
+        (source, target, at)
+        for source, target in ((conv_all, conv_in), (gate_all, gate_mix))
+        for at in range(0, conv_in.shape[1], WIDE)
+    ]
+
+    def fetch(turn):
+        source, _, at = jobs[turn]
+        return pltpu.make_async_copy(
+            source.at[:, at : at + WIDE], block_buf.at[turn % 2], block_sem.at[turn % 2]
+        )
+
+    fetch(0).start()
+    for turn, (_, target, at) in enumerate(jobs):
+        if turn + 1 < len(jobs):
+            fetch(turn + 1).start()
+        fetch(turn).wait()
+        if turn == 1:
+            out.relay()
+            out.hand_over()
+        target[:, at : at + WIDE] = matmul(normed[...], block_buf[turn % 2]).astype(target.dtype)
+    out.hand_over_last()
+    out.end()
+
+
+def run_head(call_id, tokens, gain, inproj, outproj):
+    rows, width = tokens.shape
+    inner = inproj.shape[2]
+    count = group_size(PLANE)
+    low = jnp.bfloat16
+    vmem = pl.BlockSpec(memory_space=pltpu.VMEM)
+    hbm = pl.BlockSpec(memory_space=pl.ANY)
+    return pl.pallas_call(
+        head_kernel,
+        in_specs=[vmem] * 2 + [hbm] * 3,
+        out_specs=[vmem] * 2 + [hbm] * 3,
+        out_shape=[
+            jax.ShapeDtypeStruct((rows, inner), low),
+            jax.ShapeDtypeStruct((rows, inner), jnp.float32),
+            jax.ShapeDtypeStruct((width, inner), low),
+            jax.ShapeDtypeStruct((width, inner), low),
+            jax.ShapeDtypeStruct((inner * count, width // count), low),
+        ],
+        scratch_shapes=[
+            pltpu.VMEM((rows, width), low),
+            pltpu.VMEM((2, width, WIDE), low),
+            pltpu.SemaphoreType.DMA((2,)),
+        ]
+        + [gather_sems(), gather_sems(), pltpu.SemaphoreType.DMA(())] * 3,
+        compiler_params=pltpu.CompilerParams(
+            collective_id=call_id, has_side_effects=True, vmem_limit_bytes=40 * 2**20
+        ),
+    )(tokens, gain, inproj[0], inproj[1], outproj)
 
 
 def per_device(
@@ -914,28 +1121,22 @@
     rate = (decay_rate * LOG2E).reshape(n_state, tiles, LANE)
 
     gain_mix_row, gain_ffn_row = mixgain.reshape(1, width), ffngain.reshape(1, width)
-    own_rows = rows // lax.axis_size("tp")
     hidden = gateup.shape[2]
     low = jnp.bfloat16
 
-    mix_pack = gathered_rows(
-        jnp.concatenate([inproj[0], inproj[1], jnp.transpose(outproj)], 1)
-    )
-    ffn_pack = gathered_rows(
-        jnp.concatenate([gateup[0], gateup[1], jnp.transpose(downproj)], 1)
-    )
-
     tokens_rows = tokens.reshape(rows, width)
+    ct_low = cotangent.reshape(rows, width)
+    conv_in, gate_mix, in_conv, in_gate, out_all = run_head(
+        5, tokens_rows, gain_mix_row, inproj, outproj
+    )
+    ffn_pack, conv_in = lax.optimization_barrier(
+        (jnp.concatenate([gateup[0], gateup[1], jnp.transpose(downproj)], 1), conv_in)
+    )
+    ffn_pack = gathered_rows(ffn_pack)
     hidden_in = tokens_rows.astype(jnp.float32)
     scale_one = inverse_rms(hidden_in)
     normed_one = (hidden_in * scale_one * gain_mix).astype(low)
-    ct_low = cotangent.reshape(rows, width)
-    normed_one_cols, ct_cols = swapped_columns(normed_one), swapped_columns(ct_low)
-    normed_one, normed_one_cols, ct_cols = lax.optimization_barrier(
-        (normed_one, normed_one_cols, ct_cols)
-    )
-    conv_in = matmul(normed_one, mix_pack[:, :inner]).astype(low)
-    gate_mix = matmul(normed_one, mix_pack[:, inner : 2 * inner])
+
     conv_seqs = conv_in.reshape(seqs, span, inner)
     rim_rows = passed_along(conv_seqs[:, span - (taps - 1) :], "ctx", 1)
     padded_in = jnp.concatenate([rim_rows, conv_seqs], 1).astype(jnp.float32)
@@ -948,15 +1149,7 @@
     columns = selproj.shape[1]
     select_width = -(-columns // LANE) * LANE
     select_weights = jnp.pad(selproj, ((0, 0), (0, select_width - columns)))
-    (select_cols,) = exchange(
-        ("tp",),
-        0,
-        [matmul(scan_in, select_weights)],
-        [],
-        [],
-        as_they_are,
-        [("all", (rows, select_width), jnp.float32)],
-    )
+    (select_cols,) = sum_over_tp(0, matmul(scan_in, select_weights), [])
     step_low = select_cols[:, :rank].astype(low)
     b_rows = select_cols[:, rank : rank + n_state].reshape(-1)
     c_rows = select_cols[:, rank + n_state : columns].reshape(-1)
@@ -971,17 +1164,7 @@
     mixer_core = scan_out + skip_weight[None] * scan_float
     gate_sig = jax.nn.silu(gate_mix)
     gated = (mixer_core * gate_sig).astype(low)
-    out_weights = mix_pack[:, 2 * inner :]
-    normed_two, middle = exchange(
-        ("tp",),
-        1,
-        [matmul_nt(gated, out_weights).astype(low)],
-        [tokens_rows],
-        [gain_ffn_row],
-        after_mixer,
-        [("all", (rows, width), low), ("rows", (own_rows, width), jnp.float32)],
-    )
-    normed_two_cols = swapped_columns(normed_two)
+    normed_two, middle = mixer_out(1, gated, out_all, tokens_rows, gain_ffn_row)
     gate_up = ffn_pack[:, : 2 * hidden]
     down_weights = ffn_pack[:, 2 * hidden :]
     both_ffn = matmul(normed_two, gate_up)
@@ -996,29 +1179,20 @@
     )
     ffn_all = gathered_rows(ffn_sent)
     normed_two_part = matmul_nt(ffn_grads, gate_up).astype(low)
-    normed_two_part, normed_two_cols = lax.optimization_barrier((normed_two_part, normed_two_cols))
     ffn_part = matmul_nt(activated, down_weights).astype(low)
-    middle_low, middle_grad, ffngain_part = exchange(
-        ("tp",),
-        2,
-        [normed_two_part],
-        [ct_low],
-        [middle, gain_ffn_row],
-        after_ffn_back,
-        [
-            ("all", (rows, width), low),
-            ("rows", (own_rows, width), jnp.float32),
-            ("rows", (1, width), jnp.float32),
-        ],
-    )
-    middle_cols = swapped_columns(middle_low)
-    gated_grad = matmul(middle_low, out_weights)
+    swap_now = swaps_in_kernels(width)
+    to_swap = [normed_one, normed_two, ct_low]
+    middle_low, middle_grad, ffngain_part, gated_grad, *swapped = ffn_back(
+        2, normed_two_part, ct_low, middle, gain_ffn_row, out_all, to_swap if swap_now else []
+    )
+    if not swap_now:
+        swapped = [swapped_columns(array) for array in to_swap]
+    normed_one_cols, normed_two_cols, ct_cols = swapped
     core_grad = gated_grad * gate_sig
     gate_mix_grad = (gated_grad * mixer_core * silu_slope(gate_mix)).astype(low)
     grad_skipgain = jnp.sum(core_grad * scan_float, 0)
     back_ends = scan_ends(step_size, core_grad, c_rows, rate, seqs, True)
     end_grad = from_earlier(back_ends, span_decay, -1)
-    end_grad, middle_cols = lax.optimization_barrier((end_grad, middle_cols))
     step_grad, input_grad, rate_grad, parts = scan_backward(
         end_grad, prior, step_size, scan_float, core_grad, b_rows, c_rows, rate, seqs
     )
@@ -1035,15 +1209,8 @@
         ],
         1,
     ).astype(low)
-    (select_low,) = exchange(
-        ("tp",),
-        3,
-        [select_part],
-        [],
-        [],
-        as_they_are,
-        [("all", (rows, select_width), low)],
-    )
+    select_low, *swapped = sum_over_tp(3, select_part, [middle_low] if swap_now else [])
+    (middle_cols,) = swapped if swap_now else [swapped_columns(middle_low)]
     grad_selproj = matmul_tn(select_low, scan_in)
     scan_in_grad = (
         core_grad * skip_weight[None]
@@ -1069,7 +1236,7 @@
         .reshape(rows, inner)
     )
     mix_grads = jnp.concatenate([conv_in_grad, gate_mix_grad], 1)
-    normed_one_part = matmul_nt(mix_grads, mix_pack[:, : 2 * inner])
+    normed_one_part = matmul_nt(conv_in_grad, in_conv) + matmul_nt(gate_mix_grad, in_gate)
     mixgain_part = jnp.sum(normed_one_part * hidden_in * scale_one, 0)
     normed_one_part = normed_one_part.astype(low)
     small = [

time: 589 us -> 568 us (0.964)
  Pallas kernels: 265 us -> 361 us
  waiting for transfers between devices: 123 us -> 45.9 us
  matrix products: 71.9 us -> 52.2 us
  starting transfers between devices: 28.6 us -> 11.1 us
    pallas_call x4 -> x5, Pallas kernels: 124 us -> 218 us  [the longest x1 68.2 us: ffn_back(): pl.pallas_call(functools.partial(ffn_back_kernel, len(arrays)), in_specs=...]
    all_to_all x4 -> x0, waiting for transfers between devices: 58 us -> none  [swapped_columns(): return lax.all_to_all(rows, PLANE, split_axis=1, concat_axis=0, tiled=True)]
    all_to_all x4 -> x0, starting transfers between devices: 17.5 us -> none  [swapped_columns(): return lax.all_to_all(rows, PLANE, split_axis=1, concat_axis=0, tiled=True)]
    dot_general x7 -> x4, matrix products: 39.6 us -> 23.5 us  [matmul(): return jnp.dot(left, right, preferred_element_type=jnp.float32)]
    ppermute x4, waiting for transfers between devices: 18.4 us -> 8.68 us  [passed_along(): lax.ppermute(value, axis, [(source, source + steps) for source in range(f...]
    all_gather x3 -> x2, waiting for transfers between devices: 46.2 us -> 37.1 us  [gathered_rows(): return lax.all_gather(rows, PLANE, axis=0, tiled=True)]
    unnamed x144 -> x156, local copies, waits for them, and re-layouts: 36.5 us -> 38.4 us
  transfers between devices with their start and end apart: 11 -> 6, of which waited for: 9 -> 5; matrix products, arithmetic and copies ran while one was open for 15% -> 9% of each run, Pallas kernels for 28% -> 35%
where the time goes in v5:
time: 568 us; the launch traced here: 561 us
  Pallas kernels  361 us (64%)
  local copies, waits for them, and re-layouts  54.5 us (10%)
  matrix products  52.2 us (9%)
  waiting for transfers between devices  45.9 us (8%)
  other arithmetic  21.5 us (4%)
  between operations  15.5 us (3%)
  starting transfers between devices  11.1 us (2%)
    pallas_call x1, Pallas kernels, run_tail(): pl.pallas_call(functools.partial(tail_kernel, (inner, hidden, gain_at)),...  106 us
    pallas_call x1, Pallas kernels, ffn_back(): pl.pallas_call(functools.partial(ffn_back_kernel, len(arrays)), in_specs=...  68.2 us
    pallas_call x1, Pallas kernels, run_head(): pl.pallas_call(head_kernel, in_specs=[vmem] * 2 + [hbm] * 3, out_specs=[v...  58.9 us
    pallas_call x1, Pallas kernels, mixer_out(): pl.pallas_call(mixer_out_kernel, in_specs=[vmem] * 4, out_specs=[vmem] *...  46.7 us
    pallas_call x2, Pallas kernels, sum_over_tp(): pl.pallas_call(functools.partial(sum_kernel, len(arrays)), in_specs=[vmem...  44.2 us
    unnamed x156, local copies, waits for them, and re-layouts  38.4 us
    all_gather x2, waiting for transfers between devices, gathered_rows(): return lax.all_gather(rows, PLANE, axis=0, tiled=True)  37.1 us
    dot_general x6, matrix products, matmul_nt(): lax.dot_general(left, right, (((1,), (1,)), ((), ())), preferred_element_...  28.1 us
  transfers between devices with their start and end apart: 6, of which 5 were waited for; matrix products, arithmetic and copies ran while one was open for 9% of the time, Pallas kernels for 35%

profile of v5, /device:TPU:0, one launch (start us, length us, event | category | flops | bytes accessed | tf_op | source)
XLA Modules:
  0.0 561.4 jit_solution(5334649017693254012)
XLA Ops:
  10.5 2.3 copy.41
  14.1 3.2 pad_maximum_fusion.1
  17.3 58.9 %shard_map.262 = (bf16[256,1024]{1,0:T(8,128)(2,1)S(1)}, f32[256,1024]{1,0:T(8,128)S(1)}, bf16[2048,1024]{1,0:T(8,128)(2,1)S(1)}, bf16[2048,1024]{1,0:T(8,128)(2,1)S(1)}, bf16[8192,256]{1,0:T(8,128)(2,1)}) custom-call(bf16[256,2048]{1,0:T(8,128)(2,1)S(1)} %bitcast.99, bf16[1,2048]{1,0:T(2,128)(2,1)S(1)} %reshape.114.gain.gain_row, ...), custom_call_target="tpu_custom_call" | custom-call | tf_op jit(solution)/shard_map/pallas_call | solution.py:1069
  76.2 2.0 copy-done.9
  79.2 2.1 copy-done.36
  81.5 3.4 collective-permute-start
  89.0 14.9 %shard_map.263 = f32[256,256]{1,0:T(8,128)S(1)} custom-call(f32[256,256]{1,0:T(8,128)S(1)} %fusion.33.part), custom_call_target="tpu_custom_call" | custom-call | tf_op jit(solution)/shard_map/pallas_call | solution.py:537
  105.5 2.6 compare_select_fusion
  108.1 5.3 shard_map.264
  113.3 4.7 collective-permute-start.1
  119.1 4.0 collective-permute-done.1.start_ref
  123.1 7.3 %shard_map.265 = (f32[256,16,8,128]{3,2,1,0:T(8,128)S(1)}, f32[256,1024]{1,0:T(8,128)S(1)}) custom-call(f32[2,16,8,128]{3,2,1,0:T(8,128)} %collective-permute-done.1.start_ref, f32[256,1024]{1,0:T(8,128)S(1)} %get-tuple-element.120.step_ref, f32[256,1024]{1,0:T(8,128)S(1)} %get-tuple-element.93.drive_ref.input_ref, f32[4096]{0:T(1024)S(1)} %reshape.117.rows_ref.brow_ref, ...), custom_call_target="tpu_custom_call" | custom-call | tf_op jit(solution)/shard_map/pallas_call | solution.py:194
  130.5 5.8 %copy-done.2 = f32[256,16,8,128]{3,2,1,0:T(8,128)} copy-done((f32[256,16,8,128]{3,2,1,0:T(8,128)}, f32[256,16,8,128]{3,2,1,0:T(8,128)S(1)}, u32[]{:S(2)}) %copy-start.2) | copy-done | bytes 16777240
  138.1 46.7 %shard_map.266 = (bf16[256,2048]{1,0:T(8,128)(2,1)S(1)}, f32[64,2048]{1,0:T(8,128)S(1)}) custom-call(bf16[256,1024]{1,0:T(8,128)(2,1)S(1)} %multiply_convert_fusion.4.gated, bf16[8192,256]{1,0:T(8,128)(2,1)S(1)} %copy-done.3, bf16[256,2048]{1,0:T(8,128)(2,1)S(1)} %bitcast.100, bf16[1,2048]{1,0:T(2,128)(2,1)S(1)} %reshape.120.gain), custom_call_target="tpu_custom_call" | custom-call | tf_op jit(solution)/shard_map/pallas_call | solution.py:575
  187.3 27.1 %all-gather.3.cloned.1.call-done = bf16[2048,6144]{0,1:T(8,128)(2,1)} async-done(((bf16[256,6144]{0,1:T(8,128)(2,1)}), bf16[2048,6144]{0,1:T(8,128)(2,1)}) %all-gather.3.cloned.1.call-update) | async-done | bytes 25165840 | tf_op jit(solution)/shard_map/all_gather | solution.py:365
  214.5 12.6 %fusion.2 = f32[256,4096]{1,0:T(8,128)} fusion(bf16[256,2048]{1,0:T(8,128)(2,1)} %copy-done.30, bf16[2048,6144]{0,1:T(8,128)(2,1)} %all-gather.3.cloned.1.call-done), kind=kOutput, calls=%fused_computation.2 | convolution fusion | flops 4294967296 | bytes 22020096 | tf_op jit(solution)/shard_map/dot_general | solution.py:26
  227.1 7.9 %multiply_convert_fusion.1 = (bf16[256,2048]{1,0:T(8,128)(2,1)S(1)}, bf16[256,2048]{1,0:T(8,128)(2,1)S(1)}, bf16[256,2048]{1,0:T(8,128)(2,1)S(1)}) fusion(f32[256,4096]{1,0:T(8,128)} %fusion.2, bf16[256,2048]{1,0:T(8,128)(2,1)} %bitcast.113, bf16[2048,6144]{0,1:T(8,128)(2,1)} %all-gather.3.cloned.1.call-done), kind=kOutput, calls=%fused_computation.24 | convolution fusion | flops 2155347968 | bytes 16777216 | tf_op jit(solution)/shard_map/dot_general | solution.py:26
  236.7 2.1 pad_maximum_fusion
  244.6 14.4 %fusion.11.part = bf16[256,2048]{1,0:T(8,128)(2,1)} fusion(bf16[256,4096]{1,0:T(8,128)(2,1)S(1)} %copy-done.49, bf16[2048,6144]{0,1:T(8,128)(2,1)} %all-gather.3.cloned.1.call-done), kind=kOutput, calls=%fused_computation.15 | convolution fusion | flops 4295491584 | bytes 19922944 | tf_op jit(solution)/shard_map/dot_general | solution.py:30
  259.0 68.2 %shard_map.267 = (bf16[256,2048]{1,0:T(8,128)(2,1)S(1)}, f32[64,2048]{1,0:T(8,128)S(1)}, f32[1,2048]{1,0:T(1,128)S(1)}, f32[256,1024]{1,0:T(8,128)S(1)}, bf16[20...) custom-call(bf16[256,2048]{1,0:T(8,128)(2,1)} %fusion.11.part, ...), custom_call_target="tpu_custom_call" | custom-call | tf_op jit(solution)/shard_map/pallas_call | solution.py:631
  329.1 5.2 shard_map.268
  335.9 7.9 %fusion.14.ffn_part = bf16[256,2048]{1,0:T(8,128)(2,1)} fusion(bf16[256,2048]{1,0:T(8,128)(2,1)S(1)} %copy-done.57, bf16[2048,6144]{0,1:T(8,128)(2,1)} %all-gather.3.cloned.1.call-done), kind=kOutput, calls=%fused_computation.16 | convolution fusion | flops 2148007936 | bytes 10485760 | tf_op jit(solution)/shard_map/dot_general | solution.py:30
  343.8 2.6 fusion.53
  347.7 18.9 %shard_map.269 = (f32[256,1024]{1,0:T(8,128)S(1)}, f32[256,1024]{1,0:T(8,128)S(1)}, f32[16,8,128]{2,1,0:T(8,128)S(1)}, f32[256,32,128]{2,1,0:T(8,128)S(1)}) custom-call(f32[2,16,8,128]{3,2,1,0:T(8,128)} %collective-permute-done.2.end_ref, f32[256,16,8,128]{3,2,1,0:T(8,128)} %copy-done.2, f32[256,1024]{1,0:T(8,128)S(1)} %get-tuple-element.120.step_ref, ...), custom_call_target="tpu_custom_call" | custom-call | tf_op jit(solution)/shard_map/pallas_call | solution.py:315
  366.6 2.0 copy-done.11
  371.2 3.5 reduce_sum.91
  375.9 29.3 %shard_map.270 = (bf16[256,256]{1,0:T(8,128)(2,1)S(1)}, bf16[2048,256]{1,0:T(8,128)(2,1)S(1)}) custom-call(bf16[256,256]{1,0:T(8,128)(2,1)S(1)} %maximum_maximum_fusion.part, bf16[256,2048]{1,0:T(8,128)(2,1)S(1)} %copy-done.25), custom_call_target="tpu_custom_call" | custom-call | tf_op jit(solution)/shard_map/pallas_call | solution.py:537
  409.9 3.4 collective-permute-done.3
  413.4 2.7 fusion.20
  419.3 10.0 %all-gather.5.cloned.1.call-done.ffn_all = bf16[2048,7168]{1,0:T(8,128)(2,1)} async-done(((bf16[256,7168]{1,0:T(8,128)(2,1)}), bf16[2048,7168]{1,0:T(8,128)(2,1)}) %all-gather.5.cloned.1.call-update) | async-done | bytes 29360144 | tf_op jit(solution)/shard_map/all_gather | solution.py:365
  429.3 106.0 %shard_map.271 = (bf16[256,2048]{1,0:T(8,128)(2,1)}, bf16[256,2048]{1,0:T(8,128)(2,1)}, bf16[384,1024]{1,0:T(8,128)(2,1)}, f32[16,1024]{1,0:T(8,128)}, bf16[2048...) custom-call(bf16[256,2048]{1,0:T(8,128)(2,1)} %pad_maximum_fusion.3., ...), custom_call_target="tpu_custom_call" | custom-call | tf_op jit(solution)/shard_map/pallas_call | solution.py:942
  549.7 2.1 copy.60
  (223 shorter events, 56.6 us)
Async XLA Ops:
  7.2 98.2 %copy-start = (bf16[128,1024]{1,0:T(8,128)(2,1)S(1)}, bf16[128,1024]{1,0:T(8,128)(2,1)}, u32[]{:S(2)}) copy-start(bf16[128,1024]{1,0:T(8,128)(2,1)} %param.21) | copy-start | bytes 786436
  7.2 207.3 %all-gather.3.cloned.1.call-start = ((), (), s32[]{:S(2)}) async-start(), calls=%async_computation | async-start | bytes 28311552 | tf_op jit(solution)/shard_map/all_gather | solution.py:365
  8.1 9.2 %copy-start.33 = (bf16[1,2048]{1,0:T(2,128)(2,1)}, bf16[1,2048]{1,0:T(2,128)(2,1)S(1)}, u32[]{:S(2)}) copy-start(bf16[1,2048]{1,0:T(2,128)(2,1)S(1)} %reshape.114.gain.gain_row) | copy-start | bytes 12292
  81.4 3.6 copy-start.70
  81.4 347.9 %all-gather.5.cloned.1.call-start = ((), (), s32[]{:S(2)}) async-start(), calls=%async_computation.1 | async-start | bytes 33030144 | tf_op jit(solution)/shard_map/all_gather | solution.py:365
  81.5 4.8 collective-permute-start
  105.4 12.6 %copy-start.71 = (bf16[1024]{0:T(1024)(128)(2,1)S(1)}, bf16[1024]{0:T(1024)(128)(2,1)}, u32[]{:S(2)}) copy-start(bf16[1024]{0:T(1024)(128)(2,1)} %param.24) | copy-start | bytes 6148
  105.4 12.6 %copy-start.68 = (bf16[2048]{0:T(1024)(128)(2,1)S(1)}, bf16[2048]{0:T(1024)(128)(2,1)}, u32[]{:S(2)}) copy-start(bf16[2048]{0:T(1024)(128)(2,1)} %param.26) | copy-start | bytes 12292
  113.3 9.8 %collective-permute-start.1 = (f32[2,16,8,128]{3,2,1,0:T(8,128)}, f32[2,16,8,128]{3,2,1,0:T(8,128)}, u32[]{:S(2)}, u32[]{:S(2)}) collective-permute-start(f32[2,16,8,128]{3,2,1,0:T(8,128)} %shard_map.264), channel_id=1, source_target_pairs={{0,4},{1,5},{2,6},{3,7},{8,12},{9,13},{10,14},{11,15},{16,20},{17,... | collective-permute-start | bytes 393224 | tf_op jit(solution)/shard_map/ppermute | solution.py:22
  119.1 17.1 %copy-start.13 = (f32[256,1024]{1,0:T(8,128)S(1)}, f32[256,1024]{1,0:T(8,128)}, u32[]{:S(2)}) copy-start(f32[256,1024]{1,0:T(8,128)} %copy-done.12) | copy-start | bytes 3145732
  123.1 14.9 %copy-start.3 = (bf16[8192,256]{1,0:T(8,128)(2,1)S(1)}, bf16[8192,256]{1,0:T(8,128)(2,1)}, u32[]{:S(2)}) copy-start(bf16[8192,256]{1,0:T(8,128)(2,1)} %get-tuple-element.53.out_all) | copy-start | bytes 12582916
  130.4 5.8 %copy-start.2 = (f32[256,16,8,128]{3,2,1,0:T(8,128)}, f32[256,16,8,128]{3,2,1,0:T(8,128)S(1)}, u32[]{:S(2)}) copy-start(f32[256,16,8,128]{3,2,1,0:T(8,128)S(1)} %get-tuple-element.59.prior_ref) | copy-start | bytes 50331652
  242.6 16.4 %copy-start.66 = (f32[256]{0:T(256)}, f32[256]{0:T(256)S(1)}, u32[]{:S(2)}) copy-start(f32[256]{0:T(256)S(1)} %rsqrt_bitcast_fusion) | copy-start | bytes 3076
  244.6 14.4 %copy-start.18 = (f32[64,2048]{1,0:T(8,128)S(1)}, f32[64,2048]{1,0:T(8,128)}, u32[]{:S(2)}) copy-start(f32[64,2048]{1,0:T(8,128)} %copy-done.17) | copy-start | bytes 1572868
  259.0 68.3 %copy-start.14 = (f32[256,1024]{1,0:T(8,128)S(1)}, f32[256,1024]{1,0:T(8,128)}, u32[]{:S(2)}) copy-start(f32[256,1024]{1,0:T(8,128)} %copy-done.12) | copy-start | bytes 3145732
  259.0 68.3 %copy-start.16 = (f32[256,1024]{1,0:T(8,128)S(1)}, f32[256,1024]{1,0:T(8,128)}, u32[]{:S(2)}) copy-start(f32[256,1024]{1,0:T(8,128)} %copy-done.15) | copy-start | bytes 3145732
  259.0 68.3 %copy-start.41 = (bf16[256,1024]{1,0:T(8,128)(2,1)S(1)}, bf16[256,1024]{1,0:T(8,128)(2,1)}, u32[]{:S(2)}) copy-start(bf16[256,1024]{1,0:T(8,128)(2,1)} %copy-done.40) | copy-start | bytes 1572868
  329.1 14.7 %copy-start.4 = (f32[256,1024]{1,0:T(8,128)}, f32[256,1024]{1,0:T(8,128)S(1)}, u32[]{:S(2)}) copy-start(f32[256,1024]{1,0:T(8,128)S(1)} %get-tuple-element.88.drive_ref.ograd_ref) | copy-start | bytes 3145732
  329.1 14.7 %copy-start.51 = (bf16[256,1024]{1,0:T(8,128)(2,1)}, bf16[256,1024]{1,0:T(8,128)(2,1)S(1)}, u32[]{:S(2)}) copy-start(bf16[256,1024]{1,0:T(8,128)(2,1)S(1)} %get-tuple-element.98) | copy-start | bytes 1572868
  329.1 6.8 %copy-start.57 = (bf16[256,2048]{1,0:T(8,128)(2,1)S(1)}, bf16[256,2048]{1,0:T(8,128)(2,1)}, u32[]{:S(2)}) copy-start(bf16[256,2048]{1,0:T(8,128)(2,1)} %copy-done.56) | copy-start | bytes 3145732
  334.3 9.4 %copy-start.37 = (bf16[2048,1024]{1,0:T(8,128)(2,1)S(1)}, bf16[2048,1024]{1,0:T(8,128)(2,1)}, u32[]{:S(2)}) copy-start(bf16[2048,1024]{1,0:T(8,128)(2,1)} %copy-done.36) | copy-start | bytes 12582916
  334.3 12.1 %collective-permute-start.2 = (f32[2,16,8,128]{3,2,1,0:T(8,128)}, f32[2,16,8,128]{3,2,1,0:T(8,128)}, u32[]{:S(2)}, u32[]{:S(2)}) collective-permute-start(f32[2,16,8,128]{3,2,1,0:T(8,128)} %shard_map.268), channel_id=1, source_target_pairs={{4,0},{5,1},{6,2},{7,3},{12,8},{13,9},{14,10},{15,11},{20,16},{21,... | collective-permute-start | bytes 393224 | tf_op jit(solution)/shard_map/ppermute | solution.py:22
  374.7 30.5 %copy-start.55 = (bf16[1024,160]{0,1:T(8,128)(2,1)S(1)}, bf16[1024,160]{0,1:T(8,128)(2,1)}, u32[]{:S(2)}) copy-start(bf16[1024,160]{0,1:T(8,128)(2,1)} %param.20) | copy-start | bytes 983044
  375.0 30.5 %copy-start.6 = (f32[256,1024]{1,0:T(8,128)S(1)}, f32[256,1024]{1,0:T(8,128)}, u32[]{:S(2)}) copy-start(f32[256,1024]{1,0:T(8,128)} %copy-done.4) | copy-start | bytes 3145732
  375.1 30.5 %copy-start.29 = (f32[256,1024]{1,0:T(8,128)S(1)}, f32[256,1024]{1,0:T(8,128)}, u32[]{:S(2)}) copy-start(f32[256,1024]{1,0:T(8,128)} %copy-done.28) | copy-start | bytes 3145732
  375.1 30.5 %copy-start.44 = (f32[2,128,1024]{2,1,0:T(8,128)S(1)}, f32[2,128,1024]{2,1,0:T(8,128)}, u32[]{:S(2)}) copy-start(f32[2,128,1024]{2,1,0:T(8,128)} %copy-done.43) | copy-start | bytes 3145732
  406.6 6.6 %collective-permute-start.3 = (f32[2,3,1024]{2,1,0:T(4,128)S(1)}, f32[2,3,1024]{2,1,0:T(4,128)S(1)}, u32[]{:S(2)}, u32[]{:S(2)}) collective-permute-start(f32[2,3,1024]{2,1,0:T(4,128)S(1)} %pad_add_fusion.1), channel_id=1, source_target_pairs={{4,0},{5,1},{6,2},{7,3},{12,8},{13,9},{14,10},{15,11},{20,16},{21,... | collective-permute-start | bytes 73736 | tf_op jit(solution)/shard_map/ppermute | solution.py:22
  409.2 4.1 copy-start.10
  409.7 3.6 copy-start.50
  409.8 3.6 copy-start.67
  539.9 4.4 copy-start.61
  541.3 4.0 copy-start.60
  (48 other events, 87.3 us)
Sparse Core Ops, SparseCore 0:
  81.5 132.9 all-gather.2
  239.0 190.2 all-gather.4

commit v6 on v5

--- a/solution.py
+++ b/solution.py
@@ -509,9 +509,11 @@
     return width // group_size(PLANE) % LANE == 0
 
 
-def sum_kernel(n_swaps, part, *refs):
+def sum_kernel(n_rows, n_swaps, part, *refs):
+    own_rows, refs = refs[:n_rows], refs[n_rows:]
     arrays, refs = refs[:n_swaps], refs[n_swaps:]
     total, refs = refs[0], refs[1:]
+    all_rows, refs = refs[:n_rows], refs[n_rows:]
     swapped, refs = refs[:n_swaps], refs[n_swaps:]
     slots, send_sem, recv_sem, *refs = refs
     group = Group(("tp",), send_sem, recv_sem)
@@ -523,27 +525,38 @@
     copies = group.scatter(part, slots, 0)
     if n_swaps:
         swap.begin()
+    spreads = []
+    for which, (own, gathered) in enumerate(zip(own_rows, all_rows)):
+        group.own(gathered)[...] = own[...]
+        spreads += group.spread(gathered, 2 + which)
     finish(copies)
     group.own(total)[...] = group.total(part, slots).astype(total.dtype)
     finish(group.spread(total, 1))
+    finish(spreads)
     if n_swaps:
         swap.end()
 
 
-def sum_over_tp(call_id, part, arrays):
+def sum_over_tp(call_id, part, own_rows, arrays):
     count = group_size(("tp",))
     vmem = pl.BlockSpec(memory_space=pltpu.VMEM)
-    sems = pltpu.SemaphoreType.DMA((2, count - 1))
+    operands = [part, *own_rows, *arrays]
+    sems = pltpu.SemaphoreType.DMA((2 + len(own_rows), count - 1))
     return pl.pallas_call(
-        functools.partial(sum_kernel, len(arrays)),
-        in_specs=[vmem] * (1 + len(arrays)),
-        out_specs=[vmem] * (1 + len(arrays)),
-        out_shape=[jax.ShapeDtypeStruct(part.shape, part.dtype)] + swap_shapes(arrays),
+        functools.partial(sum_kernel, len(own_rows), len(arrays)),
+        in_specs=[vmem] * len(operands),
+        out_specs=[vmem] * len(operands),
+        out_shape=[jax.ShapeDtypeStruct(part.shape, part.dtype)]
+        + [
+            jax.ShapeDtypeStruct((own.shape[0] * count,) + own.shape[1:], own.dtype)
+            for own in own_rows
+        ]
+        + swap_shapes(arrays),
         scratch_shapes=[slots_for(part, count), sems, sems] + swap_scratch(arrays),
         compiler_params=pltpu.CompilerParams(
             collective_id=call_id, has_side_effects=True, vmem_limit_bytes=40 * 2**20
         ),
-    )(part, *arrays)
+    )(*operands)
 
 
 def mixer_out_kernel(
@@ -646,6 +659,364 @@
     )(part, ct, middle, gain, out_all, *arrays)
 
 
+def send_on(source, target, send_sem, recv_sem, ctx):
+    return pltpu.make_async_remote_copy(
+        src_ref=source,
+        dst_ref=target,
+        send_sem=send_sem,
+        recv_sem=recv_sem,
+        device_id={"ctx": ctx},
+        device_id_type=pl.DeviceIdType.MESH,
+    )
+
+
+def forward_pair_kernel(
+    n_state,
+    tiles,
+    groups,
+    blocks,
+    seqs,
+    step_ref,
+    input_ref,
+    brow_ref,
+    crow_ref,
+    rate_ref,
+    prior_ref,
+    mixed_ref,
+    carried,
+    ends,
+    starts,
+    prior_buf,
+    step_held,
+    input_held,
+    mixed_held,
+    prior_sem,
+    send_sem,
+    recv_sem,
+):
+    place = lax.axis_index("ctx")
+    greet([(("ctx",), [1 - place])])
+
+    def hand_on(seq):
+        return send_on(ends.at[seq], starts.at[seq], send_sem.at[seq], recv_sem.at[seq], 1)
+
+    def store(block):
+        slot = lax.rem(block, 2)
+        rows = groups * SUB
+        return pltpu.make_async_copy(
+            prior_buf.at[slot],
+            prior_ref.at[pl.ds(pl.multiple_of(block * rows, rows), rows)],
+            prior_sem.at[slot],
+        )
+
+    @pl.loop(0, seqs)
+    def _(seq):
+        @pl.when(place == 0)
+        def _():
+            carried[...] = jnp.zeros_like(carried)
+
+        @pl.when(place == 1)
+        def _():
+            hand_on(seq).wait_recv()
+            carried[...] = starts[seq]
+
+        @pl.loop(0, blocks)
+        def _(inner_block):
+            block = seq * blocks + inner_block
+            slot = lax.rem(block, 2)
+
+            @pl.when(block >= 2)
+            def _():
+                store(block - 2).wait()
+
+            def one(turn, states):
+                group = block * groups + turn
+                states = list(states)
+                stage_in(step_ref, group, step_held)
+                stage_in(input_ref, group, input_held)
+                for at in range(SUB):
+                    step = token_row(step_held, at, tiles)
+                    drive = step * token_row(input_held, at, tiles)
+                    mixed = [None] * 2
+                    for n in range(n_state):
+                        where = (group * SUB + at) * n_state + n
+                        prior_buf[slot, turn * SUB + at, n] = states[n]
+                        decay = jnp.exp2(step * rate_ref[n])
+                        states[n] = decay * states[n] + drive * brow_ref[where]
+                        term = states[n] * crow_ref[where]
+                        mixed[n % 2] = term if mixed[n % 2] is None else mixed[n % 2] + term
+                    mixed_held[pl.ds(at, tiles, stride=SUB), :] = mixed[0] + mixed[1]
+                stage_out(mixed_held, mixed_ref, group)
+                return tuple(states)
+
+            states = lax.fori_loop(0, groups, one, tuple(carried[n] for n in range(n_state)))
+            for n in range(n_state):
+                carried[n] = states[n]
+            store(block).start()
+
+        @pl.when(place == 0)
+        def _():
+            ends[seq] = carried[...]
+            hand_on(seq).start()
+
+    for block in range(max(0, seqs * blocks - 2), seqs * blocks):
+        store(block).wait()
+
+    @pl.when(place == 0)
+    def _():
+        @pl.loop(0, seqs)
+        def _(seq):
+            hand_on(seq).wait_send()
+
+
+def scan_forward_pair(call_id, step, inputs, b_rows, c_rows, rate, seqs):
+    n_state, tiles, _ = rate.shape
+    tokens, inner = step.shape
+    all_groups = tokens // SUB
+    groups = math.gcd(all_groups // seqs, 4)
+    blocks = all_groups // seqs // groups
+    vmem = pl.BlockSpec(memory_space=pltpu.VMEM)
+    smem = pl.BlockSpec(memory_space=pltpu.SMEM)
+    full = jnp.float32
+    held = pltpu.VMEM((tiles * SUB, LANE), full)
+    boundary = pltpu.VMEM((seqs, n_state, tiles, LANE), full)
+    dma = pltpu.SemaphoreType.DMA
+    return pl.pallas_call(
+        functools.partial(forward_pair_kernel, n_state, tiles, groups, blocks, seqs),
+        in_specs=[vmem, vmem, smem, smem, vmem],
+        out_specs=[pl.BlockSpec(memory_space=pl.ANY), vmem],
+        out_shape=[
+            jax.ShapeDtypeStruct((tokens, n_state, tiles, LANE), full),
+            jax.ShapeDtypeStruct(step.shape, full),
+        ],
+        scratch_shapes=[
+            pltpu.VMEM((n_state, tiles, LANE), full),
+            boundary,
+            boundary,
+            pltpu.VMEM((2, groups * SUB, n_state, tiles, LANE), full),
+            held,
+            held,
+            held,
+            dma((2,)),
+            dma((seqs,)),
+            dma((seqs,)),
+        ],
+        compiler_params=pltpu.CompilerParams(
+            collective_id=call_id, has_side_effects=True, vmem_limit_bytes=40 * 2**20
+        ),
+    )(step, inputs, b_rows, c_rows, rate)
+
+
+def backward_pair_kernel(
+    n_state,
+    tiles,
+    groups,
+    blocks,
+    seqs,
+    step_ref,
+    input_ref,
+    ograd_ref,
+    brow_ref,
+    crow_ref,
+    rate_ref,
+    picks_ref,
+    ffn_part,
+    middle,
+    prior_ref,
+    step_grad_ref,
+    input_grad_ref,
+    rate_grad_ref,
+    part_ref,
+    layer_rows,
+    carried,
+    ends,
+    starts,
+    prior_buf,
+    step_held,
+    input_held,
+    ograd_held,
+    step_grad_held,
+    input_grad_held,
+    ffn_slots,
+    prior_sem,
+    send_sem,
+    recv_sem,
+    tp_send,
+    tp_recv,
+):
+    place = lax.axis_index("ctx")
+    tp = Group(("tp",), tp_send, tp_recv)
+    greet([(("ctx",), [1 - place]), (("tp",), tp.others)])
+    ffn_sent = tp.scatter(ffn_part, ffn_slots, 0)
+
+    def hand_on(seq):
+        return send_on(ends.at[seq], starts.at[seq], send_sem.at[seq], recv_sem.at[seq], 0)
+
+    def fetch(turn):
+        seq = lax.div(turn, blocks)
+        block = seq * blocks + blocks - 1 - lax.rem(turn, blocks)
+        slot = lax.rem(turn, 2)
+        rows = groups * SUB
+        return pltpu.make_async_copy(
+            prior_ref.at[pl.ds(pl.multiple_of(block * rows, rows), rows)],
+            prior_buf.at[slot],
+            prior_sem.at[slot],
+        )
+
+    fetch(0).start()
+    rate_grad_ref[...] = jnp.zeros_like(rate_grad_ref)
+
+    @pl.when(place == 1)
+    def _():
+        @pl.loop(0, seqs)
+        def _(seq):
+            def one(turn, grads):
+                group = (seq + 1) * blocks * groups - 1 - turn
+                grads = list(grads)
+                stage_in(step_ref, group, step_held)
+                stage_in(ograd_ref, group, ograd_held)
+                for at in range(SUB - 1, -1, -1):
+                    step = token_row(step_held, at, tiles)
+                    ograd = token_row(ograd_held, at, tiles)
+                    for n in range(n_state):
+                        row = crow_ref[(group * SUB + at) * n_state + n]
+                        grads[n] = jnp.exp2(step * rate_ref[n]) * (grads[n] + ograd * row)
+                return tuple(grads)
+
+            zero = jnp.zeros((tiles, LANE), jnp.float32)
+            grads = lax.fori_loop(0, blocks * groups, one, (zero,) * n_state)
+            for n in range(n_state):
+                ends[seq, n] = grads[n]
+            hand_on(seq).start()
+
+    @pl.loop(0, seqs)
+    def _(seq):
+        @pl.when(place == 1)
+        def _():
+            carried[...] = jnp.zeros_like(carried)
+
+        @pl.when(place == 0)
+        def _():
+            hand_on(seq).wait_recv()
+            carried[...] = starts[seq]
+
+        @pl.loop(0, blocks)
+        def _(inner_block):
+            turn = seq * blocks + inner_block
+            slot = lax.rem(turn, 2)
+            first_group = (seq * blocks + blocks - 1 - inner_block) * groups
+
+            @pl.when(turn + 1 < seqs * blocks)
+            def _():
+                fetch(turn + 1).start()
+
+            fetch(turn).wait()
+
+            def one(back, grads):
+                inner_group = groups - 1 - back
+                group = first_group + inner_group
+                grads = list(grads)
+                stage_in(step_ref, group, step_held)
+                stage_in(input_ref, group, input_held)
+                stage_in(ograd_ref, group, ograd_held)
+                for at in range(SUB - 1, -1, -1):
+                    step = token_row(step_held, at, tiles)
+                    value = token_row(input_held, at, tiles)
+                    ograd = token_row(ograd_held, at, tiles)
+                    drive = step * value
+                    along_b = None
+                    along_rate = None
+                    brow_parts, crow_parts = [], []
+                    for n in range(n_state):
+                        where = (group * SUB + at) * n_state + n
+                        brow, crow = brow_ref[where], crow_ref[where]
+                        rate = rate_ref[n]
+                        decay = jnp.exp2(step * rate)
+                        grad = ograd * crow + grads[n]
+                        kept = decay * prior_buf[slot, inner_group * SUB + at, n]
+                        state = kept + drive * brow
+                        decay_term = grad * kept
+                        grads[n] = decay * grad
+                        rate_grad_ref[n] += decay_term * step
+                        by_rate, by_brow = decay_term * rate, grad * brow
+                        along_rate = by_rate if along_rate is None else along_rate + by_rate
+                        along_b = by_brow if along_b is None else along_b + by_brow
+                        brow_parts.append(grad * drive)
+                        crow_parts.append(ograd * state)
+                    step_grad_held[pl.ds(at, tiles, stride=SUB), :] = (
+                        along_rate * LN2 + along_b * value
+                    )
+                    input_grad_held[pl.ds(at, tiles, stride=SUB), :] = along_b * step
+                    parts = jnp.concatenate(brow_parts + crow_parts, 0).astype(jnp.bfloat16)
+                    part_ref[group * SUB + at] = jnp.dot(
+                        picks_ref[...], parts, preferred_element_type=jnp.float32
+                    )
+                stage_out(step_grad_held, step_grad_ref, group)
+                stage_out(input_grad_held, input_grad_ref, group)
+                return tuple(grads)
+
+            grads = lax.fori_loop(0, groups, one, tuple(carried[n] for n in range(n_state)))
+            for n in range(n_state):
+                carried[n] = grads[n]
+
+    finish(ffn_sent)
+    layer_rows[...] = (middle[...] + tp.total(ffn_part, ffn_slots)).astype(layer_rows.dtype)
+
+    @pl.when(place == 1)
+    def _():
+        @pl.loop(0, seqs)
+        def _(seq):
+            hand_on(seq).wait_send()
+
+
+def scan_backward_pair(
+    call_id, prior, step, inputs, ograd, b_rows, c_rows, rate, seqs, ffn_part, middle
+):
+    n_state, tiles, _ = rate.shape
+    tokens, inner = step.shape
+    all_groups = tokens // SUB
+    groups = math.gcd(all_groups // seqs, 4)
+    blocks = all_groups // seqs // groups
+    tp_count = group_size(("tp",))
+    vmem = pl.BlockSpec(memory_space=pltpu.VMEM)
+    smem = pl.BlockSpec(memory_space=pltpu.SMEM)
+    full = jnp.float32
+    held = pltpu.VMEM((tiles * SUB, LANE), full)
+    boundary = pltpu.VMEM((seqs, n_state, tiles, LANE), full)
+    dma = pltpu.SemaphoreType.DMA
+    picks = jnp.repeat(jnp.eye(2 * n_state, dtype=jnp.bfloat16), tiles, 1)
+    return pl.pallas_call(
+        functools.partial(backward_pair_kernel, n_state, tiles, groups, blocks, seqs),
+        in_specs=[vmem] * 3 + [smem] * 2 + [vmem] * 4 + [pl.BlockSpec(memory_space=pl.ANY)],
+        out_specs=[vmem] * 5,
+        out_shape=[
+            jax.ShapeDtypeStruct(step.shape, full),
+            jax.ShapeDtypeStruct(step.shape, full),
+            jax.ShapeDtypeStruct(rate.shape, full),
+            jax.ShapeDtypeStruct((tokens, 2 * n_state, LANE), full),
+            jax.ShapeDtypeStruct(middle.shape, jnp.bfloat16),
+        ],
+        scratch_shapes=[
+            pltpu.VMEM((n_state, tiles, LANE), full),
+            boundary,
+            boundary,
+            pltpu.VMEM((2, groups * SUB, n_state, tiles, LANE), full),
+        ]
+        + [held] * 5
+        + [
+            slots_for(ffn_part, tp_count),
+            dma((2,)),
+            dma((seqs,)),
+            dma((seqs,)),
+            dma((1, tp_count - 1)),
+            dma((1, tp_count - 1)),
+        ],
+        compiler_params=pltpu.CompilerParams(
+            collective_id=call_id, has_side_effects=True, vmem_limit_bytes=48 * 2**20
+        ),
+    )(step, inputs, ograd, b_rows, c_rows, rate, picks, ffn_part, middle, prior)
+
+
 class PlaneGather:
     def __init__(self, own, gathered, send_sem, recv_sem):
         self.own, self.gathered = own, gathered
@@ -788,10 +1159,8 @@
     sizes,
     mix_grads,
     normed_part,
-    ffn_part,
     small,
     tokens,
-    middle_rows,
     middle_grad,
     gain_row,
     one_cols,
@@ -800,7 +1169,6 @@
     middle_cols,
     ffn_all,
     tokens_grad,
-    layer_out,
     small_sum,
     gains,
     mix_all,
@@ -809,7 +1177,6 @@
     grad_gateup,
     grad_downproj,
     normed_slots,
-    ffn_slots,
     small_slots,
     gain_slots,
     gain_own,
@@ -864,7 +1231,6 @@
 
     normed_sent = tp.scatter(normed_part, normed_slots, 0)
     gather.begin(local_sem)
-    ffn_sent = tp.scatter(ffn_part, ffn_slots, 1)
     small_sent = plane.scatter(small, small_slots, 0)
     products(
         ffn_all, down_end, gu_end, flat(two_cols), side_by_side(grad_gateup, down_end), *wide
@@ -883,7 +1249,7 @@
             gain_row[...].astype(jnp.float32),
         )
     ).astype(tokens_grad.dtype)
-    tokens_sent = tp.spread(tokens_grad, 2)
+    tokens_sent = tp.spread(tokens_grad, 1)
     finish(small_sent)
     plane.own(small_sum)[...] = plane.total(small, small_slots).astype(small_sum.dtype)
     small_sent = plane.spread(small_sum, 1)
@@ -891,14 +1257,9 @@
         ffn_all, gu_end, out_end, tall(middle_cols), one_above_other(grad_outproj, gu_end), *high
     )
     gather.hand_over_last()
-    finish(ffn_sent)
-    tp.own(layer_out)[...] = (middle_rows[...] + tp.total(ffn_part, ffn_slots)).astype(
-        layer_out.dtype
-    )
-    layer_sent = tp.spread(layer_out, 3)
     finish(small_sent)
     gain_own[...] = small_sum[pl.ds(gain_at, gain_own.shape[0]), :].astype(jnp.float32)
-    gain_sent = [tp.one(gain_own, gain_slots.at[hop], 4, hop) for hop in range(tp.count - 1)]
+    gain_sent = [tp.one(gain_own, gain_slots.at[hop], 2, hop) for hop in range(tp.count - 1)]
     gather.end()
     products(
         mix_all, 0, 2 * inner // WIDE, flat(one_cols), side_by_side(grad_inproj, 0), *wide
@@ -909,7 +1270,6 @@
         total = total + gain_slots[hop]
     gains[...] = total
     finish(tokens_sent)
-    finish(layer_sent)
 
 
 def run_tail(
@@ -917,10 +1277,8 @@
     gain_at,
     mix_grads,
     normed_part,
-    ffn_part,
     small,
     tokens,
-    middle_rows,
     middle_grad,
     gain_row,
     one_cols,
@@ -941,10 +1299,9 @@
     dma = pltpu.SemaphoreType.DMA
     return pl.pallas_call(
         functools.partial(tail_kernel, (inner, hidden, gain_at)),
-        in_specs=[vmem] * 12 + [hbm],
-        out_specs=[vmem] * 4 + [hbm] * 5,
+        in_specs=[vmem] * 10 + [hbm],
+        out_specs=[vmem] * 3 + [hbm] * 5,
         out_shape=[
-            jax.ShapeDtypeStruct(tokens.shape, low),
             jax.ShapeDtypeStruct(tokens.shape, low),
             jax.ShapeDtypeStruct(small.shape, low),
             jax.ShapeDtypeStruct((gain_rows, inner), full),
@@ -956,7 +1313,6 @@
         ],
         scratch_shapes=[
             slots_for(normed_part, tp_count),
-            slots_for(ffn_part, tp_count),
             slots_for(small, plane_count),
             pltpu.VMEM((tp_count - 1, gain_rows, inner), full),
             pltpu.VMEM((gain_rows, inner), full),
@@ -966,8 +1322,8 @@
             dma((2,)),
             dma((2,)),
             dma((2,)),
-            dma((5, tp_count - 1)),
-            dma((5, tp_count - 1)),
+            dma((3, tp_count - 1)),
+            dma((3, tp_count - 1)),
             dma((2, plane_count - 1)),
             dma((2, plane_count - 1)),
             gather_sems(),
@@ -980,10 +1336,8 @@
     )(
         mix_grads,
         normed_part,
-        ffn_part,
         small,
         tokens,
-        middle_rows,
         middle_grad,
         gain_row,
         one_cols,
@@ -1149,18 +1503,22 @@
     columns = selproj.shape[1]
     select_width = -(-columns // LANE) * LANE
     select_weights = jnp.pad(selproj, ((0, 0), (0, select_width - columns)))
-    (select_cols,) = sum_over_tp(0, matmul(scan_in, select_weights), [])
+    (select_cols,) = sum_over_tp(0, matmul(scan_in, select_weights), [], [])
     step_low = select_cols[:, :rank].astype(low)
     b_rows = select_cols[:, rank : rank + n_state].reshape(-1)
     c_rows = select_cols[:, rank + n_state : columns].reshape(-1)
     step_pre = matmul(step_low, stepproj) + step_bias[None]
     step_size = jax.nn.softplus(step_pre)
-    span_decay = jnp.exp(
-        decay_rate[None] * jnp.sum(step_size.reshape(seqs, span, inner), 1)[:, None]
-    ).reshape(seqs, n_state, tiles, LANE)
-    ends = scan_ends(step_size, scan_float, b_rows, rate, seqs, False)
-    start = from_earlier(ends, span_decay, 1)
-    prior, scan_out = scan_forward(start, step_size, scan_float, b_rows, c_rows, rate, seqs)
+    in_pairs = lax.axis_size("ctx") == 2
+    if in_pairs:
+        prior, scan_out = scan_forward_pair(6, step_size, scan_float, b_rows, c_rows, rate, seqs)
+    else:
+        span_decay = jnp.exp(
+            decay_rate[None] * jnp.sum(step_size.reshape(seqs, span, inner), 1)[:, None]
+        ).reshape(seqs, n_state, tiles, LANE)
+        ends = scan_ends(step_size, scan_float, b_rows, rate, seqs, False)
+        start = from_earlier(ends, span_decay, 1)
+        prior, scan_out = scan_forward(start, step_size, scan_float, b_rows, c_rows, rate, seqs)
     mixer_core = scan_out + skip_weight[None] * scan_float
     gate_sig = jax.nn.silu(gate_mix)
     gated = (mixer_core * gate_sig).astype(low)
@@ -1191,11 +1549,28 @@
     core_grad = gated_grad * gate_sig
     gate_mix_grad = (gated_grad * mixer_core * silu_slope(gate_mix)).astype(low)
     grad_skipgain = jnp.sum(core_grad * scan_float, 0)
-    back_ends = scan_ends(step_size, core_grad, c_rows, rate, seqs, True)
-    end_grad = from_earlier(back_ends, span_decay, -1)
-    step_grad, input_grad, rate_grad, parts = scan_backward(
-        end_grad, prior, step_size, scan_float, core_grad, b_rows, c_rows, rate, seqs
-    )
+    if in_pairs:
+        step_grad, input_grad, rate_grad, parts, layer_rows = scan_backward_pair(
+            7,
+            prior,
+            step_size,
+            scan_float,
+            core_grad,
+            b_rows,
+            c_rows,
+            rate,
+            seqs,
+            ffn_part,
+            middle,
+        )
+    else:
+        back_ends = scan_ends(step_size, core_grad, c_rows, rate, seqs, True)
+        end_grad = from_earlier(back_ends, span_decay, -1)
+        step_grad, input_grad, rate_grad, parts = scan_backward(
+            end_grad, prior, step_size, scan_float, core_grad, b_rows, c_rows, rate, seqs
+        )
+        ffn_sum = lax.psum_scatter(ffn_part, "tp", scatter_dimension=0, tiled=True)
+        layer_rows = (middle + ffn_sum.astype(jnp.float32)).astype(low)
     grad_decaylog = rate_grad.reshape(n_state, inner) * decay_rate
     pre_grad = step_grad * jax.nn.sigmoid(step_pre)
     grad_stepbias = jnp.sum(pre_grad, 0)
@@ -1209,7 +1584,9 @@
         ],
         1,
     ).astype(low)
-    select_low, *swapped = sum_over_tp(3, select_part, [middle_low] if swap_now else [])
+    select_low, layer_out, *swapped = sum_over_tp(
+        3, select_part, [layer_rows], [middle_low] if swap_now else []
+    )
     (middle_cols,) = swapped if swap_now else [swapped_columns(middle_low)]
     grad_selproj = matmul_tn(select_low, scan_in)
     scan_in_grad = (
@@ -1258,7 +1635,6 @@
     small = jnp.pad(small, ((0, -(gain_at + 16) % share + 16 - sum(sizes[-2:])), (0, 0)))
     (
         tokens_grad,
-        layer_out,
         small,
         gains,
         _,
@@ -1271,10 +1647,8 @@
         gain_at,
         mix_grads,
         normed_one_part,
-        ffn_part,
         small,
         tokens_rows,
-        middle,
         middle_grad,
         gain_mix_row,
         normed_one_cols,

time: 568 us -> 536 us (0.944)
  Pallas kernels: 361 us -> 336 us
  local copies, waits for them, and re-layouts: 54.5 us -> 46.1 us
  starting transfers between devices: 11.1 us -> 4.89 us
    pallas_call x1, Pallas kernels: 106 us -> 68.8 us  [run_tail(): pl.pallas_call(functools.partial(tail_kernel, (inner, hidden, gain_at)),...]
    unnamed x156, local copies, waits for them, and re-layouts: 38.4 us -> 27.9 us
    pallas_call x6 -> x4, Pallas kernels: 80.9 us -> 89.9 us  [the longest x2 47.4 us: sum_over_tp(): pl.pallas_call(functools.partial(sum_kernel, len(own_rows), len(arrays)),...]
    all_gather x2, waiting for transfers between devices: 37.1 us -> 45 us  [gathered_rows(): return lax.all_gather(rows, PLANE, axis=0, tiled=True)]
    ppermute x4 -> x2, waiting for transfers between devices: 8.68 us -> 1.24 us  [passed_along(): lax.ppermute(value, axis, [(source, source + steps) for source in range(f...]
    ppermute x4 -> x2, starting transfers between devices: 11.1 us -> 4.81 us  [passed_along(): lax.ppermute(value, axis, [(source, source + steps) for source in range(f...]
  transfers between devices with their start and end apart: 6 -> 4, of which waited for: 5 -> 2; matrix products, arithmetic and copies ran while one was open for 9% -> 11% of each run, Pallas kernels for 35% -> 39%
where the time goes in v6:
time: 536 us; the launch traced here: 529 us
  Pallas kernels  336 us (63%)
  matrix products  55.6 us (10%)
  waiting for transfers between devices  46.3 us (9%)
  local copies, waits for them, and re-layouts  46.1 us (9%)
  other arithmetic  24.7 us (5%)
  between operations  15.4 us (3%)
    pallas_call x1, Pallas kernels, ffn_back(): pl.pallas_call(functools.partial(ffn_back_kernel, len(arrays)), in_specs=...  72.3 us
    pallas_call x1, Pallas kernels, run_tail(): pl.pallas_call(functools.partial(tail_kernel, (inner, hidden, gain_at)),...  68.8 us
    pallas_call x1, Pallas kernels, run_head(): pl.pallas_call(head_kernel, in_specs=[vmem] * 2 + [hbm] * 3, out_specs=[v...  58.9 us
    pallas_call x2, Pallas kernels, sum_over_tp(): pl.pallas_call(functools.partial(sum_kernel, len(own_rows), len(arrays)),...  47.4 us
    pallas_call x1, Pallas kernels, mixer_out(): pl.pallas_call(mixer_out_kernel, in_specs=[vmem] * 4, out_specs=[vmem] *...  46.4 us
    all_gather x2, waiting for transfers between devices, gathered_rows(): return lax.all_gather(rows, PLANE, axis=0, tiled=True)  45 us
    dot_general x6, matrix products, matmul_nt(): lax.dot_general(left, right, (((1,), (1,)), ((), ())), preferred_element_...  30.9 us
    pallas_call x1, Pallas kernels, scan_backward_pair(): pl.pallas_call(functools.partial(backward_pair_kernel, n_state, tiles, gr...  28.4 us
  transfers between devices with their start and end apart: 4, of which 2 were waited for; matrix products, arithmetic and copies ran while one was open for 11% of the time, Pallas kernels for 39%

profile of v6, /device:TPU:0, one launch (start us, length us, event | category | flops | bytes accessed | tf_op | source)
XLA Modules:
  0.0 529.2 jit_solution(12650950849258780221)
XLA Ops:
  10.5 2.3 copy.41
  14.1 3.2 pad_maximum_fusion.1
  17.3 58.9 %shard_map.262 = (bf16[256,1024]{1,0:T(8,128)(2,1)S(1)}, f32[256,1024]{1,0:T(8,128)S(1)}, bf16[2048,1024]{1,0:T(8,128)(2,1)S(1)}, bf16[2048,1024]{1,0:T(8,128)(2,1)S(1)}, bf16[8192,256]{1,0:T(8,128)(2,1)}) custom-call(bf16[256,2048]{1,0:T(8,128)(2,1)S(1)} %bitcast.96, bf16[1,2048]{1,0:T(2,128)(2,1)S(1)} %reshape.114.gain.gain_row, ...), custom_call_target="tpu_custom_call" | custom-call | tf_op jit(solution)/shard_map/pallas_call | solution.py:1423
  76.2 2.0 copy-done.5
  79.2 2.1 copy-done.30
  81.5 3.4 collective-permute-start
  89.9 14.9 %shard_map.263 = f32[256,256]{1,0:T(8,128)S(1)} custom-call(f32[256,256]{1,0:T(8,128)S(1)} %fusion.32.part), custom_call_target="tpu_custom_call" | custom-call | tf_op jit(solution)/shard_map/pallas_call | solution.py:545
  105.2 1.7 compare_select_fusion
  106.9 14.1 %shard_map.264 = (f32[256,16,8,128]{3,2,1,0:T(8,128)}, f32[256,1024]{1,0:T(8,128)S(1)}) custom-call(f32[256,1024]{1,0:T(8,128)S(1)} %get-tuple-element.121.step_ref, f32[256,1024]{1,0:T(8,128)S(1)} %get-tuple-element.93.input_ref, f32[4096]{0:T(1024)S(1)} %reshape.117.brow_ref, f32[4096]{0:T(1024)S(1)} %reshape.118.crow_ref, f32[16,8,128]{2,1,0:T(8,128)S(1)} %bitcast.99), custom_call_target="tpu_custom_call" | custom-call | tf_op jit(solution)/shard_map/pallas_call | solution.py:784
  122.0 46.4 %shard_map.265 = (bf16[256,2048]{1,0:T(8,128)(2,1)S(1)}, f32[64,2048]{1,0:T(8,128)S(1)}) custom-call(bf16[256,1024]{1,0:T(8,128)(2,1)S(1)} %multiply_convert_fusion.4.gated, bf16[8192,256]{1,0:T(8,128)(2,1)S(1)} %copy-done.2, bf16[256,2048]{1,0:T(8,128)(2,1)S(1)} %bitcast.97, bf16[1,2048]{1,0:T(2,128)(2,1)S(1)} %reshape.120.gain), custom_call_target="tpu_custom_call" | custom-call | tf_op jit(solution)/shard_map/pallas_call | solution.py:588
  169.5 45.0 %all-gather.3.cloned.1.call-done = bf16[2048,6144]{0,1:T(8,128)(2,1)} async-done(((bf16[256,6144]{0,1:T(8,128)(2,1)}), bf16[2048,6144]{0,1:T(8,128)(2,1)}) %all-gather.3.cloned.1.call-update) | async-done | bytes 25165840 | tf_op jit(solution)/shard_map/all_gather | solution.py:365
  214.5 12.6 %fusion.2 = f32[256,4096]{1,0:T(8,128)} fusion(bf16[256,2048]{1,0:T(8,128)(2,1)} %copy-done.19, bf16[2048,6144]{0,1:T(8,128)(2,1)} %all-gather.3.cloned.1.call-done), kind=kOutput, calls=%fused_computation.2 | convolution fusion | flops 4294967296 | bytes 22020096 | tf_op jit(solution)/shard_map/dot_general | solution.py:26
  227.2 7.9 %multiply_convert_fusion.1 = (bf16[256,2048]{1,0:T(8,128)(2,1)S(1)}, bf16[256,2048]{1,0:T(8,128)(2,1)S(1)}, bf16[256,2048]{1,0:T(8,128)(2,1)S(1)}) fusion(f32[256,4096]{1,0:T(8,128)} %fusion.2, bf16[256,2048]{1,0:T(8,128)(2,1)} %bitcast.109, bf16[2048,6144]{0,1:T(8,128)(2,1)} %all-gather.3.cloned.1.call-done), kind=kOutput, calls=%fused_computation.24 | convolution fusion | flops 2155347968 | bytes 16777216 | tf_op jit(solution)/shard_map/dot_general | solution.py:26
  235.1 1.6 pad_maximum_fusion.2
  236.7 2.2 pad_maximum_fusion
  241.9 13.0 %fusion.11.part = bf16[256,2048]{1,0:T(8,128)(2,1)} fusion(bf16[256,4096]{1,0:T(8,128)(2,1)S(1)} %copy-done.46, bf16[2048,6144]{0,1:T(8,128)(2,1)} %all-gather.3.cloned.1.call-done), kind=kOutput, calls=%fused_computation.15 | convolution fusion | flops 4295491584 | bytes 19922944 | tf_op jit(solution)/shard_map/dot_general | solution.py:30
  254.9 72.3 %shard_map.266 = (bf16[256,2048]{1,0:T(8,128)(2,1)S(1)}, f32[64,2048]{1,0:T(8,128)S(1)}, f32[1,2048]{1,0:T(1,128)S(1)}, f32[256,1024]{1,0:T(8,128)S(1)}, bf16[20...) custom-call(bf16[256,2048]{1,0:T(8,128)(2,1)} %fusion.11.part, ...), custom_call_target="tpu_custom_call" | custom-call | tf_op jit(solution)/shard_map/pallas_call | solution.py:644
  328.2 2.0 multiply_reduce_fusion.1
  330.3 8.7 %fusion.14.ffn_part = bf16[256,2048]{1,0:T(8,128)(2,1)} fusion(bf16[256,2048]{1,0:T(8,128)(2,1)S(1)} %copy-done.52, bf16[2048,6144]{0,1:T(8,128)(2,1)} %all-gather.3.cloned.1.call-done), kind=kOutput, calls=%fused_computation.16 | convolution fusion | flops 2148007936 | bytes 10485760 | tf_op jit(solution)/shard_map/dot_general | solution.py:30
  339.0 28.4 %shard_map.267 = (f32[256,1024]{1,0:T(8,128)S(1)}, f32[256,1024]{1,0:T(8,128)S(1)}, f32[16,8,128]{2,1,0:T(8,128)S(1)}, f32[256,32,128]{2,1,0:T(8,128)}, bf16[64,2048]{1,0:T(8,128)(2,1)S(1)}) custom-call(f32[256,1024]{1,0:T(8,128)S(1)} %copy-done.4, f32[256,1024]{1,0:T(8,128)S(1)} %get-tuple-element.93.input_ref, ...), custom_call_target="tpu_custom_call" | custom-call | tf_op jit(solution)/shard_map/pallas_call | solution.py:988
  370.7 3.4 reduce_sum.91
  374.2 1.7 fusion.43
  376.3 32.5 %shard_map.268 = (bf16[256,256]{1,0:T(8,128)(2,1)S(1)}, bf16[256,2048]{1,0:T(8,128)(2,1)S(1)}, bf16[2048,256]{1,0:T(8,128)(2,1)S(1)}) custom-call(bf16[256,256]{1,0:T(8,128)(2,1)S(1)} %maximum_maximum_fusion.part, bf16[64,2048]{1,0:T(8,128)(2,1)S(1)} %copy-done.26, bf16[256,2048]{1,0:T(8,128)(2,1)S(1)} %copy-done.16), custom_call_target="tpu_custom_call" | custom-call | tf_op jit(solution)/shard_map/pallas_call | solution.py:545
  411.8 1.4 collective-permute-start.1
  413.3 1.5 pad_add_fusion
  417.0 2.6 fusion.50
  419.8 1.9 slice.209
  423.1 5.0 fusion.20
  428.1 4.3 concatenate.30
  434.5 68.8 %shard_map.269 = (bf16[256,2048]{1,0:T(8,128)(2,1)}, bf16[384,1024]{1,0:T(8,128)(2,1)}, f32[16,1024]{1,0:T(8,128)}, bf16[2048,2048]{1,0:T(8,128)(2,1)}, f32[2,25...) custom-call(bf16[256,2048]{1,0:T(8,128)(2,1)} %pad_maximum_fusion.3.mix_grads, ...), custom_call_target="tpu_custom_call" | custom-call | tf_op jit(solution)/shard_map/pallas_call | solution.py:1300
  506.0 1.8 slice.162
  517.5 2.1 copy.60
  (215 shorter events, 44.0 us)
Async XLA Ops:
  7.2 98.0 %copy-start = (bf16[128,1024]{1,0:T(8,128)(2,1)S(1)}, bf16[128,1024]{1,0:T(8,128)(2,1)}, u32[]{:S(2)}) copy-start(bf16[128,1024]{1,0:T(8,128)(2,1)} %param.21) | copy-start | bytes 786436
  7.2 207.3 %all-gather.3.cloned.1.call-start = ((), (), s32[]{:S(2)}) async-start(), calls=%async_computation | async-start | bytes 28311552 | tf_op jit(solution)/shard_map/all_gather | solution.py:365
  8.1 9.2 %copy-start.27 = (bf16[1,2048]{1,0:T(2,128)(2,1)}, bf16[1,2048]{1,0:T(2,128)(2,1)S(1)}, u32[]{:S(2)}) copy-start(bf16[1,2048]{1,0:T(2,128)(2,1)S(1)} %reshape.114.gain.gain_row) | copy-start | bytes 12292
  81.4 3.6 copy-start.67
  81.4 3.6 copy-start.68
  81.4 3.6 copy-start.65
  81.4 353.0 %all-gather.5.cloned.1.call-start = ((), (), s32[]{:S(2)}) async-start(), calls=%async_computation.1 | async-start | bytes 33030144 | tf_op jit(solution)/shard_map/all_gather | solution.py:365
  81.5 4.8 collective-permute-start
  104.8 16.2 %copy-start.13 = (f32[256,256]{1,0:T(8,128)}, f32[256,256]{1,0:T(8,128)S(1)}, u32[]{:S(2)}) copy-start(f32[256,256]{1,0:T(8,128)S(1)} %shard_map.263) | copy-start | bytes 786436
  105.2 15.9 %copy-start.7 = (f32[256,1024]{1,0:T(8,128)S(1)}, f32[256,1024]{1,0:T(8,128)}, u32[]{:S(2)}) copy-start(f32[256,1024]{1,0:T(8,128)} %copy-done.6) | copy-start | bytes 3145732
  105.2 15.9 %copy-start.37 = (bf16[256,1024]{1,0:T(8,128)(2,1)S(1)}, bf16[256,1024]{1,0:T(8,128)(2,1)}, u32[]{:S(2)}) copy-start(bf16[256,1024]{1,0:T(8,128)(2,1)} %copy-done.36) | copy-start | bytes 1572868
  106.9 14.5 %copy-start.3 = (f32[256,1024]{1,0:T(8,128)}, f32[256,1024]{1,0:T(8,128)S(1)}, u32[]{:S(2)}) copy-start(f32[256,1024]{1,0:T(8,128)S(1)} %get-tuple-element.121.step_ref) | copy-start | bytes 3145732
  106.9 15.1 %copy-start.2 = (bf16[8192,256]{1,0:T(8,128)(2,1)S(1)}, bf16[8192,256]{1,0:T(8,128)(2,1)}, u32[]{:S(2)}) copy-start(bf16[8192,256]{1,0:T(8,128)(2,1)} %get-tuple-element.54.out_all) | copy-start | bytes 12582916
  169.5 85.4 %copy-start.11 = (f32[64,2048]{1,0:T(8,128)}, f32[64,2048]{1,0:T(8,128)S(1)}, u32[]{:S(2)}) copy-start(f32[64,2048]{1,0:T(8,128)S(1)} %get-tuple-element.58.middle) | copy-start | bytes 1572868
  240.6 14.3 %copy-start.63 = (f32[256]{0:T(256)}, f32[256]{0:T(256)S(1)}, u32[]{:S(2)}) copy-start(f32[256]{0:T(256)S(1)} %rsqrt_bitcast_fusion) | copy-start | bytes 3076
  254.9 73.3 %copy-start.8 = (f32[256,1024]{1,0:T(8,128)S(1)}, f32[256,1024]{1,0:T(8,128)}, u32[]{:S(2)}) copy-start(f32[256,1024]{1,0:T(8,128)} %copy-done.6) | copy-start | bytes 3145732
  254.9 73.3 %copy-start.10 = (f32[256,1024]{1,0:T(8,128)S(1)}, f32[256,1024]{1,0:T(8,128)}, u32[]{:S(2)}) copy-start(f32[256,1024]{1,0:T(8,128)} %copy-done.9) | copy-start | bytes 3145732
  254.9 73.3 %copy-start.38 = (bf16[256,1024]{1,0:T(8,128)(2,1)S(1)}, bf16[256,1024]{1,0:T(8,128)(2,1)}, u32[]{:S(2)}) copy-start(bf16[256,1024]{1,0:T(8,128)(2,1)} %copy-done.36) | copy-start | bytes 1572868
  330.3 8.7 %copy-start.4 = (f32[256,1024]{1,0:T(8,128)S(1)}, f32[256,1024]{1,0:T(8,128)}, u32[]{:S(2)}) copy-start(f32[256,1024]{1,0:T(8,128)} %copy-done.3) | copy-start | bytes 3145732
  330.3 8.7 %copy-start.12 = (f32[64,2048]{1,0:T(8,128)S(1)}, f32[64,2048]{1,0:T(8,128)}, u32[]{:S(2)}) copy-start(f32[64,2048]{1,0:T(8,128)} %copy-done.11) | copy-start | bytes 1572868
  374.2 34.6 %copy-start.33 = (f32[256,1024]{1,0:T(8,128)S(1)}, f32[256,1024]{1,0:T(8,128)}, u32[]{:S(2)}) copy-start(f32[256,1024]{1,0:T(8,128)} %copy-done.32) | copy-start | bytes 3145732
  374.2 34.6 %copy-start.35 = (f32[2,131,1024]{2,1,0:T(8,128)S(1)}, f32[2,131,1024]{2,1,0:T(8,128)}, u32[]{:S(2)}) copy-start(f32[2,131,1024]{2,1,0:T(8,128)} %copy-done.34) | copy-start | bytes 3219460
  374.2 34.6 %copy-start.50 = (f32[256,1024]{1,0:T(8,128)S(1)}, f32[256,1024]{1,0:T(8,128)}, u32[]{:S(2)}) copy-start(f32[256,1024]{1,0:T(8,128)} %get-tuple-element.107) | copy-start | bytes 3145732
  374.2 34.6 %copy-start.56 = (bf16[1024,160]{0,1:T(8,128)(2,1)S(1)}, bf16[1024,160]{0,1:T(8,128)(2,1)}, u32[]{:S(2)}) copy-start(bf16[1024,160]{0,1:T(8,128)(2,1)} %param.20) | copy-start | bytes 983044
  411.8 4.0 copy-start.39
  411.8 9.9 %collective-permute-start.1 = (f32[2,3,1024]{2,1,0:T(4,128)}, f32[2,3,1024]{2,1,0:T(4,128)}, u32[]{:S(2)}, u32[]{:S(2)}) collective-permute-start(f32[2,3,1024]{2,1,0:T(4,128)} %pad_add_fusion.1), channel_id=1, source_target_pairs={{4,0},{5,1},{6,2},{7,3},{12,8},{13,9},{14,10},{15,11},{20,16},{21,... | collective-permute-start | bytes 73736 | tf_op jit(solution)/shard_map/ppermute | solution.py:22
  413.3 3.6 copy-start.31
  416.9 4.7 copy-start.71
  416.9 4.7 copy-start.70
  416.9 4.7 copy-start.69
  428.1 5.3 %copy-start.49 = (bf16[256,1024]{1,0:T(8,128)(2,1)S(1)}, bf16[256,1024]{1,0:T(8,128)(2,1)}, u32[]{:S(2)}) copy-start(bf16[256,1024]{1,0:T(8,128)(2,1)} %get-tuple-element.98) | copy-start | bytes 1572868
  509.1 4.0 copy-start.54
  (45 other events, 93.4 us)
Sparse Core Ops, SparseCore 0:
  81.5 132.9 all-gather.2
  239.0 190.2 all-gather.4

commit v7 on v6

--- a/solution.py
+++ b/solution.py
@@ -509,66 +509,98 @@
     return width // group_size(PLANE) % LANE == 0
 
 
-def sum_kernel(n_rows, n_swaps, part, *refs):
+def sum_kernel(n_rows, n_swaps, n_gathers, part, *refs):
     own_rows, refs = refs[:n_rows], refs[n_rows:]
     arrays, refs = refs[:n_swaps], refs[n_swaps:]
+    shards, refs = refs[:n_gathers], refs[n_gathers:]
     total, refs = refs[0], refs[1:]
     all_rows, refs = refs[:n_rows], refs[n_rows:]
     swapped, refs = refs[:n_swaps], refs[n_swaps:]
+    gathered, refs = refs[:n_gathers], refs[n_gathers:]
     slots, send_sem, recv_sem, *refs = refs
     group = Group(("tp",), send_sem, recv_sem)
+    greeted = [(("tp",), group.others)]
     if n_swaps:
-        swap = Swap(arrays, swapped, *refs)
-        greet([(("tp",), group.others), (PLANE, swap.plane.others)])
-    else:
-        greet([(("tp",), group.others)])
+        swap = Swap(arrays, swapped, *refs[:3])
+        greeted.append((PLANE, swap.plane.others))
+        refs = refs[3:]
+    if n_gathers:
+        gather = PlaneGather(shards[0], gathered[0], *refs[:2])
+        if not n_swaps:
+            greeted.append((PLANE, gather.others))
+    greet(greeted)
     copies = group.scatter(part, slots, 0)
     if n_swaps:
         swap.begin()
+    if n_gathers:
+        gather.begin(refs[2])
     spreads = []
-    for which, (own, gathered) in enumerate(zip(own_rows, all_rows)):
-        group.own(gathered)[...] = own[...]
-        spreads += group.spread(gathered, 2 + which)
+    for which, (own, everything) in enumerate(zip(own_rows, all_rows)):
+        group.own(everything)[...] = own[...]
+        spreads += group.spread(everything, 2 + which)
     finish(copies)
     group.own(total)[...] = group.total(part, slots).astype(total.dtype)
-    finish(group.spread(total, 1))
+    copies = group.spread(total, 1)
+    if n_gathers:
+        gather.relay()
+        gather.hand_over()
+    finish(copies)
     finish(spreads)
     if n_swaps:
         swap.end()
-
-
-def sum_over_tp(call_id, part, own_rows, arrays):
+    if n_gathers:
+        gather.hand_over_last()
+        gather.end()
+
+
+def gathered_shape(shard):
+    return jax.ShapeDtypeStruct(
+        (shard.shape[0] * group_size(PLANE),) + shard.shape[1:], shard.dtype
+    )
+
+
+def gather_scratch():
+    return [gather_sems(), gather_sems(), pltpu.SemaphoreType.DMA(())]
+
+
+def sum_over_tp(call_id, part, own_rows, arrays, shards):
     count = group_size(("tp",))
     vmem = pl.BlockSpec(memory_space=pltpu.VMEM)
+    hbm = pl.BlockSpec(memory_space=pl.ANY)
     operands = [part, *own_rows, *arrays]
     sems = pltpu.SemaphoreType.DMA((2 + len(own_rows), count - 1))
     return pl.pallas_call(
-        functools.partial(sum_kernel, len(own_rows), len(arrays)),
-        in_specs=[vmem] * len(operands),
-        out_specs=[vmem] * len(operands),
+        functools.partial(sum_kernel, len(own_rows), len(arrays), len(shards)),
+        in_specs=[vmem] * len(operands) + [hbm] * len(shards),
+        out_specs=[vmem] * len(operands) + [hbm] * len(shards),
         out_shape=[jax.ShapeDtypeStruct(part.shape, part.dtype)]
         + [
             jax.ShapeDtypeStruct((own.shape[0] * count,) + own.shape[1:], own.dtype)
             for own in own_rows
         ]
-        + swap_shapes(arrays),
-        scratch_shapes=[slots_for(part, count), sems, sems] + swap_scratch(arrays),
+        + swap_shapes(arrays)
+        + [gathered_shape(shard) for shard in shards],
+        scratch_shapes=[slots_for(part, count), sems, sems]
+        + swap_scratch(arrays)
+        + gather_scratch() * len(shards),
         compiler_params=pltpu.CompilerParams(
             collective_id=call_id, has_side_effects=True, vmem_limit_bytes=40 * 2**20
         ),
-    )(*operands)
+    )(*operands, *shards)
 
 
 def mixer_out_kernel(
-    gated, out_all, tokens, gain, normed, middle, part, slots, send_sem, recv_sem
+    gated, out_first, out_last, tokens, gain, normed, middle, part, slots, send_sem, recv_sem
 ):
     group = Group(("tp",), send_sem, recv_sem)
-    inner = gated.shape[1]
-    share = out_all.shape[1]
+    half = gated.shape[1] // 2
+    share = out_first.shape[1]
     greet([(("tp",), group.others)])
-    for at in range(out_all.shape[0] // inner):
-        part[:, at * share : (at + 1) * share] = matmul(
-            gated[...], out_all[at * inner : (at + 1) * inner, :]
+    for at in range(out_first.shape[0] // half):
+        rows = slice(at * half, (at + 1) * half)
+        part[:, at * share : (at + 1) * share] = (
+            matmul(gated[:, :half], out_first[rows, :])
+            + matmul(gated[:, half:], out_last[rows, :])
         ).astype(part.dtype)
     finish(group.scatter(part, slots, 0))
     rows = group.own(tokens)[...].astype(jnp.float32) + group.total(part, slots)
@@ -579,7 +611,7 @@
     finish(group.spread(normed, 1))
 
 
-def mixer_out(call_id, gated, out_all, tokens, gain):
+def mixer_out(call_id, gated, out_first, out_last, tokens, gain):
     count = group_size(("tp",))
     vmem = pl.BlockSpec(memory_space=pltpu.VMEM)
     rows, width = tokens.shape
@@ -587,17 +619,17 @@
     sems = pltpu.SemaphoreType.DMA((2, count - 1))
     return pl.pallas_call(
         mixer_out_kernel,
-        in_specs=[vmem] * 4,
+        in_specs=[vmem] * 5,
         out_specs=[vmem] * 2,
         out_shape=[part, jax.ShapeDtypeStruct((rows // count, width), jnp.float32)],
         scratch_shapes=[pltpu.VMEM(part.shape, part.dtype), slots_for(part, count), sems, sems],
         compiler_params=pltpu.CompilerParams(
             collective_id=call_id, has_side_effects=True, vmem_limit_bytes=40 * 2**20
         ),
-    )(gated, out_all, tokens, gain)
-
-
-def ffn_back_kernel(n_swaps, part, ct, middle, gain, out_all, *refs):
+    )(gated, out_first, out_last, tokens, gain)
+
+
+def ffn_back_kernel(n_swaps, part, ct, middle, gain, out_first, out_last, *refs):
     arrays, refs = refs[:n_swaps], refs[n_swaps:]
     middle_low, middle_grad, gain_grad, gated_grad, *refs = refs
     swapped, refs = refs[:n_swaps], refs[n_swaps:]
@@ -622,28 +654,30 @@
     middle_grad[...] = grad
     group.own(middle_low)[...] = grad.astype(middle_low.dtype)
     finish(group.spread(middle_low, 1))
-    inner = gated_grad.shape[1]
-    share = out_all.shape[1]
-    total = None
-    for at in range(out_all.shape[0] // inner):
-        one = matmul_nt(
-            middle_low[:, at * share : (at + 1) * share], out_all[at * inner : (at + 1) * inner, :]
-        )
-        total = one if total is None else total + one
-    gated_grad[...] = total
+    half = gated_grad.shape[1] // 2
+    share = out_first.shape[1]
+    for side, weights in enumerate((out_first, out_last)):
+        total = None
+        for at in range(weights.shape[0] // half):
+            one = matmul_nt(
+                middle_low[:, at * share : (at + 1) * share],
+                weights[at * half : (at + 1) * half, :],
+            )
+            total = one if total is None else total + one
+        gated_grad[:, side * half : (side + 1) * half] = total
     if n_swaps:
         swap.end()
 
 
-def ffn_back(call_id, part, ct, middle, gain, out_all, arrays):
+def ffn_back(call_id, part, ct, middle, gain, out_first, out_last, arrays):
     count = group_size(("tp",))
     vmem = pl.BlockSpec(memory_space=pltpu.VMEM)
     rows, width = part.shape
-    inner = out_all.shape[0] // group_size(PLANE)
+    inner = 2 * out_first.shape[0] // group_size(PLANE)
     sems = pltpu.SemaphoreType.DMA((2, count - 1))
     return pl.pallas_call(
         functools.partial(ffn_back_kernel, len(arrays)),
-        in_specs=[vmem] * (5 + len(arrays)),
+        in_specs=[vmem] * (6 + len(arrays)),
         out_specs=[vmem] * (4 + len(arrays)),
         out_shape=[
             jax.ShapeDtypeStruct((rows, width), jnp.bfloat16),
@@ -656,7 +690,7 @@
         compiler_params=pltpu.CompilerParams(
             collective_id=call_id, has_side_effects=True, vmem_limit_bytes=48 * 2**20
         ),
-    )(part, ct, middle, gain, out_all, *arrays)
+    )(part, ct, middle, gain, out_first, out_last, *arrays)
 
 
 def send_on(source, target, send_sem, recv_sem, ctx):
@@ -681,8 +715,10 @@
     brow_ref,
     crow_ref,
     rate_ref,
+    shard,
     prior_ref,
     mixed_ref,
+    gathered,
     carried,
     ends,
     starts,
@@ -693,9 +729,14 @@
     prior_sem,
     send_sem,
     recv_sem,
+    gather_send,
+    gather_recv,
+    local_sem,
 ):
     place = lax.axis_index("ctx")
-    greet([(("ctx",), [1 - place])])
+    gather = PlaneGather(shard, gathered, gather_send, gather_recv)
+    greet([(PLANE, gather.others)])
+    gather.begin(local_sem)
 
     def hand_on(seq):
         return send_on(ends.at[seq], starts.at[seq], send_sem.at[seq], recv_sem.at[seq], 1)
@@ -709,8 +750,7 @@
             prior_sem.at[slot],
         )
 
-    @pl.loop(0, seqs)
-    def _(seq):
+    def one_sequence(seq):
         @pl.when(place == 0)
         def _():
             carried[...] = jnp.zeros_like(carried)
@@ -759,17 +799,24 @@
             ends[seq] = carried[...]
             hand_on(seq).start()
 
+    for seq in range(seqs):
+        one_sequence(seq)
+        if seq == 0:
+            gather.relay()
+            gather.hand_over()
+    gather.hand_over_last()
     for block in range(max(0, seqs * blocks - 2), seqs * blocks):
         store(block).wait()
 
     @pl.when(place == 0)
     def _():
-        @pl.loop(0, seqs)
-        def _(seq):
+        for seq in range(seqs):
             hand_on(seq).wait_send()
 
-
-def scan_forward_pair(call_id, step, inputs, b_rows, c_rows, rate, seqs):
+    gather.end()
+
+
+def scan_forward_pair(call_id, step, inputs, b_rows, c_rows, rate, seqs, shard):
     n_state, tiles, _ = rate.shape
     tokens, inner = step.shape
     all_groups = tokens // SUB
@@ -777,17 +824,19 @@
     blocks = all_groups // seqs // groups
     vmem = pl.BlockSpec(memory_space=pltpu.VMEM)
     smem = pl.BlockSpec(memory_space=pltpu.SMEM)
+    hbm = pl.BlockSpec(memory_space=pl.ANY)
     full = jnp.float32
     held = pltpu.VMEM((tiles * SUB, LANE), full)
     boundary = pltpu.VMEM((seqs, n_state, tiles, LANE), full)
     dma = pltpu.SemaphoreType.DMA
     return pl.pallas_call(
         functools.partial(forward_pair_kernel, n_state, tiles, groups, blocks, seqs),
-        in_specs=[vmem, vmem, smem, smem, vmem],
-        out_specs=[pl.BlockSpec(memory_space=pl.ANY), vmem],
+        in_specs=[vmem, vmem, smem, smem, vmem, hbm],
+        out_specs=[hbm, vmem, hbm],
         out_shape=[
             jax.ShapeDtypeStruct((tokens, n_state, tiles, LANE), full),
             jax.ShapeDtypeStruct(step.shape, full),
+            gathered_shape(shard),
         ],
         scratch_shapes=[
             pltpu.VMEM((n_state, tiles, LANE), full),
@@ -800,11 +849,12 @@
             dma((2,)),
             dma((seqs,)),
             dma((seqs,)),
-        ],
+        ]
+        + gather_scratch(),
         compiler_params=pltpu.CompilerParams(
             collective_id=call_id, has_side_effects=True, vmem_limit_bytes=40 * 2**20
         ),
-    )(step, inputs, b_rows, c_rows, rate)
+    )(step, inputs, b_rows, c_rows, rate, shard)
 
 
 def backward_pair_kernel(
@@ -1353,94 +1403,81 @@
     gain,
     in_conv,
     in_gate,
-    outproj,
     conv_in,
     gate_mix,
     conv_all,
     gate_all,
-    out_all,
     normed,
     block_buf,
     block_sem,
     *sems,
 ):
-    gathers = [
-        PlaneGather(own, gathered, *sems[3 * at : 3 * at + 2])
-        for at, (own, gathered) in enumerate(
-            [(in_conv, conv_all), (in_gate, gate_all), (outproj, out_all)]
-        )
-    ]
-    local_sems = sems[2::3]
-    conv, gate, out = gathers
+    conv = PlaneGather(in_conv, conv_all, *sems[:2])
+    gate = PlaneGather(in_gate, gate_all, *sems[3:5])
     greet([(PLANE, conv.others)])
-    conv.begin(local_sems[0])
-    gate.begin(local_sems[1])
+    conv.begin(sems[2])
+    gate.begin(sems[5])
     hidden_in = tokens[...].astype(jnp.float32)
-    normed[...] = (
-        hidden_in * inverse_rms(hidden_in) * gain[...].astype(jnp.float32)
-    ).astype(normed.dtype)
+    normed[...] = (hidden_in * inverse_rms(hidden_in) * gain[...].astype(jnp.float32)).astype(
+        normed.dtype
+    )
+
+    def product(source, target):
+        columns = range(0, source.shape[1], WIDE)
+
+        def fetch(turn):
+            at = columns[turn]
+            return pltpu.make_async_copy(
+                source.at[:, at : at + WIDE], block_buf.at[turn % 2], block_sem.at[turn % 2]
+            )
+
+        fetch(0).start()
+        for turn, at in enumerate(columns):
+            if turn + 1 < len(columns):
+                fetch(turn + 1).start()
+            fetch(turn).wait()
+            target[:, at : at + WIDE] = matmul(normed[...], block_buf[turn % 2]).astype(
+                target.dtype
+            )
+
     conv.relay()
     conv.hand_over()
     gate.relay()
+    conv.hand_over_last()
     gate.hand_over()
-    out.begin(local_sems[2])
-    conv.hand_over_last()
+    conv.end()
+    product(conv_all, conv_in)
     gate.hand_over_last()
-    conv.end()
     gate.end()
-    jobs = [
-        (source, target, at)
-        for source, target in ((conv_all, conv_in), (gate_all, gate_mix))
-        for at in range(0, conv_in.shape[1], WIDE)
-    ]
-
-    def fetch(turn):
-        source, _, at = jobs[turn]
-        return pltpu.make_async_copy(
-            source.at[:, at : at + WIDE], block_buf.at[turn % 2], block_sem.at[turn % 2]
-        )
-
-    fetch(0).start()
-    for turn, (_, target, at) in enumerate(jobs):
-        if turn + 1 < len(jobs):
-            fetch(turn + 1).start()
-        fetch(turn).wait()
-        if turn == 1:
-            out.relay()
-            out.hand_over()
-        target[:, at : at + WIDE] = matmul(normed[...], block_buf[turn % 2]).astype(target.dtype)
-    out.hand_over_last()
-    out.end()
-
-
-def run_head(call_id, tokens, gain, inproj, outproj):
+    product(gate_all, gate_mix)
+
+
+def run_head(call_id, tokens, gain, inproj):
     rows, width = tokens.shape
     inner = inproj.shape[2]
-    count = group_size(PLANE)
     low = jnp.bfloat16
     vmem = pl.BlockSpec(memory_space=pltpu.VMEM)
     hbm = pl.BlockSpec(memory_space=pl.ANY)
     return pl.pallas_call(
         head_kernel,
-        in_specs=[vmem] * 2 + [hbm] * 3,
-        out_specs=[vmem] * 2 + [hbm] * 3,
+        in_specs=[vmem] * 2 + [hbm] * 2,
+        out_specs=[vmem] * 2 + [hbm] * 2,
         out_shape=[
             jax.ShapeDtypeStruct((rows, inner), low),
             jax.ShapeDtypeStruct((rows, inner), jnp.float32),
             jax.ShapeDtypeStruct((width, inner), low),
             jax.ShapeDtypeStruct((width, inner), low),
-            jax.ShapeDtypeStruct((inner * count, width // count), low),
         ],
         scratch_shapes=[
             pltpu.VMEM((rows, width), low),
             pltpu.VMEM((2, width, WIDE), low),
             pltpu.SemaphoreType.DMA((2,)),
         ]
-        + [gather_sems(), gather_sems(), pltpu.SemaphoreType.DMA(())] * 3,
+        + gather_scratch() * 2,
         compiler_params=pltpu.CompilerParams(
             collective_id=call_id, has_side_effects=True, vmem_limit_bytes=40 * 2**20
         ),
-    )(tokens, gain, inproj[0], inproj[1], outproj)
+    )(tokens, gain, inproj[0], inproj[1])
 
 
 def per_device(
@@ -1480,13 +1517,10 @@
 
     tokens_rows = tokens.reshape(rows, width)
     ct_low = cotangent.reshape(rows, width)
-    conv_in, gate_mix, in_conv, in_gate, out_all = run_head(
-        5, tokens_rows, gain_mix_row, inproj, outproj
-    )
-    ffn_pack, conv_in = lax.optimization_barrier(
-        (jnp.concatenate([gateup[0], gateup[1], jnp.transpose(downproj)], 1), conv_in)
-    )
-    ffn_pack = gathered_rows(ffn_pack)
+    ffn_pack = gathered_rows(
+        jnp.concatenate([gateup[0], gateup[1], jnp.transpose(downproj)], 1)
+    )
+    conv_in, gate_mix, in_conv, in_gate = run_head(5, tokens_rows, gain_mix_row, inproj)
     hidden_in = tokens_rows.astype(jnp.float32)
     scale_one = inverse_rms(hidden_in)
     normed_one = (hidden_in * scale_one * gain_mix).astype(low)
@@ -1503,7 +1537,9 @@
     columns = selproj.shape[1]
     select_width = -(-columns // LANE) * LANE
     select_weights = jnp.pad(selproj, ((0, 0), (0, select_width - columns)))
-    (select_cols,) = sum_over_tp(0, matmul(scan_in, select_weights), [], [])
+    select_cols, out_first = sum_over_tp(
+        0, matmul(scan_in, select_weights), [], [], [outproj[: inner // 2]]
+    )
     step_low = select_cols[:, :rank].astype(low)
     b_rows = select_cols[:, rank : rank + n_state].reshape(-1)
     c_rows = select_cols[:, rank + n_state : columns].reshape(-1)
@@ -1511,7 +1547,9 @@
     step_size = jax.nn.softplus(step_pre)
     in_pairs = lax.axis_size("ctx") == 2
     if in_pairs:
-        prior, scan_out = scan_forward_pair(6, step_size, scan_float, b_rows, c_rows, rate, seqs)
+        prior, scan_out, out_last = scan_forward_pair(
+            6, step_size, scan_float, b_rows, c_rows, rate, seqs, outproj[inner // 2 :]
+        )
     else:
         span_decay = jnp.exp(
             decay_rate[None] * jnp.sum(step_size.reshape(seqs, span, inner), 1)[:, None]
@@ -1519,10 +1557,11 @@
         ends = scan_ends(step_size, scan_float, b_rows, rate, seqs, False)
         start = from_earlier(ends, span_decay, 1)
         prior, scan_out = scan_forward(start, step_size, scan_float, b_rows, c_rows, rate, seqs)
+        out_last = gathered_rows(outproj[inner // 2 :])
     mixer_core = scan_out + skip_weight[None] * scan_float
     gate_sig = jax.nn.silu(gate_mix)
     gated = (mixer_core * gate_sig).astype(low)
-    normed_two, middle = mixer_out(1, gated, out_all, tokens_rows, gain_ffn_row)
+    normed_two, middle = mixer_out(1, gated, out_first, out_last, tokens_rows, gain_ffn_row)
     gate_up = ffn_pack[:, : 2 * hidden]
     down_weights = ffn_pack[:, 2 * hidden :]
     both_ffn = matmul(normed_two, gate_up)
@@ -1541,7 +1580,14 @@
     swap_now = swaps_in_kernels(width)
     to_swap = [normed_one, normed_two, ct_low]
     middle_low, middle_grad, ffngain_part, gated_grad, *swapped = ffn_back(
-        2, normed_two_part, ct_low, middle, gain_ffn_row, out_all, to_swap if swap_now else []
+        2,
+        normed_two_part,
+        ct_low,
+        middle,
+        gain_ffn_row,
+        out_first,
+        out_last,
+        to_swap if swap_now else [],
     )
     if not swap_now:
         swapped = [swapped_columns(array) for array in to_swap]
@@ -1585,7 +1631,7 @@
         1,
     ).astype(low)
     select_low, layer_out, *swapped = sum_over_tp(
-        3, select_part, [layer_rows], [middle_low] if swap_now else []
+        3, select_part, [layer_rows], [middle_low] if swap_now else [], []
     )
     (middle_cols,) = swapped if swap_now else [swapped_columns(middle_low)]
     grad_selproj = matmul_tn(select_low, scan_in)

time: 536 us -> 531 us (level)
  waiting for transfers between devices: 46.3 us -> 1.22 us
  Pallas kernels: 336 us -> 380 us
    all_gather x2, waiting for transfers between devices: 45 us -> 0.01 us  [gathered_rows(): return lax.all_gather(rows, PLANE, axis=0, tiled=True)]
    pallas_call x4, Pallas kernels: 153 us -> 172 us  [the longest x1 68.5 us: run_head(): pl.pallas_call(head_kernel, in_specs=[vmem] * 2 + [hbm] * 2, out_specs=[v...]
    pallas_call x1, Pallas kernels: 14.1 us -> 31.9 us  [scan_forward_pair(): pl.pallas_call(functools.partial(forward_pair_kernel, n_state, tiles, gro...]
    pallas_call x1, Pallas kernels: 72.3 us -> 78.9 us  [ffn_back(): pl.pallas_call(functools.partial(ffn_back_kernel, len(arrays)), in_specs=...]
    unnamed x156 -> x160, local copies, waits for them, and re-layouts: 27.9 us -> 26.8 us
  transfers between devices with their start and end apart: 4 -> 4, of which waited for: 2 -> 1; matrix products, arithmetic and copies ran while one was open for 11% -> 11% of each run, Pallas kernels for 39% -> 59%
where the time goes in v7:
time: 531 us; the launch traced here: 525 us
  Pallas kernels  380 us (72%)
  matrix products  54 us (10%)
  local copies, waits for them, and re-layouts  43.5 us (8%)
  other arithmetic  24.3 us (5%)
  between operations  15.5 us (3%)
  starting transfers between devices  6.06 us (1%)
    pallas_call x1, Pallas kernels, ffn_back(): pl.pallas_call(functools.partial(ffn_back_kernel, len(arrays)), in_specs=...  78.9 us
    pallas_call x1, Pallas kernels, run_tail(): pl.pallas_call(functools.partial(tail_kernel, (inner, hidden, gain_at)),...  68.7 us
    pallas_call x1, Pallas kernels, run_head(): pl.pallas_call(head_kernel, in_specs=[vmem] * 2 + [hbm] * 2, out_specs=[v...  68.5 us
    pallas_call x2, Pallas kernels, sum_over_tp(): pl.pallas_call(functools.partial(sum_kernel, len(own_rows), len(arrays),...  57.7 us
    pallas_call x1, Pallas kernels, mixer_out(): pl.pallas_call(mixer_out_kernel, in_specs=[vmem] * 5, out_specs=[vmem] *...  46 us
    pallas_call x1, Pallas kernels, scan_forward_pair(): pl.pallas_call(functools.partial(forward_pair_kernel, n_state, tiles, gro...  31.9 us
    dot_general x6, matrix products, matmul_nt(): lax.dot_general(left, right, (((1,), (1,)), ((), ())), preferred_element_...  29.2 us
    pallas_call x1, Pallas kernels, scan_backward_pair(): pl.pallas_call(functools.partial(backward_pair_kernel, n_state, tiles, gr...  28.5 us
  transfers between devices with their start and end apart: 4, of which 1 were waited for; matrix products, arithmetic and copies ran while one was open for 11% of the time, Pallas kernels for 59%

profile of v7, /device:TPU:0, one launch (start us, length us, event | category | flops | bytes accessed | tf_op | source)
XLA Modules:
  0.0 524.6 jit_solution(11566939484762235862)
XLA Ops:
  7.2 1.7 fusion.46
  10.0 2.8 pad_maximum_fusion.1
  14.4 68.5 %shard_map.262 = (bf16[256,1024]{1,0:T(8,128)(2,1)S(1)}, f32[256,1024]{1,0:T(8,128)S(1)}, bf16[2048,1024]{1,0:T(8,128)(2,1)S(1)}, bf16[2048,1024]{1,0:T(8,128)(2,1)S(1)}) custom-call(bf16[256,2048]{1,0:T(8,128)(2,1)S(1)} %bitcast.96, bf16[1,2048]{1,0:T(2,128)(2,1)S(1)} %reshape.114.gain.gain_row, bf16[256,1024]{1,0:T(8,128)(2,1)S(1)} %get-tuple-element.109.in_conv, ...), custom_call_target="tpu_custom_call" | custom-call | tf_op jit(solution)/shard_map/pallas_call | solution.py:1461
  82.9 2.1 copy-done.31
  85.1 4.6 collective-permute-start
  94.4 25.2 %shard_map.263 = (f32[256,256]{1,0:T(8,128)S(1)}, bf16[4096,256]{1,0:T(8,128)(2,1)S(1)}) custom-call(f32[256,256]{1,0:T(8,128)S(1)} %fusion.32.part, bf16[512,256]{1,0:T(8,128)(2,1)S(1)} %get-tuple-element.114.refs_0_), custom_call_target="tpu_custom_call" | custom-call | tf_op jit(solution)/shard_map/pallas_call | solution.py:572
  121.3 1.7 compare_select_fusion
  123.0 31.9 %shard_map.264 = (f32[256,16,8,128]{3,2,1,0:T(8,128)}, f32[256,1024]{1,0:T(8,128)S(1)}, bf16[4096,256]{1,0:T(8,128)(2,1)S(1)}) custom-call(f32[256,1024]{1,0:T(8,128)S(1)} %get-tuple-element.123.step_ref, f32[256,1024]{1,0:T(8,128)S(1)} %get-tuple-element.93.input_ref, f32[4096]{0:T(1024)S(1)} %reshape.117.brow_ref, f32[4096]{0:T(1024)S(1)} %reshape.118.crow_ref, ...), custom_call_target="tpu_custom_call" | custom-call | tf_op jit(solution)/shard_map/pallas_call | solution.py:832
  158.6 46.0 %shard_map.265 = (bf16[256,2048]{1,0:T(8,128)(2,1)S(1)}, f32[64,2048]{1,0:T(8,128)S(1)}) custom-call(bf16[256,1024]{1,0:T(8,128)(2,1)S(1)} %multiply_convert_fusion.4.gated, bf16[4096,256]{1,0:T(8,128)(2,1)S(1)} %copy-done.3, bf16[4096,256]{1,0:T(8,128)(2,1)S(1)} %get-tuple-element.55.out_last, bf16[256,2048]{1,0:T(8,128)(2,1)S(1)} %bitcast.97, ...), custom_call_target="tpu_custom_call" | custom-call | tf_op jit(solution)/shard_map/pallas_call | solution.py:620
  205.6 12.8 %fusion.2 = f32[256,4096]{1,0:T(8,128)} fusion(bf16[256,2048]{1,0:T(8,128)(2,1)} %copy-done.19, bf16[2048,6144]{0,1:T(8,128)(2,1)} %all-gather.3.cloned.1.call-done), kind=kOutput, calls=%fused_computation.2 | convolution fusion | flops 4294967296 | bytes 22020096 | tf_op jit(solution)/shard_map/dot_general | solution.py:26
  218.5 7.9 %multiply_convert_fusion.1 = (bf16[256,2048]{1,0:T(8,128)(2,1)S(1)}, bf16[256,2048]{1,0:T(8,128)(2,1)S(1)}, bf16[256,2048]{1,0:T(8,128)(2,1)S(1)}) fusion(f32[256,4096]{1,0:T(8,128)} %fusion.2, bf16[256,2048]{1,0:T(8,128)(2,1)} %bitcast.109, bf16[2048,6144]{0,1:T(8,128)(2,1)} %all-gather.3.cloned.1.call-done), kind=kOutput, calls=%fused_computation.24 | convolution fusion | flops 2155347968 | bytes 16777216 | tf_op jit(solution)/shard_map/dot_general | solution.py:26
  226.4 1.6 pad_maximum_fusion.2
  228.0 2.2 pad_maximum_fusion
  232.5 11.3 %fusion.11.part = bf16[256,2048]{1,0:T(8,128)(2,1)} fusion(bf16[256,4096]{1,0:T(8,128)(2,1)S(1)} %copy-done.46, bf16[2048,6144]{0,1:T(8,128)(2,1)} %all-gather.3.cloned.1.call-done), kind=kOutput, calls=%fused_computation.15 | convolution fusion | flops 4295491584 | bytes 19922944 | tf_op jit(solution)/shard_map/dot_general | solution.py:30
  243.9 78.9 %shard_map.266 = (bf16[256,2048]{1,0:T(8,128)(2,1)S(1)}, f32[64,2048]{1,0:T(8,128)S(1)}, f32[1,2048]{1,0:T(1,128)S(1)}, f32[256,1024]{1,0:T(8,128)S(1)}, bf16[20...) custom-call(bf16[256,2048]{1,0:T(8,128)(2,1)} %fusion.11.part, ...), custom_call_target="tpu_custom_call" | custom-call | tf_op jit(solution)/shard_map/pallas_call | solution.py:678
  323.7 2.0 multiply_reduce_fusion.1
  325.8 8.7 %fusion.14.ffn_part = bf16[256,2048]{1,0:T(8,128)(2,1)} fusion(bf16[256,2048]{1,0:T(8,128)(2,1)S(1)} %copy-done.52, bf16[2048,6144]{0,1:T(8,128)(2,1)} %all-gather.3.cloned.1.call-done), kind=kOutput, calls=%fused_computation.16 | convolution fusion | flops 2148007936 | bytes 10485760 | tf_op jit(solution)/shard_map/dot_general | solution.py:30
  334.5 28.5 %shard_map.267 = (f32[256,1024]{1,0:T(8,128)S(1)}, f32[256,1024]{1,0:T(8,128)S(1)}, f32[16,8,128]{2,1,0:T(8,128)S(1)}, f32[256,32,128]{2,1,0:T(8,128)}, bf16[64,2048]{1,0:T(8,128)(2,1)S(1)}) custom-call(f32[256,1024]{1,0:T(8,128)S(1)} %copy-done.6, f32[256,1024]{1,0:T(8,128)S(1)} %get-tuple-element.93.input_ref, ...), custom_call_target="tpu_custom_call" | custom-call | tf_op jit(solution)/shard_map/pallas_call | solution.py:1038
  366.3 3.4 reduce_sum.91
  369.8 1.7 fusion.43
  371.9 32.5 %shard_map.268 = (bf16[256,256]{1,0:T(8,128)(2,1)S(1)}, bf16[256,2048]{1,0:T(8,128)(2,1)S(1)}, bf16[2048,256]{1,0:T(8,128)(2,1)S(1)}) custom-call(bf16[256,256]{1,0:T(8,128)(2,1)S(1)} %maximum_maximum_fusion.part, bf16[64,2048]{1,0:T(8,128)(2,1)S(1)} %copy-done.27, bf16[256,2048]{1,0:T(8,128)(2,1)S(1)} %copy-done.16), custom_call_target="tpu_custom_call" | custom-call | tf_op jit(solution)/shard_map/pallas_call | solution.py:572
  407.4 1.4 collective-permute-start.1
  408.8 1.5 pad_add_fusion
  412.5 2.6 fusion.51
  415.3 1.9 slice.217
  417.2 1.4 fusion.23
  418.6 5.0 fusion.20
  423.6 4.3 concatenate.30
  430.0 68.7 %shard_map.269 = (bf16[256,2048]{1,0:T(8,128)(2,1)}, bf16[384,1024]{1,0:T(8,128)(2,1)}, f32[16,1024]{1,0:T(8,128)}, bf16[2048,2048]{1,0:T(8,128)(2,1)}, f32[2,25...) custom-call(bf16[256,2048]{1,0:T(8,128)(2,1)} %pad_maximum_fusion.3.mix_grads, ...), custom_call_target="tpu_custom_call" | custom-call | tf_op jit(solution)/shard_map/pallas_call | solution.py:1350
  498.6 1.4 fusion.47
  501.3 1.8 slice.170
  512.9 2.1 copy.60
  (220 shorter events, 41.1 us)
Async XLA Ops:
  7.2 114.1 %copy-start = (bf16[128,1024]{1,0:T(8,128)(2,1)S(1)}, bf16[128,1024]{1,0:T(8,128)(2,1)}, u32[]{:S(2)}) copy-start(bf16[128,1024]{1,0:T(8,128)(2,1)} %param.21) | copy-start | bytes 786436
  7.2 198.4 %all-gather.3.cloned.1.call-start = ((), (), s32[]{:S(2)}) async-start(), calls=%async_computation | async-start | bytes 28311552 | tf_op jit(solution)/shard_map/all_gather | solution.py:365
  12.9 417.1 %all-gather.5.cloned.1.call-start = ((), (), s32[]{:S(2)}) async-start(), calls=%async_computation.1 | async-start | bytes 33030144 | tf_op jit(solution)/shard_map/all_gather | solution.py:365
  14.1 68.8 %copy-start.28 = (bf16[1,2048]{1,0:T(2,128)(2,1)}, bf16[1,2048]{1,0:T(2,128)(2,1)S(1)}, u32[]{:S(2)}) copy-start(bf16[1,2048]{1,0:T(2,128)(2,1)S(1)} %reshape.114.gain.gain_row) | copy-start | bytes 12292
  14.1 75.5 %copy-start.59 = (bf16[1024,16]{0,1:T(8,128)(2,1)S(1)}, bf16[1024,16]{0,1:T(8,128)(2,1)}, u32[]{:S(2)}) copy-start(bf16[1024,16]{0,1:T(8,128)(2,1)} %param.23) | copy-start | bytes 98308
  14.1 75.6 %copy-start.56 = (bf16[1024,256]{1,0:T(8,128)(2,1)S(1)}, bf16[1024,256]{1,0:T(8,128)(2,1)}, u32[]{:S(2)}) copy-start(bf16[1024,256]{1,0:T(8,128)(2,1)} %param.25) | copy-start | bytes 1572868
  14.2 75.6 %copy-start.63 = (bf16[4,1024]{1,0:T(4,128)(2,1)S(1)}, bf16[4,1024]{1,0:T(4,128)(2,1)}, u32[]{:S(2)}) copy-start(bf16[4,1024]{1,0:T(4,128)(2,1)} %param.18) | copy-start | bytes 24580
  14.2 75.6 %copy-start.68 = (bf16[1024]{0:T(1024)(128)(2,1)S(1)}, bf16[1024]{0:T(1024)(128)(2,1)}, u32[]{:S(2)}) copy-start(bf16[1024]{0:T(1024)(128)(2,1)} %param.24) | copy-start | bytes 6148
  14.2 75.6 %copy-start.69 = (bf16[1024]{0:T(1024)(128)(2,1)S(1)}, bf16[1024]{0:T(1024)(128)(2,1)}, u32[]{:S(2)}) copy-start(bf16[1024]{0:T(1024)(128)(2,1)} %param.19) | copy-start | bytes 6148
  14.2 75.6 %copy-start.70 = (bf16[1024]{0:T(1024)(128)(2,1)S(1)}, bf16[1024]{0:T(1024)(128)(2,1)}, u32[]{:S(2)}) copy-start(bf16[1024]{0:T(1024)(128)(2,1)} %param.22) | copy-start | bytes 6148
  14.2 75.6 %copy-start.67 = (bf16[2048]{0:T(1024)(128)(2,1)S(1)}, bf16[2048]{0:T(1024)(128)(2,1)}, u32[]{:S(2)}) copy-start(bf16[2048]{0:T(1024)(128)(2,1)} %param.26) | copy-start | bytes 12292
  85.0 6.7 %copy-start.7 = (bf16[2048,1024]{1,0:T(8,128)(2,1)}, bf16[2048,1024]{1,0:T(8,128)(2,1)S(1)}, u32[]{:S(2)}) copy-start(bf16[2048,1024]{1,0:T(8,128)(2,1)S(1)} %get-tuple-element.68) | copy-start | bytes 12582916
  85.0 6.7 %copy-start.8 = (f32[256,1024]{1,0:T(8,128)}, f32[256,1024]{1,0:T(8,128)S(1)}, u32[]{:S(2)}) copy-start(f32[256,1024]{1,0:T(8,128)S(1)} %get-tuple-element.53) | copy-start | bytes 3145732
  85.1 6.0 %collective-permute-start = (bf16[2,3,1024]{2,1,0:T(4,128)(2,1)S(1)}, bf16[2,3,1024]{2,1,0:T(4,128)(2,1)S(1)}, u32[]{:S(2)}, u32[]{:S(2)}) collective-permute-start(bf16[2,3,1024]{2,1,0:T(4,128)(2,1)S(1)} %slice.152), channel_id=1, source_target_pairs={{0,4},{1,5},{2,6},{3,7},{8,12},{9,13},{10,14},{11,15},{16,20},{17,... | collective-permute-start | bytes 36872 | tf_op jit(solution)/shard_map/ppermute | solution.py:22
  120.9 34.0 %copy-start.23 = (f32[256,256]{1,0:T(8,128)}, f32[256,256]{1,0:T(8,128)S(1)}, u32[]{:S(2)}) copy-start(f32[256,256]{1,0:T(8,128)S(1)} %get-tuple-element.51) | copy-start | bytes 786436
  121.2 34.6 %copy-start.9 = (f32[256,1024]{1,0:T(8,128)S(1)}, f32[256,1024]{1,0:T(8,128)}, u32[]{:S(2)}) copy-start(f32[256,1024]{1,0:T(8,128)} %copy-done.8) | copy-start | bytes 3145732
  121.3 34.6 %copy-start.38 = (bf16[256,1024]{1,0:T(8,128)(2,1)S(1)}, bf16[256,1024]{1,0:T(8,128)(2,1)}, u32[]{:S(2)}) copy-start(bf16[256,1024]{1,0:T(8,128)(2,1)} %copy-done.37) | copy-start | bytes 1572868
  205.6 38.2 %copy-start.13 = (f32[64,2048]{1,0:T(8,128)}, f32[64,2048]{1,0:T(8,128)S(1)}, u32[]{:S(2)}) copy-start(f32[64,2048]{1,0:T(8,128)S(1)} %get-tuple-element.58.middle) | copy-start | bytes 1572868
  231.2 12.6 %copy-start.65 = (f32[256]{0:T(256)}, f32[256]{0:T(256)S(1)}, u32[]{:S(2)}) copy-start(f32[256]{0:T(256)S(1)} %rsqrt_bitcast_fusion) | copy-start | bytes 3076
  243.8 79.9 %copy-start.10 = (f32[256,1024]{1,0:T(8,128)S(1)}, f32[256,1024]{1,0:T(8,128)}, u32[]{:S(2)}) copy-start(f32[256,1024]{1,0:T(8,128)} %copy-done.8) | copy-start | bytes 3145732
  243.8 79.9 %copy-start.12 = (f32[256,1024]{1,0:T(8,128)S(1)}, f32[256,1024]{1,0:T(8,128)}, u32[]{:S(2)}) copy-start(f32[256,1024]{1,0:T(8,128)} %copy-done.11) | copy-start | bytes 3145732
  243.8 79.9 %copy-start.39 = (bf16[256,1024]{1,0:T(8,128)(2,1)S(1)}, bf16[256,1024]{1,0:T(8,128)(2,1)}, u32[]{:S(2)}) copy-start(bf16[256,1024]{1,0:T(8,128)(2,1)} %copy-done.37) | copy-start | bytes 1572868
  325.8 8.7 %copy-start.6 = (f32[256,1024]{1,0:T(8,128)S(1)}, f32[256,1024]{1,0:T(8,128)}, u32[]{:S(2)}) copy-start(f32[256,1024]{1,0:T(8,128)} %copy-done.5) | copy-start | bytes 3145732
  325.8 8.7 %copy-start.14 = (f32[64,2048]{1,0:T(8,128)S(1)}, f32[64,2048]{1,0:T(8,128)}, u32[]{:S(2)}) copy-start(f32[64,2048]{1,0:T(8,128)} %copy-done.13) | copy-start | bytes 1572868
  369.8 34.6 %copy-start.34 = (f32[256,1024]{1,0:T(8,128)S(1)}, f32[256,1024]{1,0:T(8,128)}, u32[]{:S(2)}) copy-start(f32[256,1024]{1,0:T(8,128)} %copy-done.33) | copy-start | bytes 3145732
  369.8 34.6 %copy-start.36 = (f32[2,131,1024]{2,1,0:T(8,128)S(1)}, f32[2,131,1024]{2,1,0:T(8,128)}, u32[]{:S(2)}) copy-start(f32[2,131,1024]{2,1,0:T(8,128)} %copy-done.35) | copy-start | bytes 3219460
  369.8 34.6 %copy-start.50 = (f32[256,1024]{1,0:T(8,128)S(1)}, f32[256,1024]{1,0:T(8,128)}, u32[]{:S(2)}) copy-start(f32[256,1024]{1,0:T(8,128)} %get-tuple-element.107) | copy-start | bytes 3145732
  369.8 34.6 %copy-start.58 = (bf16[1024,160]{0,1:T(8,128)(2,1)S(1)}, bf16[1024,160]{0,1:T(8,128)(2,1)}, u32[]{:S(2)}) copy-start(bf16[1024,160]{0,1:T(8,128)(2,1)} %param.20) | copy-start | bytes 983044
  407.4 9.9 %collective-permute-start.1 = (f32[2,3,1024]{2,1,0:T(4,128)}, f32[2,3,1024]{2,1,0:T(4,128)}, u32[]{:S(2)}, u32[]{:S(2)}) collective-permute-start(f32[2,3,1024]{2,1,0:T(4,128)} %pad_add_fusion.1), channel_id=1, source_target_pairs={{4,0},{5,1},{6,2},{7,3},{12,8},{13,9},{14,10},{15,11},{20,16},{21,... | collective-permute-start | bytes 73736 | tf_op jit(solution)/shard_map/ppermute | solution.py:22
  412.5 4.7 copy-start.72
  412.5 4.7 copy-start.71
  423.6 5.3 %copy-start.49 = (bf16[256,1024]{1,0:T(8,128)(2,1)S(1)}, bf16[256,1024]{1,0:T(8,128)(2,1)}, u32[]{:S(2)}) copy-start(bf16[256,1024]{1,0:T(8,128)(2,1)} %get-tuple-element.98) | copy-start | bytes 1572868
  (47 other events, 96.0 us)
Sparse Core Ops, SparseCore 0:
  13.0 174.5 all-gather.2
  230.3 194.4 all-gather.4

commit v8 on v7

--- a/solution.py
+++ b/solution.py
@@ -589,60 +589,209 @@
     )(*operands, *shards)
 
 
-def mixer_out_kernel(
-    gated, out_first, out_last, tokens, gain, normed, middle, part, slots, send_sem, recv_sem
-):
+def mixer_out_kernel(n_swaps, gated, out_first, out_last, tokens, gain, *refs):
+    arrays, refs = refs[:n_swaps], refs[n_swaps:]
+    normed, middle, gated_all, *refs = refs
+    swapped, refs = refs[:n_swaps], refs[n_swaps:]
+    part, slots, send_sem, recv_sem, gather_send, gather_recv, local_sem, *refs = refs
     group = Group(("tp",), send_sem, recv_sem)
+    gather = PlaneGather(gated, gated_all, gather_send, gather_recv)
     half = gated.shape[1] // 2
     share = out_first.shape[1]
-    greet([(("tp",), group.others)])
+    greet([(("tp",), group.others), (PLANE, gather.others)])
+    gather.begin(local_sem)
     for at in range(out_first.shape[0] // half):
         rows = slice(at * half, (at + 1) * half)
         part[:, at * share : (at + 1) * share] = (
             matmul(gated[:, :half], out_first[rows, :])
             + matmul(gated[:, half:], out_last[rows, :])
         ).astype(part.dtype)
-    finish(group.scatter(part, slots, 0))
+    copies = group.scatter(part, slots, 0)
+    if n_swaps:
+        swap = Swap(arrays, swapped, *refs)
+        swap.begin()
+    finish(copies)
     rows = group.own(tokens)[...].astype(jnp.float32) + group.total(part, slots)
     middle[...] = rows
     group.own(normed)[...] = (rows * inverse_rms(rows) * gain[...].astype(jnp.float32)).astype(
         normed.dtype
     )
-    finish(group.spread(normed, 1))
-
-
-def mixer_out(call_id, gated, out_first, out_last, tokens, gain):
+    copies = group.spread(normed, 1)
+    gather.relay()
+    gather.hand_over()
+    finish(copies)
+    gather.hand_over_last()
+    gather.end()
+    if n_swaps:
+        swap.end()
+
+
+def mixer_out(call_id, gated, out_first, out_last, tokens, gain, arrays):
     count = group_size(("tp",))
     vmem = pl.BlockSpec(memory_space=pltpu.VMEM)
+    hbm = pl.BlockSpec(memory_space=pl.ANY)
     rows, width = tokens.shape
     part = jax.ShapeDtypeStruct((rows, width), jnp.bfloat16)
     sems = pltpu.SemaphoreType.DMA((2, count - 1))
     return pl.pallas_call(
-        mixer_out_kernel,
-        in_specs=[vmem] * 5,
-        out_specs=[vmem] * 2,
-        out_shape=[part, jax.ShapeDtypeStruct((rows // count, width), jnp.float32)],
-        scratch_shapes=[pltpu.VMEM(part.shape, part.dtype), slots_for(part, count), sems, sems],
+        functools.partial(mixer_out_kernel, len(arrays)),
+        in_specs=[vmem] * (5 + len(arrays)),
+        out_specs=[vmem] * 2 + [hbm] + [vmem] * len(arrays),
+        out_shape=[
+            part,
+            jax.ShapeDtypeStruct((rows // count, width), jnp.float32),
+            gathered_shape(gated),
+        ]
+        + swap_shapes(arrays),
+        scratch_shapes=[pltpu.VMEM(part.shape, part.dtype), slots_for(part, count), sems, sems]
+        + gather_scratch()
+        + swap_scratch(arrays),
         compiler_params=pltpu.CompilerParams(
             collective_id=call_id, has_side_effects=True, vmem_limit_bytes=40 * 2**20
         ),
-    )(gated, out_first, out_last, tokens, gain)
-
-
-def ffn_back_kernel(n_swaps, part, ct, middle, gain, out_first, out_last, *refs):
-    arrays, refs = refs[:n_swaps], refs[n_swaps:]
-    middle_low, middle_grad, gain_grad, gated_grad, *refs = refs
-    swapped, refs = refs[:n_swaps], refs[n_swaps:]
-    slots, send_sem, recv_sem, *refs = refs
+    )(gated, out_first, out_last, tokens, gain, *arrays)
+
+
+def ffn_kernel(swaps, normed, ct, weights, made, *refs):
+    hidden = weights.shape[1] // 3
+    if swaps:
+        *swapped, block_buf, block_sem, send_sem, recv_sem, local_sem = refs
+        swap = Swap([normed, ct], swapped, send_sem, recv_sem, local_sem)
+        greet([(PLANE, swap.plane.others)])
+        swap.begin()
+    else:
+        block_buf, block_sem = refs
+
+    def columns(j, which):
+        return pl.ds(pl.multiple_of(which * hidden + j * WIDE, WIDE), WIDE)
+
+    def fetch(j, which):
+        slot = lax.rem(j, 2)
+        return pltpu.make_async_copy(
+            weights.at[:, columns(j, which)],
+            block_buf.at[slot, which],
+            block_sem.at[slot, which],
+        )
+
+    for which in range(3):
+        fetch(0, which).start()
+
+    @pl.loop(0, hidden // WIDE)
+    def _(j):
+        slot = lax.rem(j, 2)
+
+        @pl.when(j + 1 < hidden // WIDE)
+        def _():
+            for which in range(3):
+                fetch(j + 1, which).start()
+
+        fetch(j, 0).wait()
+        gate = matmul(normed[...], block_buf[slot, 0])
+        fetch(j, 1).wait()
+        up = matmul(normed[...], block_buf[slot, 1])
+        fetch(j, 2).wait()
+        act_grad = matmul(ct[...], block_buf[slot, 2])
+        logistic = jax.nn.sigmoid(gate)
+        silu = gate * logistic
+        slope = logistic * (1.0 + gate * (1.0 - logistic))
+        made[:, columns(j, 0)] = (silu * up).astype(made.dtype)
+        made[:, columns(j, 1)] = (act_grad * up * slope).astype(made.dtype)
+        made[:, columns(j, 2)] = (act_grad * silu).astype(made.dtype)
+
+    if swaps:
+        swap.end()
+
+
+def run_ffn(call_id, normed, ct, weights, swaps):
+    rows, width = normed.shape
+    arrays = [normed, ct] if swaps else []
+    vmem = pl.BlockSpec(memory_space=pltpu.VMEM)
+    params = dict(collective_id=call_id, has_side_effects=True) if swaps else {}
+    return pl.pallas_call(
+        functools.partial(ffn_kernel, swaps),
+        in_specs=[vmem, vmem, pl.BlockSpec(memory_space=pl.ANY)],
+        out_specs=[vmem] * (1 + len(arrays)),
+        out_shape=[jax.ShapeDtypeStruct((rows, weights.shape[1]), jnp.bfloat16)]
+        + swap_shapes(arrays),
+        scratch_shapes=[
+            pltpu.VMEM((2, 3, width, WIDE), jnp.bfloat16),
+            pltpu.SemaphoreType.DMA((2, 3)),
+        ]
+        + swap_scratch(arrays),
+        compiler_params=pltpu.CompilerParams(vmem_limit_bytes=48 * 2**20, **params),
+    )(normed, ct, weights)
+
+
+def ffn_back_kernel(
+    made,
+    ct,
+    middle,
+    gain,
+    out_first,
+    out_last,
+    weights,
+    middle_low,
+    middle_grad,
+    gain_grad,
+    gated_grad,
+    ffn_part,
+    part,
+    slots,
+    wide_buf,
+    down_buf,
+    wide_sem,
+    down_sem,
+    part_send,
+    part_recv,
+    send_sem,
+    recv_sem,
+):
+    hidden = made.shape[1] // 3
+    blocks = part.shape[1] // WIDE
     group = Group(("tp",), send_sem, recv_sem)
-    if n_swaps:
-        swap = Swap(arrays, swapped, *refs)
-        greet([(("tp",), group.others), (PLANE, swap.plane.others)])
-    else:
-        greet([(("tp",), group.others)])
-    copies = group.scatter(part, slots, 0)
-    if n_swaps:
-        swap.begin()
+    greet([(("tp",), group.others)])
+
+    def fetch(j):
+        return pltpu.make_async_copy(
+            weights.at[j * WIDE : (j + 1) * WIDE, : 2 * hidden],
+            wide_buf.at[j % 2],
+            wide_sem.at[j % 2],
+        )
+
+    def fetch_down(j):
+        return pltpu.make_async_copy(
+            weights.at[j * WIDE : (j + 1) * WIDE, 2 * hidden :],
+            down_buf.at[j % 2],
+            down_sem.at[j % 2],
+        )
+
+    fetch(0).start()
+    copies = []
+    for j in range(blocks):
+        if j + 1 < blocks:
+            fetch(j + 1).start()
+        else:
+            fetch_down(0).start()
+        fetch(j).wait()
+        columns = slice(j * WIDE, (j + 1) * WIDE)
+        part[:, columns] = matmul_nt(made[:, hidden:], wide_buf[j % 2]).astype(part.dtype)
+        for hop, other in enumerate(group.others):
+            copies.append(
+                sent(
+                    rows_of(part, other, group.count).at[:, columns],
+                    slots.at[hop, :, columns],
+                    part_send.at[j, hop],
+                    part_recv.at[j, hop],
+                    device_at(("tp",), other),
+                )
+            )
+    for j in range(blocks):
+        if j + 1 < blocks:
+            fetch_down(j + 1).start()
+        fetch_down(j).wait()
+        ffn_part[:, j * WIDE : (j + 1) * WIDE] = matmul_nt(
+            made[:, :hidden], down_buf[j % 2]
+        ).astype(ffn_part.dtype)
     finish(copies)
     normed_grad = group.total(part, slots)
     rows = middle[...]
@@ -653,44 +802,56 @@
     )
     middle_grad[...] = grad
     group.own(middle_low)[...] = grad.astype(middle_low.dtype)
-    finish(group.spread(middle_low, 1))
+    finish(group.spread(middle_low, 0))
     half = gated_grad.shape[1] // 2
     share = out_first.shape[1]
-    for side, weights in enumerate((out_first, out_last)):
+    for side, shards in enumerate((out_first, out_last)):
         total = None
-        for at in range(weights.shape[0] // half):
+        for at in range(shards.shape[0] // half):
             one = matmul_nt(
                 middle_low[:, at * share : (at + 1) * share],
-                weights[at * half : (at + 1) * half, :],
+                shards[at * half : (at + 1) * half, :],
             )
             total = one if total is None else total + one
         gated_grad[:, side * half : (side + 1) * half] = total
-    if n_swaps:
-        swap.end()
-
-
-def ffn_back(call_id, part, ct, middle, gain, out_first, out_last, arrays):
+
+
+def ffn_back(call_id, made, ct, middle, gain, out_first, out_last, weights):
     count = group_size(("tp",))
     vmem = pl.BlockSpec(memory_space=pltpu.VMEM)
-    rows, width = part.shape
+    rows, width = ct.shape
+    hidden = made.shape[1] // 3
     inner = 2 * out_first.shape[0] // group_size(PLANE)
-    sems = pltpu.SemaphoreType.DMA((2, count - 1))
+    low, full = jnp.bfloat16, jnp.float32
+    part = jax.ShapeDtypeStruct((rows, width), low)
+    dma = pltpu.SemaphoreType.DMA
     return pl.pallas_call(
-        functools.partial(ffn_back_kernel, len(arrays)),
-        in_specs=[vmem] * (6 + len(arrays)),
-        out_specs=[vmem] * (4 + len(arrays)),
+        ffn_back_kernel,
+        in_specs=[vmem] * 6 + [pl.BlockSpec(memory_space=pl.ANY)],
+        out_specs=[vmem] * 5,
         out_shape=[
-            jax.ShapeDtypeStruct((rows, width), jnp.bfloat16),
-            jax.ShapeDtypeStruct((rows // count, width), jnp.float32),
-            jax.ShapeDtypeStruct((1, width), jnp.float32),
-            jax.ShapeDtypeStruct((rows, inner), jnp.float32),
-        ]
-        + swap_shapes(arrays),
-        scratch_shapes=[slots_for(part, count), sems, sems] + swap_scratch(arrays),
+            part,
+            jax.ShapeDtypeStruct((rows // count, width), full),
+            jax.ShapeDtypeStruct((1, width), full),
+            jax.ShapeDtypeStruct((rows, inner), full),
+            part,
+        ],
+        scratch_shapes=[
+            pltpu.VMEM(part.shape, low),
+            slots_for(part, count),
+            pltpu.VMEM((2, WIDE, 2 * hidden), low),
+            pltpu.VMEM((2, WIDE, hidden), low),
+            dma((2,)),
+            dma((2,)),
+            dma((width // WIDE, count - 1)),
+            dma((width // WIDE, count - 1)),
+            dma((1, count - 1)),
+            dma((1, count - 1)),
+        ],
         compiler_params=pltpu.CompilerParams(
-            collective_id=call_id, has_side_effects=True, vmem_limit_bytes=48 * 2**20
+            collective_id=call_id, has_side_effects=True, vmem_limit_bytes=52 * 2**20
         ),
-    )(part, ct, middle, gain, out_first, out_last, *arrays)
+    )(made, ct, middle, gain, out_first, out_last, weights)
 
 
 def send_on(source, target, send_sem, recv_sem, ctx):
@@ -1218,6 +1379,7 @@
     ct_cols,
     middle_cols,
     ffn_all,
+    gated_all,
     tokens_grad,
     small_sum,
     gains,
@@ -1277,7 +1439,6 @@
     high = (block_buf, block_sem, tall_buf, tall_sem)
     down_end = hidden // WIDE
     gu_end = 3 * hidden // WIDE
-    out_end = gu_end + inner // WIDE
 
     normed_sent = tp.scatter(normed_part, normed_slots, 0)
     gather.begin(local_sem)
@@ -1304,7 +1465,7 @@
     plane.own(small_sum)[...] = plane.total(small, small_slots).astype(small_sum.dtype)
     small_sent = plane.spread(small_sum, 1)
     products(
-        ffn_all, gu_end, out_end, tall(middle_cols), one_above_other(grad_outproj, gu_end), *high
+        gated_all, 0, inner // WIDE, tall(middle_cols), one_above_other(grad_outproj, 0), *high
     )
     gather.hand_over_last()
     finish(small_sent)
@@ -1336,9 +1497,10 @@
     ct_cols,
     middle_cols,
     ffn_all,
+    gated_all,
 ):
     inner = mix_grads.shape[1] // 2
-    hidden = (ffn_all.shape[1] - inner) // 3
+    hidden = ffn_all.shape[1] // 3
     share = one_cols.shape[1]
     all_rows = ffn_all.shape[0]
     tp_count, plane_count = group_size(("tp",)), group_size(PLANE)
@@ -1349,7 +1511,7 @@
     dma = pltpu.SemaphoreType.DMA
     return pl.pallas_call(
         functools.partial(tail_kernel, (inner, hidden, gain_at)),
-        in_specs=[vmem] * 10 + [hbm],
+        in_specs=[vmem] * 10 + [hbm] * 2,
         out_specs=[vmem] * 3 + [hbm] * 5,
         out_shape=[
             jax.ShapeDtypeStruct(tokens.shape, low),
@@ -1395,6 +1557,7 @@
         ct_cols,
         middle_cols,
         ffn_all,
+        gated_all,
     )
 
 
@@ -1512,7 +1675,6 @@
     rate = (decay_rate * LOG2E).reshape(n_state, tiles, LANE)
 
     gain_mix_row, gain_ffn_row = mixgain.reshape(1, width), ffngain.reshape(1, width)
-    hidden = gateup.shape[2]
     low = jnp.bfloat16
 
     tokens_rows = tokens.reshape(rows, width)
@@ -1561,37 +1723,25 @@
     mixer_core = scan_out + skip_weight[None] * scan_float
     gate_sig = jax.nn.silu(gate_mix)
     gated = (mixer_core * gate_sig).astype(low)
-    normed_two, middle = mixer_out(1, gated, out_first, out_last, tokens_rows, gain_ffn_row)
-    gate_up = ffn_pack[:, : 2 * hidden]
-    down_weights = ffn_pack[:, 2 * hidden :]
-    both_ffn = matmul(normed_two, gate_up)
-    gate_ffn, up_ffn = both_ffn[:, :hidden], both_ffn[:, hidden:]
-    activated = (jax.nn.silu(gate_ffn) * up_ffn).astype(low)
-    act_grad = matmul(ct_low, down_weights)
-    gate_grad = (act_grad * up_ffn * silu_slope(gate_ffn)).astype(low)
-    up_grad = (act_grad * jax.nn.silu(gate_ffn)).astype(low)
-    ffn_grads = jnp.concatenate([gate_grad, up_grad], 1)
-    ffn_sent, ffn_grads = lax.optimization_barrier(
-        (jnp.concatenate([activated, ffn_grads, gated], 1), ffn_grads)
-    )
-    ffn_all = gathered_rows(ffn_sent)
-    normed_two_part = matmul_nt(ffn_grads, gate_up).astype(low)
-    ffn_part = matmul_nt(activated, down_weights).astype(low)
     swap_now = swaps_in_kernels(width)
-    to_swap = [normed_one, normed_two, ct_low]
-    middle_low, middle_grad, ffngain_part, gated_grad, *swapped = ffn_back(
-        2,
-        normed_two_part,
-        ct_low,
-        middle,
-        gain_ffn_row,
+    normed_two, middle, gated_all, *swapped = mixer_out(
+        1,
+        gated,
         out_first,
         out_last,
-        to_swap if swap_now else [],
-    )
+        tokens_rows,
+        gain_ffn_row,
+        [normed_one] if swap_now else [],
+    )
+    (normed_one_cols,) = swapped if swap_now else [swapped_columns(normed_one)]
+    made, *swapped = run_ffn(8, normed_two, ct_low, ffn_pack, swap_now)
     if not swap_now:
-        swapped = [swapped_columns(array) for array in to_swap]
-    normed_one_cols, normed_two_cols, ct_cols = swapped
+        swapped = [swapped_columns(normed_two), swapped_columns(ct_low)]
+    normed_two_cols, ct_cols = swapped
+    ffn_all = gathered_rows(made)
+    middle_low, middle_grad, ffngain_part, gated_grad, ffn_part = ffn_back(
+        2, made, ct_low, middle, gain_ffn_row, out_first, out_last, ffn_pack
+    )
     core_grad = gated_grad * gate_sig
     gate_mix_grad = (gated_grad * mixer_core * silu_slope(gate_mix)).astype(low)
     grad_skipgain = jnp.sum(core_grad * scan_float, 0)
@@ -1702,6 +1852,7 @@
         ct_cols,
         middle_cols,
         ffn_all,
+        gated_all,
     )
     small = small.astype(jnp.float32)
     smalls, at = [], 0

time: 531 us -> 505 us (0.951); the launches traced: 525 us -> 504 us
  matrix products: 54 us -> 15.8 us
  Pallas kernels: 380 us -> 396 us
  local copies, waits for them, and re-layouts: 43.5 us -> 52.2 us
    dot_general x4 -> x2, matrix products: 22.7 us -> 3.01 us  [matmul(): return jnp.dot(left, right, preferred_element_type=jnp.float32)]
    dot_general x6 -> x4, matrix products: 29.2 us -> 10.6 us  [matmul_nt(): lax.dot_general(left, right, (((1,), (1,)), ((), ())), preferred_element_...]
    pallas_call x2 -> x3, Pallas kernels: 125 us -> 138 us  [the longest x1 59.5 us: ffn_back(): pl.pallas_call(ffn_back_kernel, in_specs=[vmem] * 6 + [pl.BlockSpec(memor...]
    unnamed x160 -> x159, local copies, waits for them, and re-layouts: 26.8 us -> 37.5 us
    pallas_call x1, Pallas kernels: 28.5 us -> 35 us  [scan_backward_pair(): pl.pallas_call(functools.partial(backward_pair_kernel, n_state, tiles, gr...]
  transfers between devices with their start and end apart: 4 -> 4, of which waited for: 1 -> 0; matrix products, arithmetic and copies ran while one was open for 11% -> 8% of each run, Pallas kernels for 59% -> 59%
where the time goes in v8:
time: 505 us; the launch traced here: 504 us
  Pallas kernels  396 us (78%)
  local copies, waits for them, and re-layouts  52.2 us (10%)
  other arithmetic  19 us (4%)
  matrix products  15.8 us (3%)
  between operations  15 us (3%)
  starting transfers between devices  6.04 us (1%)
    pallas_call x1, Pallas kernels, run_tail(): pl.pallas_call(functools.partial(tail_kernel, (inner, hidden, gain_at)),...  68.5 us
    pallas_call x1, Pallas kernels, run_head(): pl.pallas_call(head_kernel, in_specs=[vmem] * 2 + [hbm] * 2, out_specs=[v...  68.5 us
    pallas_call x1, Pallas kernels, ffn_back(): pl.pallas_call(ffn_back_kernel, in_specs=[vmem] * 6 + [pl.BlockSpec(memor...  59.5 us
    pallas_call x2, Pallas kernels, sum_over_tp(): pl.pallas_call(functools.partial(sum_kernel, len(own_rows), len(arrays),...  54.2 us
    pallas_call x1, Pallas kernels, mixer_out(): pl.pallas_call(functools.partial(mixer_out_kernel, len(arrays)), in_specs...  48.1 us
    unnamed x159, local copies, waits for them, and re-layouts  37.5 us
    pallas_call x1, Pallas kernels, scan_backward_pair(): pl.pallas_call(functools.partial(backward_pair_kernel, n_state, tiles, gr...  35 us
    pallas_call x1, Pallas kernels, scan_forward_pair(): pl.pallas_call(functools.partial(forward_pair_kernel, n_state, tiles, gro...  32 us
  transfers between devices with their start and end apart: 4, of which 0 were waited for; matrix products, arithmetic and copies ran while one was open for 8% of the time, Pallas kernels for 59%

profile of v8, /device:TPU:0, one launch (start us, length us, event | category | flops | bytes accessed | tf_op | source)
XLA Modules:
  0.0 504.2 jit_solution(10955698481688260364)
XLA Ops:
  7.2 1.7 slice_bitcast_fusion.1
  9.0 1.5 copy.32
  10.5 1.8 pad_maximum_fusion
  13.8 68.5 %shard_map.262 = (bf16[256,1024]{1,0:T(8,128)(2,1)S(1)}, f32[256,1024]{1,0:T(8,128)S(1)}, bf16[2048,1024]{1,0:T(8,128)(2,1)S(1)}, bf16[2048,1024]{1,0:T(8,128)(2,1)S(1)}) custom-call(bf16[256,2048]{1,0:T(8,128)(2,1)S(1)} %bitcast.92, bf16[1,2048]{1,0:T(2,128)(2,1)S(1)} %reshape.114.gain.gain_row, bf16[256,1024]{1,0:T(8,128)(2,1)S(1)} %get-tuple-element.108.in_conv, ...), custom_call_target="tpu_custom_call" | custom-call | tf_op jit(solution)/shard_map/pallas_call | solution.py:1624
  83.2 2.0 copy-done.37
  85.3 4.5 collective-permute-start
  94.2 1.4 fusion.26
  95.9 24.1 %shard_map.263 = (f32[256,256]{1,0:T(8,128)S(1)}, bf16[4096,256]{1,0:T(8,128)(2,1)S(1)}) custom-call(f32[256,256]{1,0:T(8,128)S(1)} %fusion.14.part, bf16[512,256]{1,0:T(8,128)(2,1)S(1)} %get-tuple-element.113.refs_0_), custom_call_target="tpu_custom_call" | custom-call | tf_op jit(solution)/shard_map/pallas_call | solution.py:572
  120.0 1.3 copy-done.3
  122.4 2.7 compare_select_fusion
  126.0 32.0 %shard_map.264 = (f32[256,16,8,128]{3,2,1,0:T(8,128)}, f32[256,1024]{1,0:T(8,128)S(1)}, bf16[4096,256]{1,0:T(8,128)(2,1)S(1)}) custom-call(f32[256,1024]{1,0:T(8,128)S(1)} %get-tuple-element.122.step_ref, f32[256,1024]{1,0:T(8,128)S(1)} %get-tuple-element.95.input_ref, f32[4096]{0:T(1024)S(1)} %reshape.117.brow_ref, f32[4096]{0:T(1024)S(1)} %reshape.118.crow_ref, ...), custom_call_target="tpu_custom_call" | custom-call | tf_op jit(solution)/shard_map/pallas_call | solution.py:993
  161.0 48.1 %shard_map.265 = (bf16[256,2048]{1,0:T(8,128)(2,1)S(1)}, f32[64,2048]{1,0:T(8,128)S(1)}, bf16[2048,1024]{1,0:T(8,128)(2,1)S(1)}, bf16[2048,256]{1,0:T(8,128)(2,1)S(1)}) custom-call(bf16[256,1024]{1,0:T(8,128)(2,1)S(1)} %multiply_convert_fusion.1.gated, bf16[4096,256]{1,0:T(8,128)(2,1)S(1)} %copy-done.4, bf16[4096,256]{1,0:T(8,128)(2,1)S(1)} %get-tuple-element.56.out_last, ...), custom_call_target="tpu_custom_call" | custom-call | tf_op jit(solution)/shard_map/pallas_call | solution.py:636
  209.1 2.0 copy-done.15
  216.3 30.4 %shard_map.266 = (bf16[256,6144]{1,0:T(8,128)(2,1)}, bf16[2048,256]{1,0:T(8,128)(2,1)S(1)}, bf16[2048,256]{1,0:T(8,128)(2,1)S(1)}) custom-call(bf16[256,2048]{1,0:T(8,128)(2,1)S(1)} %copy-done.24, bf16[256,2048]{1,0:T(8,128)(2,1)S(1)} %bitcast.95, bf16[2048,6144]{1,0:T(8,128)(2,1)} %all-gather.3.cloned.1.call-done.weights), custom_call_target="tpu_custom_call" | custom-call | tf_op jit(solution)/shard_map/pallas_call | solution.py:710
  251.9 59.5 %shard_map.267 = (bf16[256,2048]{1,0:T(8,128)(2,1)}, f32[64,2048]{1,0:T(8,128)S(1)}, f32[1,2048]{1,0:T(1,128)S(1)}, f32[256,1024]{1,0:T(8,128)}, bf16[256,2048]{1,0:T(8,128)(2,1)}) custom-call(bf16[256,6144]{1,0:T(8,128)(2,1)} %get-tuple-element.58.made, bf16[256,2048]{1,0:T(8,128)(2,1)} %bitcast.94, f32[64,2048]{1,0:T(8,128)S(1)} %copy-done.18, ...), custom_call_target="tpu_custom_call" | custom-call | tf_op jit(solution)/shard_map/pallas_call | solution.py:828
  311.5 3.4 multiply_reduce_fusion.1
  314.9 35.0 %shard_map.268 = (f32[256,1024]{1,0:T(8,128)S(1)}, f32[256,1024]{1,0:T(8,128)S(1)}, f32[16,8,128]{2,1,0:T(8,128)S(1)}, f32[256,32,128]{2,1,0:T(8,128)}, bf16[64,2048]{1,0:T(8,128)(2,1)S(1)}) custom-call(f32[256,1024]{1,0:T(8,128)S(1)} %get-tuple-element.122.step_ref, f32[256,1024]{1,0:T(8,128)S(1)} %get-tuple-element.95.input_ref, ...), custom_call_target="tpu_custom_call" | custom-call | tf_op jit(solution)/shard_map/pallas_call | solution.py:1199
  353.2 3.5 reduce_sum.91
  358.1 30.1 %shard_map.269 = (bf16[256,256]{1,0:T(8,128)(2,1)S(1)}, bf16[256,2048]{1,0:T(8,128)(2,1)S(1)}, bf16[2048,256]{1,0:T(8,128)(2,1)S(1)}) custom-call(bf16[256,256]{1,0:T(8,128)(2,1)S(1)} %maximum_maximum_fusion.part, bf16[64,2048]{1,0:T(8,128)(2,1)S(1)} %copy-done.33, bf16[256,2048]{1,0:T(8,128)(2,1)S(1)} %copy-done.19), custom_call_target="tpu_custom_call" | custom-call | tf_op jit(solution)/shard_map/pallas_call | solution.py:572
  388.3 2.3 multiply_reduce_fusion.2
  391.3 1.4 collective-permute-start.1
  392.7 1.5 pad_add_fusion
  396.4 2.6 fusion.32
  399.2 1.7 slice.177
  401.0 1.4 fusion.5
  402.4 5.4 %fusion.3 = (bf16[2048]{0:T(1024)(128)(2,1)S(1)}, bf16[256,2048]{1,0:T(8,128)(2,1)}) fusion(f32[256]{0:T(256)S(1)} %copy-done.68, bf16[2,128,2048]{2,1,0:T(8,128)(2,1)S(1)} %copy-done.2, f32[256,2048]{1,0:T(8,128)} %fusion.32, bf16[256,1024]{1,0:T(8,128)(2,1)S(1)} %bitcast.102, bf16[2048,1024]{1,0:T(8,128)(2,1)} %copy-done.6), kind=kOutput, calls=%fused_computation.8 | convolution fusion | flops 1076885504 | bytes 8918016 | tf_op jit(solution)/shard_map/dot_general | solution.py:30
  407.8 2.7 concatenate.21
  412.5 68.5 %shard_map.270 = (bf16[256,2048]{1,0:T(8,128)(2,1)}, bf16[384,1024]{1,0:T(8,128)(2,1)}, f32[16,1024]{1,0:T(8,128)}, bf16[2048,2048]{1,0:T(8,128)(2,1)}, f32[2,25...) custom-call(bf16[256,2048]{1,0:T(8,128)(2,1)} %pad_maximum_fusion.1.mix_grads, ...), custom_call_target="tpu_custom_call" | custom-call | tf_op jit(solution)/shard_map/pallas_call | solution.py:1512
  481.1 1.4 convert_element_type.92
  489.5 1.3 copy.51
  492.9 2.1 copy.53
  496.0 1.3 copy.54
  (214 shorter events, 42.0 us)
Async XLA Ops:
  7.2 115.1 %copy-start = (bf16[128,1024]{1,0:T(8,128)(2,1)S(1)}, bf16[128,1024]{1,0:T(8,128)(2,1)}, u32[]{:S(2)}) copy-start(bf16[128,1024]{1,0:T(8,128)(2,1)} %param.21) | copy-start | bytes 786436
  7.2 206.7 %all-gather.3.cloned.1.call-start = ((), (), s32[]{:S(2)}) async-start(), calls=%async_computation | async-start | bytes 28311552 | tf_op jit(solution)/shard_map/all_gather | solution.py:365
  12.3 400.3 %all-gather.5.cloned.1.call-start = ((), (), s32[]{:S(2)}) async-start(), calls=%async_computation.1 | async-start | bytes 28311552 | tf_op jit(solution)/shard_map/all_gather | solution.py:365
  13.5 68.8 %copy-start.34 = (bf16[1,2048]{1,0:T(2,128)(2,1)}, bf16[1,2048]{1,0:T(2,128)(2,1)S(1)}, u32[]{:S(2)}) copy-start(bf16[1,2048]{1,0:T(2,128)(2,1)S(1)} %reshape.114.gain.gain_row) | copy-start | bytes 12292
  13.5 76.6 %copy-start.61 = (bf16[1024,16]{0,1:T(8,128)(2,1)S(1)}, bf16[1024,16]{0,1:T(8,128)(2,1)}, u32[]{:S(2)}) copy-start(bf16[1024,16]{0,1:T(8,128)(2,1)} %param.23) | copy-start | bytes 98308
  13.5 76.7 %copy-start.58 = (bf16[1024,256]{1,0:T(8,128)(2,1)S(1)}, bf16[1024,256]{1,0:T(8,128)(2,1)}, u32[]{:S(2)}) copy-start(bf16[1024,256]{1,0:T(8,128)(2,1)} %param.25) | copy-start | bytes 1572868
  85.2 7.0 %copy-start.6 = (bf16[2048,1024]{1,0:T(8,128)(2,1)}, bf16[2048,1024]{1,0:T(8,128)(2,1)S(1)}, u32[]{:S(2)}) copy-start(bf16[2048,1024]{1,0:T(8,128)(2,1)S(1)} %get-tuple-element.70) | copy-start | bytes 12582916
  85.3 7.2 %collective-permute-start = (bf16[2,3,1024]{2,1,0:T(4,128)(2,1)S(1)}, bf16[2,3,1024]{2,1,0:T(4,128)(2,1)S(1)}, u32[]{:S(2)}, u32[]{:S(2)}) collective-permute-start(bf16[2,3,1024]{2,1,0:T(4,128)(2,1)S(1)} %slice.136), channel_id=1, source_target_pairs={{0,4},{1,5},{2,6},{3,7},{8,12},{9,13},{10,14},{11,15},{16,20},{17,... | collective-permute-start | bytes 36872 | tf_op jit(solution)/shard_map/ppermute | solution.py:22
  95.5 26.7 %copy-start.43 = (bf16[256,1024]{1,0:T(8,128)(2,1)}, bf16[256,1024]{1,0:T(8,128)(2,1)S(1)}, u32[]{:S(2)}) copy-start(bf16[256,1024]{1,0:T(8,128)(2,1)S(1)} %get-tuple-element.96) | copy-start | bytes 1572868
  122.3 35.7 %copy-start.10 = (f32[256,1024]{1,0:T(8,128)S(1)}, f32[256,1024]{1,0:T(8,128)}, u32[]{:S(2)}) copy-start(f32[256,1024]{1,0:T(8,128)} %copy-done.9) | copy-start | bytes 3145732
  122.3 35.7 %copy-start.44 = (bf16[256,1024]{1,0:T(8,128)(2,1)S(1)}, bf16[256,1024]{1,0:T(8,128)(2,1)}, u32[]{:S(2)}) copy-start(bf16[256,1024]{1,0:T(8,128)(2,1)} %copy-done.43) | copy-start | bytes 1572868
  251.9 59.6 %copy-start.11 = (f32[256,1024]{1,0:T(8,128)S(1)}, f32[256,1024]{1,0:T(8,128)}, u32[]{:S(2)}) copy-start(f32[256,1024]{1,0:T(8,128)} %copy-done.9) | copy-start | bytes 3145732
  251.9 59.6 %copy-start.13 = (f32[256,1024]{1,0:T(8,128)S(1)}, f32[256,1024]{1,0:T(8,128)}, u32[]{:S(2)}) copy-start(f32[256,1024]{1,0:T(8,128)} %copy-done.12) | copy-start | bytes 3145732
  251.9 59.6 %copy-start.45 = (bf16[256,1024]{1,0:T(8,128)(2,1)S(1)}, bf16[256,1024]{1,0:T(8,128)(2,1)}, u32[]{:S(2)}) copy-start(bf16[256,1024]{1,0:T(8,128)(2,1)} %copy-done.43) | copy-start | bytes 1572868
  311.5 3.4 copy-start.31
  314.9 35.0 %copy-start.7 = (f32[256,1024]{1,0:T(8,128)}, f32[256,1024]{1,0:T(8,128)S(1)}, u32[]{:S(2)}) copy-start(f32[256,1024]{1,0:T(8,128)S(1)} %get-tuple-element.92.ograd_ref) | copy-start | bytes 3145732
  353.2 3.5 copy-start.21
  353.2 3.6 copy-start.54
  356.8 31.5 %copy-start.8 = (f32[256,1024]{1,0:T(8,128)S(1)}, f32[256,1024]{1,0:T(8,128)}, u32[]{:S(2)}) copy-start(f32[256,1024]{1,0:T(8,128)} %copy-done.7) | copy-start | bytes 3145732
  356.8 31.5 %copy-start.40 = (f32[256,1024]{1,0:T(8,128)S(1)}, f32[256,1024]{1,0:T(8,128)}, u32[]{:S(2)}) copy-start(f32[256,1024]{1,0:T(8,128)} %copy-done.39) | copy-start | bytes 3145732
  356.8 31.5 %copy-start.42 = (f32[2,131,1024]{2,1,0:T(8,128)S(1)}, f32[2,131,1024]{2,1,0:T(8,128)}, u32[]{:S(2)}) copy-start(f32[2,131,1024]{2,1,0:T(8,128)} %copy-done.41) | copy-start | bytes 3219460
  356.8 31.5 %copy-start.60 = (bf16[1024,160]{0,1:T(8,128)(2,1)S(1)}, bf16[1024,160]{0,1:T(8,128)(2,1)}, u32[]{:S(2)}) copy-start(bf16[1024,160]{0,1:T(8,128)(2,1)} %param.20) | copy-start | bytes 983044
  391.3 4.0 copy-start.46
  391.3 9.7 %collective-permute-start.1 = (f32[2,3,1024]{2,1,0:T(4,128)S(1)}, f32[2,3,1024]{2,1,0:T(4,128)S(1)}, u32[]{:S(2)}, u32[]{:S(2)}) collective-permute-start(f32[2,3,1024]{2,1,0:T(4,128)S(1)} %pad_add_fusion.1), channel_id=1, source_target_pairs={{4,0},{5,1},{6,2},{7,3},{12,8},{13,9},{14,10},{15,11},{20,16},{21,... | collective-permute-start | bytes 73736 | tf_op jit(solution)/shard_map/ppermute | solution.py:22
  392.7 3.7 copy-start.38
  396.4 4.5 copy-start.69
  399.0 3.3 copy-start.68
  402.4 5.4 %copy-start.57 = (bf16[128,1024]{1,0:T(8,128)(2,1)S(1)}, bf16[128,1024]{1,0:T(8,128)(2,1)}, u32[]{:S(2)}) copy-start(bf16[128,1024]{1,0:T(8,128)(2,1)} %convolution_convert_fusion) | copy-start | bytes 786436
  407.7 3.7 copy-start.52
  482.4 6.1 %copy-start.56 = (bf16[256,2048]{1,0:T(8,128)(2,1)S(1)}, bf16[256,2048]{1,0:T(8,128)(2,1)}, u32[]{:S(2)}) copy-start(bf16[256,2048]{1,0:T(8,128)(2,1)} %get-tuple-element.80) | copy-start | bytes 3145732
  489.5 3.4 copy-start.47
  492.9 4.4 copy-start.1
  (47 other events, 78.7 us)
Sparse Core Ops, SparseCore 0:
  12.4 187.5 all-gather.2
  248.8 140.3 all-gather.4

commit v9 on v8

--- a/solution.py
+++ b/solution.py
@@ -13,6 +13,7 @@
 LN2 = math.log(2.0)
 SUB = 8
 LANE = 128
+VMEM_GRANT = 60 * 2**20
 PLANE = ("dp", "ctx")
 
 
@@ -130,7 +131,7 @@
         out_specs=pl.BlockSpec((1, n_state, tiles, LANE), lambda s: (s, 0, 0, 0)),
         out_shape=jax.ShapeDtypeStruct((seqs, n_state, tiles, LANE), jnp.float32),
         scratch_shapes=[held, held],
-        compiler_params=pltpu.CompilerParams(vmem_limit_bytes=32 * 2**20),
+        compiler_params=pltpu.CompilerParams(vmem_limit_bytes=VMEM_GRANT),
     )(step, drive, rows, rate)
 
 
@@ -213,7 +214,7 @@
             jax.ShapeDtypeStruct(step.shape, jnp.float32),
         ],
         scratch_shapes=[pltpu.VMEM((n_state, tiles, LANE), jnp.float32)] + [held] * 3,
-        compiler_params=pltpu.CompilerParams(vmem_limit_bytes=32 * 2**20),
+        compiler_params=pltpu.CompilerParams(vmem_limit_bytes=VMEM_GRANT),
     )(start, step, inputs, b_rows, c_rows, rate)
 
 
@@ -339,7 +340,7 @@
             jax.ShapeDtypeStruct((tokens, 2 * n_state, LANE), jnp.float32),
         ],
         scratch_shapes=[pltpu.VMEM((n_state, tiles, LANE), jnp.float32)] + [held] * 5,
-        compiler_params=pltpu.CompilerParams(vmem_limit_bytes=32 * 2**20),
+        compiler_params=pltpu.CompilerParams(vmem_limit_bytes=VMEM_GRANT),
     )(end_grad, prior, step, inputs, ograd, b_rows, c_rows, rate, picks)
 
 
@@ -566,7 +567,7 @@
 def sum_over_tp(call_id, part, own_rows, arrays, shards):
     count = group_size(("tp",))
     vmem = pl.BlockSpec(memory_space=pltpu.VMEM)
-    hbm = pl.BlockSpec(memory_space=pl.ANY)
+    hbm = pl.BlockSpec(memory_space=pltpu.HBM)
     operands = [part, *own_rows, *arrays]
     sems = pltpu.SemaphoreType.DMA((2 + len(own_rows), count - 1))
     return pl.pallas_call(
@@ -584,7 +585,7 @@
         + swap_scratch(arrays)
         + gather_scratch() * len(shards),
         compiler_params=pltpu.CompilerParams(
-            collective_id=call_id, has_side_effects=True, vmem_limit_bytes=40 * 2**20
+            collective_id=call_id, has_side_effects=True, vmem_limit_bytes=VMEM_GRANT
         ),
     )(*operands, *shards)
 
@@ -629,14 +630,14 @@
 def mixer_out(call_id, gated, out_first, out_last, tokens, gain, arrays):
     count = group_size(("tp",))
     vmem = pl.BlockSpec(memory_space=pltpu.VMEM)
-    hbm = pl.BlockSpec(memory_space=pl.ANY)
+    hbm = pl.BlockSpec(memory_space=pltpu.HBM)
     rows, width = tokens.shape
     part = jax.ShapeDtypeStruct((rows, width), jnp.bfloat16)
     sems = pltpu.SemaphoreType.DMA((2, count - 1))
     return pl.pallas_call(
         functools.partial(mixer_out_kernel, len(arrays)),
         in_specs=[vmem] * (5 + len(arrays)),
-        out_specs=[vmem] * 2 + [hbm] + [vmem] * len(arrays),
+        out_specs=[vmem] * 2 + [hbm] + [hbm] * len(arrays),
         out_shape=[
             part,
             jax.ShapeDtypeStruct((rows // count, width), jnp.float32),
@@ -647,7 +648,7 @@
         + gather_scratch()
         + swap_scratch(arrays),
         compiler_params=pltpu.CompilerParams(
-            collective_id=call_id, has_side_effects=True, vmem_limit_bytes=40 * 2**20
+            collective_id=call_id, has_side_effects=True, vmem_limit_bytes=VMEM_GRANT
         ),
     )(gated, out_first, out_last, tokens, gain, *arrays)
 
@@ -656,7 +657,7 @@
     hidden = weights.shape[1] // 3
     if swaps:
         *swapped, block_buf, block_sem, send_sem, recv_sem, local_sem = refs
-        swap = Swap([normed, ct], swapped, send_sem, recv_sem, local_sem)
+        swap = Swap([normed], swapped, send_sem, recv_sem, local_sem)
         greet([(PLANE, swap.plane.others)])
         swap.begin()
     else:
@@ -704,13 +705,13 @@
 
 def run_ffn(call_id, normed, ct, weights, swaps):
     rows, width = normed.shape
-    arrays = [normed, ct] if swaps else []
+    arrays = [normed] if swaps else []
     vmem = pl.BlockSpec(memory_space=pltpu.VMEM)
     params = dict(collective_id=call_id, has_side_effects=True) if swaps else {}
     return pl.pallas_call(
         functools.partial(ffn_kernel, swaps),
-        in_specs=[vmem, vmem, pl.BlockSpec(memory_space=pl.ANY)],
-        out_specs=[vmem] * (1 + len(arrays)),
+        in_specs=[vmem, vmem, pl.BlockSpec(memory_space=pltpu.HBM)],
+        out_specs=[vmem] + [pl.BlockSpec(memory_space=pltpu.HBM)] * len(arrays),
         out_shape=[jax.ShapeDtypeStruct((rows, weights.shape[1]), jnp.bfloat16)]
         + swap_shapes(arrays),
         scratch_shapes=[
@@ -718,7 +719,7 @@
             pltpu.SemaphoreType.DMA((2, 3)),
         ]
         + swap_scratch(arrays),
-        compiler_params=pltpu.CompilerParams(vmem_limit_bytes=48 * 2**20, **params),
+        compiler_params=pltpu.CompilerParams(vmem_limit_bytes=VMEM_GRANT, **params),
     )(normed, ct, weights)
 
 
@@ -827,7 +828,7 @@
     dma = pltpu.SemaphoreType.DMA
     return pl.pallas_call(
         ffn_back_kernel,
-        in_specs=[vmem] * 6 + [pl.BlockSpec(memory_space=pl.ANY)],
+        in_specs=[vmem] * 6 + [pl.BlockSpec(memory_space=pltpu.HBM)],
         out_specs=[vmem] * 5,
         out_shape=[
             part,
@@ -849,7 +850,7 @@
             dma((1, count - 1)),
         ],
         compiler_params=pltpu.CompilerParams(
-            collective_id=call_id, has_side_effects=True, vmem_limit_bytes=52 * 2**20
+            collective_id=call_id, has_side_effects=True, vmem_limit_bytes=VMEM_GRANT
         ),
     )(made, ct, middle, gain, out_first, out_last, weights)
 
@@ -985,7 +986,7 @@
     blocks = all_groups // seqs // groups
     vmem = pl.BlockSpec(memory_space=pltpu.VMEM)
     smem = pl.BlockSpec(memory_space=pltpu.SMEM)
-    hbm = pl.BlockSpec(memory_space=pl.ANY)
+    hbm = pl.BlockSpec(memory_space=pltpu.HBM)
     full = jnp.float32
     held = pltpu.VMEM((tiles * SUB, LANE), full)
     boundary = pltpu.VMEM((seqs, n_state, tiles, LANE), full)
@@ -1013,12 +1014,13 @@
         ]
         + gather_scratch(),
         compiler_params=pltpu.CompilerParams(
-            collective_id=call_id, has_side_effects=True, vmem_limit_bytes=40 * 2**20
+            collective_id=call_id, has_side_effects=True, vmem_limit_bytes=VMEM_GRANT
         ),
     )(step, inputs, b_rows, c_rows, rate, shard)
 
 
 def backward_pair_kernel(
+    n_swaps,
     n_state,
     tiles,
     groups,
@@ -1034,30 +1036,23 @@
     ffn_part,
     middle,
     prior_ref,
-    step_grad_ref,
-    input_grad_ref,
-    rate_grad_ref,
-    part_ref,
-    layer_rows,
-    carried,
-    ends,
-    starts,
-    prior_buf,
-    step_held,
-    input_held,
-    ograd_held,
-    step_grad_held,
-    input_grad_held,
-    ffn_slots,
-    prior_sem,
-    send_sem,
-    recv_sem,
-    tp_send,
-    tp_recv,
+    *refs,
 ):
+    arrays, refs = refs[:n_swaps], refs[n_swaps:]
+    step_grad_ref, input_grad_ref, rate_grad_ref, part_ref, *refs = refs
+    layer_first, layer_last, *refs = refs
+    swapped, refs = refs[:n_swaps], refs[n_swaps:]
+    carried, ends, starts, prior_buf, step_held, input_held, ograd_held, *refs = refs
+    step_grad_held, input_grad_held, ffn_slots, prior_sem, send_sem, recv_sem, *refs = refs
+    tp_send, tp_recv, *refs = refs
     place = lax.axis_index("ctx")
     tp = Group(("tp",), tp_send, tp_recv)
-    greet([(("ctx",), [1 - place]), (("tp",), tp.others)])
+    if n_swaps:
+        swap = Swap(arrays, swapped, *refs)
+        greet([(PLANE, swap.plane.others), (("tp",), tp.others)])
+        swap.begin()
+    else:
+        greet([(("ctx",), [1 - place]), (("tp",), tp.others)])
     ffn_sent = tp.scatter(ffn_part, ffn_slots, 0)
 
     def hand_on(seq):
@@ -1171,7 +1166,9 @@
                 carried[n] = grads[n]
 
     finish(ffn_sent)
-    layer_rows[...] = (middle[...] + tp.total(ffn_part, ffn_slots)).astype(layer_rows.dtype)
+    layer_rows = (middle[...] + tp.total(ffn_part, ffn_slots)).astype(layer_first.dtype)
+    half = layer_first.shape[1]
+    layer_first[...], layer_last[...] = layer_rows[:, :half], layer_rows[:, half:]
 
     @pl.when(place == 1)
     def _():
@@ -1179,9 +1176,12 @@
         def _(seq):
             hand_on(seq).wait_send()
 
+    if n_swaps:
+        swap.end()
+
 
 def scan_backward_pair(
-    call_id, prior, step, inputs, ograd, b_rows, c_rows, rate, seqs, ffn_part, middle
+    call_id, prior, step, inputs, ograd, b_rows, c_rows, rate, seqs, ffn_part, middle, arrays
 ):
     n_state, tiles, _ = rate.shape
     tokens, inner = step.shape
@@ -1191,22 +1191,28 @@
     tp_count = group_size(("tp",))
     vmem = pl.BlockSpec(memory_space=pltpu.VMEM)
     smem = pl.BlockSpec(memory_space=pltpu.SMEM)
+    hbm = pl.BlockSpec(memory_space=pltpu.HBM)
     full = jnp.float32
     held = pltpu.VMEM((tiles * SUB, LANE), full)
     boundary = pltpu.VMEM((seqs, n_state, tiles, LANE), full)
     dma = pltpu.SemaphoreType.DMA
+    layer_half = jax.ShapeDtypeStruct((middle.shape[0], middle.shape[1] // 2), jnp.bfloat16)
     picks = jnp.repeat(jnp.eye(2 * n_state, dtype=jnp.bfloat16), tiles, 1)
     return pl.pallas_call(
-        functools.partial(backward_pair_kernel, n_state, tiles, groups, blocks, seqs),
-        in_specs=[vmem] * 3 + [smem] * 2 + [vmem] * 4 + [pl.BlockSpec(memory_space=pl.ANY)],
-        out_specs=[vmem] * 5,
+        functools.partial(
+            backward_pair_kernel, len(arrays), n_state, tiles, groups, blocks, seqs
+        ),
+        in_specs=[vmem] * 3 + [smem] * 2 + [vmem] * 4 + [hbm] + [vmem] * len(arrays),
+        out_specs=[vmem] * 6 + [hbm] * len(arrays),
         out_shape=[
             jax.ShapeDtypeStruct(step.shape, full),
             jax.ShapeDtypeStruct(step.shape, full),
             jax.ShapeDtypeStruct(rate.shape, full),
             jax.ShapeDtypeStruct((tokens, 2 * n_state, LANE), full),
-            jax.ShapeDtypeStruct(middle.shape, jnp.bfloat16),
-        ],
+            layer_half,
+            layer_half,
+        ]
+        + swap_shapes(arrays),
         scratch_shapes=[
             pltpu.VMEM((n_state, tiles, LANE), full),
             boundary,
@@ -1221,11 +1227,12 @@
             dma((seqs,)),
             dma((1, tp_count - 1)),
             dma((1, tp_count - 1)),
-        ],
+        ]
+        + swap_scratch(arrays),
         compiler_params=pltpu.CompilerParams(
-            collective_id=call_id, has_side_effects=True, vmem_limit_bytes=48 * 2**20
+            collective_id=call_id, has_side_effects=True, vmem_limit_bytes=VMEM_GRANT
         ),
-    )(step, inputs, ograd, b_rows, c_rows, rate, picks, ffn_part, middle, prior)
+    )(step, inputs, ograd, b_rows, c_rows, rate, picks, ffn_part, middle, prior, *arrays)
 
 
 class PlaneGather:
@@ -1366,14 +1373,31 @@
         store(j, j % 2).wait()
 
 
+SMALL_ROWS = 32
+GAIN_ROWS = 16
+
+
 def tail_kernel(
-    sizes,
-    mix_grads,
-    normed_part,
-    small,
+    swaps,
+    conv_grad,
+    gate_grad,
+    convkern,
+    convbias,
+    stepbias,
+    decaylog,
+    skipgain,
+    ffngain,
+    layer_rows,
+    middle_low,
+    step_low,
+    pre_low,
+    select_low,
+    scan_in,
     tokens,
     middle_grad,
     gain_row,
+    in_conv,
+    in_gate,
     one_cols,
     two_cols,
     ct_cols,
@@ -1381,23 +1405,37 @@
     ffn_all,
     gated_all,
     tokens_grad,
-    small_sum,
+    layer_out,
+    vectors_sum,
+    step_sum,
+    select_sum,
     gains,
     mix_all,
     grad_inproj,
     grad_outproj,
     grad_gateup,
     grad_downproj,
+    mix_own,
+    normed_part,
+    small,
+    small_sum,
     normed_slots,
     small_slots,
     gain_slots,
     gain_own,
+    vectors_own,
+    cols,
+    in_buf,
     block_buf,
     wide_buf,
     tall_buf,
+    cols_sem,
+    in_sem,
     block_sem,
     wide_sem,
     tall_sem,
+    part_send,
+    part_recv,
     tp_send,
     tp_recv,
     plane_send,
@@ -1405,22 +1443,94 @@
     gather_send,
     gather_recv,
     local_sem,
+    *swap_sems,
 ):
-    inner, hidden, gain_at = sizes
+    inner = conv_grad.shape[1]
+    hidden = ffn_all.shape[1] // 3
+    width = tokens.shape[1]
+    rank = step_low.shape[1]
     tp = Group(("tp",), tp_send, tp_recv)
     plane = Group(PLANE, plane_send, plane_recv)
-    gather = PlaneGather(mix_grads, mix_all, gather_send, gather_recv)
+    gather = PlaneGather(mix_own, mix_all, gather_send, gather_recv)
+    sources = (one_cols, two_cols, ct_cols) if swaps else (one_cols, two_cols, ct_cols, middle_cols)
+    loads = [
+        pltpu.make_async_copy(source, cols.at[at], cols_sem.at[at])
+        for at, source in enumerate(sources)
+    ]
+    if swaps:
+        swap = Swap([middle_low], [cols.at[3]], *swap_sems)
+
+    def fetch(j):
+        slot = j % 2
+        rows = slice(j * WIDE, (j + 1) * WIDE)
+        return [
+            pltpu.make_async_copy(source.at[rows, :], in_buf.at[slot, at], in_sem.at[slot, at])
+            for at, source in enumerate((in_conv, in_gate))
+        ]
+
+    for copy in fetch(0) + loads:
+        copy.start()
+    mix_own[:, :inner] = conv_grad[...]
+    mix_own[:, inner:] = gate_grad[...]
     greet([(("tp",), tp.others), (PLANE, plane.others)])
-
-    def flat(lhs):
-        return lambda block: lax.dot_general(
-            lhs[...], block, (((0,), (0,)), ((), ())), preferred_element_type=jnp.float32
+    gather.begin(local_sem)
+    if swaps:
+        swap.begin()
+
+    small[...] = jnp.zeros_like(small)
+    vectors_own[...] = jnp.zeros_like(vectors_own)
+    at = 0
+    for vector in (convkern, convbias, stepbias, decaylog, skipgain):
+        vectors_own[at : at + vector.shape[0], :] = vector[...]
+        at += vector.shape[0]
+    at = SMALL_ROWS - GAIN_ROWS + 10
+    for row in range(width // inner):
+        vectors_own[at + row : at + row + 1, :] = ffngain[:, row * inner : (row + 1) * inner]
+    hidden_in = tokens[...].astype(jnp.float32)
+    unit_rows = hidden_in * inverse_rms(hidden_in)
+    blocks = width // WIDE
+    normed_sent = []
+    for j in range(blocks):
+        if j + 1 < blocks:
+            for copy in fetch(j + 1):
+                copy.start()
+        finish(fetch(j))
+        columns = slice(j * WIDE, (j + 1) * WIDE)
+        block = matmul_nt(conv_grad[...], in_buf[j % 2, 0]) + matmul_nt(
+            gate_grad[...], in_buf[j % 2, 1]
         )
-
-    def tall(rhs):
-        return lambda block: lax.dot_general(
-            block, rhs[...], (((0,), (0,)), ((), ())), preferred_element_type=jnp.float32
-        )
+        normed_part[:, columns] = block.astype(normed_part.dtype)
+        for hop, other in enumerate(tp.others):
+            normed_sent.append(
+                sent(
+                    rows_of(normed_part, other, tp.count).at[:, columns],
+                    normed_slots.at[hop, :, columns],
+                    part_send.at[j, hop],
+                    part_recv.at[j, hop],
+                    device_at(("tp",), other),
+                )
+            )
+        gain_grad = jnp.sum(block * unit_rows[:, columns], 0, keepdims=True)
+        row, at = divmod(j * WIDE, inner)
+        row += SMALL_ROWS - GAIN_ROWS + 8
+        vectors_own[row : row + 1, at : at + WIDE] = gain_grad
+    tp.own(layer_out)[...] = layer_rows[...]
+    layer_sent = tp.spread(layer_out, 2)
+    small[:SMALL_ROWS, :] = vectors_own[...].astype(small.dtype)
+    small[SMALL_ROWS : SMALL_ROWS + rank, :] = matmul_tn(step_low[...], pre_low[...]).astype(
+        small.dtype
+    )
+    selected = select_sum.shape[0]
+    small[SMALL_ROWS + rank : SMALL_ROWS + rank + selected, :] = matmul_tn(
+        select_low[...], scan_in[...]
+    )[:selected].astype(small.dtype)
+    small_sent = plane.scatter(small, small_slots, 0)
+
+    def flat(at):
+        return lambda block: matmul_tn(cols[at], block)
+
+    def tall(at):
+        return lambda block: matmul_tn(block, cols[at])
 
     def side_by_side(ref, first):
         per = ref.shape[2] // WIDE
@@ -1432,22 +1542,17 @@
 
         return target
 
-    def one_above_other(ref, first):
-        return lambda j: ref.at[pl.ds(pl.multiple_of((j - first) * WIDE, WIDE), WIDE), :]
+    def one_above_other(ref):
+        return lambda j: ref.at[pl.ds(pl.multiple_of(j * WIDE, WIDE), WIDE), :]
 
     wide = (block_buf, block_sem, wide_buf, wide_sem)
     high = (block_buf, block_sem, tall_buf, tall_sem)
     down_end = hidden // WIDE
     gu_end = 3 * hidden // WIDE
-
-    normed_sent = tp.scatter(normed_part, normed_slots, 0)
-    gather.begin(local_sem)
-    small_sent = plane.scatter(small, small_slots, 0)
-    products(
-        ffn_all, down_end, gu_end, flat(two_cols), side_by_side(grad_gateup, down_end), *wide
-    )
+    finish(loads)
+    products(ffn_all, 0, down_end, tall(2), one_above_other(grad_downproj), *high)
     gather.relay()
-    products(ffn_all, 0, down_end, tall(ct_cols), one_above_other(grad_downproj, 0), *high)
+    products(ffn_all, down_end, gu_end, flat(1), side_by_side(grad_gateup, down_end), *wide)
     gather.hand_over()
     finish(normed_sent)
     hidden_in = tp.own(tokens)[...].astype(jnp.float32)
@@ -1460,38 +1565,51 @@
             gain_row[...].astype(jnp.float32),
         )
     ).astype(tokens_grad.dtype)
-    tokens_sent = tp.spread(tokens_grad, 1)
+    tokens_sent = tp.spread(tokens_grad, 0)
     finish(small_sent)
     plane.own(small_sum)[...] = plane.total(small, small_slots).astype(small_sum.dtype)
     small_sent = plane.spread(small_sum, 1)
-    products(
-        gated_all, 0, inner // WIDE, tall(middle_cols), one_above_other(grad_outproj, 0), *high
-    )
     gather.hand_over_last()
+    if swaps:
+        swap.end()
+    products(gated_all, 0, inner // WIDE, tall(3), one_above_other(grad_outproj), *high)
     finish(small_sent)
-    gain_own[...] = small_sum[pl.ds(gain_at, gain_own.shape[0]), :].astype(jnp.float32)
-    gain_sent = [tp.one(gain_own, gain_slots.at[hop], 2, hop) for hop in range(tp.count - 1)]
+    gain_own[...] = small_sum[SMALL_ROWS - GAIN_ROWS : SMALL_ROWS, :].astype(jnp.float32)
+    gain_sent = [tp.one(gain_own, gain_slots.at[hop], 1, hop) for hop in range(tp.count - 1)]
+    vectors_sum[...] = small_sum[:SMALL_ROWS, :].astype(jnp.float32)
+    step_sum[...] = small_sum[SMALL_ROWS : SMALL_ROWS + rank, :].astype(jnp.float32)
+    select_sum[...] = small_sum[SMALL_ROWS + rank : SMALL_ROWS + rank + selected, :].astype(
+        jnp.float32
+    )
     gather.end()
-    products(
-        mix_all, 0, 2 * inner // WIDE, flat(one_cols), side_by_side(grad_inproj, 0), *wide
-    )
+    products(mix_all, 0, 2 * inner // WIDE, flat(0), side_by_side(grad_inproj, 0), *wide)
     finish(gain_sent)
     total = gain_own[...]
     for hop in range(tp.count - 1):
         total = total + gain_slots[hop]
     gains[...] = total
     finish(tokens_sent)
+    finish(layer_sent)
 
 
 def run_tail(
     call_id,
-    gain_at,
-    mix_grads,
-    normed_part,
-    small,
+    selected,
+    swaps,
+    conv_grad,
+    gate_grad,
+    vectors,
+    layer_rows,
+    middle_low,
+    step_low,
+    pre_low,
+    select_low,
+    scan_in,
     tokens,
     middle_grad,
     gain_row,
+    in_conv,
+    in_gate,
     one_cols,
     two_cols,
     ct_cols,
@@ -1499,24 +1617,31 @@
     ffn_all,
     gated_all,
 ):
-    inner = mix_grads.shape[1] // 2
+    rows, inner = conv_grad.shape
+    rank = step_low.shape[1]
     hidden = ffn_all.shape[1] // 3
+    width = tokens.shape[1]
     share = one_cols.shape[1]
     all_rows = ffn_all.shape[0]
     tp_count, plane_count = group_size(("tp",)), group_size(PLANE)
     low, full = jnp.bfloat16, jnp.float32
     vmem = pl.BlockSpec(memory_space=pltpu.VMEM)
-    hbm = pl.BlockSpec(memory_space=pl.ANY)
-    gain_rows = 16
+    hbm = pl.BlockSpec(memory_space=pltpu.HBM)
     dma = pltpu.SemaphoreType.DMA
+    small_rows = SMALL_ROWS + rank + selected
+    small = jax.ShapeDtypeStruct((small_rows + -small_rows % (16 * plane_count), inner), low)
+    part = jax.ShapeDtypeStruct((rows, width), low)
     return pl.pallas_call(
-        functools.partial(tail_kernel, (inner, hidden, gain_at)),
-        in_specs=[vmem] * 10 + [hbm] * 2,
-        out_specs=[vmem] * 3 + [hbm] * 5,
+        functools.partial(tail_kernel, swaps),
+        in_specs=[vmem] * 17 + [hbm] * 8,
+        out_specs=[vmem] * 6 + [hbm] * 5,
         out_shape=[
             jax.ShapeDtypeStruct(tokens.shape, low),
-            jax.ShapeDtypeStruct(small.shape, low),
-            jax.ShapeDtypeStruct((gain_rows, inner), full),
+            jax.ShapeDtypeStruct((rows, width // 2), low),
+            jax.ShapeDtypeStruct((SMALL_ROWS, inner), full),
+            jax.ShapeDtypeStruct((rank, inner), full),
+            jax.ShapeDtypeStruct((selected, inner), full),
+            jax.ShapeDtypeStruct((GAIN_ROWS, inner), full),
             jax.ShapeDtypeStruct((all_rows, 2 * inner), low),
             jax.ShapeDtypeStruct((2, share, inner), full),
             jax.ShapeDtypeStruct((inner, share), full),
@@ -1524,34 +1649,52 @@
             jax.ShapeDtypeStruct((hidden, share), full),
         ],
         scratch_shapes=[
-            slots_for(normed_part, tp_count),
+            pltpu.VMEM((rows, 2 * inner), low),
+            pltpu.VMEM(part.shape, low),
+            pltpu.VMEM(small.shape, low),
+            pltpu.VMEM(small.shape, low),
+            slots_for(part, tp_count),
             slots_for(small, plane_count),
-            pltpu.VMEM((tp_count - 1, gain_rows, inner), full),
-            pltpu.VMEM((gain_rows, inner), full),
+            pltpu.VMEM((tp_count - 1, GAIN_ROWS, inner), full),
+            pltpu.VMEM((GAIN_ROWS, inner), full),
+            pltpu.VMEM((SMALL_ROWS, inner), full),
+            pltpu.VMEM((4, all_rows, share), low),
+            pltpu.VMEM((2, 2, WIDE, inner), low),
             pltpu.VMEM((2, all_rows, WIDE), low),
             pltpu.VMEM((2, share, WIDE), full),
             pltpu.VMEM((2, WIDE, share), full),
+            dma((4,)),
+            dma((2, 2)),
             dma((2,)),
             dma((2,)),
             dma((2,)),
+            dma((width // WIDE, tp_count - 1)),
+            dma((width // WIDE, tp_count - 1)),
             dma((3, tp_count - 1)),
             dma((3, tp_count - 1)),
             dma((2, plane_count - 1)),
             dma((2, plane_count - 1)),
-            gather_sems(),
-            gather_sems(),
-            dma(()),
-        ],
+        ]
+        + gather_scratch()
+        + (swap_scratch([tokens]) if swaps else []),
         compiler_params=pltpu.CompilerParams(
-            collective_id=call_id, has_side_effects=True, vmem_limit_bytes=56 * 2**20
+            collective_id=call_id, has_side_effects=True, vmem_limit_bytes=VMEM_GRANT
         ),
     )(
-        mix_grads,
-        normed_part,
-        small,
+        conv_grad,
+        gate_grad,
+        *vectors,
+        layer_rows,
+        middle_low,
+        step_low,
+        pre_low,
+        select_low,
+        scan_in,
         tokens,
         middle_grad,
         gain_row,
+        in_conv,
+        in_gate,
         one_cols,
         two_cols,
         ct_cols,
@@ -1561,24 +1704,64 @@
     )
 
 
+class SplitSwap:
+    def __init__(self, array, swapped, plane_send, plane_recv, tp_send, tp_recv, local_sem):
+        self.plane, self.tp = Group(PLANE, plane_send, plane_recv), Group(("tp",), tp_send, tp_recv)
+        self.array, self.swapped, self.local_sem = array, swapped, local_sem
+        rows = array.shape[0] // self.tp.count
+        self.rows = pl.ds(pl.multiple_of(self.tp.me * rows, rows), rows)
+
+    def columns(self, index):
+        share = self.swapped.shape[2]
+        return self.array.at[self.rows, pl.ds(pl.multiple_of(index * share, share), share)]
+
+    def begin(self):
+        mine = self.swapped.at[self.plane.me, self.rows, :]
+        self.local = pltpu.make_async_copy(
+            self.columns(self.plane.me), mine, self.local_sem
+        )
+        self.local.start()
+        self.copies = [
+            self.plane.one(self.columns(other), mine, 0, hop)
+            for hop, other in enumerate(self.plane.others)
+        ]
+
+    def pass_on(self):
+        finish(self.copies)
+        self.local.wait()
+        here = self.swapped.at[:, self.rows, :]
+        self.copies = [self.tp.one(here, here, 0, hop) for hop in range(self.tp.count - 1)]
+
+    def end(self):
+        finish(self.copies)
+
+
 def head_kernel(
+    swaps,
     tokens,
     gain,
+    ct,
     in_conv,
     in_gate,
     conv_in,
     gate_mix,
     conv_all,
     gate_all,
-    normed,
-    block_buf,
-    block_sem,
-    *sems,
+    *refs,
 ):
+    if swaps:
+        swapped, *refs = refs
+    normed, block_buf, block_sem, *sems = refs
     conv = PlaneGather(in_conv, conv_all, *sems[:2])
     gate = PlaneGather(in_gate, gate_all, *sems[3:5])
-    greet([(PLANE, conv.others)])
+    if swaps:
+        swap = SplitSwap(ct, swapped, *sems[6:])
+        greet([(PLANE, conv.others), (("tp",), swap.tp.others)])
+    else:
+        greet([(PLANE, conv.others)])
     conv.begin(sems[2])
+    if swaps:
+        swap.begin()
     gate.begin(sems[5])
     hidden_in = tokens[...].astype(jnp.float32)
     normed[...] = (hidden_in * inverse_rms(hidden_in) * gain[...].astype(jnp.float32)).astype(
@@ -1605,6 +1788,8 @@
 
     conv.relay()
     conv.hand_over()
+    if swaps:
+        swap.pass_on()
     gate.relay()
     conv.hand_over_last()
     gate.hand_over()
@@ -1613,34 +1798,48 @@
     gate.hand_over_last()
     gate.end()
     product(gate_all, gate_mix)
-
-
-def run_head(call_id, tokens, gain, inproj):
+    if swaps:
+        swap.end()
+
+
+def run_head(call_id, tokens, gain, ct, inproj, swaps):
     rows, width = tokens.shape
     inner = inproj.shape[2]
     low = jnp.bfloat16
     vmem = pl.BlockSpec(memory_space=pltpu.VMEM)
-    hbm = pl.BlockSpec(memory_space=pl.ANY)
+    hbm = pl.BlockSpec(memory_space=pltpu.HBM)
+    count, tp_count = group_size(PLANE), group_size(("tp",))
+    dma = pltpu.SemaphoreType.DMA
+    swap_sems = [
+        dma((1, count - 1)),
+        dma((1, count - 1)),
+        dma((1, tp_count - 1)),
+        dma((1, tp_count - 1)),
+        dma(()),
+    ]
+    swapped = [jax.ShapeDtypeStruct((count, rows, width // count), low)]
     return pl.pallas_call(
-        head_kernel,
-        in_specs=[vmem] * 2 + [hbm] * 2,
-        out_specs=[vmem] * 2 + [hbm] * 2,
+        functools.partial(head_kernel, swaps),
+        in_specs=[vmem] * 3 + [hbm] * 2,
+        out_specs=[vmem] * 2 + [hbm] * (3 if swaps else 2),
         out_shape=[
             jax.ShapeDtypeStruct((rows, inner), low),
             jax.ShapeDtypeStruct((rows, inner), jnp.float32),
             jax.ShapeDtypeStruct((width, inner), low),
             jax.ShapeDtypeStruct((width, inner), low),
-        ],
+        ]
+        + (swapped if swaps else []),
         scratch_shapes=[
             pltpu.VMEM((rows, width), low),
             pltpu.VMEM((2, width, WIDE), low),
             pltpu.SemaphoreType.DMA((2,)),
         ]
-        + gather_scratch() * 2,
+        + gather_scratch() * 2
+        + (swap_sems if swaps else []),
         compiler_params=pltpu.CompilerParams(
-            collective_id=call_id, has_side_effects=True, vmem_limit_bytes=40 * 2**20
+            collective_id=call_id, has_side_effects=True, vmem_limit_bytes=VMEM_GRANT
         ),
-    )(tokens, gain, inproj[0], inproj[1])
+    )(tokens, gain, ct, inproj[0], inproj[1])
 
 
 def per_device(
@@ -1682,7 +1881,11 @@
     ffn_pack = gathered_rows(
         jnp.concatenate([gateup[0], gateup[1], jnp.transpose(downproj)], 1)
     )
-    conv_in, gate_mix, in_conv, in_gate = run_head(5, tokens_rows, gain_mix_row, inproj)
+    swap_now = swaps_in_kernels(width)
+    conv_in, gate_mix, in_conv, in_gate, *swapped = run_head(
+        5, tokens_rows, gain_mix_row, ct_low, inproj, swap_now
+    )
+    ct_cols = swapped[0].reshape(-1, swapped[0].shape[2]) if swapped else swapped_columns(ct_low)
     hidden_in = tokens_rows.astype(jnp.float32)
     scale_one = inverse_rms(hidden_in)
     normed_one = (hidden_in * scale_one * gain_mix).astype(low)
@@ -1723,7 +1926,6 @@
     mixer_core = scan_out + skip_weight[None] * scan_float
     gate_sig = jax.nn.silu(gate_mix)
     gated = (mixer_core * gate_sig).astype(low)
-    swap_now = swaps_in_kernels(width)
     normed_two, middle, gated_all, *swapped = mixer_out(
         1,
         gated,
@@ -1735,9 +1937,7 @@
     )
     (normed_one_cols,) = swapped if swap_now else [swapped_columns(normed_one)]
     made, *swapped = run_ffn(8, normed_two, ct_low, ffn_pack, swap_now)
-    if not swap_now:
-        swapped = [swapped_columns(normed_two), swapped_columns(ct_low)]
-    normed_two_cols, ct_cols = swapped
+    (normed_two_cols,) = swapped or [swapped_columns(normed_two)]
     ffn_all = gathered_rows(made)
     middle_low, middle_grad, ffngain_part, gated_grad, ffn_part = ffn_back(
         2, made, ct_low, middle, gain_ffn_row, out_first, out_last, ffn_pack
@@ -1746,7 +1946,7 @@
     gate_mix_grad = (gated_grad * mixer_core * silu_slope(gate_mix)).astype(low)
     grad_skipgain = jnp.sum(core_grad * scan_float, 0)
     if in_pairs:
-        step_grad, input_grad, rate_grad, parts, layer_rows = scan_backward_pair(
+        step_grad, input_grad, rate_grad, parts, *layer_rows = scan_backward_pair(
             7,
             prior,
             step_size,
@@ -1758,6 +1958,7 @@
             seqs,
             ffn_part,
             middle,
+            [],
         )
     else:
         back_ends = scan_ends(step_size, core_grad, c_rows, rate, seqs, True)
@@ -1766,12 +1967,11 @@
             end_grad, prior, step_size, scan_float, core_grad, b_rows, c_rows, rate, seqs
         )
         ffn_sum = lax.psum_scatter(ffn_part, "tp", scatter_dimension=0, tiled=True)
-        layer_rows = (middle + ffn_sum.astype(jnp.float32)).astype(low)
+        layer_rows = jnp.split((middle + ffn_sum.astype(jnp.float32)).astype(low), 2, 1)
     grad_decaylog = rate_grad.reshape(n_state, inner) * decay_rate
     pre_grad = step_grad * jax.nn.sigmoid(step_pre)
     grad_stepbias = jnp.sum(pre_grad, 0)
     pre_low = pre_grad.astype(low)
-    grad_stepproj = matmul_tn(step_low, pre_low)
     select_part = jnp.concatenate(
         [
             matmul_nt(pre_low, stepproj),
@@ -1780,11 +1980,7 @@
         ],
         1,
     ).astype(low)
-    select_low, layer_out, *swapped = sum_over_tp(
-        3, select_part, [layer_rows], [middle_low] if swap_now else [], []
-    )
-    (middle_cols,) = swapped if swap_now else [swapped_columns(middle_low)]
-    grad_selproj = matmul_tn(select_low, scan_in)
+    select_low, layer_first = sum_over_tp(3, select_part, layer_rows[:1], [], [])
     scan_in_grad = (
         core_grad * skip_weight[None]
         + input_grad
@@ -1808,30 +2004,20 @@
         .astype(low)
         .reshape(rows, inner)
     )
-    mix_grads = jnp.concatenate([conv_in_grad, gate_mix_grad], 1)
-    normed_one_part = matmul_nt(conv_in_grad, in_conv) + matmul_nt(gate_mix_grad, in_gate)
-    mixgain_part = jnp.sum(normed_one_part * hidden_in * scale_one, 0)
-    normed_one_part = normed_one_part.astype(low)
-    small = [
+    vectors = [
         grad_convkern,
         grad_convbias[None],
         grad_stepbias[None],
         grad_decaylog,
         grad_skipgain[None],
-        grad_stepproj,
-        grad_selproj[:columns],
-        mixgain_part.reshape(-1, inner),
-        ffngain_part.reshape(-1, inner),
+        ffngain_part,
     ]
-    sizes = [part.shape[0] for part in small]
-    gain_at = sum(sizes[:-2]) + -sum(sizes[:-2]) % 16
-    small.insert(-2, jnp.zeros((gain_at - sum(sizes[:-2]), inner), jnp.float32))
-    small = jnp.concatenate(small, 0).astype(low)
-    share = 16 * group_size(PLANE)
-    small = jnp.pad(small, ((0, -(gain_at + 16) % share + 16 - sum(sizes[-2:])), (0, 0)))
     (
         tokens_grad,
-        small,
+        layer_last,
+        vectors,
+        grad_stepproj,
+        grad_selproj,
         gains,
         _,
         grad_inproj,
@@ -1840,40 +2026,44 @@
         grad_downproj,
     ) = run_tail(
         4,
-        gain_at,
-        mix_grads,
-        normed_one_part,
-        small,
+        columns,
+        swap_now,
+        conv_in_grad,
+        gate_mix_grad,
+        vectors,
+        layer_rows[1],
+        middle_low,
+        step_low,
+        pre_low,
+        select_low,
+        scan_in,
         tokens_rows,
         middle_grad,
         gain_mix_row,
+        in_conv,
+        in_gate,
         normed_one_cols,
         normed_two_cols,
         ct_cols,
-        middle_cols,
+        normed_two_cols if swap_now else swapped_columns(middle_low),
         ffn_all,
         gated_all,
     )
-    small = small.astype(jnp.float32)
-    smalls, at = [], 0
-    for size in sizes[:-2]:
-        smalls.append(small[at : at + size])
-        at += size
-    gains = gains[: sum(sizes[-2:])].reshape(2, width)
+    at = taps + 2
     return (
-        layer_out.reshape(tokens.shape),
+        jnp.concatenate([layer_first, layer_last], 1).reshape(tokens.shape),
         tokens_grad.reshape(tokens.shape),
-        gains[0],
+        gains[8:10].reshape(width),
         grad_inproj,
-        smalls[0],
-        smalls[1][0],
-        jnp.transpose(smalls[6]),
-        smalls[5],
-        smalls[2][0],
-        jnp.transpose(smalls[3]),
-        smalls[4][0],
+        vectors[:taps],
+        vectors[taps],
+        jnp.transpose(grad_selproj),
+        grad_stepproj,
+        vectors[taps + 1],
+        jnp.transpose(vectors[at : at + n_state]),
+        vectors[at + n_state],
         grad_outproj,
-        gains[1],
+        gains[10:12].reshape(width),
         grad_gateup,
         grad_downproj,
     )

time: 505 us -> 493 us (0.976)
  local copies, waits for them, and re-layouts: 52.2 us -> 28 us
  Pallas kernels: 396 us -> 411 us
  matrix products: 15.8 us -> 6.82 us
  other arithmetic: 19 us -> 24.5 us
    pallas_call x3, Pallas kernels: 172 us -> 199 us  [the longest x1 85.1 us: run_head(): pl.pallas_call(functools.partial(head_kernel, swaps), in_specs=[vmem] * 3...]
    unnamed x159 -> x74, local copies, waits for them, and re-layouts: 37.5 us -> 13.7 us
    pallas_call x1, Pallas kernels: 30.4 us -> 18.3 us  [run_ffn(): pl.pallas_call(functools.partial(ffn_kernel, swaps), in_specs=[vmem, vmem...]
    pallas_call x2, Pallas kernels: 54.2 us -> 45.5 us  [sum_over_tp(): pl.pallas_call(functools.partial(sum_kernel, len(own_rows), len(arrays),...]
    dot_general x4 -> x2, matrix products: 10.6 us -> 2.77 us  [matmul_nt(): lax.dot_general(left, right, (((1,), (1,)), ((), ())), preferred_element_...]
  transfers between devices with their start and end apart: 4 -> 4, of which waited for: 0 -> 1; matrix products, arithmetic and copies ran while one was open for 8% -> 8% of each run, Pallas kernels for 59% -> 64%
where the time goes in v9:
time: 493 us; the launch traced here: 491 us
  Pallas kernels  411 us (83%)
  local copies, waits for them, and re-layouts  28 us (6%)
  other arithmetic  24.5 us (5%)
  between operations  14.6 us (3%)
  matrix products  6.82 us (1%)
    pallas_call x1, Pallas kernels, run_head(): pl.pallas_call(functools.partial(head_kernel, swaps), in_specs=[vmem] * 3...  85.1 us
    pallas_call x1, Pallas kernels, run_tail(): pl.pallas_call(functools.partial(tail_kernel, swaps), in_specs=[vmem] * 1...  77.3 us
    pallas_call x1, Pallas kernels, ffn_back(): pl.pallas_call(ffn_back_kernel, in_specs=[vmem] * 6 + [pl.BlockSpec(memor...  61.5 us
    pallas_call x1, Pallas kernels, mixer_out(): pl.pallas_call(functools.partial(mixer_out_kernel, len(arrays)), in_specs...  52.7 us
    pallas_call x2, Pallas kernels, sum_over_tp(): pl.pallas_call(functools.partial(sum_kernel, len(own_rows), len(arrays),...  45.5 us
    pallas_call x1, Pallas kernels, scan_backward_pair(): pl.pallas_call(functools.partial(backward_pair_kernel, len(arrays), n_sta...  36.6 us
    pallas_call x1, Pallas kernels, scan_forward_pair(): pl.pallas_call(functools.partial(forward_pair_kernel, n_state, tiles, gro...  34.3 us
    pallas_call x1, Pallas kernels, run_ffn(): pl.pallas_call(functools.partial(ffn_kernel, swaps), in_specs=[vmem, vmem...  18.3 us
  transfers between devices with their start and end apart: 4, of which 1 were waited for; matrix products, arithmetic and copies ran while one was open for 8% of the time, Pallas kernels for 64%

profile of v9, /device:TPU:0, one launch (start us, length us, event | category | flops | bytes accessed | tf_op | source)
XLA Modules:
  0.0 491.4 jit_solution(16563582834144772336)
XLA Ops:
  7.3 1.6 copy.32
  9.3 1.8 pad_maximum_fusion
  12.4 1.0 slice_bitcast_fusion.2
  13.4 85.1 %shard_map.262 = (bf16[256,1024]{1,0:T(8,128)(2,1)}, f32[256,1024]{1,0:T(8,128)}, bf16[2048,1024]{1,0:T(8,128)(2,1)}, bf16[2048,1024]{1,0:T(8,128)(2,1)}, bf16[8,256,256]{2,1,0:T(8,128)(2,1)}) custom-call(bf16[256,2048]{1,0:T(8,128)(2,1)} %bitcast.88, bf16[1,2048]{1,0:T(2,128)(2,1)} %reshape.110.gain.gain_row, bf16[256,2048]{1,0:T(8,128)(2,1)} %bitcast.91, ...), custom_call_target="tpu_custom_call" | custom-call | tf_op jit(solution)/shard_map/pallas_call | solution.py:1821
  99.3 2.7 collective-permute-start
  103.2 1.3 multiply_convert_fusion.refs_0_
  106.5 1.8 fusion.20
  109.3 24.8 %shard_map.263 = (f32[256,256]{1,0:T(8,128)}, bf16[4096,256]{1,0:T(8,128)(2,1)}) custom-call(f32[256,256]{1,0:T(8,128)} %fusion.10.part, bf16[512,256]{1,0:T(8,128)(2,1)} %get-tuple-element.114.refs_0_), custom_call_target="tpu_custom_call" | custom-call | tf_op jit(solution)/shard_map/pallas_call | solution.py:573
  134.1 1.1 fusion.23
  136.6 3.0 compare_select_fusion
  139.6 34.3 %shard_map.264 = (f32[256,16,8,128]{3,2,1,0:T(8,128)}, f32[256,1024]{1,0:T(8,128)}, bf16[4096,256]{1,0:T(8,128)(2,1)}) custom-call(f32[256,1024]{1,0:T(8,128)} %get-tuple-element.126.step_ref, f32[256,1024]{1,0:T(8,128)} %get-tuple-element.99.input_ref, f32[4096]{0:T(1024)} %reshape.114.brow_ref, f32[4096]{0:T(1024)} %reshape.115.crow_ref, ...), custom_call_target="tpu_custom_call" | custom-call | tf_op jit(solution)/shard_map/pallas_call | solution.py:994
  173.9 2.4 multiply_convert_fusion.2.gated
  176.3 52.7 %shard_map.265 = (bf16[256,2048]{1,0:T(8,128)(2,1)}, f32[64,2048]{1,0:T(8,128)}, bf16[2048,1024]{1,0:T(8,128)(2,1)}, bf16[2048,256]{1,0:T(8,128)(2,1)}) custom-call(bf16[256,1024]{1,0:T(8,128)(2,1)} %multiply_convert_fusion.2.gated, bf16[4096,256]{1,0:T(8,128)(2,1)} %get-tuple-element.58.out_first, bf16[4096,256]{1,0:T(8,128)(2,1)} %get-tuple-element.59.out_last, ...), custom_call_target="tpu_custom_call" | custom-call | tf_op jit(solution)/shard_map/pallas_call | solution.py:637
  229.0 18.3 %shard_map.266 = (bf16[256,6144]{1,0:T(8,128)(2,1)}, bf16[2048,256]{1,0:T(8,128)(2,1)}) custom-call(bf16[256,2048]{1,0:T(8,128)(2,1)} %get-tuple-element.60.normed, bf16[256,2048]{1,0:T(8,128)(2,1)} %bitcast.92, bf16[2048,6144]{1,0:T(8,128)(2,1)} %all-gather.3.cloned.1.call-done.weights), custom_call_target="tpu_custom_call" | custom-call | tf_op jit(solution)/shard_map/pallas_call | solution.py:711
  248.7 1.5 slice.147.step_low
  250.2 61.5 %shard_map.267 = (bf16[256,2048]{1,0:T(8,128)(2,1)}, f32[64,2048]{1,0:T(8,128)}, f32[1,2048]{1,0:T(1,128)}, f32[256,1024]{1,0:T(8,128)}, bf16[256,2048]{1,0:T(8,128)(2,1)}) custom-call(bf16[256,6144]{1,0:T(8,128)(2,1)} %get-tuple-element.61.made, bf16[256,2048]{1,0:T(8,128)(2,1)} %bitcast.93, f32[64,2048]{1,0:T(8,128)} %get-tuple-element.62.middle, ...), custom_call_target="tpu_custom_call" | custom-call | tf_op jit(solution)/shard_map/pallas_call | solution.py:829
  311.7 3.9 multiply_reduce_fusion.1
  315.6 36.6 %shard_map.268 = (f32[256,1024]{1,0:T(8,128)}, f32[256,1024]{1,0:T(8,128)}, f32[16,8,128]{2,1,0:T(8,128)}, f32[256,32,128]{2,1,0:T(8,128)}, bf16[64,1024]{1,0:T(8,128)(2,1)}, /*index=5*/bf16[64,1024]{1,0:T(8,128)(2,1)}) custom-call(f32[256,1024]{1,0:T(8,128)} %get-tuple-element.126.step_ref, f32[256,1024]{1,0:T(8,128)} %get-tuple-element.99.input_ref, ...), custom_call_target="tpu_custom_call" | custom-call | tf_op jit(solution)/shard_map/pallas_call | solution.py:1201
  352.2 3.4 reduce_sum.82
  355.7 2.2 fusion.17
  358.9 20.7 %shard_map.269 = (bf16[256,256]{1,0:T(8,128)(2,1)}, bf16[256,1024]{1,0:T(8,128)(2,1)}) custom-call(bf16[256,256]{1,0:T(8,128)(2,1)} %maximum_maximum_fusion.part, bf16[64,1024]{1,0:T(8,128)(2,1)} %get-tuple-element.68.refs_0_), custom_call_target="tpu_custom_call" | custom-call | tf_op jit(solution)/shard_map/pallas_call | solution.py:573
  379.6 2.5 multiply_reduce_fusion.5
  382.7 1.4 collective-permute-start.1
  386.6 2.0 collective-permute-done.1
  389.5 77.3 %shard_map.270 = (bf16[256,2048]{1,0:T(8,128)(2,1)}, bf16[256,1024]{1,0:T(8,128)(2,1)}, f32[32,1024]{1,0:T(8,128)}, f32[128,1024]{1,0:T(8,128)}, f32[160,1024]{1...) custom-call(bf16[256,1024]{1,0:T(8,128)(2,1)} %bitcast.96, ...), custom_call_target="tpu_custom_call" | custom-call | tf_op jit(solution)/shard_map/pallas_call | solution.py:1634
  466.9 1.5 fusion.24
  468.3 1.4 slice.111
  469.7 1.5 slice_bitcast_fusion.4
  472.1 2.3 pad_maximum_fusion.1
  475.9 1.3 copy.51
  480.2 2.1 copy.55
  483.3 1.3 copy.56
  (110 shorter events, 20.6 us)
Async XLA Ops:
  7.2 129.4 %copy-start = (bf16[128,1024]{1,0:T(8,128)(2,1)S(1)}, bf16[128,1024]{1,0:T(8,128)(2,1)}, u32[]{:S(2)}) copy-start(bf16[128,1024]{1,0:T(8,128)(2,1)} %param.21) | copy-start | bytes 786436
  7.2 1.9 copy-start.7
  7.2 221.8 %all-gather.3.cloned.1.call-start = ((), (), s32[]{:S(2)}) async-start(), calls=%async_computation | async-start | bytes 28311552 | tf_op jit(solution)/shard_map/all_gather | solution.py:366
  11.1 378.4 %all-gather.5.cloned.1.call-start = ((), (), s32[]{:S(2)}) async-start(), calls=%async_computation.1 | async-start | bytes 28311552 | tf_op jit(solution)/shard_map/all_gather | solution.py:366
  13.4 88.6 %copy-start.1 = (bf16[2,128,2048]{2,1,0:T(8,128)(2,1)S(1)}, bf16[2,128,2048]{2,1,0:T(8,128)(2,1)}, u32[]{:S(2)}) copy-start(bf16[2,128,2048]{2,1,0:T(8,128)(2,1)} %param.15) | copy-start | bytes 3145732
  13.4 89.0 %copy-start.20 = (bf16[1024,16]{0,1:T(8,128)(2,1)S(1)}, bf16[1024,16]{0,1:T(8,128)(2,1)}, u32[]{:S(2)}) copy-start(bf16[1024,16]{0,1:T(8,128)(2,1)} %param.23) | copy-start | bytes 98308
  13.4 89.0 %copy-start.16 = (bf16[1024,256]{1,0:T(8,128)(2,1)S(1)}, bf16[1024,256]{1,0:T(8,128)(2,1)}, u32[]{:S(2)}) copy-start(bf16[1024,256]{1,0:T(8,128)(2,1)} %param.25) | copy-start | bytes 1572868
  99.3 6.6 %collective-permute-start = (bf16[2,3,1024]{2,1,0:T(4,128)(2,1)S(1)}, bf16[2,3,1024]{2,1,0:T(4,128)(2,1)S(1)}, u32[]{:S(2)}, u32[]{:S(2)}) collective-permute-start(bf16[2,3,1024]{2,1,0:T(4,128)(2,1)S(1)} %slice.118), channel_id=1, source_target_pairs={{0,4},{1,5},{2,6},{3,7},{8,12},{9,13},{10,14},{11,15},{16,20},{17,... | collective-permute-start | bytes 36872 | tf_op jit(solution)/shard_map/ppermute | solution.py:23
  102.0 2.5 copy-start.25
  102.0 2.5 copy-start.28
  102.0 2.5 copy-start.29
  102.0 2.6 copy-start.30
  102.0 2.6 copy-start.27
  102.1 3.8 copy-start.15
  106.5 1.8 copy-start.19
  108.3 203.4 %copy-start.2 = (bf16[256,1024]{1,0:T(8,128)(2,1)}, bf16[256,1024]{1,0:T(8,128)(2,1)S(1)}, u32[]{:S(2)}) copy-start(bf16[256,1024]{1,0:T(8,128)(2,1)S(1)} %get-tuple-element.100.scan_in) | copy-start | bytes 1572868
  136.6 37.3 %copy-start.5 = (f32[256,1024]{1,0:T(8,128)S(1)}, f32[256,1024]{1,0:T(8,128)}, u32[]{:S(2)}) copy-start(f32[256,1024]{1,0:T(8,128)} %get-tuple-element.57) | copy-start | bytes 3145732
  352.2 3.5 copy-start.10
  355.6 2.5 copy-start.31
  355.6 23.9 %copy-start.4 = (f32[256,1024]{1,0:T(8,128)S(1)}, f32[256,1024]{1,0:T(8,128)}, u32[]{:S(2)}) copy-start(f32[256,1024]{1,0:T(8,128)} %get-tuple-element.98.ograd_ref) | copy-start | bytes 3145732
  357.9 24.2 %copy-start.3 = (bf16[256,1024]{1,0:T(8,128)(2,1)}, bf16[256,1024]{1,0:T(8,128)(2,1)S(1)}, u32[]{:S(2)}) copy-start(bf16[256,1024]{1,0:T(8,128)(2,1)S(1)} %get-tuple-element.103.pre_low) | copy-start | bytes 1572868
  379.6 2.5 copy-start.24
  382.6 2.0 copy-start.21
  382.7 2.0 copy-start.22
  382.7 5.9 %collective-permute-start.1 = (f32[2,3,1024]{2,1,0:T(4,128)S(1)}, f32[2,3,1024]{2,1,0:T(4,128)S(1)}, u32[]{:S(2)}, u32[]{:S(2)}) collective-permute-start(f32[2,3,1024]{2,1,0:T(4,128)S(1)} %pad_add_fusion.1), channel_id=1, source_target_pairs={{4,0},{5,1},{6,2},{7,3},{12,8},{13,9},{14,10},{15,11},{20,16},{21,... | collective-permute-start | bytes 73736 | tf_op jit(solution)/shard_map/ppermute | solution.py:23
  389.5 82.5 %copy-start.18 = (bf16[256,1024]{1,0:T(8,128)(2,1)S(1)}, bf16[256,1024]{1,0:T(8,128)(2,1)}, u32[]{:S(2)}) copy-start(bf16[256,1024]{1,0:T(8,128)(2,1)} %get-tuple-element.69) | copy-start | bytes 1572868
  466.8 8.1 %copy-start.13 = (bf16[256,2048]{1,0:T(8,128)(2,1)S(1)}, bf16[256,2048]{1,0:T(8,128)(2,1)}, u32[]{:S(2)}) copy-start(bf16[256,2048]{1,0:T(8,128)(2,1)} %get-tuple-element.84) | copy-start | bytes 3145732
  472.1 3.8 copy-start.9
  475.9 2.4 copy-start.17
  475.9 3.1 copy-start.12
  477.4 2.7 copy-start.6
  480.2 3.1 copy-start.8
  (4 other events, 5.0 us)
Sparse Core Ops, SparseCore 0:
  11.2 175.1 all-gather.2
  247.5 130.9 all-gather.4

commit v10 on v9

--- a/solution.py
+++ b/solution.py
@@ -468,6 +468,116 @@
     return math.prod(lax.axis_size(axis) for axis in axes)
 
 
+def line_of_four():
+    me = lax.axis_index("tp")
+    near = me + 1 - 2 * lax.rem(me, 2)
+    return me, near, lax.rem(me + 2, 4), lax.rem(near + 2, 4)
+
+
+class LineSum:
+    def __init__(self, part, near_slots, far_slot, passed, send_sem, recv_sem):
+        self.part, self.near_slots, self.far_slot = part, near_slots, far_slot
+        self.passed, self.send_sem, self.recv_sem = passed, send_sem, recv_sem
+        self.me, self.near, self.far, self.cross = line_of_four()
+        self.blocks = send_sem.shape[1]
+        self.copies = []
+
+    def columns(self, j):
+        wide = self.part.shape[1] // self.blocks
+        return slice(j * wide, (j + 1) * wide)
+
+    def rows(self, index):
+        return rows_of(self.part, index, 4)
+
+    def send(self, source, target, which, j, where):
+        copy = sent(
+            source.at[:, self.columns(j)],
+            target.at[:, self.columns(j)],
+            self.send_sem.at[which, j],
+            self.recv_sem.at[which, j],
+            {"tp": where},
+        )
+        self.copies.append((which, copy))
+        return copy
+
+    def begin(self, j):
+        first = self.send(self.rows(self.cross), self.near_slots.at[0], 0, j, self.near)
+        self.send(self.rows(self.near), self.near_slots.at[1], 1, j, self.near)
+        return first
+
+    def pass_on(self, j, first):
+        first.wait_recv()
+        columns = self.columns(j)
+        self.passed[:, columns] = (
+            self.rows(self.far)[:, columns].astype(jnp.float32)
+            + self.near_slots[0, :, columns].astype(jnp.float32)
+        ).astype(self.passed.dtype)
+        self.send(self.passed, self.far_slot, 2, j, self.far)
+
+    def total(self):
+        for which, copy in self.copies:
+            copy.wait_send()
+            if which:
+                copy.wait_recv()
+        return (
+            self.rows(self.me)[...].astype(jnp.float32)
+            + self.near_slots[1].astype(jnp.float32)
+            + self.far_slot[...].astype(jnp.float32)
+        )
+
+    def pass_all(self, firsts):
+        for j, first in enumerate(firsts):
+            self.pass_on(j, first)
+
+
+def line_sum_scratch(part, blocks):
+    share = (part.shape[0] // 4,) + part.shape[1:]
+    sems = pltpu.SemaphoreType.DMA((3, blocks))
+    return [
+        pltpu.VMEM((2,) + share, part.dtype),
+        pltpu.VMEM(share, part.dtype),
+        pltpu.VMEM(share, part.dtype),
+        sems,
+        sems,
+    ]
+
+
+class LineSpread:
+    def __init__(self, ref, send_sem, recv_sem):
+        self.ref, self.send_sem, self.recv_sem = ref, send_sem, recv_sem
+        self.me, self.near, self.far, self.cross = line_of_four()
+
+    def send(self, owner, half, which, where):
+        rows = rows_of(self.ref, owner, 4)
+        if half is not None:
+            wide = self.ref.shape[1] // 2
+            rows = rows.at[:, half * wide : (half + 1) * wide]
+        return sent(rows, rows, self.send_sem.at[which], self.recv_sem.at[which], {"tp": where})
+
+    def begin(self):
+        self.across = [self.send(self.me, half, half, self.far) for half in range(2)]
+        self.within = [self.send(self.me, None, 2, self.near)]
+
+    def pass_on(self):
+        for half, copy in enumerate(self.across):
+            copy.wait_recv()
+            self.within.append(self.send(self.far, half, 3 + half, self.near))
+
+    def end(self):
+        for copy in self.across:
+            copy.wait_send()
+        finish(self.within)
+
+    def run(self):
+        self.begin()
+        self.pass_on()
+        self.end()
+
+
+def line_spread_scratch():
+    return [pltpu.SemaphoreType.DMA((5,)), pltpu.SemaphoreType.DMA((5,))]
+
+
 class Swap:
     def __init__(self, arrays, swapped, send_sem, recv_sem, local_sem):
         plane = Group(PLANE, send_sem, recv_sem)
@@ -510,50 +620,6 @@
     return width // group_size(PLANE) % LANE == 0
 
 
-def sum_kernel(n_rows, n_swaps, n_gathers, part, *refs):
-    own_rows, refs = refs[:n_rows], refs[n_rows:]
-    arrays, refs = refs[:n_swaps], refs[n_swaps:]
-    shards, refs = refs[:n_gathers], refs[n_gathers:]
-    total, refs = refs[0], refs[1:]
-    all_rows, refs = refs[:n_rows], refs[n_rows:]
-    swapped, refs = refs[:n_swaps], refs[n_swaps:]
-    gathered, refs = refs[:n_gathers], refs[n_gathers:]
-    slots, send_sem, recv_sem, *refs = refs
-    group = Group(("tp",), send_sem, recv_sem)
-    greeted = [(("tp",), group.others)]
-    if n_swaps:
-        swap = Swap(arrays, swapped, *refs[:3])
-        greeted.append((PLANE, swap.plane.others))
-        refs = refs[3:]
-    if n_gathers:
-        gather = PlaneGather(shards[0], gathered[0], *refs[:2])
-        if not n_swaps:
-            greeted.append((PLANE, gather.others))
-    greet(greeted)
-    copies = group.scatter(part, slots, 0)
-    if n_swaps:
-        swap.begin()
-    if n_gathers:
-        gather.begin(refs[2])
-    spreads = []
-    for which, (own, everything) in enumerate(zip(own_rows, all_rows)):
-        group.own(everything)[...] = own[...]
-        spreads += group.spread(everything, 2 + which)
-    finish(copies)
-    group.own(total)[...] = group.total(part, slots).astype(total.dtype)
-    copies = group.spread(total, 1)
-    if n_gathers:
-        gather.relay()
-        gather.hand_over()
-    finish(copies)
-    finish(spreads)
-    if n_swaps:
-        swap.end()
-    if n_gathers:
-        gather.hand_over_last()
-        gather.end()
-
-
 def gathered_shape(shard):
     return jax.ShapeDtypeStruct(
         (shard.shape[0] * group_size(PLANE),) + shard.shape[1:], shard.dtype
@@ -564,79 +630,165 @@
     return [gather_sems(), gather_sems(), pltpu.SemaphoreType.DMA(())]
 
 
-def sum_over_tp(call_id, part, own_rows, arrays, shards):
-    count = group_size(("tp",))
-    vmem = pl.BlockSpec(memory_space=pltpu.VMEM)
-    hbm = pl.BlockSpec(memory_space=pltpu.HBM)
-    operands = [part, *own_rows, *arrays]
-    sems = pltpu.SemaphoreType.DMA((2 + len(own_rows), count - 1))
-    return pl.pallas_call(
-        functools.partial(sum_kernel, len(own_rows), len(arrays), len(shards)),
-        in_specs=[vmem] * len(operands) + [hbm] * len(shards),
-        out_specs=[vmem] * len(operands) + [hbm] * len(shards),
-        out_shape=[jax.ShapeDtypeStruct(part.shape, part.dtype)]
-        + [
-            jax.ShapeDtypeStruct((own.shape[0] * count,) + own.shape[1:], own.dtype)
-            for own in own_rows
-        ]
-        + swap_shapes(arrays)
-        + [gathered_shape(shard) for shard in shards],
-        scratch_shapes=[slots_for(part, count), sems, sems]
-        + swap_scratch(arrays)
-        + gather_scratch() * len(shards),
-        compiler_params=pltpu.CompilerParams(
-            collective_id=call_id, has_side_effects=True, vmem_limit_bytes=VMEM_GRANT
-        ),
-    )(*operands, *shards)
-
-
-def mixer_out_kernel(n_swaps, gated, out_first, out_last, tokens, gain, *refs):
-    arrays, refs = refs[:n_swaps], refs[n_swaps:]
-    normed, middle, gated_all, *refs = refs
-    swapped, refs = refs[:n_swaps], refs[n_swaps:]
-    part, slots, send_sem, recv_sem, gather_send, gather_recv, local_sem, *refs = refs
+def product_in_blocks(left, source, target, block_buf, block_sem):
+    columns = range(0, source.shape[1], WIDE)
+
+    def fetch(turn):
+        at = columns[turn]
+        return pltpu.make_async_copy(
+            source.at[:, at : at + WIDE], block_buf.at[turn % 2], block_sem.at[turn % 2]
+        )
+
+    fetch(0).start()
+    for turn, at in enumerate(columns):
+        if turn + 1 < len(columns):
+            fetch(turn + 1).start()
+        fetch(turn).wait()
+        target[:, at : at + WIDE] = matmul(left[...], block_buf[turn % 2]).astype(target.dtype)
+
+
+def select_kernel(
+    part,
+    normed,
+    shard,
+    total,
+    product,
+    gathered,
+    slots,
+    send_sem,
+    recv_sem,
+    block_buf,
+    block_sem,
+    gather_send,
+    gather_recv,
+    local_sem,
+):
     group = Group(("tp",), send_sem, recv_sem)
-    gather = PlaneGather(gated, gated_all, gather_send, gather_recv)
-    half = gated.shape[1] // 2
-    share = out_first.shape[1]
+    gather = PlaneGather(shard, gathered, gather_send, gather_recv)
     greet([(("tp",), group.others), (PLANE, gather.others)])
     gather.begin(local_sem)
-    for at in range(out_first.shape[0] // half):
-        rows = slice(at * half, (at + 1) * half)
-        part[:, at * share : (at + 1) * share] = (
-            matmul(gated[:, :half], out_first[rows, :])
-            + matmul(gated[:, half:], out_last[rows, :])
-        ).astype(part.dtype)
-    copies = group.scatter(part, slots, 0)
-    if n_swaps:
-        swap = Swap(arrays, swapped, *refs)
-        swap.begin()
-    finish(copies)
-    rows = group.own(tokens)[...].astype(jnp.float32) + group.total(part, slots)
-    middle[...] = rows
-    group.own(normed)[...] = (rows * inverse_rms(rows) * gain[...].astype(jnp.float32)).astype(
-        normed.dtype
-    )
-    copies = group.spread(normed, 1)
+    finish(group.scatter(part, slots, 0))
+    group.own(total)[...] = group.total(part, slots).astype(total.dtype)
+    copies = group.spread(total, 1)
     gather.relay()
     gather.hand_over()
     finish(copies)
     gather.hand_over_last()
     gather.end()
+    product_in_blocks(normed, gathered, product, block_buf, block_sem)
+
+
+def run_select(call_id, part, normed, shard):
+    count = group_size(("tp",))
+    vmem = pl.BlockSpec(memory_space=pltpu.VMEM)
+    hbm = pl.BlockSpec(memory_space=pltpu.HBM)
+    sems = pltpu.SemaphoreType.DMA((2, count - 1))
+    rows, width = normed.shape
+    return pl.pallas_call(
+        select_kernel,
+        in_specs=[vmem, vmem, hbm],
+        out_specs=[vmem, vmem, hbm],
+        out_shape=[
+            jax.ShapeDtypeStruct(part.shape, part.dtype),
+            jax.ShapeDtypeStruct((rows, shard.shape[1]), jnp.float32),
+            gathered_shape(shard),
+        ],
+        scratch_shapes=[
+            slots_for(part, count),
+            sems,
+            sems,
+            pltpu.VMEM((2, width, WIDE), jnp.bfloat16),
+            pltpu.SemaphoreType.DMA((2,)),
+        ]
+        + gather_scratch(),
+        compiler_params=pltpu.CompilerParams(
+            collective_id=call_id, has_side_effects=True, vmem_limit_bytes=VMEM_GRANT
+        ),
+    )(part, normed, shard)
+
+
+def sum_kernel(part, own_rows, total, all_rows, slots, send_sem, recv_sem, *line_sems):
+    group = Group(("tp",), send_sem, recv_sem)
+    rows = LineSpread(all_rows, *line_sems)
+    greet([(("tp",), group.others)])
+    copies = group.scatter(part, slots, 0)
+    group.own(all_rows)[...] = own_rows[...]
+    rows.begin()
+    finish(copies)
+    group.own(total)[...] = group.total(part, slots).astype(total.dtype)
+    copies = group.spread(total, 1)
+    rows.pass_on()
+    finish(copies)
+    rows.end()
+
+
+def sum_over_tp(call_id, part, own_rows):
+    count = group_size(("tp",))
+    vmem = pl.BlockSpec(memory_space=pltpu.VMEM)
+    sems = pltpu.SemaphoreType.DMA((2, count - 1))
+    return pl.pallas_call(
+        sum_kernel,
+        in_specs=[vmem] * 2,
+        out_specs=[vmem] * 2,
+        out_shape=[
+            jax.ShapeDtypeStruct(part.shape, part.dtype),
+            jax.ShapeDtypeStruct((own_rows.shape[0] * count, own_rows.shape[1]), own_rows.dtype),
+        ],
+        scratch_shapes=[slots_for(part, count), sems, sems] + line_spread_scratch(),
+        compiler_params=pltpu.CompilerParams(
+            collective_id=call_id, has_side_effects=True, vmem_limit_bytes=VMEM_GRANT
+        ),
+    )(part, own_rows)
+
+
+def mixer_out_kernel(n_swaps, gated, out_all, tokens, gain, *refs):
+    arrays, refs = refs[:n_swaps], refs[n_swaps:]
+    normed, middle, gated_all, *refs = refs
+    swapped, refs = refs[:n_swaps], refs[n_swaps:]
+    part, refs = refs[0], refs[1:]
+    line = LineSum(part, *refs[:5])
+    spread = LineSpread(normed, *refs[5:7])
+    gather_send, gather_recv, local_sem, *refs = refs[7:]
+    group = Group(("tp",), None, None)
+    gather = PlaneGather(gated, gated_all, gather_send, gather_recv)
+    inner = gated.shape[1]
+    share = out_all.shape[1]
+    greet([(("tp",), group.others), (PLANE, gather.others)])
+    gather.begin(local_sem)
+    for at in range(out_all.shape[0] // inner):
+        part[:, at * share : (at + 1) * share] = matmul(
+            gated[...], out_all[at * inner : (at + 1) * inner, :]
+        ).astype(part.dtype)
+    firsts = [line.begin(j) for j in range(line.blocks)]
+    if n_swaps:
+        swap = Swap(arrays, swapped, *refs)
+        swap.begin()
+    line.pass_all(firsts)
+    rows = group.own(tokens)[...].astype(jnp.float32) + line.total()
+    middle[...] = rows
+    group.own(normed)[...] = (rows * inverse_rms(rows) * gain[...].astype(jnp.float32)).astype(
+        normed.dtype
+    )
+    spread.begin()
+    gather.relay()
+    gather.hand_over()
+    spread.pass_on()
+    spread.end()
+    gather.hand_over_last()
+    gather.end()
     if n_swaps:
         swap.end()
 
 
-def mixer_out(call_id, gated, out_first, out_last, tokens, gain, arrays):
+def mixer_out(call_id, gated, out_all, tokens, gain, arrays):
     count = group_size(("tp",))
     vmem = pl.BlockSpec(memory_space=pltpu.VMEM)
     hbm = pl.BlockSpec(memory_space=pltpu.HBM)
     rows, width = tokens.shape
     part = jax.ShapeDtypeStruct((rows, width), jnp.bfloat16)
-    sems = pltpu.SemaphoreType.DMA((2, count - 1))
     return pl.pallas_call(
         functools.partial(mixer_out_kernel, len(arrays)),
-        in_specs=[vmem] * (5 + len(arrays)),
+        in_specs=[vmem] * (4 + len(arrays)),
         out_specs=[vmem] * 2 + [hbm] + [hbm] * len(arrays),
         out_shape=[
             part,
@@ -644,13 +796,15 @@
             gathered_shape(gated),
         ]
         + swap_shapes(arrays),
-        scratch_shapes=[pltpu.VMEM(part.shape, part.dtype), slots_for(part, count), sems, sems]
+        scratch_shapes=[pltpu.VMEM(part.shape, part.dtype)]
+        + line_sum_scratch(part, 2)
+        + line_spread_scratch()
         + gather_scratch()
         + swap_scratch(arrays),
         compiler_params=pltpu.CompilerParams(
             collective_id=call_id, has_side_effects=True, vmem_limit_bytes=VMEM_GRANT
         ),
-    )(gated, out_first, out_last, tokens, gain, *arrays)
+    )(gated, out_all, tokens, gain, *arrays)
 
 
 def ffn_kernel(swaps, normed, ct, weights, made, *refs):
@@ -728,8 +882,7 @@
     ct,
     middle,
     gain,
-    out_first,
-    out_last,
+    out_all,
     weights,
     middle_low,
     middle_grad,
@@ -737,19 +890,17 @@
     gated_grad,
     ffn_part,
     part,
-    slots,
     wide_buf,
     down_buf,
     wide_sem,
     down_sem,
-    part_send,
-    part_recv,
-    send_sem,
-    recv_sem,
+    *sems,
 ):
     hidden = made.shape[1] // 3
     blocks = part.shape[1] // WIDE
-    group = Group(("tp",), send_sem, recv_sem)
+    group = Group(("tp",), None, None)
+    line = LineSum(part, *sems[:5])
+    spread = LineSpread(middle_low, *sems[5:])
     greet([(("tp",), group.others)])
 
     def fetch(j):
@@ -767,7 +918,7 @@
         )
 
     fetch(0).start()
-    copies = []
+    firsts = []
     for j in range(blocks):
         if j + 1 < blocks:
             fetch(j + 1).start()
@@ -776,16 +927,7 @@
         fetch(j).wait()
         columns = slice(j * WIDE, (j + 1) * WIDE)
         part[:, columns] = matmul_nt(made[:, hidden:], wide_buf[j % 2]).astype(part.dtype)
-        for hop, other in enumerate(group.others):
-            copies.append(
-                sent(
-                    rows_of(part, other, group.count).at[:, columns],
-                    slots.at[hop, :, columns],
-                    part_send.at[j, hop],
-                    part_recv.at[j, hop],
-                    device_at(("tp",), other),
-                )
-            )
+        firsts.append(line.begin(j))
     for j in range(blocks):
         if j + 1 < blocks:
             fetch_down(j + 1).start()
@@ -793,8 +935,8 @@
         ffn_part[:, j * WIDE : (j + 1) * WIDE] = matmul_nt(
             made[:, :hidden], down_buf[j % 2]
         ).astype(ffn_part.dtype)
-    finish(copies)
-    normed_grad = group.total(part, slots)
+        line.pass_on(j, firsts[j])
+    normed_grad = line.total()
     rows = middle[...]
     scale = inverse_rms(rows)
     gain_grad[...] = jnp.sum(normed_grad * rows * scale, 0, keepdims=True)
@@ -803,32 +945,30 @@
     )
     middle_grad[...] = grad
     group.own(middle_low)[...] = grad.astype(middle_low.dtype)
-    finish(group.spread(middle_low, 0))
-    half = gated_grad.shape[1] // 2
-    share = out_first.shape[1]
-    for side, shards in enumerate((out_first, out_last)):
-        total = None
-        for at in range(shards.shape[0] // half):
-            one = matmul_nt(
-                middle_low[:, at * share : (at + 1) * share],
-                shards[at * half : (at + 1) * half, :],
-            )
-            total = one if total is None else total + one
-        gated_grad[:, side * half : (side + 1) * half] = total
-
-
-def ffn_back(call_id, made, ct, middle, gain, out_first, out_last, weights):
+    spread.run()
+    inner = gated_grad.shape[1]
+    share = out_all.shape[1]
+    total = None
+    for at in range(out_all.shape[0] // inner):
+        one = matmul_nt(
+            middle_low[:, at * share : (at + 1) * share], out_all[at * inner : (at + 1) * inner, :]
+        )
+        total = one if total is None else total + one
+    gated_grad[...] = total
+
+
+def ffn_back(call_id, made, ct, middle, gain, out_all, weights):
     count = group_size(("tp",))
     vmem = pl.BlockSpec(memory_space=pltpu.VMEM)
     rows, width = ct.shape
     hidden = made.shape[1] // 3
-    inner = 2 * out_first.shape[0] // group_size(PLANE)
+    inner = out_all.shape[0] // group_size(PLANE)
     low, full = jnp.bfloat16, jnp.float32
     part = jax.ShapeDtypeStruct((rows, width), low)
     dma = pltpu.SemaphoreType.DMA
     return pl.pallas_call(
         ffn_back_kernel,
-        in_specs=[vmem] * 6 + [pl.BlockSpec(memory_space=pltpu.HBM)],
+        in_specs=[vmem] * 5 + [pl.BlockSpec(memory_space=pltpu.HBM)],
         out_specs=[vmem] * 5,
         out_shape=[
             part,
@@ -839,20 +979,17 @@
         ],
         scratch_shapes=[
             pltpu.VMEM(part.shape, low),
-            slots_for(part, count),
             pltpu.VMEM((2, WIDE, 2 * hidden), low),
             pltpu.VMEM((2, WIDE, hidden), low),
             dma((2,)),
             dma((2,)),
-            dma((width // WIDE, count - 1)),
-            dma((width // WIDE, count - 1)),
-            dma((1, count - 1)),
-            dma((1, count - 1)),
-        ],
+        ]
+        + line_sum_scratch(part, width // WIDE)
+        + line_spread_scratch(),
         compiler_params=pltpu.CompilerParams(
             collective_id=call_id, has_side_effects=True, vmem_limit_bytes=VMEM_GRANT
         ),
-    )(made, ct, middle, gain, out_first, out_last, weights)
+    )(made, ct, middle, gain, out_all, weights)
 
 
 def send_on(source, target, send_sem, recv_sem, ctx):
@@ -1419,7 +1556,6 @@
     normed_part,
     small,
     small_sum,
-    normed_slots,
     small_slots,
     gain_slots,
     gain_own,
@@ -1434,8 +1570,6 @@
     block_sem,
     wide_sem,
     tall_sem,
-    part_send,
-    part_recv,
     tp_send,
     tp_recv,
     plane_send,
@@ -1443,7 +1577,7 @@
     gather_send,
     gather_recv,
     local_sem,
-    *swap_sems,
+    *sems,
 ):
     inner = conv_grad.shape[1]
     hidden = ffn_all.shape[1] // 3
@@ -1451,6 +1585,10 @@
     rank = step_low.shape[1]
     tp = Group(("tp",), tp_send, tp_recv)
     plane = Group(PLANE, plane_send, plane_recv)
+    line = LineSum(normed_part, *sems[:5])
+    tokens_spread = LineSpread(tokens_grad, *sems[5:7])
+    layer_spread = LineSpread(layer_out, *sems[7:9])
+    swap_sems = sems[9:]
     gather = PlaneGather(mix_own, mix_all, gather_send, gather_recv)
     sources = (one_cols, two_cols, ct_cols) if swaps else (one_cols, two_cols, ct_cols, middle_cols)
     loads = [
@@ -1489,7 +1627,7 @@
     hidden_in = tokens[...].astype(jnp.float32)
     unit_rows = hidden_in * inverse_rms(hidden_in)
     blocks = width // WIDE
-    normed_sent = []
+    firsts = []
     for j in range(blocks):
         if j + 1 < blocks:
             for copy in fetch(j + 1):
@@ -1500,22 +1638,13 @@
             gate_grad[...], in_buf[j % 2, 1]
         )
         normed_part[:, columns] = block.astype(normed_part.dtype)
-        for hop, other in enumerate(tp.others):
-            normed_sent.append(
-                sent(
-                    rows_of(normed_part, other, tp.count).at[:, columns],
-                    normed_slots.at[hop, :, columns],
-                    part_send.at[j, hop],
-                    part_recv.at[j, hop],
-                    device_at(("tp",), other),
-                )
-            )
+        firsts.append(line.begin(j))
         gain_grad = jnp.sum(block * unit_rows[:, columns], 0, keepdims=True)
         row, at = divmod(j * WIDE, inner)
         row += SMALL_ROWS - GAIN_ROWS + 8
         vectors_own[row : row + 1, at : at + WIDE] = gain_grad
     tp.own(layer_out)[...] = layer_rows[...]
-    layer_sent = tp.spread(layer_out, 2)
+    layer_spread.begin()
     small[:SMALL_ROWS, :] = vectors_own[...].astype(small.dtype)
     small[SMALL_ROWS : SMALL_ROWS + rank, :] = matmul_tn(step_low[...], pre_low[...]).astype(
         small.dtype
@@ -1525,6 +1654,7 @@
         select_low[...], scan_in[...]
     )[:selected].astype(small.dtype)
     small_sent = plane.scatter(small, small_slots, 0)
+    line.pass_all(firsts)
 
     def flat(at):
         return lambda block: matmul_tn(cols[at], block)
@@ -1554,28 +1684,29 @@
     gather.relay()
     products(ffn_all, down_end, gu_end, flat(1), side_by_side(grad_gateup, down_end), *wide)
     gather.hand_over()
-    finish(normed_sent)
+    layer_spread.pass_on()
     hidden_in = tp.own(tokens)[...].astype(jnp.float32)
     tp.own(tokens_grad)[...] = (
         middle_grad[...]
         + norm_back(
-            tp.total(normed_part, normed_slots),
+            line.total(),
             hidden_in,
             inverse_rms(hidden_in),
             gain_row[...].astype(jnp.float32),
         )
     ).astype(tokens_grad.dtype)
-    tokens_sent = tp.spread(tokens_grad, 0)
+    tokens_spread.begin()
     finish(small_sent)
     plane.own(small_sum)[...] = plane.total(small, small_slots).astype(small_sum.dtype)
     small_sent = plane.spread(small_sum, 1)
     gather.hand_over_last()
     if swaps:
         swap.end()
+    tokens_spread.pass_on()
     products(gated_all, 0, inner // WIDE, tall(3), one_above_other(grad_outproj), *high)
     finish(small_sent)
     gain_own[...] = small_sum[SMALL_ROWS - GAIN_ROWS : SMALL_ROWS, :].astype(jnp.float32)
-    gain_sent = [tp.one(gain_own, gain_slots.at[hop], 1, hop) for hop in range(tp.count - 1)]
+    gain_sent = [tp.one(gain_own, gain_slots.at[hop], 0, hop) for hop in range(tp.count - 1)]
     vectors_sum[...] = small_sum[:SMALL_ROWS, :].astype(jnp.float32)
     step_sum[...] = small_sum[SMALL_ROWS : SMALL_ROWS + rank, :].astype(jnp.float32)
     select_sum[...] = small_sum[SMALL_ROWS + rank : SMALL_ROWS + rank + selected, :].astype(
@@ -1588,8 +1719,8 @@
     for hop in range(tp.count - 1):
         total = total + gain_slots[hop]
     gains[...] = total
-    finish(tokens_sent)
-    finish(layer_sent)
+    tokens_spread.end()
+    layer_spread.end()
 
 
 def run_tail(
@@ -1653,7 +1784,6 @@
             pltpu.VMEM(part.shape, low),
             pltpu.VMEM(small.shape, low),
             pltpu.VMEM(small.shape, low),
-            slots_for(part, tp_count),
             slots_for(small, plane_count),
             pltpu.VMEM((tp_count - 1, GAIN_ROWS, inner), full),
             pltpu.VMEM((GAIN_ROWS, inner), full),
@@ -1668,14 +1798,14 @@
             dma((2,)),
             dma((2,)),
             dma((2,)),
-            dma((width // WIDE, tp_count - 1)),
-            dma((width // WIDE, tp_count - 1)),
-            dma((3, tp_count - 1)),
-            dma((3, tp_count - 1)),
+            dma((1, tp_count - 1)),
+            dma((1, tp_count - 1)),
             dma((2, plane_count - 1)),
             dma((2, plane_count - 1)),
         ]
         + gather_scratch()
+        + line_sum_scratch(part, width // WIDE)
+        + line_spread_scratch() * 2
         + (swap_scratch([tokens]) if swaps else []),
         compiler_params=pltpu.CompilerParams(
             collective_id=call_id, has_side_effects=True, vmem_limit_bytes=VMEM_GRANT
@@ -1742,69 +1872,41 @@
     gain,
     ct,
     in_conv,
-    in_gate,
     conv_in,
-    gate_mix,
     conv_all,
-    gate_all,
     *refs,
 ):
     if swaps:
         swapped, *refs = refs
     normed, block_buf, block_sem, *sems = refs
     conv = PlaneGather(in_conv, conv_all, *sems[:2])
-    gate = PlaneGather(in_gate, gate_all, *sems[3:5])
     if swaps:
-        swap = SplitSwap(ct, swapped, *sems[6:])
+        swap = SplitSwap(ct, swapped, *sems[3:])
         greet([(PLANE, conv.others), (("tp",), swap.tp.others)])
     else:
         greet([(PLANE, conv.others)])
     conv.begin(sems[2])
     if swaps:
         swap.begin()
-    gate.begin(sems[5])
     hidden_in = tokens[...].astype(jnp.float32)
     normed[...] = (hidden_in * inverse_rms(hidden_in) * gain[...].astype(jnp.float32)).astype(
         normed.dtype
     )
 
-    def product(source, target):
-        columns = range(0, source.shape[1], WIDE)
-
-        def fetch(turn):
-            at = columns[turn]
-            return pltpu.make_async_copy(
-                source.at[:, at : at + WIDE], block_buf.at[turn % 2], block_sem.at[turn % 2]
-            )
-
-        fetch(0).start()
-        for turn, at in enumerate(columns):
-            if turn + 1 < len(columns):
-                fetch(turn + 1).start()
-            fetch(turn).wait()
-            target[:, at : at + WIDE] = matmul(normed[...], block_buf[turn % 2]).astype(
-                target.dtype
-            )
-
     conv.relay()
     conv.hand_over()
+    conv.hand_over_last()
     if swaps:
         swap.pass_on()
-    gate.relay()
-    conv.hand_over_last()
-    gate.hand_over()
     conv.end()
-    product(conv_all, conv_in)
-    gate.hand_over_last()
-    gate.end()
-    product(gate_all, gate_mix)
+    product_in_blocks(normed, conv_all, conv_in, block_buf, block_sem)
     if swaps:
         swap.end()
 
 
-def run_head(call_id, tokens, gain, ct, inproj, swaps):
+def run_head(call_id, tokens, gain, ct, shard, swaps):
     rows, width = tokens.shape
-    inner = inproj.shape[2]
+    inner = shard.shape[1]
     low = jnp.bfloat16
     vmem = pl.BlockSpec(memory_space=pltpu.VMEM)
     hbm = pl.BlockSpec(memory_space=pltpu.HBM)
@@ -1820,12 +1922,10 @@
     swapped = [jax.ShapeDtypeStruct((count, rows, width // count), low)]
     return pl.pallas_call(
         functools.partial(head_kernel, swaps),
-        in_specs=[vmem] * 3 + [hbm] * 2,
-        out_specs=[vmem] * 2 + [hbm] * (3 if swaps else 2),
+        in_specs=[vmem] * 3 + [hbm],
+        out_specs=[vmem] + [hbm] * (2 if swaps else 1),
         out_shape=[
             jax.ShapeDtypeStruct((rows, inner), low),
-            jax.ShapeDtypeStruct((rows, inner), jnp.float32),
-            jax.ShapeDtypeStruct((width, inner), low),
             jax.ShapeDtypeStruct((width, inner), low),
         ]
         + (swapped if swaps else []),
@@ -1834,12 +1934,12 @@
             pltpu.VMEM((2, width, WIDE), low),
             pltpu.SemaphoreType.DMA((2,)),
         ]
-        + gather_scratch() * 2
+        + gather_scratch()
         + (swap_sems if swaps else []),
         compiler_params=pltpu.CompilerParams(
             collective_id=call_id, has_side_effects=True, vmem_limit_bytes=VMEM_GRANT
         ),
-    )(tokens, gain, ct, inproj[0], inproj[1])
+    )(tokens, gain, ct, shard)
 
 
 def per_device(
@@ -1882,8 +1982,8 @@
         jnp.concatenate([gateup[0], gateup[1], jnp.transpose(downproj)], 1)
     )
     swap_now = swaps_in_kernels(width)
-    conv_in, gate_mix, in_conv, in_gate, *swapped = run_head(
-        5, tokens_rows, gain_mix_row, ct_low, inproj, swap_now
+    conv_in, in_conv, *swapped = run_head(
+        5, tokens_rows, gain_mix_row, ct_low, inproj[0], swap_now
     )
     ct_cols = swapped[0].reshape(-1, swapped[0].shape[2]) if swapped else swapped_columns(ct_low)
     hidden_in = tokens_rows.astype(jnp.float32)
@@ -1902,8 +2002,8 @@
     columns = selproj.shape[1]
     select_width = -(-columns // LANE) * LANE
     select_weights = jnp.pad(selproj, ((0, 0), (0, select_width - columns)))
-    select_cols, out_first = sum_over_tp(
-        0, matmul(scan_in, select_weights), [], [], [outproj[: inner // 2]]
+    select_cols, gate_mix, in_gate = run_select(
+        0, matmul(scan_in, select_weights), normed_one, inproj[1]
     )
     step_low = select_cols[:, :rank].astype(low)
     b_rows = select_cols[:, rank : rank + n_state].reshape(-1)
@@ -1912,8 +2012,8 @@
     step_size = jax.nn.softplus(step_pre)
     in_pairs = lax.axis_size("ctx") == 2
     if in_pairs:
-        prior, scan_out, out_last = scan_forward_pair(
-            6, step_size, scan_float, b_rows, c_rows, rate, seqs, outproj[inner // 2 :]
+        prior, scan_out, out_all = scan_forward_pair(
+            6, step_size, scan_float, b_rows, c_rows, rate, seqs, outproj
         )
     else:
         span_decay = jnp.exp(
@@ -1922,15 +2022,14 @@
         ends = scan_ends(step_size, scan_float, b_rows, rate, seqs, False)
         start = from_earlier(ends, span_decay, 1)
         prior, scan_out = scan_forward(start, step_size, scan_float, b_rows, c_rows, rate, seqs)
-        out_last = gathered_rows(outproj[inner // 2 :])
+        out_all = gathered_rows(outproj)
     mixer_core = scan_out + skip_weight[None] * scan_float
     gate_sig = jax.nn.silu(gate_mix)
     gated = (mixer_core * gate_sig).astype(low)
     normed_two, middle, gated_all, *swapped = mixer_out(
         1,
         gated,
-        out_first,
-        out_last,
+        out_all,
         tokens_rows,
         gain_ffn_row,
         [normed_one] if swap_now else [],
@@ -1940,7 +2039,7 @@
     (normed_two_cols,) = swapped or [swapped_columns(normed_two)]
     ffn_all = gathered_rows(made)
     middle_low, middle_grad, ffngain_part, gated_grad, ffn_part = ffn_back(
-        2, made, ct_low, middle, gain_ffn_row, out_first, out_last, ffn_pack
+        2, made, ct_low, middle, gain_ffn_row, out_all, ffn_pack
     )
     core_grad = gated_grad * gate_sig
     gate_mix_grad = (gated_grad * mixer_core * silu_slope(gate_mix)).astype(low)
@@ -1980,7 +2079,7 @@
         ],
         1,
     ).astype(low)
-    select_low, layer_first = sum_over_tp(3, select_part, layer_rows[:1], [], [])
+    select_low, layer_first = sum_over_tp(3, select_part, layer_rows[0])
     scan_in_grad = (
         core_grad * skip_weight[None]
         + input_grad

time: 493 us -> 496 us (level)
    pallas_call x1, Pallas kernels: 85.1 us -> 62.7 us  [run_head(): pl.pallas_call(functools.partial(head_kernel, swaps), in_specs=[vmem] * 3...]
    pallas_call x1, Pallas kernels: 34.3 us -> 46.2 us  [scan_forward_pair(): pl.pallas_call(functools.partial(forward_pair_kernel, n_state, tiles, gro...]
    pallas_call x3, Pallas kernels: 107 us -> 118 us  [the longest x1 52.2 us: ffn_back(): pl.pallas_call(ffn_back_kernel, in_specs=[vmem] * 5 + [pl.BlockSpec(memor...]
    pallas_call x1, Pallas kernels: 36.6 us -> 30.3 us  [scan_backward_pair(): pl.pallas_call(functools.partial(backward_pair_kernel, len(arrays), n_sta...]
    unnamed x74 -> x72, local copies, waits for them, and re-layouts: 13.7 us -> 13.7 us
  transfers between devices with their start and end apart: 4 -> 4, of which waited for: 1 -> 2; matrix products, arithmetic and copies ran while one was open for 8% -> 7% of each run, Pallas kernels for 64% -> 63%
where the time goes in v10:
time: 496 us; the launch traced here: 495 us
  Pallas kernels  410 us (83%)
  local copies, waits for them, and re-layouts  27.3 us (6%)
  other arithmetic  25.2 us (5%)
  between operations  14.6 us (3%)
  matrix products  6.82 us (1%)
  starting transfers between devices  5.77 us (1%)
    pallas_call x1, Pallas kernels, run_tail(): pl.pallas_call(functools.partial(tail_kernel, swaps), in_specs=[vmem] * 1...  79.8 us
    pallas_call x1, Pallas kernels, run_head(): pl.pallas_call(functools.partial(head_kernel, swaps), in_specs=[vmem] * 3...  62.7 us
    pallas_call x1, Pallas kernels, mixer_out(): pl.pallas_call(functools.partial(mixer_out_kernel, len(arrays)), in_specs...  55.2 us
    pallas_call x1, Pallas kernels, ffn_back(): pl.pallas_call(ffn_back_kernel, in_specs=[vmem] * 5 + [pl.BlockSpec(memor...  52.2 us
    pallas_call x1, Pallas kernels, run_select(): pl.pallas_call(select_kernel, in_specs=[vmem, vmem, hbm], out_specs=[vmem...  48.4 us
    pallas_call x1, Pallas kernels, scan_forward_pair(): pl.pallas_call(functools.partial(forward_pair_kernel, n_state, tiles, gro...  46.2 us
    pallas_call x1, Pallas kernels, scan_backward_pair(): pl.pallas_call(functools.partial(backward_pair_kernel, len(arrays), n_sta...  30.3 us
    pallas_call x1, Pallas kernels, run_ffn(): pl.pallas_call(functools.partial(ffn_kernel, swaps), in_specs=[vmem, vmem...  17.8 us
  transfers between devices with their start and end apart: 4, of which 2 were waited for; matrix products, arithmetic and copies ran while one was open for 7% of the time, Pallas kernels for 63%

profile of v10, /device:TPU:0, one launch (start us, length us, event | category | flops | bytes accessed | tf_op | source)
XLA Modules:
  0.0 494.8 jit_solution(14897563658382999722)
XLA Ops:
  7.3 1.6 copy.32
  9.3 1.8 pad_maximum_fusion
  13.4 62.7 %shard_map.262 = (bf16[256,1024]{1,0:T(8,128)(2,1)}, bf16[2048,1024]{1,0:T(8,128)(2,1)}, bf16[8,256,256]{2,1,0:T(8,128)(2,1)}) custom-call(bf16[256,2048]{1,0:T(8,128)(2,1)} %bitcast.88, bf16[1,2048]{1,0:T(2,128)(2,1)} %reshape.110.gain.gain_row, bf16[256,2048]{1,0:T(8,128)(2,1)} %bitcast.91, bf16[256,1024]{1,0:T(8,128)(2,1)} %get-tuple-element.109.in_conv), custom_call_target="tpu_custom_call" | custom-call | tf_op jit(solution)/shard_map/pallas_call | solution.py:1923
  77.1 4.3 collective-permute-start
  81.7 1.3 multiply_convert_fusion.normed.refs_0_
  85.0 1.8 fusion.20
  87.8 48.4 %shard_map.263 = (f32[256,256]{1,0:T(8,128)}, f32[256,1024]{1,0:T(8,128)}, bf16[2048,1024]{1,0:T(8,128)(2,1)}) custom-call(f32[256,256]{1,0:T(8,128)} %fusion.10.part, bf16[256,2048]{1,0:T(8,128)(2,1)} %multiply_convert_fusion.normed.refs_0_, bf16[256,1024]{1,0:T(8,128)(2,1)} %get-tuple-element.108.shard), custom_call_target="tpu_custom_call" | custom-call | tf_op jit(solution)/shard_map/pallas_call | solution.py:687
  136.2 1.1 fusion.22
  138.7 3.0 compare_select_fusion
  141.8 46.2 %shard_map.264 = (f32[256,16,8,128]{3,2,1,0:T(8,128)}, f32[256,1024]{1,0:T(8,128)}, bf16[8192,256]{1,0:T(8,128)(2,1)}) custom-call(f32[256,1024]{1,0:T(8,128)} %get-tuple-element.122.step_ref, f32[256,1024]{1,0:T(8,128)} %get-tuple-element.97.input_ref, f32[4096]{0:T(1024)} %reshape.114.brow_ref, f32[4096]{0:T(1024)} %reshape.115.crow_ref, ...), custom_call_target="tpu_custom_call" | custom-call | tf_op jit(solution)/shard_map/pallas_call | solution.py:1131
  188.0 2.4 multiply_convert_fusion.2.gated
  190.3 55.2 %shard_map.265 = (bf16[256,2048]{1,0:T(8,128)(2,1)}, f32[64,2048]{1,0:T(8,128)}, bf16[2048,1024]{1,0:T(8,128)(2,1)}, bf16[2048,256]{1,0:T(8,128)(2,1)}) custom-call(bf16[256,1024]{1,0:T(8,128)(2,1)} %multiply_convert_fusion.2.gated, bf16[8192,256]{1,0:T(8,128)(2,1)} %get-tuple-element.57.out_all, bf16[256,2048]{1,0:T(8,128)(2,1)} %bitcast.89, ...), custom_call_target="tpu_custom_call" | custom-call | tf_op jit(solution)/shard_map/pallas_call | solution.py:789
  245.5 17.8 %shard_map.266 = (bf16[256,6144]{1,0:T(8,128)(2,1)}, bf16[2048,256]{1,0:T(8,128)(2,1)}) custom-call(bf16[256,2048]{1,0:T(8,128)(2,1)} %get-tuple-element.58.normed, bf16[256,2048]{1,0:T(8,128)(2,1)} %bitcast.92, bf16[2048,6144]{1,0:T(8,128)(2,1)} %all-gather.3.cloned.1.call-done.weights), custom_call_target="tpu_custom_call" | custom-call | tf_op jit(solution)/shard_map/pallas_call | solution.py:865
  264.7 1.5 slice.139.step_low
  266.2 52.2 %shard_map.267 = (bf16[256,2048]{1,0:T(8,128)(2,1)}, f32[64,2048]{1,0:T(8,128)}, f32[1,2048]{1,0:T(1,128)}, f32[256,1024]{1,0:T(8,128)}, bf16[256,2048]{1,0:T(8,128)(2,1)}) custom-call(bf16[256,6144]{1,0:T(8,128)(2,1)} %get-tuple-element.59.made, bf16[256,2048]{1,0:T(8,128)(2,1)} %bitcast.93, f32[64,2048]{1,0:T(8,128)} %get-tuple-element.60.middle, ...), custom_call_target="tpu_custom_call" | custom-call | tf_op jit(solution)/shard_map/pallas_call | solution.py:969
  318.4 4.5 multiply_reduce_fusion.1
  322.9 30.3 %shard_map.268 = (f32[256,1024]{1,0:T(8,128)}, f32[256,1024]{1,0:T(8,128)}, f32[16,8,128]{2,1,0:T(8,128)}, f32[256,32,128]{2,1,0:T(8,128)}, bf16[64,1024]{1,0:T(8,128)(2,1)}, /*index=5*/bf16[64,1024]{1,0:T(8,128)(2,1)}) custom-call(f32[256,1024]{1,0:T(8,128)} %get-tuple-element.122.step_ref, f32[256,1024]{1,0:T(8,128)} %get-tuple-element.97.input_ref, ...), custom_call_target="tpu_custom_call" | custom-call | tf_op jit(solution)/shard_map/pallas_call | solution.py:1338
  353.3 3.5 reduce_sum.82
  356.8 2.2 fusion.17
  360.0 17.6 %shard_map.269 = (bf16[256,256]{1,0:T(8,128)(2,1)}, bf16[256,1024]{1,0:T(8,128)(2,1)}) custom-call(bf16[256,256]{1,0:T(8,128)(2,1)} %maximum_maximum_fusion.part, bf16[64,1024]{1,0:T(8,128)(2,1)} %get-tuple-element.66.own_rows), custom_call_target="tpu_custom_call" | custom-call | tf_op jit(solution)/shard_map/pallas_call | solution.py:729
  377.6 2.5 multiply_reduce_fusion.5
  380.7 1.4 collective-permute-start.1
  384.6 2.7 collective-permute-done.1
  388.2 2.1 all-gather.5.cloned.1.call-done.ffn_all
  390.4 79.8 %shard_map.270 = (bf16[256,2048]{1,0:T(8,128)(2,1)}, bf16[256,1024]{1,0:T(8,128)(2,1)}, f32[32,1024]{1,0:T(8,128)}, f32[128,1024]{1,0:T(8,128)}, f32[160,1024]{1...) custom-call(bf16[256,1024]{1,0:T(8,128)(2,1)} %bitcast.96, ...), custom_call_target="tpu_custom_call" | custom-call | tf_op jit(solution)/shard_map/pallas_call | solution.py:1765
  470.2 1.5 fusion.23
  471.7 1.4 slice.103
  473.0 1.5 slice_bitcast_fusion.4
  475.4 2.3 pad_maximum_fusion.1
  479.3 1.3 copy.51
  483.5 2.1 copy.55
  486.6 1.3 copy.56
  (107 shorter events, 20.9 us)
Async XLA Ops:
  7.2 131.6 %copy-start = (bf16[128,1024]{1,0:T(8,128)(2,1)S(1)}, bf16[128,1024]{1,0:T(8,128)(2,1)}, u32[]{:S(2)}) copy-start(bf16[128,1024]{1,0:T(8,128)(2,1)} %param.21) | copy-start | bytes 786436
  7.2 1.9 copy-start.7
  7.2 238.3 %all-gather.3.cloned.1.call-start = ((), (), s32[]{:S(2)}) async-start(), calls=%async_computation | async-start | bytes 28311552 | tf_op jit(solution)/shard_map/all_gather | solution.py:366
  11.1 379.3 %all-gather.5.cloned.1.call-start = ((), (), s32[]{:S(2)}) async-start(), calls=%async_computation.1 | async-start | bytes 28311552 | tf_op jit(solution)/shard_map/all_gather | solution.py:366
  12.4 69.0 %copy-start.1 = (bf16[2,128,2048]{2,1,0:T(8,128)(2,1)S(1)}, bf16[2,128,2048]{2,1,0:T(8,128)(2,1)}, u32[]{:S(2)}) copy-start(bf16[2,128,2048]{2,1,0:T(8,128)(2,1)} %param.15) | copy-start | bytes 3145732
  13.4 68.3 %copy-start.19 = (bf16[1024,16]{0,1:T(8,128)(2,1)S(1)}, bf16[1024,16]{0,1:T(8,128)(2,1)}, u32[]{:S(2)}) copy-start(bf16[1024,16]{0,1:T(8,128)(2,1)} %param.23) | copy-start | bytes 98308
  76.2 6.8 %copy-start.24 = (bf16[4,1024]{1,0:T(4,128)(2,1)S(1)}, bf16[4,1024]{1,0:T(4,128)(2,1)}, u32[]{:S(2)}) copy-start(bf16[4,1024]{1,0:T(4,128)(2,1)} %param.18) | copy-start | bytes 24580
  76.2 6.8 %copy-start.27 = (bf16[1024]{0:T(1024)(128)(2,1)S(1)}, bf16[1024]{0:T(1024)(128)(2,1)}, u32[]{:S(2)}) copy-start(bf16[1024]{0:T(1024)(128)(2,1)} %param.24) | copy-start | bytes 6148
  76.2 6.8 %copy-start.28 = (bf16[1024]{0:T(1024)(128)(2,1)S(1)}, bf16[1024]{0:T(1024)(128)(2,1)}, u32[]{:S(2)}) copy-start(bf16[1024]{0:T(1024)(128)(2,1)} %param.19) | copy-start | bytes 6148
  76.2 6.9 %copy-start.29 = (bf16[1024]{0:T(1024)(128)(2,1)S(1)}, bf16[1024]{0:T(1024)(128)(2,1)}, u32[]{:S(2)}) copy-start(bf16[1024]{0:T(1024)(128)(2,1)} %param.22) | copy-start | bytes 6148
  76.2 6.9 %copy-start.26 = (bf16[2048]{0:T(1024)(128)(2,1)S(1)}, bf16[2048]{0:T(1024)(128)(2,1)}, u32[]{:S(2)}) copy-start(bf16[2048]{0:T(1024)(128)(2,1)} %param.26) | copy-start | bytes 12292
  76.2 8.1 %copy-start.15 = (bf16[256,1024]{1,0:T(8,128)(2,1)S(1)}, bf16[256,1024]{1,0:T(8,128)(2,1)}, u32[]{:S(2)}) copy-start(bf16[256,1024]{1,0:T(8,128)(2,1)} %get-tuple-element.53) | copy-start | bytes 1572868
  77.1 7.3 %collective-permute-start = (bf16[2,3,1024]{2,1,0:T(4,128)(2,1)S(1)}, bf16[2,3,1024]{2,1,0:T(4,128)(2,1)S(1)}, u32[]{:S(2)}, u32[]{:S(2)}) collective-permute-start(bf16[2,3,1024]{2,1,0:T(4,128)(2,1)S(1)} %slice.110), channel_id=1, source_target_pairs={{0,4},{1,5},{2,6},{3,7},{8,12},{9,13},{10,14},{11,15},{16,20},{17,... | collective-permute-start | bytes 36872 | tf_op jit(solution)/shard_map/ppermute | solution.py:23
  85.0 1.8 copy-start.18
  86.8 231.7 %copy-start.2 = (bf16[256,1024]{1,0:T(8,128)(2,1)}, bf16[256,1024]{1,0:T(8,128)(2,1)S(1)}, u32[]{:S(2)}) copy-start(bf16[256,1024]{1,0:T(8,128)(2,1)S(1)} %get-tuple-element.98.scan_in) | copy-start | bytes 1572868
  138.7 49.2 %copy-start.5 = (f32[256,1024]{1,0:T(8,128)S(1)}, f32[256,1024]{1,0:T(8,128)}, u32[]{:S(2)}) copy-start(f32[256,1024]{1,0:T(8,128)} %get-tuple-element.56) | copy-start | bytes 3145732
  353.3 3.5 copy-start.10
  356.8 2.5 copy-start.30
  356.8 20.8 %copy-start.4 = (f32[256,1024]{1,0:T(8,128)S(1)}, f32[256,1024]{1,0:T(8,128)}, u32[]{:S(2)}) copy-start(f32[256,1024]{1,0:T(8,128)} %get-tuple-element.96.ograd_ref) | copy-start | bytes 3145732
  359.0 21.1 %copy-start.3 = (bf16[256,1024]{1,0:T(8,128)(2,1)}, bf16[256,1024]{1,0:T(8,128)(2,1)S(1)}, u32[]{:S(2)}) copy-start(bf16[256,1024]{1,0:T(8,128)(2,1)S(1)} %get-tuple-element.101.pre_low) | copy-start | bytes 1572868
  377.6 2.5 copy-start.23
  380.7 2.0 copy-start.20
  380.7 2.0 copy-start.21
  380.7 6.6 %collective-permute-start.1 = (f32[2,3,1024]{2,1,0:T(4,128)S(1)}, f32[2,3,1024]{2,1,0:T(4,128)S(1)}, u32[]{:S(2)}, u32[]{:S(2)}) collective-permute-start(f32[2,3,1024]{2,1,0:T(4,128)S(1)} %pad_add_fusion.1), channel_id=1, source_target_pairs={{4,0},{5,1},{6,2},{7,3},{12,8},{13,9},{14,10},{15,11},{20,16},{21,... | collective-permute-start | bytes 73736 | tf_op jit(solution)/shard_map/ppermute | solution.py:23
  390.4 85.0 %copy-start.17 = (bf16[256,1024]{1,0:T(8,128)(2,1)S(1)}, bf16[256,1024]{1,0:T(8,128)(2,1)}, u32[]{:S(2)}) copy-start(bf16[256,1024]{1,0:T(8,128)(2,1)} %get-tuple-element.67) | copy-start | bytes 1572868
  470.2 8.1 %copy-start.13 = (bf16[256,2048]{1,0:T(8,128)(2,1)S(1)}, bf16[256,2048]{1,0:T(8,128)(2,1)}, u32[]{:S(2)}) copy-start(bf16[256,2048]{1,0:T(8,128)(2,1)} %get-tuple-element.82) | copy-start | bytes 3145732
  475.4 3.8 copy-start.9
  479.2 1.5 copy-start.14
  479.3 2.4 copy-start.16
  479.3 3.1 copy-start.12
  480.8 2.7 copy-start.6
  483.5 3.1 copy-start.8
  (3 other events, 3.5 us)
Sparse Core Ops, SparseCore 0:
  11.2 175.6 all-gather.2
  263.5 126.8 all-gather.4

commit v11 on v10

--- a/solution.py
+++ b/solution.py
@@ -1524,6 +1524,7 @@
     decaylog,
     skipgain,
     ffngain,
+    layer_first,
     layer_rows,
     middle_low,
     step_low,
@@ -1587,7 +1588,8 @@
     plane = Group(PLANE, plane_send, plane_recv)
     line = LineSum(normed_part, *sems[:5])
     tokens_spread = LineSpread(tokens_grad, *sems[5:7])
-    layer_spread = LineSpread(layer_out, *sems[7:9])
+    layer_last = layer_out.at[:, width // 2 :]
+    layer_spread = LineSpread(layer_last, *sems[7:9])
     swap_sems = sems[9:]
     gather = PlaneGather(mix_own, mix_all, gather_send, gather_recv)
     sources = (one_cols, two_cols, ct_cols) if swaps else (one_cols, two_cols, ct_cols, middle_cols)
@@ -1612,8 +1614,6 @@
     mix_own[:, inner:] = gate_grad[...]
     greet([(("tp",), tp.others), (PLANE, plane.others)])
     gather.begin(local_sem)
-    if swaps:
-        swap.begin()
 
     small[...] = jnp.zeros_like(small)
     vectors_own[...] = jnp.zeros_like(vectors_own)
@@ -1643,7 +1643,8 @@
         row, at = divmod(j * WIDE, inner)
         row += SMALL_ROWS - GAIN_ROWS + 8
         vectors_own[row : row + 1, at : at + WIDE] = gain_grad
-    tp.own(layer_out)[...] = layer_rows[...]
+    layer_out[:, : width // 2] = layer_first[...]
+    rows_of(layer_last, tp.me, tp.count)[...] = layer_rows[...]
     layer_spread.begin()
     small[:SMALL_ROWS, :] = vectors_own[...].astype(small.dtype)
     small[SMALL_ROWS : SMALL_ROWS + rank, :] = matmul_tn(step_low[...], pre_low[...]).astype(
@@ -1684,6 +1685,11 @@
     gather.relay()
     products(ffn_all, down_end, gu_end, flat(1), side_by_side(grad_gateup, down_end), *wide)
     gather.hand_over()
+    finish(small_sent)
+    plane.own(small_sum)[...] = plane.total(small, small_slots).astype(small_sum.dtype)
+    small_sent = plane.spread(small_sum, 1)
+    if swaps:
+        swap.begin()
     layer_spread.pass_on()
     hidden_in = tp.own(tokens)[...].astype(jnp.float32)
     tp.own(tokens_grad)[...] = (
@@ -1696,14 +1702,10 @@
         )
     ).astype(tokens_grad.dtype)
     tokens_spread.begin()
-    finish(small_sent)
-    plane.own(small_sum)[...] = plane.total(small, small_slots).astype(small_sum.dtype)
-    small_sent = plane.spread(small_sum, 1)
     gather.hand_over_last()
-    if swaps:
-        swap.end()
+    gather.end()
+    products(mix_all, 0, 2 * inner // WIDE, flat(0), side_by_side(grad_inproj, 0), *wide)
     tokens_spread.pass_on()
-    products(gated_all, 0, inner // WIDE, tall(3), one_above_other(grad_outproj), *high)
     finish(small_sent)
     gain_own[...] = small_sum[SMALL_ROWS - GAIN_ROWS : SMALL_ROWS, :].astype(jnp.float32)
     gain_sent = [tp.one(gain_own, gain_slots.at[hop], 0, hop) for hop in range(tp.count - 1)]
@@ -1712,8 +1714,9 @@
     select_sum[...] = small_sum[SMALL_ROWS + rank : SMALL_ROWS + rank + selected, :].astype(
         jnp.float32
     )
-    gather.end()
-    products(mix_all, 0, 2 * inner // WIDE, flat(0), side_by_side(grad_inproj, 0), *wide)
+    if swaps:
+        swap.end()
+    products(gated_all, 0, inner // WIDE, tall(3), one_above_other(grad_outproj), *high)
     finish(gain_sent)
     total = gain_own[...]
     for hop in range(tp.count - 1):
@@ -1730,6 +1733,7 @@
     conv_grad,
     gate_grad,
     vectors,
+    layer_first,
     layer_rows,
     middle_low,
     step_low,
@@ -1764,11 +1768,11 @@
     part = jax.ShapeDtypeStruct((rows, width), low)
     return pl.pallas_call(
         functools.partial(tail_kernel, swaps),
-        in_specs=[vmem] * 17 + [hbm] * 8,
+        in_specs=[vmem] * 18 + [hbm] * 8,
         out_specs=[vmem] * 6 + [hbm] * 5,
         out_shape=[
             jax.ShapeDtypeStruct(tokens.shape, low),
-            jax.ShapeDtypeStruct((rows, width // 2), low),
+            jax.ShapeDtypeStruct(tokens.shape, low),
             jax.ShapeDtypeStruct((SMALL_ROWS, inner), full),
             jax.ShapeDtypeStruct((rank, inner), full),
             jax.ShapeDtypeStruct((selected, inner), full),
@@ -1814,6 +1818,7 @@
         conv_grad,
         gate_grad,
         *vectors,
+        layer_first,
         layer_rows,
         middle_low,
         step_low,
@@ -1978,13 +1983,14 @@
 
     tokens_rows = tokens.reshape(rows, width)
     ct_low = cotangent.reshape(rows, width)
-    ffn_pack = gathered_rows(
-        jnp.concatenate([gateup[0], gateup[1], jnp.transpose(downproj)], 1)
-    )
     swap_now = swaps_in_kernels(width)
     conv_in, in_conv, *swapped = run_head(
         5, tokens_rows, gain_mix_row, ct_low, inproj[0], swap_now
     )
+    ffn_pack, conv_in = lax.optimization_barrier(
+        (jnp.concatenate([gateup[0], gateup[1], jnp.transpose(downproj)], 1), conv_in)
+    )
+    ffn_pack = gathered_rows(ffn_pack)
     ct_cols = swapped[0].reshape(-1, swapped[0].shape[2]) if swapped else swapped_columns(ct_low)
     hidden_in = tokens_rows.astype(jnp.float32)
     scale_one = inverse_rms(hidden_in)
@@ -2113,7 +2119,7 @@
     ]
     (
         tokens_grad,
-        layer_last,
+        layer_out,
         vectors,
         grad_stepproj,
         grad_selproj,
@@ -2130,6 +2136,7 @@
         conv_in_grad,
         gate_mix_grad,
         vectors,
+        layer_first,
         layer_rows[1],
         middle_low,
         step_low,
@@ -2150,7 +2157,7 @@
     )
     at = taps + 2
     return (
-        jnp.concatenate([layer_first, layer_last], 1).reshape(tokens.shape),
+        layer_out.reshape(tokens.shape),
         tokens_grad.reshape(tokens.shape),
         gains[8:10].reshape(width),
         grad_inproj,

time: 496 us -> 501 us (1.010)
    pallas_call x1, Pallas kernels: 62.7 us -> 49.6 us  [run_head(): pl.pallas_call(functools.partial(head_kernel, swaps), in_specs=[vmem] * 3...]
    pallas_call x1, Pallas kernels: 55.2 us -> 67.4 us  [mixer_out(): pl.pallas_call(functools.partial(mixer_out_kernel, len(arrays)), in_specs...]
    unnamed x72 -> x69, local copies, waits for them, and re-layouts: 13.7 us -> 16.2 us
  transfers between devices with their start and end apart: 4 -> 4, of which waited for: 2 -> 3; matrix products, arithmetic and copies ran while one was open for 7% -> 7% of each run, Pallas kernels for 63% -> 53%
where the time goes in v11:
time: 501 us; the launch traced here: 500 us
  Pallas kernels  410 us (82%)
  local copies, waits for them, and re-layouts  30.9 us (6%)
  other arithmetic  23.1 us (5%)
  between operations  14.6 us (3%)
  waiting for transfers between devices  9.22 us (2%)
  matrix products  6.83 us (1%)
    pallas_call x1, Pallas kernels, run_tail(): pl.pallas_call(functools.partial(tail_kernel, swaps), in_specs=[vmem] * 1...  77.9 us
    pallas_call x1, Pallas kernels, mixer_out(): pl.pallas_call(functools.partial(mixer_out_kernel, len(arrays)), in_specs...  67.4 us
    pallas_call x1, Pallas kernels, ffn_back(): pl.pallas_call(ffn_back_kernel, in_specs=[vmem] * 5 + [pl.BlockSpec(memor...  51.1 us
    pallas_call x1, Pallas kernels, run_head(): pl.pallas_call(functools.partial(head_kernel, swaps), in_specs=[vmem] * 3...  49.6 us
    pallas_call x1, Pallas kernels, run_select(): pl.pallas_call(select_kernel, in_specs=[vmem, vmem, hbm], out_specs=[vmem...  48.5 us
    pallas_call x1, Pallas kernels, scan_forward_pair(): pl.pallas_call(functools.partial(forward_pair_kernel, n_state, tiles, gro...  48.5 us
    pallas_call x1, Pallas kernels, scan_backward_pair(): pl.pallas_call(functools.partial(backward_pair_kernel, len(arrays), n_sta...  31.9 us
    pallas_call x1, Pallas kernels, run_ffn(): pl.pallas_call(functools.partial(ffn_kernel, swaps), in_specs=[vmem, vmem...  19.4 us
  transfers between devices with their start and end apart: 4, of which 3 were waited for; matrix products, arithmetic and copies ran while one was open for 7% of the time, Pallas kernels for 53%

profile of v11, /device:TPU:0, one launch (start us, length us, event | category | flops | bytes accessed | tf_op | source)
XLA Modules:
  0.0 499.8 jit_solution(1121079647343049915)
XLA Ops:
  7.2 1.3 reshape.110.gain.gain_row
  8.6 1.6 copy.32
  10.2 2.2 slice_bitcast_fusion.2
  12.6 1.8 pad_maximum_fusion
  14.4 49.6 %shard_map.262 = (bf16[256,1024]{1,0:T(8,128)(2,1)}, bf16[2048,1024]{1,0:T(8,128)(2,1)}, bf16[8,256,256]{2,1,0:T(8,128)(2,1)}) custom-call(bf16[256,2048]{1,0:T(8,128)(2,1)} %bitcast.88, bf16[1,2048]{1,0:T(2,128)(2,1)} %reshape.110.gain.gain_row, bf16[256,2048]{1,0:T(8,128)(2,1)} %bitcast.91, bf16[256,1024]{1,0:T(8,128)(2,1)} %get-tuple-element.113.in_conv), custom_call_target="tpu_custom_call" | custom-call | tf_op jit(solution)/shard_map/pallas_call | solution.py:1928
  65.1 3.4 collective-permute-start
  72.1 1.8 fusion.20
  74.9 48.5 %shard_map.263 = (f32[256,256]{1,0:T(8,128)}, f32[256,1024]{1,0:T(8,128)}, bf16[2048,1024]{1,0:T(8,128)(2,1)}) custom-call(f32[256,256]{1,0:T(8,128)} %fusion.10.part, bf16[256,2048]{1,0:T(8,128)(2,1)} %multiply_convert_fusion.normed.refs_0_, bf16[256,1024]{1,0:T(8,128)(2,1)} %get-tuple-element.112.shard), custom_call_target="tpu_custom_call" | custom-call | tf_op jit(solution)/shard_map/pallas_call | solution.py:687
  126.0 3.0 compare_select_fusion
  129.0 48.5 %shard_map.264 = (f32[256,16,8,128]{3,2,1,0:T(8,128)}, f32[256,1024]{1,0:T(8,128)}, bf16[8192,256]{1,0:T(8,128)(2,1)}) custom-call(f32[256,1024]{1,0:T(8,128)} %get-tuple-element.126.step_ref, f32[256,1024]{1,0:T(8,128)} %get-tuple-element.101.input_ref, f32[4096]{0:T(1024)} %reshape.114.brow_ref, f32[4096]{0:T(1024)} %reshape.115.crow_ref, ...), custom_call_target="tpu_custom_call" | custom-call | tf_op jit(solution)/shard_map/pallas_call | solution.py:1131
  177.5 2.5 multiply_convert_fusion.2.gated
  179.9 67.4 %shard_map.265 = (bf16[256,2048]{1,0:T(8,128)(2,1)}, f32[64,2048]{1,0:T(8,128)}, bf16[2048,1024]{1,0:T(8,128)(2,1)}, bf16[2048,256]{1,0:T(8,128)(2,1)}) custom-call(bf16[256,1024]{1,0:T(8,128)(2,1)} %multiply_convert_fusion.2.gated, bf16[8192,256]{1,0:T(8,128)(2,1)} %get-tuple-element.60.out_all, bf16[256,2048]{1,0:T(8,128)(2,1)} %bitcast.89, ...), custom_call_target="tpu_custom_call" | custom-call | tf_op jit(solution)/shard_map/pallas_call | solution.py:789
  247.3 3.0 all-gather.3.cloned.1.call-done.weights
  250.4 19.4 %shard_map.266 = (bf16[256,6144]{1,0:T(8,128)(2,1)}, bf16[2048,256]{1,0:T(8,128)(2,1)}) custom-call(bf16[256,2048]{1,0:T(8,128)(2,1)} %get-tuple-element.61.normed, bf16[256,2048]{1,0:T(8,128)(2,1)} %bitcast.92, bf16[2048,6144]{1,0:T(8,128)(2,1)} %all-gather.3.cloned.1.call-done.weights), custom_call_target="tpu_custom_call" | custom-call | tf_op jit(solution)/shard_map/pallas_call | solution.py:865
  271.2 1.5 slice.139.step_low
  272.7 51.1 %shard_map.267 = (bf16[256,2048]{1,0:T(8,128)(2,1)}, f32[64,2048]{1,0:T(8,128)}, f32[1,2048]{1,0:T(1,128)}, f32[256,1024]{1,0:T(8,128)}, bf16[256,2048]{1,0:T(8,128)(2,1)}) custom-call(bf16[256,6144]{1,0:T(8,128)(2,1)} %get-tuple-element.63.made, bf16[256,2048]{1,0:T(8,128)(2,1)} %bitcast.93, f32[64,2048]{1,0:T(8,128)} %get-tuple-element.64.middle, ...), custom_call_target="tpu_custom_call" | custom-call | tf_op jit(solution)/shard_map/pallas_call | solution.py:969
  323.9 4.5 multiply_reduce_fusion.1
  328.4 31.9 %shard_map.268 = (f32[256,1024]{1,0:T(8,128)}, f32[256,1024]{1,0:T(8,128)}, f32[16,8,128]{2,1,0:T(8,128)}, f32[256,32,128]{2,1,0:T(8,128)}, bf16[64,1024]{1,0:T(8,128)(2,1)}, /*index=5*/bf16[64,1024]{1,0:T(8,128)(2,1)}) custom-call(f32[256,1024]{1,0:T(8,128)} %get-tuple-element.126.step_ref, f32[256,1024]{1,0:T(8,128)} %get-tuple-element.101.input_ref, ...), custom_call_target="tpu_custom_call" | custom-call | tf_op jit(solution)/shard_map/pallas_call | solution.py:1338
  360.3 3.6 reduce_sum.82
  364.0 2.2 fusion.17
  367.2 15.8 %shard_map.269 = (bf16[256,256]{1,0:T(8,128)(2,1)}, bf16[256,1024]{1,0:T(8,128)(2,1)}) custom-call(bf16[256,256]{1,0:T(8,128)(2,1)} %maximum_maximum_fusion.part, bf16[64,1024]{1,0:T(8,128)(2,1)} %get-tuple-element.71.own_rows), custom_call_target="tpu_custom_call" | custom-call | tf_op jit(solution)/shard_map/pallas_call | solution.py:729
  383.0 2.5 multiply_reduce_fusion.5
  386.1 1.4 collective-permute-start.1
  390.0 2.7 collective-permute-done.1
  393.6 3.4 all-gather.5.cloned.1.call-done.ffn_all
  397.1 77.9 %shard_map.270 = (bf16[256,2048]{1,0:T(8,128)(2,1)}, bf16[256,2048]{1,0:T(8,128)(2,1)}, f32[32,1024]{1,0:T(8,128)}, f32[128,1024]{1,0:T(8,128)}, f32[160,1024]{1...) custom-call(bf16[256,1024]{1,0:T(8,128)(2,1)} %bitcast.96, ...), custom_call_target="tpu_custom_call" | custom-call | tf_op jit(solution)/shard_map/pallas_call | solution.py:1769
  475.0 1.5 fusion.23
  476.5 1.4 slice.103
  477.8 1.5 slice_bitcast_fusion.4
  480.8 2.5 copy.51
  484.2 1.3 copy.53
  488.5 2.1 copy.57
  (103 shorter events, 22.2 us)
Async XLA Ops:
  7.2 118.8 %copy-start = (bf16[128,1024]{1,0:T(8,128)(2,1)S(1)}, bf16[128,1024]{1,0:T(8,128)(2,1)}, u32[]{:S(2)}) copy-start(bf16[128,1024]{1,0:T(8,128)(2,1)} %param.21) | copy-start | bytes 786436
  7.2 243.2 %all-gather.3.cloned.1.call-start = ((), (), s32[]{:S(2)}) async-start(), calls=%async_computation | async-start | bytes 28311552 | tf_op jit(solution)/shard_map/all_gather | solution.py:366
  8.6 3.9 copy-start.7
  64.0 4.4 copy-start.23
  64.0 4.4 copy-start.1
  64.0 4.7 copy-start.17
  64.1 6.0 %copy-start.22 = (bf16[4,1024]{1,0:T(4,128)(2,1)S(1)}, bf16[4,1024]{1,0:T(4,128)(2,1)}, u32[]{:S(2)}) copy-start(bf16[4,1024]{1,0:T(4,128)(2,1)} %param.18) | copy-start | bytes 24580
  64.1 6.0 %copy-start.25 = (bf16[1024]{0:T(1024)(128)(2,1)S(1)}, bf16[1024]{0:T(1024)(128)(2,1)}, u32[]{:S(2)}) copy-start(bf16[1024]{0:T(1024)(128)(2,1)} %param.24) | copy-start | bytes 6148
  64.1 6.0 %copy-start.26 = (bf16[1024]{0:T(1024)(128)(2,1)S(1)}, bf16[1024]{0:T(1024)(128)(2,1)}, u32[]{:S(2)}) copy-start(bf16[1024]{0:T(1024)(128)(2,1)} %param.19) | copy-start | bytes 6148
  64.1 6.0 %copy-start.27 = (bf16[1024]{0:T(1024)(128)(2,1)S(1)}, bf16[1024]{0:T(1024)(128)(2,1)}, u32[]{:S(2)}) copy-start(bf16[1024]{0:T(1024)(128)(2,1)} %param.22) | copy-start | bytes 6148
  64.1 6.1 %copy-start.24 = (bf16[2048]{0:T(1024)(128)(2,1)S(1)}, bf16[2048]{0:T(1024)(128)(2,1)}, u32[]{:S(2)}) copy-start(bf16[2048]{0:T(1024)(128)(2,1)} %param.26) | copy-start | bytes 12292
  64.1 333.0 %all-gather.5.cloned.1.call-start = ((), (), s32[]{:S(2)}) async-start(), calls=%async_computation.1 | async-start | bytes 28311552 | tf_op jit(solution)/shard_map/all_gather | solution.py:366
  65.1 6.4 %collective-permute-start = (bf16[2,3,1024]{2,1,0:T(4,128)(2,1)S(1)}, bf16[2,3,1024]{2,1,0:T(4,128)(2,1)S(1)}, u32[]{:S(2)}, u32[]{:S(2)}) collective-permute-start(bf16[2,3,1024]{2,1,0:T(4,128)(2,1)S(1)} %slice.110), channel_id=1, source_target_pairs={{0,4},{1,5},{2,6},{3,7},{8,12},{9,13},{10,14},{11,15},{16,20},{17,... | collective-permute-start | bytes 36872 | tf_op jit(solution)/shard_map/ppermute | solution.py:23
  70.1 2.0 copy-start.20
  72.1 1.8 copy-start.16
  73.9 250.0 %copy-start.2 = (bf16[256,1024]{1,0:T(8,128)(2,1)}, bf16[256,1024]{1,0:T(8,128)(2,1)S(1)}, u32[]{:S(2)}) copy-start(bf16[256,1024]{1,0:T(8,128)(2,1)S(1)} %get-tuple-element.102.scan_in) | copy-start | bytes 1572868
  126.0 51.5 %copy-start.5 = (f32[256,1024]{1,0:T(8,128)S(1)}, f32[256,1024]{1,0:T(8,128)}, u32[]{:S(2)}) copy-start(f32[256,1024]{1,0:T(8,128)} %get-tuple-element.59) | copy-start | bytes 3145732
  360.3 3.6 copy-start.10
  363.9 2.5 copy-start.28
  363.9 19.0 %copy-start.4 = (f32[256,1024]{1,0:T(8,128)S(1)}, f32[256,1024]{1,0:T(8,128)}, u32[]{:S(2)}) copy-start(f32[256,1024]{1,0:T(8,128)} %get-tuple-element.100.ograd_ref) | copy-start | bytes 3145732
  366.2 19.3 %copy-start.3 = (bf16[256,1024]{1,0:T(8,128)(2,1)}, bf16[256,1024]{1,0:T(8,128)(2,1)S(1)}, u32[]{:S(2)}) copy-start(bf16[256,1024]{1,0:T(8,128)(2,1)S(1)} %get-tuple-element.105.pre_low) | copy-start | bytes 1572868
  383.0 2.5 copy-start.21
  386.1 2.0 copy-start.18
  386.1 2.0 copy-start.19
  386.1 6.6 %collective-permute-start.1 = (f32[2,3,1024]{2,1,0:T(4,128)S(1)}, f32[2,3,1024]{2,1,0:T(4,128)S(1)}, u32[]{:S(2)}, u32[]{:S(2)}) collective-permute-start(f32[2,3,1024]{2,1,0:T(4,128)S(1)} %pad_add_fusion.1), channel_id=1, source_target_pairs={{4,0},{5,1},{6,2},{7,3},{12,8},{13,9},{14,10},{15,11},{20,16},{21,... | collective-permute-start | bytes 73736 | tf_op jit(solution)/shard_map/ppermute | solution.py:23
  475.0 8.3 %copy-start.12 = (bf16[256,2048]{1,0:T(8,128)(2,1)S(1)}, bf16[256,2048]{1,0:T(8,128)(2,1)}, u32[]{:S(2)}) copy-start(bf16[256,2048]{1,0:T(8,128)(2,1)} %get-tuple-element.86) | copy-start | bytes 3145732
  480.8 3.4 copy-start.9
  484.2 1.5 copy-start.13
  484.2 2.4 copy-start.15
  484.2 3.1 copy-start.11
  485.8 2.7 copy-start.6
  488.5 3.1 copy-start.8
  (1 other events, 1.0 us)
Sparse Core Ops, SparseCore 0:
  64.2 186.1 all-gather.2
  269.9 127.0 all-gather.4

commit v12 on v11

--- a/solution.py
+++ b/solution.py
@@ -603,6 +603,55 @@
         finish(self.copies)
 
 
+class SplitSwap:
+    def __init__(self, array, swapped, plane_send, plane_recv, tp_send, tp_recv, local_sem):
+        self.plane, self.tp = Group(PLANE, plane_send, plane_recv), Group(("tp",), tp_send, tp_recv)
+        self.array, self.swapped, self.local_sem = array, swapped, local_sem
+        rows = array.shape[0] // self.tp.count
+        self.rows = pl.ds(pl.multiple_of(self.tp.me * rows, rows), rows)
+
+    def columns(self, index):
+        share = self.swapped.shape[2]
+        return self.array.at[self.rows, pl.ds(pl.multiple_of(index * share, share), share)]
+
+    def begin(self):
+        mine = self.swapped.at[self.plane.me, self.rows, :]
+        self.local = pltpu.make_async_copy(
+            self.columns(self.plane.me), mine, self.local_sem
+        )
+        self.local.start()
+        self.copies = [
+            self.plane.one(self.columns(other), mine, 0, hop)
+            for hop, other in enumerate(self.plane.others)
+        ]
+
+    def pass_on(self):
+        finish(self.copies)
+        self.local.wait()
+        here = self.swapped.at[:, self.rows, :]
+        self.copies = [self.tp.one(here, here, 0, hop) for hop in range(self.tp.count - 1)]
+
+    def end(self):
+        finish(self.copies)
+
+
+def split_scratch(arrays):
+    dma = pltpu.SemaphoreType.DMA
+    count, tp_count = group_size(PLANE), group_size(("tp",))
+    sems = [dma((1, count - 1))] * 2 + [dma((1, tp_count - 1))] * 2 + [dma(())]
+    return sems if arrays else []
+
+
+def split_shapes(arrays):
+    count = group_size(PLANE)
+    return [
+        jax.ShapeDtypeStruct(
+            (count, array.shape[0], array.shape[1] // count), array.dtype
+        )
+        for array in arrays
+    ]
+
+
 def swap_scratch(arrays):
     sems = pltpu.SemaphoreType.DMA((len(arrays), group_size(PLANE) - 1))
     return [sems, sems, pltpu.SemaphoreType.DMA((len(arrays),))] if arrays else []
@@ -647,52 +696,50 @@
         target[:, at : at + WIDE] = matmul(left[...], block_buf[turn % 2]).astype(target.dtype)
 
 
-def select_kernel(
-    part,
-    normed,
-    shard,
-    total,
-    product,
-    gathered,
-    slots,
-    send_sem,
-    recv_sem,
-    block_buf,
-    block_sem,
-    gather_send,
-    gather_recv,
-    local_sem,
-):
+def select_kernel(n_swaps, part, normed, shard, *refs):
+    arrays, refs = refs[:n_swaps], refs[n_swaps:]
+    total, product, gathered, *refs = refs
+    swapped, refs = refs[:n_swaps], refs[n_swaps:]
+    slots, send_sem, recv_sem, block_buf, block_sem, *refs = refs
+    gather_send, gather_recv, local_sem, *swap_sems = refs
     group = Group(("tp",), send_sem, recv_sem)
     gather = PlaneGather(shard, gathered, gather_send, gather_recv)
     greet([(("tp",), group.others), (PLANE, gather.others)])
     gather.begin(local_sem)
+    if n_swaps:
+        swap = SplitSwap(arrays[0], swapped[0], *swap_sems)
+        swap.begin()
     finish(group.scatter(part, slots, 0))
     group.own(total)[...] = group.total(part, slots).astype(total.dtype)
     copies = group.spread(total, 1)
     gather.relay()
     gather.hand_over()
     finish(copies)
+    if n_swaps:
+        swap.pass_on()
     gather.hand_over_last()
     gather.end()
     product_in_blocks(normed, gathered, product, block_buf, block_sem)
-
-
-def run_select(call_id, part, normed, shard):
+    if n_swaps:
+        swap.end()
+
+
+def run_select(call_id, part, normed, shard, arrays):
     count = group_size(("tp",))
     vmem = pl.BlockSpec(memory_space=pltpu.VMEM)
     hbm = pl.BlockSpec(memory_space=pltpu.HBM)
     sems = pltpu.SemaphoreType.DMA((2, count - 1))
     rows, width = normed.shape
     return pl.pallas_call(
-        select_kernel,
-        in_specs=[vmem, vmem, hbm],
-        out_specs=[vmem, vmem, hbm],
+        functools.partial(select_kernel, len(arrays)),
+        in_specs=[vmem, vmem, hbm] + [vmem] * len(arrays),
+        out_specs=[vmem, vmem, hbm] + [hbm] * len(arrays),
         out_shape=[
             jax.ShapeDtypeStruct(part.shape, part.dtype),
             jax.ShapeDtypeStruct((rows, shard.shape[1]), jnp.float32),
             gathered_shape(shard),
-        ],
+        ]
+        + split_shapes(arrays),
         scratch_shapes=[
             slots_for(part, count),
             sems,
@@ -700,11 +747,12 @@
             pltpu.VMEM((2, width, WIDE), jnp.bfloat16),
             pltpu.SemaphoreType.DMA((2,)),
         ]
-        + gather_scratch(),
+        + gather_scratch()
+        + split_scratch(arrays),
         compiler_params=pltpu.CompilerParams(
             collective_id=call_id, has_side_effects=True, vmem_limit_bytes=VMEM_GRANT
         ),
-    )(part, normed, shard)
+    )(part, normed, shard, *arrays)
 
 
 def sum_kernel(part, own_rows, total, all_rows, slots, send_sem, recv_sem, *line_sems):
@@ -741,81 +789,63 @@
     )(part, own_rows)
 
 
-def mixer_out_kernel(n_swaps, gated, out_all, tokens, gain, *refs):
-    arrays, refs = refs[:n_swaps], refs[n_swaps:]
-    normed, middle, gated_all, *refs = refs
-    swapped, refs = refs[:n_swaps], refs[n_swaps:]
-    part, refs = refs[0], refs[1:]
-    line = LineSum(part, *refs[:5])
-    spread = LineSpread(normed, *refs[5:7])
-    gather_send, gather_recv, local_sem, *refs = refs[7:]
+def mixer_out_kernel(gated, out_all, tokens, gain, normed, middle, part, *sems):
+    line = LineSum(part, *sems[:5])
+    spread = LineSpread(normed, *sems[5:])
     group = Group(("tp",), None, None)
-    gather = PlaneGather(gated, gated_all, gather_send, gather_recv)
     inner = gated.shape[1]
     share = out_all.shape[1]
-    greet([(("tp",), group.others), (PLANE, gather.others)])
-    gather.begin(local_sem)
+    greet([(("tp",), group.others)])
     for at in range(out_all.shape[0] // inner):
         part[:, at * share : (at + 1) * share] = matmul(
             gated[...], out_all[at * inner : (at + 1) * inner, :]
         ).astype(part.dtype)
-    firsts = [line.begin(j) for j in range(line.blocks)]
-    if n_swaps:
-        swap = Swap(arrays, swapped, *refs)
-        swap.begin()
-    line.pass_all(firsts)
+    line.pass_all([line.begin(j) for j in range(line.blocks)])
     rows = group.own(tokens)[...].astype(jnp.float32) + line.total()
     middle[...] = rows
     group.own(normed)[...] = (rows * inverse_rms(rows) * gain[...].astype(jnp.float32)).astype(
         normed.dtype
     )
     spread.begin()
-    gather.relay()
-    gather.hand_over()
     spread.pass_on()
     spread.end()
-    gather.hand_over_last()
-    gather.end()
-    if n_swaps:
-        swap.end()
-
-
-def mixer_out(call_id, gated, out_all, tokens, gain, arrays):
+
+
+def mixer_out(call_id, gated, out_all, tokens, gain):
     count = group_size(("tp",))
     vmem = pl.BlockSpec(memory_space=pltpu.VMEM)
-    hbm = pl.BlockSpec(memory_space=pltpu.HBM)
     rows, width = tokens.shape
     part = jax.ShapeDtypeStruct((rows, width), jnp.bfloat16)
     return pl.pallas_call(
-        functools.partial(mixer_out_kernel, len(arrays)),
-        in_specs=[vmem] * (4 + len(arrays)),
-        out_specs=[vmem] * 2 + [hbm] + [hbm] * len(arrays),
-        out_shape=[
-            part,
-            jax.ShapeDtypeStruct((rows // count, width), jnp.float32),
-            gathered_shape(gated),
-        ]
-        + swap_shapes(arrays),
+        mixer_out_kernel,
+        in_specs=[vmem] * 4,
+        out_specs=[vmem] * 2,
+        out_shape=[part, jax.ShapeDtypeStruct((rows // count, width), jnp.float32)],
         scratch_shapes=[pltpu.VMEM(part.shape, part.dtype)]
         + line_sum_scratch(part, 2)
-        + line_spread_scratch()
-        + gather_scratch()
-        + swap_scratch(arrays),
+        + line_spread_scratch(),
         compiler_params=pltpu.CompilerParams(
             collective_id=call_id, has_side_effects=True, vmem_limit_bytes=VMEM_GRANT
         ),
-    )(gated, out_all, tokens, gain, *arrays)
-
-
-def ffn_kernel(swaps, normed, ct, weights, made, *refs):
+    )(gated, out_all, tokens, gain)
+
+
+def ffn_kernel(
+    normed,
+    ct,
+    weights,
+    shard,
+    made,
+    gathered,
+    block_buf,
+    block_sem,
+    gather_send,
+    gather_recv,
+    local_sem,
+):
     hidden = weights.shape[1] // 3
-    if swaps:
-        *swapped, block_buf, block_sem, send_sem, recv_sem, local_sem = refs
-        swap = Swap([normed], swapped, send_sem, recv_sem, local_sem)
-        greet([(PLANE, swap.plane.others)])
-        swap.begin()
-    else:
-        block_buf, block_sem = refs
+    blocks = hidden // WIDE
+    gather = PlaneGather(shard, gathered, gather_send, gather_recv)
 
     def columns(j, which):
         return pl.ds(pl.multiple_of(which * hidden + j * WIDE, WIDE), WIDE)
@@ -830,12 +860,13 @@
 
     for which in range(3):
         fetch(0, which).start()
-
-    @pl.loop(0, hidden // WIDE)
-    def _(j):
+    greet([(PLANE, gather.others)])
+    gather.begin(local_sem)
+
+    def one_block(j):
         slot = lax.rem(j, 2)
 
-        @pl.when(j + 1 < hidden // WIDE)
+        @pl.when(j + 1 < blocks)
         def _():
             for which in range(3):
                 fetch(j + 1, which).start()
@@ -853,55 +884,62 @@
         made[:, columns(j, 1)] = (act_grad * up * slope).astype(made.dtype)
         made[:, columns(j, 2)] = (act_grad * silu).astype(made.dtype)
 
-    if swaps:
-        swap.end()
-
-
-def run_ffn(call_id, normed, ct, weights, swaps):
+    pl.loop(0, blocks // 2)(one_block)
+    gather.relay()
+    gather.hand_over()
+    pl.loop(blocks // 2, blocks)(one_block)
+    gather.hand_over_last()
+    gather.end()
+
+
+def run_ffn(call_id, normed, ct, weights, shard):
     rows, width = normed.shape
-    arrays = [normed] if swaps else []
     vmem = pl.BlockSpec(memory_space=pltpu.VMEM)
-    params = dict(collective_id=call_id, has_side_effects=True) if swaps else {}
+    hbm = pl.BlockSpec(memory_space=pltpu.HBM)
     return pl.pallas_call(
-        functools.partial(ffn_kernel, swaps),
-        in_specs=[vmem, vmem, pl.BlockSpec(memory_space=pltpu.HBM)],
-        out_specs=[vmem] + [pl.BlockSpec(memory_space=pltpu.HBM)] * len(arrays),
-        out_shape=[jax.ShapeDtypeStruct((rows, weights.shape[1]), jnp.bfloat16)]
-        + swap_shapes(arrays),
+        ffn_kernel,
+        in_specs=[vmem, vmem, hbm, hbm],
+        out_specs=[vmem, hbm],
+        out_shape=[
+            jax.ShapeDtypeStruct((rows, weights.shape[1]), jnp.bfloat16),
+            gathered_shape(shard),
+        ],
         scratch_shapes=[
             pltpu.VMEM((2, 3, width, WIDE), jnp.bfloat16),
             pltpu.SemaphoreType.DMA((2, 3)),
         ]
-        + swap_scratch(arrays),
-        compiler_params=pltpu.CompilerParams(vmem_limit_bytes=VMEM_GRANT, **params),
-    )(normed, ct, weights)
+        + gather_scratch(),
+        compiler_params=pltpu.CompilerParams(
+            collective_id=call_id, has_side_effects=True, vmem_limit_bytes=VMEM_GRANT
+        ),
+    )(normed, ct, weights, shard)
 
 
 def ffn_back_kernel(
+    n_swaps,
     made,
     ct,
     middle,
     gain,
     out_all,
     weights,
-    middle_low,
-    middle_grad,
-    gain_grad,
-    gated_grad,
-    ffn_part,
-    part,
-    wide_buf,
-    down_buf,
-    wide_sem,
-    down_sem,
-    *sems,
+    *refs,
 ):
+    arrays, refs = refs[:n_swaps], refs[n_swaps:]
+    middle_low, middle_grad, gain_grad, gated_grad, ffn_part, *refs = refs
+    swapped, refs = refs[:n_swaps], refs[n_swaps:]
+    part, wide_buf, down_buf, wide_sem, down_sem, *sems = refs
     hidden = made.shape[1] // 3
     blocks = part.shape[1] // WIDE
     group = Group(("tp",), None, None)
     line = LineSum(part, *sems[:5])
-    spread = LineSpread(middle_low, *sems[5:])
-    greet([(("tp",), group.others)])
+    spread = LineSpread(middle_low, *sems[5:7])
+    if n_swaps:
+        swap = Swap(arrays, swapped, *sems[7:])
+        greet([(("tp",), group.others), (PLANE, swap.plane.others)])
+        swap.begin()
+    else:
+        greet([(("tp",), group.others)])
 
     def fetch(j):
         return pltpu.make_async_copy(
@@ -955,11 +993,14 @@
         )
         total = one if total is None else total + one
     gated_grad[...] = total
-
-
-def ffn_back(call_id, made, ct, middle, gain, out_all, weights):
+    if n_swaps:
+        swap.end()
+
+
+def ffn_back(call_id, made, ct, middle, gain, out_all, weights, arrays):
     count = group_size(("tp",))
     vmem = pl.BlockSpec(memory_space=pltpu.VMEM)
+    hbm = pl.BlockSpec(memory_space=pltpu.HBM)
     rows, width = ct.shape
     hidden = made.shape[1] // 3
     inner = out_all.shape[0] // group_size(PLANE)
@@ -967,16 +1008,17 @@
     part = jax.ShapeDtypeStruct((rows, width), low)
     dma = pltpu.SemaphoreType.DMA
     return pl.pallas_call(
-        ffn_back_kernel,
-        in_specs=[vmem] * 5 + [pl.BlockSpec(memory_space=pltpu.HBM)],
-        out_specs=[vmem] * 5,
+        functools.partial(ffn_back_kernel, len(arrays)),
+        in_specs=[vmem] * 5 + [hbm] + [vmem] * len(arrays),
+        out_specs=[vmem] * 5 + [hbm] * len(arrays),
         out_shape=[
             part,
             jax.ShapeDtypeStruct((rows // count, width), full),
             jax.ShapeDtypeStruct((1, width), full),
             jax.ShapeDtypeStruct((rows, inner), full),
             part,
-        ],
+        ]
+        + swap_shapes(arrays),
         scratch_shapes=[
             pltpu.VMEM(part.shape, low),
             pltpu.VMEM((2, WIDE, 2 * hidden), low),
@@ -985,11 +1027,12 @@
             dma((2,)),
         ]
         + line_sum_scratch(part, width // WIDE)
-        + line_spread_scratch(),
+        + line_spread_scratch()
+        + swap_scratch(arrays),
         compiler_params=pltpu.CompilerParams(
             collective_id=call_id, has_side_effects=True, vmem_limit_bytes=VMEM_GRANT
         ),
-    )(made, ct, middle, gain, out_all, weights)
+    )(made, ct, middle, gain, out_all, weights, *arrays)
 
 
 def send_on(source, target, send_sem, recv_sem, ctx):
@@ -1004,6 +1047,7 @@
 
 
 def forward_pair_kernel(
+    n_swaps,
     n_state,
     tiles,
     groups,
@@ -1015,27 +1059,23 @@
     crow_ref,
     rate_ref,
     shard,
-    prior_ref,
-    mixed_ref,
-    gathered,
-    carried,
-    ends,
-    starts,
-    prior_buf,
-    step_held,
-    input_held,
-    mixed_held,
-    prior_sem,
-    send_sem,
-    recv_sem,
-    gather_send,
-    gather_recv,
-    local_sem,
+    *refs,
 ):
+    arrays, refs = refs[:n_swaps], refs[n_swaps:]
+    prior_ref, mixed_ref, gathered, *refs = refs
+    swapped, refs = refs[:n_swaps], refs[n_swaps:]
+    carried, ends, starts, prior_buf, step_held, input_held, mixed_held, *refs = refs
+    prior_sem, send_sem, recv_sem, gather_send, gather_recv, local_sem, *swap_sems = refs
     place = lax.axis_index("ctx")
     gather = PlaneGather(shard, gathered, gather_send, gather_recv)
-    greet([(PLANE, gather.others)])
-    gather.begin(local_sem)
+    if n_swaps:
+        swap = SplitSwap(arrays[0], swapped[0], *swap_sems)
+        greet([(PLANE, gather.others), (("tp",), swap.tp.others)])
+        gather.begin(local_sem)
+        swap.begin()
+    else:
+        greet([(PLANE, gather.others)])
+        gather.begin(local_sem)
 
     def hand_on(seq):
         return send_on(ends.at[seq], starts.at[seq], send_sem.at[seq], recv_sem.at[seq], 1)
@@ -1103,6 +1143,8 @@
         if seq == 0:
             gather.relay()
             gather.hand_over()
+            if n_swaps:
+                swap.pass_on()
     gather.hand_over_last()
     for block in range(max(0, seqs * blocks - 2), seqs * blocks):
         store(block).wait()
@@ -1113,9 +1155,13 @@
             hand_on(seq).wait_send()
 
     gather.end()
-
-
-def scan_forward_pair(call_id, step, inputs, b_rows, c_rows, rate, seqs, shard):
+    if n_swaps:
+        swap.end()
+
+
+def scan_forward_pair(
+    call_id, step, inputs, b_rows, c_rows, rate, seqs, shard, arrays
+):
     n_state, tiles, _ = rate.shape
     tokens, inner = step.shape
     all_groups = tokens // SUB
@@ -1129,14 +1175,17 @@
     boundary = pltpu.VMEM((seqs, n_state, tiles, LANE), full)
     dma = pltpu.SemaphoreType.DMA
     return pl.pallas_call(
-        functools.partial(forward_pair_kernel, n_state, tiles, groups, blocks, seqs),
-        in_specs=[vmem, vmem, smem, smem, vmem, hbm],
-        out_specs=[hbm, vmem, hbm],
+        functools.partial(
+            forward_pair_kernel, len(arrays), n_state, tiles, groups, blocks, seqs
+        ),
+        in_specs=[vmem, vmem, smem, smem, vmem, hbm] + [vmem] * len(arrays),
+        out_specs=[hbm, vmem, hbm] + [hbm] * len(arrays),
         out_shape=[
             jax.ShapeDtypeStruct((tokens, n_state, tiles, LANE), full),
             jax.ShapeDtypeStruct(step.shape, full),
             gathered_shape(shard),
-        ],
+        ]
+        + split_shapes(arrays),
         scratch_shapes=[
             pltpu.VMEM((n_state, tiles, LANE), full),
             boundary,
@@ -1149,11 +1198,12 @@
             dma((seqs,)),
             dma((seqs,)),
         ]
-        + gather_scratch(),
+        + gather_scratch()
+        + split_scratch(arrays),
         compiler_params=pltpu.CompilerParams(
             collective_id=call_id, has_side_effects=True, vmem_limit_bytes=VMEM_GRANT
         ),
-    )(step, inputs, b_rows, c_rows, rate, shard)
+    )(step, inputs, b_rows, c_rows, rate, shard, *arrays)
 
 
 def backward_pair_kernel(
@@ -1839,112 +1889,56 @@
     )
 
 
-class SplitSwap:
-    def __init__(self, array, swapped, plane_send, plane_recv, tp_send, tp_recv, local_sem):
-        self.plane, self.tp = Group(PLANE, plane_send, plane_recv), Group(("tp",), tp_send, tp_recv)
-        self.array, self.swapped, self.local_sem = array, swapped, local_sem
-        rows = array.shape[0] // self.tp.count
-        self.rows = pl.ds(pl.multiple_of(self.tp.me * rows, rows), rows)
-
-    def columns(self, index):
-        share = self.swapped.shape[2]
-        return self.array.at[self.rows, pl.ds(pl.multiple_of(index * share, share), share)]
-
-    def begin(self):
-        mine = self.swapped.at[self.plane.me, self.rows, :]
-        self.local = pltpu.make_async_copy(
-            self.columns(self.plane.me), mine, self.local_sem
-        )
-        self.local.start()
-        self.copies = [
-            self.plane.one(self.columns(other), mine, 0, hop)
-            for hop, other in enumerate(self.plane.others)
-        ]
-
-    def pass_on(self):
-        finish(self.copies)
-        self.local.wait()
-        here = self.swapped.at[:, self.rows, :]
-        self.copies = [self.tp.one(here, here, 0, hop) for hop in range(self.tp.count - 1)]
-
-    def end(self):
-        finish(self.copies)
-
-
 def head_kernel(
-    swaps,
     tokens,
     gain,
-    ct,
-    in_conv,
+    shard,
     conv_in,
-    conv_all,
-    *refs,
+    gathered,
+    normed,
+    block_buf,
+    block_sem,
+    gather_send,
+    gather_recv,
+    local_sem,
 ):
-    if swaps:
-        swapped, *refs = refs
-    normed, block_buf, block_sem, *sems = refs
-    conv = PlaneGather(in_conv, conv_all, *sems[:2])
-    if swaps:
-        swap = SplitSwap(ct, swapped, *sems[3:])
-        greet([(PLANE, conv.others), (("tp",), swap.tp.others)])
-    else:
-        greet([(PLANE, conv.others)])
-    conv.begin(sems[2])
-    if swaps:
-        swap.begin()
+    gather = PlaneGather(shard, gathered, gather_send, gather_recv)
+    greet([(PLANE, gather.others)])
+    gather.begin(local_sem)
     hidden_in = tokens[...].astype(jnp.float32)
     normed[...] = (hidden_in * inverse_rms(hidden_in) * gain[...].astype(jnp.float32)).astype(
         normed.dtype
     )
-
-    conv.relay()
-    conv.hand_over()
-    conv.hand_over_last()
-    if swaps:
-        swap.pass_on()
-    conv.end()
-    product_in_blocks(normed, conv_all, conv_in, block_buf, block_sem)
-    if swaps:
-        swap.end()
-
-
-def run_head(call_id, tokens, gain, ct, shard, swaps):
+    gather.relay()
+    gather.hand_over()
+    gather.hand_over_last()
+    gather.end()
+    product_in_blocks(normed, gathered, conv_in, block_buf, block_sem)
+
+
+def run_head(call_id, tokens, gain, shard):
     rows, width = tokens.shape
-    inner = shard.shape[1]
     low = jnp.bfloat16
     vmem = pl.BlockSpec(memory_space=pltpu.VMEM)
     hbm = pl.BlockSpec(memory_space=pltpu.HBM)
-    count, tp_count = group_size(PLANE), group_size(("tp",))
-    dma = pltpu.SemaphoreType.DMA
-    swap_sems = [
-        dma((1, count - 1)),
-        dma((1, count - 1)),
-        dma((1, tp_count - 1)),
-        dma((1, tp_count - 1)),
-        dma(()),
-    ]
-    swapped = [jax.ShapeDtypeStruct((count, rows, width // count), low)]
     return pl.pallas_call(
-        functools.partial(head_kernel, swaps),
-        in_specs=[vmem] * 3 + [hbm],
-        out_specs=[vmem] + [hbm] * (2 if swaps else 1),
+        head_kernel,
+        in_specs=[vmem] * 2 + [hbm],
+        out_specs=[vmem, hbm],
         out_shape=[
-            jax.ShapeDtypeStruct((rows, inner), low),
-            jax.ShapeDtypeStruct((width, inner), low),
-        ]
-        + (swapped if swaps else []),
+            jax.ShapeDtypeStruct((rows, shard.shape[1]), low),
+            gathered_shape(shard),
+        ],
         scratch_shapes=[
             pltpu.VMEM((rows, width), low),
             pltpu.VMEM((2, width, WIDE), low),
             pltpu.SemaphoreType.DMA((2,)),
         ]
-        + gather_scratch()
-        + (swap_sems if swaps else []),
+        + gather_scratch(),
         compiler_params=pltpu.CompilerParams(
             collective_id=call_id, has_side_effects=True, vmem_limit_bytes=VMEM_GRANT
         ),
-    )(tokens, gain, ct, shard)
+    )(tokens, gain, shard)
 
 
 def per_device(
@@ -1984,14 +1978,11 @@
     tokens_rows = tokens.reshape(rows, width)
     ct_low = cotangent.reshape(rows, width)
     swap_now = swaps_in_kernels(width)
-    conv_in, in_conv, *swapped = run_head(
-        5, tokens_rows, gain_mix_row, ct_low, inproj[0], swap_now
-    )
+    conv_in, in_conv = run_head(5, tokens_rows, gain_mix_row, inproj[0])
     ffn_pack, conv_in = lax.optimization_barrier(
         (jnp.concatenate([gateup[0], gateup[1], jnp.transpose(downproj)], 1), conv_in)
     )
     ffn_pack = gathered_rows(ffn_pack)
-    ct_cols = swapped[0].reshape(-1, swapped[0].shape[2]) if swapped else swapped_columns(ct_low)
     hidden_in = tokens_rows.astype(jnp.float32)
     scale_one = inverse_rms(hidden_in)
     normed_one = (hidden_in * scale_one * gain_mix).astype(low)
@@ -2008,9 +1999,20 @@
     columns = selproj.shape[1]
     select_width = -(-columns // LANE) * LANE
     select_weights = jnp.pad(selproj, ((0, 0), (0, select_width - columns)))
-    select_cols, gate_mix, in_gate = run_select(
-        0, matmul(scan_in, select_weights), normed_one, inproj[1]
+    select_cols, gate_mix, in_gate, *swapped = run_select(
+        0,
+        matmul(scan_in, select_weights),
+        normed_one,
+        inproj[1],
+        [ct_low] if swap_now else [],
     )
+
+    def columns_of(swapped, array):
+        if not swapped:
+            return swapped_columns(array)
+        return swapped[0].reshape(-1, swapped[0].shape[-1])
+
+    ct_cols = columns_of(swapped, ct_low)
     step_low = select_cols[:, :rank].astype(low)
     b_rows = select_cols[:, rank : rank + n_state].reshape(-1)
     c_rows = select_cols[:, rank + n_state : columns].reshape(-1)
@@ -2018,8 +2020,16 @@
     step_size = jax.nn.softplus(step_pre)
     in_pairs = lax.axis_size("ctx") == 2
     if in_pairs:
-        prior, scan_out, out_all = scan_forward_pair(
-            6, step_size, scan_float, b_rows, c_rows, rate, seqs, outproj
+        prior, scan_out, out_all, *swapped = scan_forward_pair(
+            6,
+            step_size,
+            scan_float,
+            b_rows,
+            c_rows,
+            rate,
+            seqs,
+            outproj,
+            [normed_one] if swap_now else [],
         )
     else:
         span_decay = jnp.exp(
@@ -2028,25 +2038,25 @@
         ends = scan_ends(step_size, scan_float, b_rows, rate, seqs, False)
         start = from_earlier(ends, span_decay, 1)
         prior, scan_out = scan_forward(start, step_size, scan_float, b_rows, c_rows, rate, seqs)
-        out_all = gathered_rows(outproj)
+        out_all, swapped = gathered_rows(outproj), []
+    normed_one_cols = columns_of(swapped, normed_one)
     mixer_core = scan_out + skip_weight[None] * scan_float
     gate_sig = jax.nn.silu(gate_mix)
     gated = (mixer_core * gate_sig).astype(low)
-    normed_two, middle, gated_all, *swapped = mixer_out(
-        1,
-        gated,
+    normed_two, middle = mixer_out(1, gated, out_all, tokens_rows, gain_ffn_row)
+    made, gated_all = run_ffn(8, normed_two, ct_low, ffn_pack, gated)
+    ffn_all = gathered_rows(made)
+    middle_low, middle_grad, ffngain_part, gated_grad, ffn_part, *swapped = ffn_back(
+        2,
+        made,
+        ct_low,
+        middle,
+        gain_ffn_row,
         out_all,
-        tokens_rows,
-        gain_ffn_row,
-        [normed_one] if swap_now else [],
+        ffn_pack,
+        [normed_two] if swap_now else [],
     )
-    (normed_one_cols,) = swapped if swap_now else [swapped_columns(normed_one)]
-    made, *swapped = run_ffn(8, normed_two, ct_low, ffn_pack, swap_now)
-    (normed_two_cols,) = swapped or [swapped_columns(normed_two)]
-    ffn_all = gathered_rows(made)
-    middle_low, middle_grad, ffngain_part, gated_grad, ffn_part = ffn_back(
-        2, made, ct_low, middle, gain_ffn_row, out_all, ffn_pack
-    )
+    normed_two_cols = columns_of(swapped, normed_two)
     core_grad = gated_grad * gate_sig
     gate_mix_grad = (gated_grad * mixer_core * silu_slope(gate_mix)).astype(low)
     grad_skipgain = jnp.sum(core_grad * scan_float, 0)

time: 501 us -> 503 us (level)
  transfers between devices with their start and end apart: 4 -> 4, of which waited for: 3 -> 2; matrix products, arithmetic and copies ran while one was open for 7% -> 7% of each run, Pallas kernels for 53% -> 53%
where the time goes in v12:
time: 503 us; the launch traced here: 501 us
  Pallas kernels  409 us (81%)
  local copies, waits for them, and re-layouts  30.9 us (6%)
  other arithmetic  22.3 us (4%)
  between operations  14.6 us (3%)
  waiting for transfers between devices  13.1 us (3%)
  matrix products  6.73 us (1%)
    pallas_call x1, Pallas kernels, run_tail(): pl.pallas_call(functools.partial(tail_kernel, swaps), in_specs=[vmem] * 1...  77.9 us
    pallas_call x1, Pallas kernels, scan_forward_pair(): pl.pallas_call(functools.partial(forward_pair_kernel, len(arrays), n_stat...  62.5 us
    pallas_call x1, Pallas kernels, run_select(): pl.pallas_call(functools.partial(select_kernel, len(arrays)), in_specs=[v...  56.7 us
    pallas_call x1, Pallas kernels, ffn_back(): pl.pallas_call(functools.partial(ffn_back_kernel, len(arrays)), in_specs=...  54.2 us
    pallas_call x1, Pallas kernels, mixer_out(): pl.pallas_call(mixer_out_kernel, in_specs=[vmem] * 4, out_specs=[vmem] *...  46.4 us
    pallas_call x1, Pallas kernels, run_ffn(): pl.pallas_call(ffn_kernel, in_specs=[vmem, vmem, hbm, hbm], out_specs=[vm...  33.2 us
    pallas_call x1, Pallas kernels, scan_backward_pair(): pl.pallas_call(functools.partial(backward_pair_kernel, len(arrays), n_sta...  31.5 us
    pallas_call x1, Pallas kernels, run_head(): pl.pallas_call(head_kernel, in_specs=[vmem] * 2 + [hbm], out_specs=[vmem,...  29.9 us
  transfers between devices with their start and end apart: 4, of which 2 were waited for; matrix products, arithmetic and copies ran while one was open for 7% of the time, Pallas kernels for 53%

profile of v12, /device:TPU:0, one launch (start us, length us, event | category | flops | bytes accessed | tf_op | source)
XLA Modules:
  0.0 501.4 jit_solution(16386060600737222347)
XLA Ops:
  7.2 1.3 reshape.113.gain.gain_row
  8.6 1.6 copy.32
  10.2 2.2 slice_bitcast_fusion.2
  12.6 1.8 pad_maximum_fusion
  14.4 29.9 %shard_map.262 = (bf16[256,1024]{1,0:T(8,128)(2,1)}, bf16[2048,1024]{1,0:T(8,128)(2,1)}) custom-call(bf16[256,2048]{1,0:T(8,128)(2,1)} %bitcast.89, bf16[1,2048]{1,0:T(2,128)(2,1)} %reshape.113.gain.gain_row, bf16[256,1024]{1,0:T(8,128)(2,1)} %get-tuple-element.113.shard), custom_call_target="tpu_custom_call" | custom-call | tf_op jit(solution)/shard_map/pallas_call | solution.py:1924
  45.3 3.4 collective-permute-start
  52.4 1.8 fusion.20
  55.2 56.7 %shard_map.263 = (f32[256,256]{1,0:T(8,128)}, f32[256,1024]{1,0:T(8,128)}, bf16[2048,1024]{1,0:T(8,128)(2,1)}, bf16[8,256,256]{2,1,0:T(8,128)(2,1)}) custom-call(f32[256,256]{1,0:T(8,128)} %fusion.10.part, bf16[256,2048]{1,0:T(8,128)(2,1)} %multiply_convert_fusion.normed.refs_0_, bf16[256,1024]{1,0:T(8,128)(2,1)} %get-tuple-element.112.shard, ...), custom_call_target="tpu_custom_call" | custom-call | tf_op jit(solution)/shard_map/pallas_call | solution.py:733
  114.4 2.9 compare_select_fusion
  117.3 62.5 %shard_map.264 = (f32[256,16,8,128]{3,2,1,0:T(8,128)}, f32[256,1024]{1,0:T(8,128)}, bf16[8192,256]{1,0:T(8,128)(2,1)}, bf16[8,256,256]{2,1,0:T(8,128)(2,1)}) custom-call(f32[256,1024]{1,0:T(8,128)} %get-tuple-element.126.step_ref, f32[256,1024]{1,0:T(8,128)} %get-tuple-element.101.input_ref, f32[4096]{0:T(1024)} %reshape.117.brow_ref, ...), custom_call_target="tpu_custom_call" | custom-call | tf_op jit(solution)/shard_map/pallas_call | solution.py:1177
  179.8 2.4 multiply_convert_fusion.2.gated.shard
  182.2 46.4 %shard_map.265 = (bf16[256,2048]{1,0:T(8,128)(2,1)}, f32[64,2048]{1,0:T(8,128)}) custom-call(bf16[256,1024]{1,0:T(8,128)(2,1)} %multiply_convert_fusion.2.gated.shard, bf16[8192,256]{1,0:T(8,128)(2,1)} %get-tuple-element.60.out_all, bf16[256,2048]{1,0:T(8,128)(2,1)} %bitcast.90, bf16[1,2048]{1,0:T(2,128)(2,1)} %reshape.120.gain), custom_call_target="tpu_custom_call" | custom-call | tf_op jit(solution)/shard_map/pallas_call | solution.py:819
  228.6 33.2 %shard_map.266 = (bf16[256,6144]{1,0:T(8,128)(2,1)}, bf16[2048,1024]{1,0:T(8,128)(2,1)}) custom-call(bf16[256,2048]{1,0:T(8,128)(2,1)} %get-tuple-element.61.normed.refs_0_, bf16[256,2048]{1,0:T(8,128)(2,1)} %bitcast.93, bf16[2048,6144]{1,0:T(8,128)(2,1)} %all-gather.3.cloned.1.call-done.weights, bf16[256,1024]{1,0:T(8,128)(2,1)} %multiply_convert_fusion.2.gated.shard), custom_call_target="tpu_custom_call" | custom-call | tf_op jit(solution)/shard_map/pallas_call | solution.py:899
  263.2 1.5 slice.139.step_low
  264.8 54.2 %shard_map.267 = (bf16[256,2048]{1,0:T(8,128)(2,1)}, f32[64,2048]{1,0:T(8,128)}, f32[1,2048]{1,0:T(1,128)}, f32[256,1024]{1,0:T(8,128)}, bf16[256,2048]{1,0:T(8,128)(2,1)}, /*index=5*/bf16[2048,256]{1,0:T(8,128)(2,1)}) custom-call(bf16[256,6144]{1,0:T(8,128)(2,1)} %get-tuple-element.63.made, bf16[256,2048]{1,0:T(8,128)(2,1)} %bitcast.94, ...), custom_call_target="tpu_custom_call" | custom-call | tf_op jit(solution)/shard_map/pallas_call | solution.py:1010
  319.0 3.9 multiply_reduce_fusion.1
  322.9 31.5 %shard_map.268 = (f32[256,1024]{1,0:T(8,128)}, f32[256,1024]{1,0:T(8,128)}, f32[16,8,128]{2,1,0:T(8,128)}, f32[256,32,128]{2,1,0:T(8,128)}, bf16[64,1024]{1,0:T(8,128)(2,1)}, /*index=5*/bf16[64,1024]{1,0:T(8,128)(2,1)}) custom-call(f32[256,1024]{1,0:T(8,128)} %get-tuple-element.126.step_ref, f32[256,1024]{1,0:T(8,128)} %get-tuple-element.101.input_ref, ...), custom_call_target="tpu_custom_call" | custom-call | tf_op jit(solution)/shard_map/pallas_call | solution.py:1388
  354.4 3.4 reduce_sum.82
  357.9 2.2 fusion.17
  361.1 16.7 %shard_map.269 = (bf16[256,256]{1,0:T(8,128)(2,1)}, bf16[256,1024]{1,0:T(8,128)(2,1)}) custom-call(bf16[256,256]{1,0:T(8,128)(2,1)} %maximum_maximum_fusion.part, bf16[64,1024]{1,0:T(8,128)(2,1)} %get-tuple-element.71.own_rows), custom_call_target="tpu_custom_call" | custom-call | tf_op jit(solution)/shard_map/pallas_call | solution.py:777
  377.8 2.5 multiply_reduce_fusion.5
  380.9 1.4 collective-permute-start.1
  384.8 2.7 collective-permute-done.1
  388.4 10.3 %all-gather.5.cloned.1.call-done.ffn_all = bf16[2048,6144]{1,0:T(8,128)(2,1)} async-done(((bf16[256,6144]{1,0:T(8,128)(2,1)}), bf16[2048,6144]{1,0:T(8,128)(2,1)}) %all-gather.5.cloned.1.call-update) | async-done | bytes 25165840 | tf_op jit(solution)/shard_map/all_gather | solution.py:366
  398.7 77.9 %shard_map.270 = (bf16[256,2048]{1,0:T(8,128)(2,1)}, bf16[256,2048]{1,0:T(8,128)(2,1)}, f32[32,1024]{1,0:T(8,128)}, f32[128,1024]{1,0:T(8,128)}, f32[160,1024]{1...) custom-call(bf16[256,1024]{1,0:T(8,128)(2,1)} %bitcast.97, ...), custom_call_target="tpu_custom_call" | custom-call | tf_op jit(solution)/shard_map/pallas_call | solution.py:1819
  476.6 1.5 fusion.23
  478.1 1.4 slice.103
  479.5 1.5 slice_bitcast_fusion.4
  482.5 2.5 copy.51
  485.9 1.3 copy.53
  490.1 2.1 copy.57
  493.3 1.3 copy.58
  (103 shorter events, 20.8 us)
Async XLA Ops:
  7.2 107.2 %copy-start = (bf16[128,1024]{1,0:T(8,128)(2,1)S(1)}, bf16[128,1024]{1,0:T(8,128)(2,1)}, u32[]{:S(2)}) copy-start(bf16[128,1024]{1,0:T(8,128)(2,1)} %param.21) | copy-start | bytes 786436
  7.2 221.4 %all-gather.3.cloned.1.call-start = ((), (), s32[]{:S(2)}) async-start(), calls=%async_computation | async-start | bytes 28311552 | tf_op jit(solution)/shard_map/all_gather | solution.py:366
  8.6 3.9 copy-start.7
  14.4 34.4 %copy-start.23 = (bf16[2048]{0:T(1024)(128)(2,1)S(1)}, bf16[2048]{0:T(1024)(128)(2,1)}, u32[]{:S(2)}) copy-start(bf16[2048]{0:T(1024)(128)(2,1)} %param.16) | copy-start | bytes 12292
  14.4 34.4 %copy-start.1 = (bf16[2,128,2048]{2,1,0:T(8,128)(2,1)S(1)}, bf16[2,128,2048]{2,1,0:T(8,128)(2,1)}, u32[]{:S(2)}) copy-start(bf16[2,128,2048]{2,1,0:T(8,128)(2,1)} %param.15) | copy-start | bytes 3145732
  44.3 4.8 copy-start.17
  44.3 6.1 %copy-start.22 = (bf16[4,1024]{1,0:T(4,128)(2,1)S(1)}, bf16[4,1024]{1,0:T(4,128)(2,1)}, u32[]{:S(2)}) copy-start(bf16[4,1024]{1,0:T(4,128)(2,1)} %param.18) | copy-start | bytes 24580
  44.3 6.1 %copy-start.25 = (bf16[1024]{0:T(1024)(128)(2,1)S(1)}, bf16[1024]{0:T(1024)(128)(2,1)}, u32[]{:S(2)}) copy-start(bf16[1024]{0:T(1024)(128)(2,1)} %param.24) | copy-start | bytes 6148
  44.4 6.1 %copy-start.26 = (bf16[1024]{0:T(1024)(128)(2,1)S(1)}, bf16[1024]{0:T(1024)(128)(2,1)}, u32[]{:S(2)}) copy-start(bf16[1024]{0:T(1024)(128)(2,1)} %param.19) | copy-start | bytes 6148
  44.4 6.1 %copy-start.27 = (bf16[1024]{0:T(1024)(128)(2,1)S(1)}, bf16[1024]{0:T(1024)(128)(2,1)}, u32[]{:S(2)}) copy-start(bf16[1024]{0:T(1024)(128)(2,1)} %param.22) | copy-start | bytes 6148
  44.4 6.1 %copy-start.24 = (bf16[2048]{0:T(1024)(128)(2,1)S(1)}, bf16[2048]{0:T(1024)(128)(2,1)}, u32[]{:S(2)}) copy-start(bf16[2048]{0:T(1024)(128)(2,1)} %param.26) | copy-start | bytes 12292
  44.4 354.4 %all-gather.5.cloned.1.call-start = ((), (), s32[]{:S(2)}) async-start(), calls=%async_computation.1 | async-start | bytes 28311552 | tf_op jit(solution)/shard_map/all_gather | solution.py:366
  45.3 6.4 %collective-permute-start = (bf16[2,3,1024]{2,1,0:T(4,128)(2,1)S(1)}, bf16[2,3,1024]{2,1,0:T(4,128)(2,1)S(1)}, u32[]{:S(2)}, u32[]{:S(2)}) collective-permute-start(bf16[2,3,1024]{2,1,0:T(4,128)(2,1)S(1)} %slice.110), channel_id=1, source_target_pairs={{0,4},{1,5},{2,6},{3,7},{8,12},{9,13},{10,14},{11,15},{16,20},{17,... | collective-permute-start | bytes 36872 | tf_op jit(solution)/shard_map/ppermute | solution.py:23
  50.4 2.0 copy-start.20
  52.4 1.8 copy-start.16
  54.2 264.8 %copy-start.2 = (bf16[256,1024]{1,0:T(8,128)(2,1)}, bf16[256,1024]{1,0:T(8,128)(2,1)S(1)}, u32[]{:S(2)}) copy-start(bf16[256,1024]{1,0:T(8,128)(2,1)S(1)} %get-tuple-element.102.scan_in) | copy-start | bytes 1572868
  117.3 62.5 %copy-start.5 = (f32[256,1024]{1,0:T(8,128)S(1)}, f32[256,1024]{1,0:T(8,128)}, u32[]{:S(2)}) copy-start(f32[256,1024]{1,0:T(8,128)} %get-tuple-element.59) | copy-start | bytes 3145732
  354.4 3.5 copy-start.10
  357.9 2.5 copy-start.28
  357.9 19.9 %copy-start.4 = (f32[256,1024]{1,0:T(8,128)S(1)}, f32[256,1024]{1,0:T(8,128)}, u32[]{:S(2)}) copy-start(f32[256,1024]{1,0:T(8,128)} %get-tuple-element.100.ograd_ref) | copy-start | bytes 3145732
  360.1 20.2 %copy-start.3 = (bf16[256,1024]{1,0:T(8,128)(2,1)}, bf16[256,1024]{1,0:T(8,128)(2,1)S(1)}, u32[]{:S(2)}) copy-start(bf16[256,1024]{1,0:T(8,128)(2,1)S(1)} %get-tuple-element.105.pre_low) | copy-start | bytes 1572868
  377.8 2.5 copy-start.21
  380.9 2.0 copy-start.18
  380.9 2.0 copy-start.19
  380.9 6.6 %collective-permute-start.1 = (f32[2,3,1024]{2,1,0:T(4,128)S(1)}, f32[2,3,1024]{2,1,0:T(4,128)S(1)}, u32[]{:S(2)}, u32[]{:S(2)}) collective-permute-start(f32[2,3,1024]{2,1,0:T(4,128)S(1)} %pad_add_fusion.1), channel_id=1, source_target_pairs={{4,0},{5,1},{6,2},{7,3},{12,8},{13,9},{14,10},{15,11},{20,16},{21,... | collective-permute-start | bytes 73736 | tf_op jit(solution)/shard_map/ppermute | solution.py:23
  476.6 8.3 %copy-start.12 = (bf16[256,2048]{1,0:T(8,128)(2,1)S(1)}, bf16[256,2048]{1,0:T(8,128)(2,1)}, u32[]{:S(2)}) copy-start(bf16[256,2048]{1,0:T(8,128)(2,1)} %get-tuple-element.86) | copy-start | bytes 3145732
  482.5 3.4 copy-start.9
  485.9 1.5 copy-start.13
  485.9 2.4 copy-start.15
  485.9 3.1 copy-start.11
  487.4 2.7 copy-start.6
  490.1 3.1 copy-start.8
  (1 other events, 1.0 us)
Sparse Core Ops, SparseCore 0:
  44.5 164.9 all-gather.2
  262.0 136.7 all-gather.4

commit v13 on v11

--- a/solution.py
+++ b/solution.py
@@ -648,26 +648,14 @@
 
 
 def select_kernel(
-    part,
-    normed,
-    shard,
-    total,
-    product,
-    gathered,
-    slots,
-    send_sem,
-    recv_sem,
-    block_buf,
-    block_sem,
-    gather_send,
-    gather_recv,
-    local_sem,
+    part, shard, total, gathered, slots, send_sem, recv_sem, gather_send, gather_recv, local_sem
 ):
     group = Group(("tp",), send_sem, recv_sem)
     gather = PlaneGather(shard, gathered, gather_send, gather_recv)
     greet([(("tp",), group.others), (PLANE, gather.others)])
+    copies = group.scatter(part, slots, 0)
     gather.begin(local_sem)
-    finish(group.scatter(part, slots, 0))
+    finish(copies)
     group.own(total)[...] = group.total(part, slots).astype(total.dtype)
     copies = group.spread(total, 1)
     gather.relay()
@@ -675,36 +663,23 @@
     finish(copies)
     gather.hand_over_last()
     gather.end()
-    product_in_blocks(normed, gathered, product, block_buf, block_sem)
-
-
-def run_select(call_id, part, normed, shard):
+
+
+def run_select(call_id, part, shard):
     count = group_size(("tp",))
     vmem = pl.BlockSpec(memory_space=pltpu.VMEM)
     hbm = pl.BlockSpec(memory_space=pltpu.HBM)
     sems = pltpu.SemaphoreType.DMA((2, count - 1))
-    rows, width = normed.shape
     return pl.pallas_call(
         select_kernel,
-        in_specs=[vmem, vmem, hbm],
-        out_specs=[vmem, vmem, hbm],
-        out_shape=[
-            jax.ShapeDtypeStruct(part.shape, part.dtype),
-            jax.ShapeDtypeStruct((rows, shard.shape[1]), jnp.float32),
-            gathered_shape(shard),
-        ],
-        scratch_shapes=[
-            slots_for(part, count),
-            sems,
-            sems,
-            pltpu.VMEM((2, width, WIDE), jnp.bfloat16),
-            pltpu.SemaphoreType.DMA((2,)),
-        ]
-        + gather_scratch(),
+        in_specs=[vmem, hbm],
+        out_specs=[vmem, hbm],
+        out_shape=[jax.ShapeDtypeStruct(part.shape, part.dtype), gathered_shape(shard)],
+        scratch_shapes=[slots_for(part, count), sems, sems] + gather_scratch(),
         compiler_params=pltpu.CompilerParams(
             collective_id=call_id, has_side_effects=True, vmem_limit_bytes=VMEM_GRANT
         ),
-    )(part, normed, shard)
+    )(part, shard)
 
 
 def sum_kernel(part, own_rows, total, all_rows, slots, send_sem, recv_sem, *line_sems):
@@ -741,7 +716,7 @@
     )(part, own_rows)
 
 
-def mixer_out_kernel(n_swaps, gated, out_all, tokens, gain, *refs):
+def mixer_out_kernel(n_swaps, gated, out_first, out_last, tokens, gain, *refs):
     arrays, refs = refs[:n_swaps], refs[n_swaps:]
     normed, middle, gated_all, *refs = refs
     swapped, refs = refs[:n_swaps], refs[n_swaps:]
@@ -751,13 +726,15 @@
     gather_send, gather_recv, local_sem, *refs = refs[7:]
     group = Group(("tp",), None, None)
     gather = PlaneGather(gated, gated_all, gather_send, gather_recv)
-    inner = gated.shape[1]
-    share = out_all.shape[1]
+    half = gated.shape[1] // 2
+    share = out_first.shape[1]
     greet([(("tp",), group.others), (PLANE, gather.others)])
     gather.begin(local_sem)
-    for at in range(out_all.shape[0] // inner):
-        part[:, at * share : (at + 1) * share] = matmul(
-            gated[...], out_all[at * inner : (at + 1) * inner, :]
+    for at in range(out_first.shape[0] // half):
+        rows = slice(at * half, (at + 1) * half)
+        part[:, at * share : (at + 1) * share] = (
+            matmul(gated[:, :half], out_first[rows, :])
+            + matmul(gated[:, half:], out_last[rows, :])
         ).astype(part.dtype)
     firsts = [line.begin(j) for j in range(line.blocks)]
     if n_swaps:
@@ -780,7 +757,7 @@
         swap.end()
 
 
-def mixer_out(call_id, gated, out_all, tokens, gain, arrays):
+def mixer_out(call_id, gated, out_first, out_last, tokens, gain, arrays):
     count = group_size(("tp",))
     vmem = pl.BlockSpec(memory_space=pltpu.VMEM)
     hbm = pl.BlockSpec(memory_space=pltpu.HBM)
@@ -788,7 +765,7 @@
     part = jax.ShapeDtypeStruct((rows, width), jnp.bfloat16)
     return pl.pallas_call(
         functools.partial(mixer_out_kernel, len(arrays)),
-        in_specs=[vmem] * (4 + len(arrays)),
+        in_specs=[vmem] * (5 + len(arrays)),
         out_specs=[vmem] * 2 + [hbm] + [hbm] * len(arrays),
         out_shape=[
             part,
@@ -804,14 +781,14 @@
         compiler_params=pltpu.CompilerParams(
             collective_id=call_id, has_side_effects=True, vmem_limit_bytes=VMEM_GRANT
         ),
-    )(gated, out_all, tokens, gain, *arrays)
+    )(gated, out_first, out_last, tokens, gain, *arrays)
 
 
 def ffn_kernel(swaps, normed, ct, weights, made, *refs):
     hidden = weights.shape[1] // 3
     if swaps:
         *swapped, block_buf, block_sem, send_sem, recv_sem, local_sem = refs
-        swap = Swap([normed], swapped, send_sem, recv_sem, local_sem)
+        swap = Swap([ct], swapped, send_sem, recv_sem, local_sem)
         greet([(PLANE, swap.plane.others)])
         swap.begin()
     else:
@@ -859,7 +836,7 @@
 
 def run_ffn(call_id, normed, ct, weights, swaps):
     rows, width = normed.shape
-    arrays = [normed] if swaps else []
+    arrays = [ct] if swaps else []
     vmem = pl.BlockSpec(memory_space=pltpu.VMEM)
     params = dict(collective_id=call_id, has_side_effects=True) if swaps else {}
     return pl.pallas_call(
@@ -878,30 +855,31 @@
 
 
 def ffn_back_kernel(
+    n_swaps,
     made,
     ct,
     middle,
     gain,
-    out_all,
+    out_first,
+    out_last,
     weights,
-    middle_low,
-    middle_grad,
-    gain_grad,
-    gated_grad,
-    ffn_part,
-    part,
-    wide_buf,
-    down_buf,
-    wide_sem,
-    down_sem,
-    *sems,
+    *refs,
 ):
+    arrays, refs = refs[:n_swaps], refs[n_swaps:]
+    middle_low, middle_grad, gain_grad, gated_grad, ffn_part, *refs = refs
+    swapped, refs = refs[:n_swaps], refs[n_swaps:]
+    part, wide_buf, down_buf, wide_sem, down_sem, *sems = refs
     hidden = made.shape[1] // 3
     blocks = part.shape[1] // WIDE
     group = Group(("tp",), None, None)
     line = LineSum(part, *sems[:5])
-    spread = LineSpread(middle_low, *sems[5:])
-    greet([(("tp",), group.others)])
+    spread = LineSpread(middle_low, *sems[5:7])
+    if n_swaps:
+        swap = Swap(arrays, swapped, *sems[7:])
+        greet([(("tp",), group.others), (PLANE, swap.plane.others)])
+        swap.begin()
+    else:
+        greet([(("tp",), group.others)])
 
     def fetch(j):
         return pltpu.make_async_copy(
@@ -946,37 +924,43 @@
     middle_grad[...] = grad
     group.own(middle_low)[...] = grad.astype(middle_low.dtype)
     spread.run()
-    inner = gated_grad.shape[1]
-    share = out_all.shape[1]
-    total = None
-    for at in range(out_all.shape[0] // inner):
-        one = matmul_nt(
-            middle_low[:, at * share : (at + 1) * share], out_all[at * inner : (at + 1) * inner, :]
-        )
-        total = one if total is None else total + one
-    gated_grad[...] = total
-
-
-def ffn_back(call_id, made, ct, middle, gain, out_all, weights):
+    half = gated_grad.shape[1] // 2
+    share = out_first.shape[1]
+    for side, shards in enumerate((out_first, out_last)):
+        total = None
+        for at in range(shards.shape[0] // half):
+            one = matmul_nt(
+                middle_low[:, at * share : (at + 1) * share],
+                shards[at * half : (at + 1) * half, :],
+            )
+            total = one if total is None else total + one
+        gated_grad[:, side * half : (side + 1) * half] = total
+    if n_swaps:
+        swap.end()
+
+
+def ffn_back(call_id, made, ct, middle, gain, out_first, out_last, weights, arrays):
     count = group_size(("tp",))
     vmem = pl.BlockSpec(memory_space=pltpu.VMEM)
+    hbm = pl.BlockSpec(memory_space=pltpu.HBM)
     rows, width = ct.shape
     hidden = made.shape[1] // 3
-    inner = out_all.shape[0] // group_size(PLANE)
+    inner = 2 * out_first.shape[0] // group_size(PLANE)
     low, full = jnp.bfloat16, jnp.float32
     part = jax.ShapeDtypeStruct((rows, width), low)
     dma = pltpu.SemaphoreType.DMA
     return pl.pallas_call(
-        ffn_back_kernel,
-        in_specs=[vmem] * 5 + [pl.BlockSpec(memory_space=pltpu.HBM)],
-        out_specs=[vmem] * 5,
+        functools.partial(ffn_back_kernel, len(arrays)),
+        in_specs=[vmem] * 6 + [hbm] + [vmem] * len(arrays),
+        out_specs=[vmem] * 5 + [hbm] * len(arrays),
         out_shape=[
             part,
             jax.ShapeDtypeStruct((rows // count, width), full),
             jax.ShapeDtypeStruct((1, width), full),
             jax.ShapeDtypeStruct((rows, inner), full),
             part,
-        ],
+        ]
+        + swap_shapes(arrays),
         scratch_shapes=[
             pltpu.VMEM(part.shape, low),
             pltpu.VMEM((2, WIDE, 2 * hidden), low),
@@ -985,11 +969,12 @@
             dma((2,)),
         ]
         + line_sum_scratch(part, width // WIDE)
-        + line_spread_scratch(),
+        + line_spread_scratch()
+        + swap_scratch(arrays),
         compiler_params=pltpu.CompilerParams(
             collective_id=call_id, has_side_effects=True, vmem_limit_bytes=VMEM_GRANT
         ),
-    )(made, ct, middle, gain, out_all, weights)
+    )(made, ct, middle, gain, out_first, out_last, weights, *arrays)
 
 
 def send_on(source, target, send_sem, recv_sem, ctx):
@@ -1015,23 +1000,11 @@
     crow_ref,
     rate_ref,
     shard,
-    prior_ref,
-    mixed_ref,
-    gathered,
-    carried,
-    ends,
-    starts,
-    prior_buf,
-    step_held,
-    input_held,
-    mixed_held,
-    prior_sem,
-    send_sem,
-    recv_sem,
-    gather_send,
-    gather_recv,
-    local_sem,
+    *refs,
 ):
+    prior_ref, mixed_ref, gathered, *refs = refs
+    carried, ends, starts, prior_buf, step_held, input_held, mixed_held, *refs = refs
+    prior_sem, send_sem, recv_sem, gather_send, gather_recv, local_sem = refs
     place = lax.axis_index("ctx")
     gather = PlaneGather(shard, gathered, gather_send, gather_recv)
     greet([(PLANE, gather.others)])
@@ -1115,7 +1088,9 @@
     gather.end()
 
 
-def scan_forward_pair(call_id, step, inputs, b_rows, c_rows, rate, seqs, shard):
+def scan_forward_pair(
+    call_id, step, inputs, b_rows, c_rows, rate, seqs, shard
+):
     n_state, tiles, _ = rate.shape
     tokens, inner = step.shape
     all_groups = tokens // SUB
@@ -1129,7 +1104,9 @@
     boundary = pltpu.VMEM((seqs, n_state, tiles, LANE), full)
     dma = pltpu.SemaphoreType.DMA
     return pl.pallas_call(
-        functools.partial(forward_pair_kernel, n_state, tiles, groups, blocks, seqs),
+        functools.partial(
+            forward_pair_kernel, n_state, tiles, groups, blocks, seqs
+        ),
         in_specs=[vmem, vmem, smem, smem, vmem, hbm],
         out_specs=[hbm, vmem, hbm],
         out_shape=[
@@ -1839,112 +1816,67 @@
     )
 
 
-class SplitSwap:
-    def __init__(self, array, swapped, plane_send, plane_recv, tp_send, tp_recv, local_sem):
-        self.plane, self.tp = Group(PLANE, plane_send, plane_recv), Group(("tp",), tp_send, tp_recv)
-        self.array, self.swapped, self.local_sem = array, swapped, local_sem
-        rows = array.shape[0] // self.tp.count
-        self.rows = pl.ds(pl.multiple_of(self.tp.me * rows, rows), rows)
-
-    def columns(self, index):
-        share = self.swapped.shape[2]
-        return self.array.at[self.rows, pl.ds(pl.multiple_of(index * share, share), share)]
-
-    def begin(self):
-        mine = self.swapped.at[self.plane.me, self.rows, :]
-        self.local = pltpu.make_async_copy(
-            self.columns(self.plane.me), mine, self.local_sem
-        )
-        self.local.start()
-        self.copies = [
-            self.plane.one(self.columns(other), mine, 0, hop)
-            for hop, other in enumerate(self.plane.others)
-        ]
-
-    def pass_on(self):
-        finish(self.copies)
-        self.local.wait()
-        here = self.swapped.at[:, self.rows, :]
-        self.copies = [self.tp.one(here, here, 0, hop) for hop in range(self.tp.count - 1)]
-
-    def end(self):
-        finish(self.copies)
-
-
 def head_kernel(
-    swaps,
     tokens,
     gain,
-    ct,
     in_conv,
+    in_gate,
     conv_in,
+    gate_mix,
     conv_all,
-    *refs,
+    gate_all,
+    normed,
+    block_buf,
+    block_sem,
+    *sems,
 ):
-    if swaps:
-        swapped, *refs = refs
-    normed, block_buf, block_sem, *sems = refs
     conv = PlaneGather(in_conv, conv_all, *sems[:2])
-    if swaps:
-        swap = SplitSwap(ct, swapped, *sems[3:])
-        greet([(PLANE, conv.others), (("tp",), swap.tp.others)])
-    else:
-        greet([(PLANE, conv.others)])
+    gate = PlaneGather(in_gate, gate_all, *sems[3:5])
+    greet([(PLANE, conv.others)])
     conv.begin(sems[2])
-    if swaps:
-        swap.begin()
+    gate.begin(sems[5])
     hidden_in = tokens[...].astype(jnp.float32)
     normed[...] = (hidden_in * inverse_rms(hidden_in) * gain[...].astype(jnp.float32)).astype(
         normed.dtype
     )
-
     conv.relay()
     conv.hand_over()
+    gate.relay()
     conv.hand_over_last()
-    if swaps:
-        swap.pass_on()
+    gate.hand_over()
     conv.end()
     product_in_blocks(normed, conv_all, conv_in, block_buf, block_sem)
-    if swaps:
-        swap.end()
-
-
-def run_head(call_id, tokens, gain, ct, shard, swaps):
+    gate.hand_over_last()
+    gate.end()
+    product_in_blocks(normed, gate_all, gate_mix, block_buf, block_sem)
+
+
+def run_head(call_id, tokens, gain, inproj):
     rows, width = tokens.shape
-    inner = shard.shape[1]
+    inner = inproj.shape[2]
     low = jnp.bfloat16
     vmem = pl.BlockSpec(memory_space=pltpu.VMEM)
     hbm = pl.BlockSpec(memory_space=pltpu.HBM)
-    count, tp_count = group_size(PLANE), group_size(("tp",))
-    dma = pltpu.SemaphoreType.DMA
-    swap_sems = [
-        dma((1, count - 1)),
-        dma((1, count - 1)),
-        dma((1, tp_count - 1)),
-        dma((1, tp_count - 1)),
-        dma(()),
-    ]
-    swapped = [jax.ShapeDtypeStruct((count, rows, width // count), low)]
     return pl.pallas_call(
-        functools.partial(head_kernel, swaps),
-        in_specs=[vmem] * 3 + [hbm],
-        out_specs=[vmem] + [hbm] * (2 if swaps else 1),
+        head_kernel,
+        in_specs=[vmem] * 2 + [hbm] * 2,
+        out_specs=[vmem] * 2 + [hbm] * 2,
         out_shape=[
             jax.ShapeDtypeStruct((rows, inner), low),
+            jax.ShapeDtypeStruct((rows, inner), jnp.float32),
             jax.ShapeDtypeStruct((width, inner), low),
-        ]
-        + (swapped if swaps else []),
+            jax.ShapeDtypeStruct((width, inner), low),
+        ],
         scratch_shapes=[
             pltpu.VMEM((rows, width), low),
             pltpu.VMEM((2, width, WIDE), low),
             pltpu.SemaphoreType.DMA((2,)),
         ]
-        + gather_scratch()
-        + (swap_sems if swaps else []),
+        + gather_scratch() * 2,
         compiler_params=pltpu.CompilerParams(
             collective_id=call_id, has_side_effects=True, vmem_limit_bytes=VMEM_GRANT
         ),
-    )(tokens, gain, ct, shard)
+    )(tokens, gain, inproj[0], inproj[1])
 
 
 def per_device(
@@ -1984,14 +1916,10 @@
     tokens_rows = tokens.reshape(rows, width)
     ct_low = cotangent.reshape(rows, width)
     swap_now = swaps_in_kernels(width)
-    conv_in, in_conv, *swapped = run_head(
-        5, tokens_rows, gain_mix_row, ct_low, inproj[0], swap_now
+    ffn_pack = gathered_rows(
+        jnp.concatenate([gateup[0], gateup[1], jnp.transpose(downproj)], 1)
     )
-    ffn_pack, conv_in = lax.optimization_barrier(
-        (jnp.concatenate([gateup[0], gateup[1], jnp.transpose(downproj)], 1), conv_in)
-    )
-    ffn_pack = gathered_rows(ffn_pack)
-    ct_cols = swapped[0].reshape(-1, swapped[0].shape[2]) if swapped else swapped_columns(ct_low)
+    conv_in, gate_mix, in_conv, in_gate = run_head(5, tokens_rows, gain_mix_row, inproj)
     hidden_in = tokens_rows.astype(jnp.float32)
     scale_one = inverse_rms(hidden_in)
     normed_one = (hidden_in * scale_one * gain_mix).astype(low)
@@ -2008,9 +1936,13 @@
     columns = selproj.shape[1]
     select_width = -(-columns // LANE) * LANE
     select_weights = jnp.pad(selproj, ((0, 0), (0, select_width - columns)))
-    select_cols, gate_mix, in_gate = run_select(
-        0, matmul(scan_in, select_weights), normed_one, inproj[1]
-    )
+    select_cols, out_first = run_select(0, matmul(scan_in, select_weights), outproj[: inner // 2])
+
+    def columns_of(swapped, array):
+        if not swapped:
+            return swapped_columns(array)
+        return swapped[0].reshape(-1, swapped[0].shape[-1])
+
     step_low = select_cols[:, :rank].astype(low)
     b_rows = select_cols[:, rank : rank + n_state].reshape(-1)
     c_rows = select_cols[:, rank + n_state : columns].reshape(-1)
@@ -2018,8 +1950,15 @@
     step_size = jax.nn.softplus(step_pre)
     in_pairs = lax.axis_size("ctx") == 2
     if in_pairs:
-        prior, scan_out, out_all = scan_forward_pair(
-            6, step_size, scan_float, b_rows, c_rows, rate, seqs, outproj
+        prior, scan_out, out_last = scan_forward_pair(
+            6,
+            step_size,
+            scan_float,
+            b_rows,
+            c_rows,
+            rate,
+            seqs,
+            outproj[inner // 2 :],
         )
     else:
         span_decay = jnp.exp(
@@ -2028,25 +1967,35 @@
         ends = scan_ends(step_size, scan_float, b_rows, rate, seqs, False)
         start = from_earlier(ends, span_decay, 1)
         prior, scan_out = scan_forward(start, step_size, scan_float, b_rows, c_rows, rate, seqs)
-        out_all = gathered_rows(outproj)
+        out_last = gathered_rows(outproj[inner // 2 :])
     mixer_core = scan_out + skip_weight[None] * scan_float
     gate_sig = jax.nn.silu(gate_mix)
     gated = (mixer_core * gate_sig).astype(low)
     normed_two, middle, gated_all, *swapped = mixer_out(
         1,
         gated,
-        out_all,
+        out_first,
+        out_last,
         tokens_rows,
         gain_ffn_row,
         [normed_one] if swap_now else [],
     )
-    (normed_one_cols,) = swapped if swap_now else [swapped_columns(normed_one)]
+    normed_one_cols = columns_of(swapped, normed_one)
     made, *swapped = run_ffn(8, normed_two, ct_low, ffn_pack, swap_now)
-    (normed_two_cols,) = swapped or [swapped_columns(normed_two)]
+    ct_cols = columns_of(swapped, ct_low)
     ffn_all = gathered_rows(made)
-    middle_low, middle_grad, ffngain_part, gated_grad, ffn_part = ffn_back(
-        2, made, ct_low, middle, gain_ffn_row, out_all, ffn_pack
+    middle_low, middle_grad, ffngain_part, gated_grad, ffn_part, *swapped = ffn_back(
+        2,
+        made,
+        ct_low,
+        middle,
+        gain_ffn_row,
+        out_first,
+        out_last,
+        ffn_pack,
+        [normed_two] if swap_now else [],
     )
+    normed_two_cols = columns_of(swapped, normed_two)
     core_grad = gated_grad * gate_sig
     gate_mix_grad = (gated_grad * mixer_core * silu_slope(gate_mix)).astype(low)
     grad_skipgain = jnp.sum(core_grad * scan_float, 0)

time: 501 us -> 476 us (0.950)
  Pallas kernels: 410 us -> 381 us
    pallas_call x1, Pallas kernels: 67.4 us -> 47.9 us  [mixer_out(): pl.pallas_call(functools.partial(mixer_out_kernel, len(arrays)), in_specs...]
    pallas_call x1, Pallas kernels: 48.5 us -> 35.4 us  [scan_forward_pair(): pl.pallas_call(functools.partial(forward_pair_kernel, n_state, tiles, gro...]
    unnamed x69 -> x73, local copies, waits for them, and re-layouts: 16.2 us -> 16.2 us
  transfers between devices with their start and end apart: 4 -> 4, of which waited for: 3 -> 2; matrix products, arithmetic and copies ran while one was open for 7% -> 8% of each run, Pallas kernels for 53% -> 60%
where the time goes in v13:
time: 476 us; the launch traced here: 475 us
  Pallas kernels  381 us (80%)
  local copies, waits for them, and re-layouts  30.5 us (6%)
  other arithmetic  22.3 us (5%)
  between operations  14.6 us (3%)
  waiting for transfers between devices  13.8 us (3%)
  matrix products  7.08 us (1%)
  starting transfers between devices  6.04 us (1%)
    pallas_call x1, Pallas kernels, run_tail(): pl.pallas_call(functools.partial(tail_kernel, swaps), in_specs=[vmem] * 1...  77.9 us
    pallas_call x1, Pallas kernels, run_head(): pl.pallas_call(head_kernel, in_specs=[vmem] * 2 + [hbm] * 2, out_specs=[v...  74.6 us
    pallas_call x1, Pallas kernels, ffn_back(): pl.pallas_call(functools.partial(ffn_back_kernel, len(arrays)), in_specs=...  52.7 us
    pallas_call x1, Pallas kernels, mixer_out(): pl.pallas_call(functools.partial(mixer_out_kernel, len(arrays)), in_specs...  47.9 us
    pallas_call x1, Pallas kernels, scan_forward_pair(): pl.pallas_call(functools.partial(forward_pair_kernel, n_state, tiles, gro...  35.4 us
    pallas_call x1, Pallas kernels, scan_backward_pair(): pl.pallas_call(functools.partial(backward_pair_kernel, len(arrays), n_sta...  32 us
    pallas_call x1, Pallas kernels, run_select(): pl.pallas_call(select_kernel, in_specs=[vmem, hbm], out_specs=[vmem, hbm]...  25.4 us
    pallas_call x1, Pallas kernels, run_ffn(): pl.pallas_call(functools.partial(ffn_kernel, swaps), in_specs=[vmem, vmem...  18.7 us
  transfers between devices with their start and end apart: 4, of which 2 were waited for; matrix products, arithmetic and copies ran while one was open for 8% of the time, Pallas kernels for 60%

profile of v13, /device:TPU:0, one launch (start us, length us, event | category | flops | bytes accessed | tf_op | source)
XLA Modules:
  0.0 474.8 jit_solution(7941290681875007862)
XLA Ops:
  7.3 1.6 copy.32
  9.3 1.8 pad_maximum_fusion
  13.4 74.6 %shard_map.262 = (bf16[256,1024]{1,0:T(8,128)(2,1)}, f32[256,1024]{1,0:T(8,128)}, bf16[2048,1024]{1,0:T(8,128)(2,1)}, bf16[2048,1024]{1,0:T(8,128)(2,1)}) custom-call(bf16[256,2048]{1,0:T(8,128)(2,1)} %bitcast.87, bf16[1,2048]{1,0:T(2,128)(2,1)} %reshape.107.gain.gain_row, bf16[256,1024]{1,0:T(8,128)(2,1)} %get-tuple-element.112.in_conv, ...), custom_call_target="tpu_custom_call" | custom-call | tf_op jit(solution)/shard_map/pallas_call | solution.py:1860
  88.8 4.5 collective-permute-start
  94.6 1.3 multiply_convert_fusion.refs_0_
  97.9 1.8 fusion.20
  100.7 25.4 %shard_map.263 = (f32[256,256]{1,0:T(8,128)}, bf16[4096,256]{1,0:T(8,128)(2,1)}) custom-call(f32[256,256]{1,0:T(8,128)} %fusion.10.part, bf16[512,256]{1,0:T(8,128)(2,1)} %get-tuple-element.114.shard), custom_call_target="tpu_custom_call" | custom-call | tf_op jit(solution)/shard_map/pallas_call | solution.py:673
  126.1 1.1 fusion.23
  128.6 3.0 compare_select_fusion
  131.6 35.4 %shard_map.264 = (f32[256,16,8,128]{3,2,1,0:T(8,128)}, f32[256,1024]{1,0:T(8,128)}, bf16[4096,256]{1,0:T(8,128)(2,1)}) custom-call(f32[256,1024]{1,0:T(8,128)} %get-tuple-element.126.step_ref, f32[256,1024]{1,0:T(8,128)} %get-tuple-element.99.input_ref, f32[4096]{0:T(1024)} %reshape.110.brow_ref, f32[4096]{0:T(1024)} %reshape.111.crow_ref, ...), custom_call_target="tpu_custom_call" | custom-call | tf_op jit(solution)/shard_map/pallas_call | solution.py:1106
  167.0 2.4 multiply_convert_fusion.2.gated
  169.4 47.9 %shard_map.265 = (bf16[256,2048]{1,0:T(8,128)(2,1)}, f32[64,2048]{1,0:T(8,128)}, bf16[2048,1024]{1,0:T(8,128)(2,1)}, bf16[2048,256]{1,0:T(8,128)(2,1)}) custom-call(bf16[256,1024]{1,0:T(8,128)(2,1)} %multiply_convert_fusion.2.gated, bf16[4096,256]{1,0:T(8,128)(2,1)} %get-tuple-element.58.out_first, bf16[4096,256]{1,0:T(8,128)(2,1)} %get-tuple-element.59.out_last, ...), custom_call_target="tpu_custom_call" | custom-call | tf_op jit(solution)/shard_map/pallas_call | solution.py:766
  217.3 18.7 %shard_map.266 = (bf16[256,6144]{1,0:T(8,128)(2,1)}, bf16[2048,256]{1,0:T(8,128)(2,1)}) custom-call(bf16[256,2048]{1,0:T(8,128)(2,1)} %get-tuple-element.60.normed.refs_0_, bf16[256,2048]{1,0:T(8,128)(2,1)} %bitcast.92, bf16[2048,6144]{1,0:T(8,128)(2,1)} %all-gather.3.cloned.1.call-done.weights), custom_call_target="tpu_custom_call" | custom-call | tf_op jit(solution)/shard_map/pallas_call | solution.py:842
  237.4 1.5 slice.147.step_low
  239.0 52.7 %shard_map.267 = (bf16[256,2048]{1,0:T(8,128)(2,1)}, f32[64,2048]{1,0:T(8,128)}, f32[1,2048]{1,0:T(1,128)}, f32[256,1024]{1,0:T(8,128)}, bf16[256,2048]{1,0:T(8,128)(2,1)}, /*index=5*/bf16[2048,256]{1,0:T(8,128)(2,1)}) custom-call(bf16[256,6144]{1,0:T(8,128)(2,1)} %get-tuple-element.61.made, bf16[256,2048]{1,0:T(8,128)(2,1)} %bitcast.93, ...), custom_call_target="tpu_custom_call" | custom-call | tf_op jit(solution)/shard_map/pallas_call | solution.py:952
  291.6 3.9 multiply_reduce_fusion.1
  295.5 32.0 %shard_map.268 = (f32[256,1024]{1,0:T(8,128)}, f32[256,1024]{1,0:T(8,128)}, f32[16,8,128]{2,1,0:T(8,128)}, f32[256,32,128]{2,1,0:T(8,128)}, bf16[64,1024]{1,0:T(8,128)(2,1)}, /*index=5*/bf16[64,1024]{1,0:T(8,128)(2,1)}) custom-call(f32[256,1024]{1,0:T(8,128)} %get-tuple-element.126.step_ref, f32[256,1024]{1,0:T(8,128)} %get-tuple-element.99.input_ref, ...), custom_call_target="tpu_custom_call" | custom-call | tf_op jit(solution)/shard_map/pallas_call | solution.py:1315
  327.5 3.4 reduce_sum.82
  331.0 2.2 fusion.17
  334.2 16.0 %shard_map.269 = (bf16[256,256]{1,0:T(8,128)(2,1)}, bf16[256,1024]{1,0:T(8,128)(2,1)}) custom-call(bf16[256,256]{1,0:T(8,128)(2,1)} %maximum_maximum_fusion.part, bf16[64,1024]{1,0:T(8,128)(2,1)} %get-tuple-element.69.own_rows), custom_call_target="tpu_custom_call" | custom-call | tf_op jit(solution)/shard_map/pallas_call | solution.py:704
  350.3 2.7 multiply_reduce_fusion.5
  353.6 1.4 collective-permute-start.1
  357.5 2.7 collective-permute-done.1
  361.1 11.0 %all-gather.5.cloned.1.call-done.ffn_all = bf16[2048,6144]{1,0:T(8,128)(2,1)} async-done(((bf16[256,6144]{1,0:T(8,128)(2,1)}), bf16[2048,6144]{1,0:T(8,128)(2,1)}) %all-gather.5.cloned.1.call-update) | async-done | bytes 25165840 | tf_op jit(solution)/shard_map/all_gather | solution.py:366
  372.1 77.9 %shard_map.270 = (bf16[256,2048]{1,0:T(8,128)(2,1)}, bf16[256,2048]{1,0:T(8,128)(2,1)}, f32[32,1024]{1,0:T(8,128)}, f32[128,1024]{1,0:T(8,128)}, f32[160,1024]{1...) custom-call(bf16[256,1024]{1,0:T(8,128)(2,1)} %bitcast.94, ...), custom_call_target="tpu_custom_call" | custom-call | tf_op jit(solution)/shard_map/pallas_call | solution.py:1746
  450.0 1.5 fusion.24
  451.5 1.4 slice.111
  452.9 1.5 slice_bitcast_fusion.4
  455.9 2.5 copy.51
  459.3 1.3 copy.53
  463.5 2.1 copy.57
  466.6 1.3 copy.58
  (108 shorter events, 21.6 us)
Async XLA Ops:
  7.2 121.4 %copy-start = (bf16[128,1024]{1,0:T(8,128)(2,1)S(1)}, bf16[128,1024]{1,0:T(8,128)(2,1)}, u32[]{:S(2)}) copy-start(bf16[128,1024]{1,0:T(8,128)(2,1)} %param.21) | copy-start | bytes 786436
  7.2 1.9 copy-start.7
  7.2 210.1 %all-gather.3.cloned.1.call-start = ((), (), s32[]{:S(2)}) async-start(), calls=%async_computation | async-start | bytes 28311552 | tf_op jit(solution)/shard_map/all_gather | solution.py:366
  11.1 361.0 %all-gather.5.cloned.1.call-start = ((), (), s32[]{:S(2)}) async-start(), calls=%async_computation.1 | async-start | bytes 28311552 | tf_op jit(solution)/shard_map/all_gather | solution.py:366
  12.4 81.0 %copy-start.1 = (bf16[2,128,2048]{2,1,0:T(8,128)(2,1)S(1)}, bf16[2,128,2048]{2,1,0:T(8,128)(2,1)}, u32[]{:S(2)}) copy-start(bf16[2,128,2048]{2,1,0:T(8,128)(2,1)} %param.15) | copy-start | bytes 3145732
  13.4 80.3 %copy-start.19 = (bf16[1024,16]{0,1:T(8,128)(2,1)S(1)}, bf16[1024,16]{0,1:T(8,128)(2,1)}, u32[]{:S(2)}) copy-start(bf16[1024,16]{0,1:T(8,128)(2,1)} %param.23) | copy-start | bytes 98308
  13.4 80.4 %copy-start.16 = (bf16[1024,256]{1,0:T(8,128)(2,1)S(1)}, bf16[1024,256]{1,0:T(8,128)(2,1)}, u32[]{:S(2)}) copy-start(bf16[1024,256]{1,0:T(8,128)(2,1)} %param.25) | copy-start | bytes 1572868
  88.8 8.4 %collective-permute-start = (bf16[2,3,1024]{2,1,0:T(4,128)(2,1)S(1)}, bf16[2,3,1024]{2,1,0:T(4,128)(2,1)S(1)}, u32[]{:S(2)}, u32[]{:S(2)}) collective-permute-start(bf16[2,3,1024]{2,1,0:T(4,128)(2,1)S(1)} %slice.118), channel_id=1, source_target_pairs={{0,4},{1,5},{2,6},{3,7},{8,12},{9,13},{10,14},{11,15},{16,20},{17,... | collective-permute-start | bytes 36872 | tf_op jit(solution)/shard_map/ppermute | solution.py:23
  93.4 2.5 copy-start.24
  93.4 2.5 copy-start.27
  93.4 2.5 copy-start.28
  93.4 2.6 copy-start.29
  93.4 2.6 copy-start.26
  93.4 3.8 copy-start.15
  97.9 1.8 copy-start.18
  99.7 191.9 %copy-start.2 = (bf16[256,1024]{1,0:T(8,128)(2,1)}, bf16[256,1024]{1,0:T(8,128)(2,1)S(1)}, u32[]{:S(2)}) copy-start(bf16[256,1024]{1,0:T(8,128)(2,1)S(1)} %get-tuple-element.100.scan_in) | copy-start | bytes 1572868
  128.6 38.4 %copy-start.5 = (f32[256,1024]{1,0:T(8,128)S(1)}, f32[256,1024]{1,0:T(8,128)}, u32[]{:S(2)}) copy-start(f32[256,1024]{1,0:T(8,128)} %get-tuple-element.57) | copy-start | bytes 3145732
  327.5 3.5 copy-start.10
  330.9 2.5 copy-start.30
  331.0 19.3 %copy-start.4 = (f32[256,1024]{1,0:T(8,128)S(1)}, f32[256,1024]{1,0:T(8,128)}, u32[]{:S(2)}) copy-start(f32[256,1024]{1,0:T(8,128)} %get-tuple-element.98.ograd_ref) | copy-start | bytes 3145732
  333.2 19.8 %copy-start.3 = (bf16[256,1024]{1,0:T(8,128)(2,1)}, bf16[256,1024]{1,0:T(8,128)(2,1)S(1)}, u32[]{:S(2)}) copy-start(bf16[256,1024]{1,0:T(8,128)(2,1)S(1)} %get-tuple-element.103.pre_low) | copy-start | bytes 1572868
  350.2 2.8 copy-start.23
  353.6 2.0 copy-start.20
  353.6 2.0 copy-start.21
  353.6 6.6 %collective-permute-start.1 = (f32[2,3,1024]{2,1,0:T(4,128)S(1)}, f32[2,3,1024]{2,1,0:T(4,128)S(1)}, u32[]{:S(2)}, u32[]{:S(2)}) collective-permute-start(f32[2,3,1024]{2,1,0:T(4,128)S(1)} %pad_add_fusion.1), channel_id=1, source_target_pairs={{4,0},{5,1},{6,2},{7,3},{12,8},{13,9},{14,10},{15,11},{20,16},{21,... | collective-permute-start | bytes 73736 | tf_op jit(solution)/shard_map/ppermute | solution.py:23
  450.0 8.3 %copy-start.13 = (bf16[256,2048]{1,0:T(8,128)(2,1)S(1)}, bf16[256,2048]{1,0:T(8,128)(2,1)}, u32[]{:S(2)}) copy-start(bf16[256,2048]{1,0:T(8,128)(2,1)} %get-tuple-element.84) | copy-start | bytes 3145732
  455.9 3.4 copy-start.9
  459.3 1.5 copy-start.14
  459.3 2.4 copy-start.17
  459.3 3.1 copy-start.12
  460.8 2.7 copy-start.6
  463.5 3.1 copy-start.8
  (3 other events, 3.5 us)
Sparse Core Ops, SparseCore 0:
  11.2 175.7 all-gather.2
  236.2 135.8 all-gather.4

commit v14 on v13

--- a/solution.py
+++ b/solution.py
@@ -1617,6 +1617,8 @@
         normed_part[:, columns] = block.astype(normed_part.dtype)
         firsts.append(line.begin(j))
         gain_grad = jnp.sum(block * unit_rows[:, columns], 0, keepdims=True)
+        if j:
+            line.pass_on(j - 1, firsts[j - 1])
         row, at = divmod(j * WIDE, inner)
         row += SMALL_ROWS - GAIN_ROWS + 8
         vectors_own[row : row + 1, at : at + WIDE] = gain_grad
@@ -1632,7 +1634,7 @@
         select_low[...], scan_in[...]
     )[:selected].astype(small.dtype)
     small_sent = plane.scatter(small, small_slots, 0)
-    line.pass_all(firsts)
+    line.pass_on(blocks - 1, firsts[-1])
 
     def flat(at):
         return lambda block: matmul_tn(cols[at], block)
@@ -1658,16 +1660,11 @@
     down_end = hidden // WIDE
     gu_end = 3 * hidden // WIDE
     finish(loads)
+    gu_middle = (down_end + gu_end) // 2
+    to_gateup = side_by_side(grad_gateup, down_end)
     products(ffn_all, 0, down_end, tall(2), one_above_other(grad_downproj), *high)
     gather.relay()
-    products(ffn_all, down_end, gu_end, flat(1), side_by_side(grad_gateup, down_end), *wide)
-    gather.hand_over()
-    finish(small_sent)
-    plane.own(small_sum)[...] = plane.total(small, small_slots).astype(small_sum.dtype)
-    small_sent = plane.spread(small_sum, 1)
-    if swaps:
-        swap.begin()
-    layer_spread.pass_on()
+    products(ffn_all, down_end, gu_middle, flat(1), to_gateup, *wide)
     hidden_in = tp.own(tokens)[...].astype(jnp.float32)
     tp.own(tokens_grad)[...] = (
         middle_grad[...]
@@ -1679,10 +1676,18 @@
         )
     ).astype(tokens_grad.dtype)
     tokens_spread.begin()
+    layer_spread.pass_on()
+    gather.hand_over()
+    finish(small_sent)
+    plane.own(small_sum)[...] = plane.total(small, small_slots).astype(small_sum.dtype)
+    small_sent = plane.spread(small_sum, 1)
+    if swaps:
+        swap.begin()
+    products(ffn_all, gu_middle, gu_end, flat(1), to_gateup, *wide)
+    tokens_spread.pass_on()
     gather.hand_over_last()
     gather.end()
     products(mix_all, 0, 2 * inner // WIDE, flat(0), side_by_side(grad_inproj, 0), *wide)
-    tokens_spread.pass_on()
     finish(small_sent)
     gain_own[...] = small_sum[SMALL_ROWS - GAIN_ROWS : SMALL_ROWS, :].astype(jnp.float32)
     gain_sent = [tp.one(gain_own, gain_slots.at[hop], 0, hop) for hop in range(tp.count - 1)]
@@ -1816,6 +1821,9 @@
     )
 
 
+BORDER = 16
+
+
 def head_kernel(
     tokens,
     gain,
@@ -1823,13 +1831,29 @@
     in_gate,
     conv_in,
     gate_mix,
+    border,
     conv_all,
     gate_all,
     normed,
     block_buf,
     block_sem,
+    border_send,
+    border_recv,
     *sems,
 ):
+    place, places = lax.axis_index("ctx"), lax.axis_size("ctx")
+    seqs = border.shape[0] // BORDER
+    span = conv_in.shape[0] // seqs
+
+    def to_next(seq):
+        return send_on(
+            conv_in.at[pl.ds((seq + 1) * span - BORDER, BORDER), :],
+            border.at[pl.ds(seq * BORDER, BORDER), :],
+            border_send.at[seq],
+            border_recv.at[seq],
+            place + 1,
+        )
+
     conv = PlaneGather(in_conv, conv_all, *sems[:2])
     gate = PlaneGather(in_gate, gate_all, *sems[3:5])
     greet([(PLANE, conv.others)])
@@ -1846,12 +1870,32 @@
     gate.hand_over()
     conv.end()
     product_in_blocks(normed, conv_all, conv_in, block_buf, block_sem)
+
+    @pl.when(place == 0)
+    def _():
+        border[...] = jnp.zeros_like(border)
+
+    @pl.when(place < places - 1)
+    def _():
+        for seq in range(seqs):
+            to_next(seq).start()
+
     gate.hand_over_last()
     gate.end()
     product_in_blocks(normed, gate_all, gate_mix, block_buf, block_sem)
 
-
-def run_head(call_id, tokens, gain, inproj):
+    @pl.when(place < places - 1)
+    def _():
+        for seq in range(seqs):
+            to_next(seq).wait_send()
+
+    @pl.when(place > 0)
+    def _():
+        for seq in range(seqs):
+            to_next(seq).wait_recv()
+
+
+def run_head(call_id, tokens, gain, inproj, seqs):
     rows, width = tokens.shape
     inner = inproj.shape[2]
     low = jnp.bfloat16
@@ -1860,10 +1904,11 @@
     return pl.pallas_call(
         head_kernel,
         in_specs=[vmem] * 2 + [hbm] * 2,
-        out_specs=[vmem] * 2 + [hbm] * 2,
+        out_specs=[vmem] * 3 + [hbm] * 2,
         out_shape=[
             jax.ShapeDtypeStruct((rows, inner), low),
             jax.ShapeDtypeStruct((rows, inner), jnp.float32),
+            jax.ShapeDtypeStruct((seqs * BORDER, inner), low),
             jax.ShapeDtypeStruct((width, inner), low),
             jax.ShapeDtypeStruct((width, inner), low),
         ],
@@ -1871,6 +1916,8 @@
             pltpu.VMEM((rows, width), low),
             pltpu.VMEM((2, width, WIDE), low),
             pltpu.SemaphoreType.DMA((2,)),
+            pltpu.SemaphoreType.DMA((seqs,)),
+            pltpu.SemaphoreType.DMA((seqs,)),
         ]
         + gather_scratch() * 2,
         compiler_params=pltpu.CompilerParams(
@@ -1919,13 +1966,15 @@
     ffn_pack = gathered_rows(
         jnp.concatenate([gateup[0], gateup[1], jnp.transpose(downproj)], 1)
     )
-    conv_in, gate_mix, in_conv, in_gate = run_head(5, tokens_rows, gain_mix_row, inproj)
+    conv_in, gate_mix, border, in_conv, in_gate = run_head(
+        5, tokens_rows, gain_mix_row, inproj, seqs
+    )
     hidden_in = tokens_rows.astype(jnp.float32)
     scale_one = inverse_rms(hidden_in)
     normed_one = (hidden_in * scale_one * gain_mix).astype(low)
 
     conv_seqs = conv_in.reshape(seqs, span, inner)
-    rim_rows = passed_along(conv_seqs[:, span - (taps - 1) :], "ctx", 1)
+    rim_rows = border.reshape(seqs, BORDER, inner)[:, BORDER - (taps - 1) :]
     padded_in = jnp.concatenate([rim_rows, conv_seqs], 1).astype(jnp.float32)
     conv_out = kernel_bias[None, None]
     for offset in range(taps):

time: 476 us -> 475 us (level)
    unnamed x73 -> x71, local copies, waits for them, and re-layouts: 16.2 us -> 16.1 us
  transfers between devices with their start and end apart: 4 -> 3, of which waited for: 2 -> 2; matrix products, arithmetic and copies ran while one was open for 8% -> 8% of each run, Pallas kernels for 60% -> 62%
where the time goes in v14:
time: 475 us; the launch traced here: 473 us
  Pallas kernels  385 us (81%)
  local copies, waits for them, and re-layouts  30.5 us (6%)
  other arithmetic  23.8 us (5%)
  between operations  14.5 us (3%)
  waiting for transfers between devices  10.8 us (2%)
  matrix products  6.89 us (1%)
    pallas_call x1, Pallas kernels, run_head(): pl.pallas_call(head_kernel, in_specs=[vmem] * 2 + [hbm] * 2, out_specs=[v...  76.2 us
    pallas_call x1, Pallas kernels, run_tail(): pl.pallas_call(functools.partial(tail_kernel, swaps), in_specs=[vmem] * 1...  75.6 us
    pallas_call x1, Pallas kernels, ffn_back(): pl.pallas_call(functools.partial(ffn_back_kernel, len(arrays)), in_specs=...  54.3 us
    pallas_call x1, Pallas kernels, mixer_out(): pl.pallas_call(functools.partial(mixer_out_kernel, len(arrays)), in_specs...  47.5 us
    pallas_call x1, Pallas kernels, scan_forward_pair(): pl.pallas_call(functools.partial(forward_pair_kernel, n_state, tiles, gro...  34.3 us
    pallas_call x1, Pallas kernels, scan_backward_pair(): pl.pallas_call(functools.partial(backward_pair_kernel, len(arrays), n_sta...  31.8 us
    pallas_call x1, Pallas kernels, run_select(): pl.pallas_call(select_kernel, in_specs=[vmem, hbm], out_specs=[vmem, hbm]...  28.9 us
    pallas_call x1, Pallas kernels, run_ffn(): pl.pallas_call(functools.partial(ffn_kernel, swaps), in_specs=[vmem, vmem...  18.2 us
  transfers between devices with their start and end apart: 3, of which 2 were waited for; matrix products, arithmetic and copies ran while one was open for 8% of the time, Pallas kernels for 62%

profile of v14, /device:TPU:0, one launch (start us, length us, event | category | flops | bytes accessed | tf_op | source)
XLA Modules:
  0.0 473.0 jit_solution(7867842942246363399)
XLA Ops:
  7.3 1.6 copy.32
  9.3 1.8 pad_maximum_fusion
  14.7 76.2 %shard_map.262 = (bf16[256,1024]{1,0:T(8,128)(2,1)}, f32[256,1024]{1,0:T(8,128)}, bf16[32,1024]{1,0:T(8,128)(2,1)}, bf16[2048,1024]{1,0:T(8,128)(2,1)}, bf16[2048,1024]{1,0:T(8,128)(2,1)}) custom-call(bf16[256,2048]{1,0:T(8,128)(2,1)} %bitcast.88, bf16[1,2048]{1,0:T(2,128)(2,1)} %reshape.110.gain.gain_row, bf16[256,1024]{1,0:T(8,128)(2,1)} %get-tuple-element.114.in_conv, ...), custom_call_target="tpu_custom_call" | custom-call | tf_op jit(solution)/shard_map/pallas_call | solution.py:1904
  91.7 1.2 maximum_convert_fusion
  94.3 1.8 fusion.20
  97.1 28.9 %shard_map.263 = (f32[256,256]{1,0:T(8,128)}, bf16[4096,256]{1,0:T(8,128)(2,1)}) custom-call(f32[256,256]{1,0:T(8,128)} %fusion.10.part, bf16[512,256]{1,0:T(8,128)(2,1)} %get-tuple-element.116.shard), custom_call_target="tpu_custom_call" | custom-call | tf_op jit(solution)/shard_map/pallas_call | solution.py:673
  126.0 1.1 fusion.23
  128.5 3.0 compare_select_fusion
  131.5 34.3 %shard_map.264 = (f32[256,16,8,128]{3,2,1,0:T(8,128)}, f32[256,1024]{1,0:T(8,128)}, bf16[4096,256]{1,0:T(8,128)(2,1)}) custom-call(f32[256,1024]{1,0:T(8,128)} %get-tuple-element.128.step_ref, f32[256,1024]{1,0:T(8,128)} %get-tuple-element.101.input_ref, f32[4096]{0:T(1024)} %reshape.114.brow_ref, f32[4096]{0:T(1024)} %reshape.115.crow_ref, ...), custom_call_target="tpu_custom_call" | custom-call | tf_op jit(solution)/shard_map/pallas_call | solution.py:1106
  166.1 2.9 multiply_convert_fusion.2.gated
  168.9 1.3 multiply_convert_fusion.refs_0_
  170.2 47.5 %shard_map.265 = (bf16[256,2048]{1,0:T(8,128)(2,1)}, f32[64,2048]{1,0:T(8,128)}, bf16[2048,1024]{1,0:T(8,128)(2,1)}, bf16[2048,256]{1,0:T(8,128)(2,1)}) custom-call(bf16[256,1024]{1,0:T(8,128)(2,1)} %multiply_convert_fusion.2.gated, bf16[4096,256]{1,0:T(8,128)(2,1)} %get-tuple-element.60.out_first, bf16[4096,256]{1,0:T(8,128)(2,1)} %get-tuple-element.61.out_last, ...), custom_call_target="tpu_custom_call" | custom-call | tf_op jit(solution)/shard_map/pallas_call | solution.py:766
  217.7 18.2 %shard_map.266 = (bf16[256,6144]{1,0:T(8,128)(2,1)}, bf16[2048,256]{1,0:T(8,128)(2,1)}) custom-call(bf16[256,2048]{1,0:T(8,128)(2,1)} %get-tuple-element.62.normed.refs_0_, bf16[256,2048]{1,0:T(8,128)(2,1)} %bitcast.93, bf16[2048,6144]{1,0:T(8,128)(2,1)} %all-gather.3.cloned.1.call-done.weights), custom_call_target="tpu_custom_call" | custom-call | tf_op jit(solution)/shard_map/pallas_call | solution.py:842
  236.0 1.5 slice.147.step_low
  238.9 54.3 %shard_map.267 = (bf16[256,2048]{1,0:T(8,128)(2,1)}, f32[64,2048]{1,0:T(8,128)}, f32[1,2048]{1,0:T(1,128)}, f32[256,1024]{1,0:T(8,128)}, bf16[256,2048]{1,0:T(8,128)(2,1)}, /*index=5*/bf16[2048,256]{1,0:T(8,128)(2,1)}) custom-call(bf16[256,6144]{1,0:T(8,128)(2,1)} %get-tuple-element.63.made, bf16[256,2048]{1,0:T(8,128)(2,1)} %bitcast.94, ...), custom_call_target="tpu_custom_call" | custom-call | tf_op jit(solution)/shard_map/pallas_call | solution.py:952
  293.3 3.9 multiply_reduce_fusion.1
  297.2 31.8 %shard_map.268 = (f32[256,1024]{1,0:T(8,128)}, f32[256,1024]{1,0:T(8,128)}, f32[16,8,128]{2,1,0:T(8,128)}, f32[256,32,128]{2,1,0:T(8,128)}, bf16[64,1024]{1,0:T(8,128)(2,1)}, /*index=5*/bf16[64,1024]{1,0:T(8,128)(2,1)}) custom-call(f32[256,1024]{1,0:T(8,128)} %get-tuple-element.128.step_ref, f32[256,1024]{1,0:T(8,128)} %get-tuple-element.101.input_ref, ...), custom_call_target="tpu_custom_call" | custom-call | tf_op jit(solution)/shard_map/pallas_call | solution.py:1315
  329.0 3.4 reduce_sum.82
  332.5 2.2 fusion.17
  335.7 18.2 %shard_map.269 = (bf16[256,256]{1,0:T(8,128)(2,1)}, bf16[256,1024]{1,0:T(8,128)(2,1)}) custom-call(bf16[256,256]{1,0:T(8,128)(2,1)} %maximum_maximum_fusion.part, bf16[64,1024]{1,0:T(8,128)(2,1)} %get-tuple-element.71.own_rows), custom_call_target="tpu_custom_call" | custom-call | tf_op jit(solution)/shard_map/pallas_call | solution.py:704
  353.9 2.5 multiply_reduce_fusion.5
  357.0 1.4 collective-permute-start
  360.9 2.7 collective-permute-done
  364.6 8.0 %all-gather.5.cloned.1.call-done.ffn_all = bf16[2048,6144]{1,0:T(8,128)(2,1)} async-done(((bf16[256,6144]{1,0:T(8,128)(2,1)}), bf16[2048,6144]{1,0:T(8,128)(2,1)}) %all-gather.5.cloned.1.call-update) | async-done | bytes 25165840 | tf_op jit(solution)/shard_map/all_gather | solution.py:366
  372.6 75.6 %shard_map.270 = (bf16[256,2048]{1,0:T(8,128)(2,1)}, bf16[256,2048]{1,0:T(8,128)(2,1)}, f32[32,1024]{1,0:T(8,128)}, f32[128,1024]{1,0:T(8,128)}, f32[160,1024]{1...) custom-call(bf16[256,1024]{1,0:T(8,128)(2,1)} %bitcast.95, ...), custom_call_target="tpu_custom_call" | custom-call | tf_op jit(solution)/shard_map/pallas_call | solution.py:1751
  448.2 1.5 fusion.24
  449.7 1.4 slice.111
  451.0 1.5 slice_bitcast_fusion.4
  454.0 2.5 copy.51
  457.5 1.3 copy.53
  461.7 2.1 copy.57
  464.8 1.3 copy.58
  (104 shorter events, 21.5 us)
Async XLA Ops:
  7.2 121.3 %copy-start = (bf16[128,1024]{1,0:T(8,128)(2,1)S(1)}, bf16[128,1024]{1,0:T(8,128)(2,1)}, u32[]{:S(2)}) copy-start(bf16[128,1024]{1,0:T(8,128)(2,1)} %param.21) | copy-start | bytes 786436
  7.2 1.9 copy-start.7
  7.2 210.5 %all-gather.3.cloned.1.call-start = ((), (), s32[]{:S(2)}) async-start(), calls=%async_computation | async-start | bytes 28311552 | tf_op jit(solution)/shard_map/all_gather | solution.py:366
  11.1 1.3 copy-start.26
  11.1 1.3 copy-start.27
  11.1 1.3 copy-start.28
  11.1 1.3 copy-start.25
  11.1 1.9 copy-start.18
  11.1 2.6 copy-start.11
  11.1 361.4 %all-gather.5.cloned.1.call-start = ((), (), s32[]{:S(2)}) async-start(), calls=%async_computation.1 | async-start | bytes 28311552 | tf_op jit(solution)/shard_map/all_gather | solution.py:366
  14.7 78.2 %copy-start.23 = (bf16[4,1024]{1,0:T(4,128)(2,1)S(1)}, bf16[4,1024]{1,0:T(4,128)(2,1)}, u32[]{:S(2)}) copy-start(bf16[4,1024]{1,0:T(4,128)(2,1)} %param.18) | copy-start | bytes 24580
  14.7 78.2 %copy-start.15 = (bf16[1024,256]{1,0:T(8,128)(2,1)S(1)}, bf16[1024,256]{1,0:T(8,128)(2,1)}, u32[]{:S(2)}) copy-start(bf16[1024,256]{1,0:T(8,128)(2,1)} %param.25) | copy-start | bytes 1572868
  93.0 1.3 copy-start.21
  94.3 1.8 copy-start.17
  96.1 197.2 %copy-start.2 = (bf16[256,1024]{1,0:T(8,128)(2,1)}, bf16[256,1024]{1,0:T(8,128)(2,1)S(1)}, u32[]{:S(2)}) copy-start(bf16[256,1024]{1,0:T(8,128)(2,1)S(1)} %get-tuple-element.102.scan_in) | copy-start | bytes 1572868
  128.5 37.3 %copy-start.1 = (bf16[2,128,2048]{2,1,0:T(8,128)(2,1)S(1)}, bf16[2,128,2048]{2,1,0:T(8,128)(2,1)}, u32[]{:S(2)}) copy-start(bf16[2,128,2048]{2,1,0:T(8,128)(2,1)} %param.15) | copy-start | bytes 3145732
  238.9 54.4 %copy-start.5 = (f32[256,1024]{1,0:T(8,128)S(1)}, f32[256,1024]{1,0:T(8,128)}, u32[]{:S(2)}) copy-start(f32[256,1024]{1,0:T(8,128)} %get-tuple-element.59) | copy-start | bytes 3145732
  329.0 3.5 copy-start.10
  332.5 2.5 copy-start.29
  332.5 21.4 %copy-start.4 = (f32[256,1024]{1,0:T(8,128)S(1)}, f32[256,1024]{1,0:T(8,128)}, u32[]{:S(2)}) copy-start(f32[256,1024]{1,0:T(8,128)} %get-tuple-element.100.ograd_ref) | copy-start | bytes 3145732
  334.7 21.8 %copy-start.3 = (bf16[256,1024]{1,0:T(8,128)(2,1)}, bf16[256,1024]{1,0:T(8,128)(2,1)S(1)}, u32[]{:S(2)}) copy-start(bf16[256,1024]{1,0:T(8,128)(2,1)S(1)} %get-tuple-element.105.pre_low) | copy-start | bytes 1572868
  353.9 2.6 copy-start.22
  357.0 2.0 copy-start.19
  357.0 2.0 copy-start.20
  357.0 6.6 %collective-permute-start = (f32[2,3,1024]{2,1,0:T(4,128)S(1)}, f32[2,3,1024]{2,1,0:T(4,128)S(1)}, u32[]{:S(2)}, u32[]{:S(2)}) collective-permute-start(f32[2,3,1024]{2,1,0:T(4,128)S(1)} %pad_add_fusion.1), channel_id=1, source_target_pairs={{4,0},{5,1},{6,2},{7,3},{12,8},{13,9},{14,10},{15,11},{20,16},{21,... | collective-permute-start | bytes 73736 | tf_op jit(solution)/shard_map/ppermute | solution.py:23
  448.2 8.3 %copy-start.13 = (bf16[256,2048]{1,0:T(8,128)(2,1)S(1)}, bf16[256,2048]{1,0:T(8,128)(2,1)}, u32[]{:S(2)}) copy-start(bf16[256,2048]{1,0:T(8,128)(2,1)} %get-tuple-element.86) | copy-start | bytes 3145732
  454.0 3.4 copy-start.9
  457.5 1.5 copy-start.14
  457.5 2.4 copy-start.16
  457.5 3.1 copy-start.12
  459.0 2.7 copy-start.6
  461.7 3.1 copy-start.8
  (1 other events, 0.7 us)
Sparse Core Ops, SparseCore 0:
  11.3 180.4 all-gather.2
  236.1 136.4 all-gather.4

commit v15 on v14

--- a/solution.py
+++ b/solution.py
@@ -1487,6 +1487,103 @@
         store(j, j % 2).wait()
 
 
+class PlaneSum:
+    def __init__(self, array, total, *refs):
+        self.array, self.result = array, total
+        self.hands_on = relayed()
+        if not self.hands_on:
+            self.slots, send_sem, recv_sem = refs
+            self.group = Group(PLANE, send_sem, recv_sem)
+            return
+        self.core_slot, self.pair, self.chip_slots, *self.sems = refs
+        dp, ctx = lax.axis_index("dp"), lax.axis_index("ctx")
+        self.half = lax.rem(dp, 2)
+        self.other_core = {"dp": dp + 1 - 2 * self.half, "ctx": ctx}
+        over_y, over_x = lax.rem(dp + 2, 4), 1 - ctx
+        self.quarter = lax.div(dp, 2) * 2 + ctx
+        self.chips = [
+            ({"dp": a, "ctx": b}, lax.div(a, 2) * 2 + b)
+            for a, b in ((dp, over_x), (over_y, ctx), (over_y, over_x))
+        ]
+
+    def to_core(self, source, target, which):
+        core_send, core_recv = self.sems[:2]
+        return sent(
+            source, target, core_send.at[which], core_recv.at[which], self.other_core
+        )
+
+    def to_chip(self, source, target, which, at):
+        chip_send, chip_recv = self.sems[2:]
+        return sent(
+            source,
+            target,
+            chip_send.at[which, at],
+            chip_recv.at[which, at],
+            self.chips[at][0],
+        )
+
+    def begin(self):
+        if not self.hands_on:
+            self.copies = self.group.scatter(self.array, self.slots, 0)
+            return
+        self.copies = [self.to_core(rows_of(self.array, 1 - self.half, 2), self.core_slot, 0)]
+
+    def add_pair(self):
+        if not self.hands_on:
+            return
+        finish(self.copies)
+        self.pair[...] = (
+            rows_of(self.array, self.half, 2)[...].astype(jnp.float32)
+            + self.core_slot[...].astype(jnp.float32)
+        ).astype(self.pair.dtype)
+        self.copies = [
+            self.to_chip(rows_of(self.pair, index, 4), self.chip_slots.at[at], 0, at)
+            for at, (_, index) in enumerate(self.chips)
+        ]
+
+    def add_all(self):
+        finish(self.copies)
+        if not self.hands_on:
+            self.group.own(self.result)[...] = self.group.total(self.array, self.slots).astype(
+                self.result.dtype
+            )
+            self.copies = self.group.spread(self.result, 1)
+            return
+        total = rows_of(self.pair, self.quarter, 4)[...].astype(jnp.float32)
+        for at in range(3):
+            total = total + self.chip_slots[at].astype(jnp.float32)
+        mine = rows_of(self.result, self.half * 4 + self.quarter, 8)
+        mine[...] = total.astype(self.result.dtype)
+        self.copies = [self.to_chip(mine, mine, 1, at) for at in range(3)]
+
+    def hand_over(self):
+        if not self.hands_on:
+            return
+        finish(self.copies)
+        half = rows_of(self.result, self.half, 2)
+        self.copies = [self.to_core(half, half, 1)]
+
+    def end(self):
+        finish(self.copies)
+
+
+def plane_sum_scratch(array):
+    dma = pltpu.SemaphoreType.DMA
+    count = group_size(PLANE)
+    if not relayed():
+        return [slots_for(array, count), dma((2, count - 1)), dma((2, count - 1))]
+    rows, width = array.shape
+    return [
+        pltpu.VMEM((rows // 2, width), array.dtype),
+        pltpu.VMEM((rows // 2, width), array.dtype),
+        pltpu.VMEM((3, rows // 8, width), array.dtype),
+        dma((2,)),
+        dma((2,)),
+        dma((2, 3)),
+        dma((2, 3)),
+    ]
+
+
 SMALL_ROWS = 32
 GAIN_ROWS = 16
 
@@ -1534,7 +1631,6 @@
     normed_part,
     small,
     small_sum,
-    small_slots,
     gain_slots,
     gain_own,
     vectors_own,
@@ -1550,8 +1646,6 @@
     tall_sem,
     tp_send,
     tp_recv,
-    plane_send,
-    plane_recv,
     gather_send,
     gather_recv,
     local_sem,
@@ -1562,12 +1656,13 @@
     width = tokens.shape[1]
     rank = step_low.shape[1]
     tp = Group(("tp",), tp_send, tp_recv)
-    plane = Group(PLANE, plane_send, plane_recv)
     line = LineSum(normed_part, *sems[:5])
     tokens_spread = LineSpread(tokens_grad, *sems[5:7])
     layer_last = layer_out.at[:, width // 2 :]
     layer_spread = LineSpread(layer_last, *sems[7:9])
-    swap_sems = sems[9:]
+    count = 7 if relayed() else 3
+    small_total = PlaneSum(small, small_sum, *sems[9 : 9 + count])
+    swap_sems = sems[9 + count :]
     gather = PlaneGather(mix_own, mix_all, gather_send, gather_recv)
     sources = (one_cols, two_cols, ct_cols) if swaps else (one_cols, two_cols, ct_cols, middle_cols)
     loads = [
@@ -1589,7 +1684,7 @@
         copy.start()
     mix_own[:, :inner] = conv_grad[...]
     mix_own[:, inner:] = gate_grad[...]
-    greet([(("tp",), tp.others), (PLANE, plane.others)])
+    greet([(("tp",), tp.others), (PLANE, gather.others)])
     gather.begin(local_sem)
 
     small[...] = jnp.zeros_like(small)
@@ -1633,7 +1728,7 @@
     small[SMALL_ROWS + rank : SMALL_ROWS + rank + selected, :] = matmul_tn(
         select_low[...], scan_in[...]
     )[:selected].astype(small.dtype)
-    small_sent = plane.scatter(small, small_slots, 0)
+    small_total.begin()
     line.pass_on(blocks - 1, firsts[-1])
 
     def flat(at):
@@ -1664,6 +1759,7 @@
     to_gateup = side_by_side(grad_gateup, down_end)
     products(ffn_all, 0, down_end, tall(2), one_above_other(grad_downproj), *high)
     gather.relay()
+    small_total.add_pair()
     products(ffn_all, down_end, gu_middle, flat(1), to_gateup, *wide)
     hidden_in = tp.own(tokens)[...].astype(jnp.float32)
     tp.own(tokens_grad)[...] = (
@@ -1678,17 +1774,16 @@
     tokens_spread.begin()
     layer_spread.pass_on()
     gather.hand_over()
-    finish(small_sent)
-    plane.own(small_sum)[...] = plane.total(small, small_slots).astype(small_sum.dtype)
-    small_sent = plane.spread(small_sum, 1)
+    small_total.add_all()
     if swaps:
         swap.begin()
     products(ffn_all, gu_middle, gu_end, flat(1), to_gateup, *wide)
     tokens_spread.pass_on()
     gather.hand_over_last()
+    small_total.hand_over()
     gather.end()
     products(mix_all, 0, 2 * inner // WIDE, flat(0), side_by_side(grad_inproj, 0), *wide)
-    finish(small_sent)
+    small_total.end()
     gain_own[...] = small_sum[SMALL_ROWS - GAIN_ROWS : SMALL_ROWS, :].astype(jnp.float32)
     gain_sent = [tp.one(gain_own, gain_slots.at[hop], 0, hop) for hop in range(tp.count - 1)]
     vectors_sum[...] = small_sum[:SMALL_ROWS, :].astype(jnp.float32)
@@ -1770,7 +1865,6 @@
             pltpu.VMEM(part.shape, low),
             pltpu.VMEM(small.shape, low),
             pltpu.VMEM(small.shape, low),
-            slots_for(small, plane_count),
             pltpu.VMEM((tp_count - 1, GAIN_ROWS, inner), full),
             pltpu.VMEM((GAIN_ROWS, inner), full),
             pltpu.VMEM((SMALL_ROWS, inner), full),
@@ -1786,12 +1880,11 @@
             dma((2,)),
             dma((1, tp_count - 1)),
             dma((1, tp_count - 1)),
-            dma((2, plane_count - 1)),
-            dma((2, plane_count - 1)),
         ]
         + gather_scratch()
         + line_sum_scratch(part, width // WIDE)
         + line_spread_scratch() * 2
+        + plane_sum_scratch(small)
         + (swap_scratch([tokens]) if swaps else []),
         compiler_params=pltpu.CompilerParams(
             collective_id=call_id, has_side_effects=True, vmem_limit_bytes=VMEM_GRANT

time: 475 us -> 474 us (level)
  no operation moved by 1% of the time
where the time goes in v15:
time: 474 us; the launch traced here: 473 us
  Pallas kernels  385 us (81%)
  local copies, waits for them, and re-layouts  30.5 us (6%)
  other arithmetic  23.8 us (5%)
  between operations  14.5 us (3%)
  waiting for transfers between devices  10.8 us (2%)
  matrix products  6.89 us (1%)
    pallas_call x1, Pallas kernels, run_head(): pl.pallas_call(head_kernel, in_specs=[vmem] * 2 + [hbm] * 2, out_specs=[v...  76.2 us
    pallas_call x1, Pallas kernels, run_tail(): pl.pallas_call(functools.partial(tail_kernel, swaps), in_specs=[vmem] * 1...  75.9 us
    pallas_call x1, Pallas kernels, ffn_back(): pl.pallas_call(functools.partial(ffn_back_kernel, len(arrays)), in_specs=...  54.3 us
    pallas_call x1, Pallas kernels, mixer_out(): pl.pallas_call(functools.partial(mixer_out_kernel, len(arrays)), in_specs...  47.5 us
    pallas_call x1, Pallas kernels, scan_forward_pair(): pl.pallas_call(functools.partial(forward_pair_kernel, n_state, tiles, gro...  34.3 us
    pallas_call x1, Pallas kernels, scan_backward_pair(): pl.pallas_call(functools.partial(backward_pair_kernel, len(arrays), n_sta...  31.8 us
    pallas_call x1, Pallas kernels, run_select(): pl.pallas_call(select_kernel, in_specs=[vmem, hbm], out_specs=[vmem, hbm]...  28.9 us
    pallas_call x1, Pallas kernels, run_ffn(): pl.pallas_call(functools.partial(ffn_kernel, swaps), in_specs=[vmem, vmem...  18.2 us
  transfers between devices with their start and end apart: 3, of which 2 were waited for; matrix products, arithmetic and copies ran while one was open for 8% of the time, Pallas kernels for 62%

profile of v15, /device:TPU:0, one launch (start us, length us, event | category | flops | bytes accessed | tf_op | source)
XLA Modules:
  0.0 473.2 jit_solution(7320556456565499134)
XLA Ops:
  7.3 1.6 copy.32
  9.3 1.8 pad_maximum_fusion
  14.7 76.2 %shard_map.262 = (bf16[256,1024]{1,0:T(8,128)(2,1)}, f32[256,1024]{1,0:T(8,128)}, bf16[32,1024]{1,0:T(8,128)(2,1)}, bf16[2048,1024]{1,0:T(8,128)(2,1)}, bf16[2048,1024]{1,0:T(8,128)(2,1)}) custom-call(bf16[256,2048]{1,0:T(8,128)(2,1)} %bitcast.88, bf16[1,2048]{1,0:T(2,128)(2,1)} %reshape.110.gain.gain_row, bf16[256,1024]{1,0:T(8,128)(2,1)} %get-tuple-element.114.in_conv, ...), custom_call_target="tpu_custom_call" | custom-call | tf_op jit(solution)/shard_map/pallas_call | solution.py:1997
  91.7 1.2 maximum_convert_fusion
  94.3 1.8 fusion.20
  97.1 28.9 %shard_map.263 = (f32[256,256]{1,0:T(8,128)}, bf16[4096,256]{1,0:T(8,128)(2,1)}) custom-call(f32[256,256]{1,0:T(8,128)} %fusion.10.part, bf16[512,256]{1,0:T(8,128)(2,1)} %get-tuple-element.116.shard), custom_call_target="tpu_custom_call" | custom-call | tf_op jit(solution)/shard_map/pallas_call | solution.py:673
  126.0 1.1 fusion.23
  128.5 3.0 compare_select_fusion
  131.5 34.3 %shard_map.264 = (f32[256,16,8,128]{3,2,1,0:T(8,128)}, f32[256,1024]{1,0:T(8,128)}, bf16[4096,256]{1,0:T(8,128)(2,1)}) custom-call(f32[256,1024]{1,0:T(8,128)} %get-tuple-element.128.step_ref, f32[256,1024]{1,0:T(8,128)} %get-tuple-element.101.input_ref, f32[4096]{0:T(1024)} %reshape.114.brow_ref, f32[4096]{0:T(1024)} %reshape.115.crow_ref, ...), custom_call_target="tpu_custom_call" | custom-call | tf_op jit(solution)/shard_map/pallas_call | solution.py:1106
  166.1 2.9 multiply_convert_fusion.2.gated
  168.9 1.3 multiply_convert_fusion.refs_0_
  170.2 47.5 %shard_map.265 = (bf16[256,2048]{1,0:T(8,128)(2,1)}, f32[64,2048]{1,0:T(8,128)}, bf16[2048,1024]{1,0:T(8,128)(2,1)}, bf16[2048,256]{1,0:T(8,128)(2,1)}) custom-call(bf16[256,1024]{1,0:T(8,128)(2,1)} %multiply_convert_fusion.2.gated, bf16[4096,256]{1,0:T(8,128)(2,1)} %get-tuple-element.60.out_first, bf16[4096,256]{1,0:T(8,128)(2,1)} %get-tuple-element.61.out_last, ...), custom_call_target="tpu_custom_call" | custom-call | tf_op jit(solution)/shard_map/pallas_call | solution.py:766
  217.7 18.2 %shard_map.266 = (bf16[256,6144]{1,0:T(8,128)(2,1)}, bf16[2048,256]{1,0:T(8,128)(2,1)}) custom-call(bf16[256,2048]{1,0:T(8,128)(2,1)} %get-tuple-element.62.normed.refs_0_, bf16[256,2048]{1,0:T(8,128)(2,1)} %bitcast.93, bf16[2048,6144]{1,0:T(8,128)(2,1)} %all-gather.3.cloned.1.call-done.weights), custom_call_target="tpu_custom_call" | custom-call | tf_op jit(solution)/shard_map/pallas_call | solution.py:842
  236.0 1.5 slice.147.step_low
  238.9 54.3 %shard_map.267 = (bf16[256,2048]{1,0:T(8,128)(2,1)}, f32[64,2048]{1,0:T(8,128)}, f32[1,2048]{1,0:T(1,128)}, f32[256,1024]{1,0:T(8,128)}, bf16[256,2048]{1,0:T(8,128)(2,1)}, /*index=5*/bf16[2048,256]{1,0:T(8,128)(2,1)}) custom-call(bf16[256,6144]{1,0:T(8,128)(2,1)} %get-tuple-element.63.made, bf16[256,2048]{1,0:T(8,128)(2,1)} %bitcast.94, ...), custom_call_target="tpu_custom_call" | custom-call | tf_op jit(solution)/shard_map/pallas_call | solution.py:952
  293.3 3.9 multiply_reduce_fusion.1
  297.2 31.8 %shard_map.268 = (f32[256,1024]{1,0:T(8,128)}, f32[256,1024]{1,0:T(8,128)}, f32[16,8,128]{2,1,0:T(8,128)}, f32[256,32,128]{2,1,0:T(8,128)}, bf16[64,1024]{1,0:T(8,128)(2,1)}, /*index=5*/bf16[64,1024]{1,0:T(8,128)(2,1)}) custom-call(f32[256,1024]{1,0:T(8,128)} %get-tuple-element.128.step_ref, f32[256,1024]{1,0:T(8,128)} %get-tuple-element.101.input_ref, ...), custom_call_target="tpu_custom_call" | custom-call | tf_op jit(solution)/shard_map/pallas_call | solution.py:1315
  329.0 3.4 reduce_sum.82
  332.5 2.2 fusion.17
  335.7 18.2 %shard_map.269 = (bf16[256,256]{1,0:T(8,128)(2,1)}, bf16[256,1024]{1,0:T(8,128)(2,1)}) custom-call(bf16[256,256]{1,0:T(8,128)(2,1)} %maximum_maximum_fusion.part, bf16[64,1024]{1,0:T(8,128)(2,1)} %get-tuple-element.71.own_rows), custom_call_target="tpu_custom_call" | custom-call | tf_op jit(solution)/shard_map/pallas_call | solution.py:704
  353.9 2.5 multiply_reduce_fusion.5
  357.0 1.4 collective-permute-start
  360.9 2.7 collective-permute-done
  364.6 8.0 %all-gather.5.cloned.1.call-done.ffn_all = bf16[2048,6144]{1,0:T(8,128)(2,1)} async-done(((bf16[256,6144]{1,0:T(8,128)(2,1)}), bf16[2048,6144]{1,0:T(8,128)(2,1)}) %all-gather.5.cloned.1.call-update) | async-done | bytes 25165840 | tf_op jit(solution)/shard_map/all_gather | solution.py:366
  372.6 75.9 %shard_map.270 = (bf16[256,2048]{1,0:T(8,128)(2,1)}, bf16[256,2048]{1,0:T(8,128)(2,1)}, f32[32,1024]{1,0:T(8,128)}, f32[128,1024]{1,0:T(8,128)}, f32[160,1024]{1...) custom-call(bf16[256,1024]{1,0:T(8,128)(2,1)} %bitcast.95, ...), custom_call_target="tpu_custom_call" | custom-call | tf_op jit(solution)/shard_map/pallas_call | solution.py:1846
  448.5 1.5 fusion.24
  450.0 1.4 slice.111
  451.3 1.5 slice_bitcast_fusion.4
  454.3 2.5 copy.51
  457.7 1.3 copy.53
  462.0 2.1 copy.57
  465.1 1.3 copy.58
  (104 shorter events, 21.5 us)
Async XLA Ops:
  7.2 121.3 %copy-start = (bf16[128,1024]{1,0:T(8,128)(2,1)S(1)}, bf16[128,1024]{1,0:T(8,128)(2,1)}, u32[]{:S(2)}) copy-start(bf16[128,1024]{1,0:T(8,128)(2,1)} %param.21) | copy-start | bytes 786436
  7.2 1.9 copy-start.7
  7.2 210.5 %all-gather.3.cloned.1.call-start = ((), (), s32[]{:S(2)}) async-start(), calls=%async_computation | async-start | bytes 28311552 | tf_op jit(solution)/shard_map/all_gather | solution.py:366
  11.1 1.3 copy-start.26
  11.1 1.3 copy-start.27
  11.1 1.3 copy-start.28
  11.1 1.3 copy-start.25
  11.1 1.9 copy-start.18
  11.1 2.6 copy-start.11
  11.1 361.4 %all-gather.5.cloned.1.call-start = ((), (), s32[]{:S(2)}) async-start(), calls=%async_computation.1 | async-start | bytes 28311552 | tf_op jit(solution)/shard_map/all_gather | solution.py:366
  14.7 78.2 %copy-start.23 = (bf16[4,1024]{1,0:T(4,128)(2,1)S(1)}, bf16[4,1024]{1,0:T(4,128)(2,1)}, u32[]{:S(2)}) copy-start(bf16[4,1024]{1,0:T(4,128)(2,1)} %param.18) | copy-start | bytes 24580
  14.7 78.2 %copy-start.15 = (bf16[1024,256]{1,0:T(8,128)(2,1)S(1)}, bf16[1024,256]{1,0:T(8,128)(2,1)}, u32[]{:S(2)}) copy-start(bf16[1024,256]{1,0:T(8,128)(2,1)} %param.25) | copy-start | bytes 1572868
  93.0 1.3 copy-start.21
  94.3 1.8 copy-start.17
  96.1 197.2 %copy-start.2 = (bf16[256,1024]{1,0:T(8,128)(2,1)}, bf16[256,1024]{1,0:T(8,128)(2,1)S(1)}, u32[]{:S(2)}) copy-start(bf16[256,1024]{1,0:T(8,128)(2,1)S(1)} %get-tuple-element.102.scan_in) | copy-start | bytes 1572868
  128.5 37.3 %copy-start.1 = (bf16[2,128,2048]{2,1,0:T(8,128)(2,1)S(1)}, bf16[2,128,2048]{2,1,0:T(8,128)(2,1)}, u32[]{:S(2)}) copy-start(bf16[2,128,2048]{2,1,0:T(8,128)(2,1)} %param.15) | copy-start | bytes 3145732
  238.9 54.4 %copy-start.5 = (f32[256,1024]{1,0:T(8,128)S(1)}, f32[256,1024]{1,0:T(8,128)}, u32[]{:S(2)}) copy-start(f32[256,1024]{1,0:T(8,128)} %get-tuple-element.59) | copy-start | bytes 3145732
  329.0 3.5 copy-start.10
  332.5 2.5 copy-start.29
  332.5 21.4 %copy-start.4 = (f32[256,1024]{1,0:T(8,128)S(1)}, f32[256,1024]{1,0:T(8,128)}, u32[]{:S(2)}) copy-start(f32[256,1024]{1,0:T(8,128)} %get-tuple-element.100.ograd_ref) | copy-start | bytes 3145732
  334.7 21.8 %copy-start.3 = (bf16[256,1024]{1,0:T(8,128)(2,1)}, bf16[256,1024]{1,0:T(8,128)(2,1)S(1)}, u32[]{:S(2)}) copy-start(bf16[256,1024]{1,0:T(8,128)(2,1)S(1)} %get-tuple-element.105.pre_low) | copy-start | bytes 1572868
  353.9 2.6 copy-start.22
  357.0 2.0 copy-start.19
  357.0 2.0 copy-start.20
  357.0 6.6 %collective-permute-start = (f32[2,3,1024]{2,1,0:T(4,128)S(1)}, f32[2,3,1024]{2,1,0:T(4,128)S(1)}, u32[]{:S(2)}, u32[]{:S(2)}) collective-permute-start(f32[2,3,1024]{2,1,0:T(4,128)S(1)} %pad_add_fusion.1), channel_id=1, source_target_pairs={{4,0},{5,1},{6,2},{7,3},{12,8},{13,9},{14,10},{15,11},{20,16},{21,... | collective-permute-start | bytes 73736 | tf_op jit(solution)/shard_map/ppermute | solution.py:23
  448.5 8.3 %copy-start.13 = (bf16[256,2048]{1,0:T(8,128)(2,1)S(1)}, bf16[256,2048]{1,0:T(8,128)(2,1)}, u32[]{:S(2)}) copy-start(bf16[256,2048]{1,0:T(8,128)(2,1)} %get-tuple-element.86) | copy-start | bytes 3145732
  454.3 3.4 copy-start.9
  457.7 1.5 copy-start.14
  457.7 2.4 copy-start.16
  457.7 3.1 copy-start.12
  459.2 2.7 copy-start.6
  462.0 3.1 copy-start.8
  (1 other events, 0.7 us)
Sparse Core Ops, SparseCore 0:
  11.3 180.4 all-gather.2
  236.1 136.4 all-gather.4

commit v16 on v15

--- a/solution.py
+++ b/solution.py
@@ -647,39 +647,28 @@
         target[:, at : at + WIDE] = matmul(left[...], block_buf[turn % 2]).astype(target.dtype)
 
 
-def select_kernel(
-    part, shard, total, gathered, slots, send_sem, recv_sem, gather_send, gather_recv, local_sem
-):
+def select_kernel(part, total, slots, send_sem, recv_sem):
     group = Group(("tp",), send_sem, recv_sem)
-    gather = PlaneGather(shard, gathered, gather_send, gather_recv)
-    greet([(("tp",), group.others), (PLANE, gather.others)])
-    copies = group.scatter(part, slots, 0)
-    gather.begin(local_sem)
-    finish(copies)
+    greet([(("tp",), group.others)])
+    finish(group.scatter(part, slots, 0))
     group.own(total)[...] = group.total(part, slots).astype(total.dtype)
-    copies = group.spread(total, 1)
-    gather.relay()
-    gather.hand_over()
-    finish(copies)
-    gather.hand_over_last()
-    gather.end()
-
-
-def run_select(call_id, part, shard):
+    finish(group.spread(total, 1))
+
+
+def run_select(call_id, part):
     count = group_size(("tp",))
     vmem = pl.BlockSpec(memory_space=pltpu.VMEM)
-    hbm = pl.BlockSpec(memory_space=pltpu.HBM)
     sems = pltpu.SemaphoreType.DMA((2, count - 1))
     return pl.pallas_call(
         select_kernel,
-        in_specs=[vmem, hbm],
-        out_specs=[vmem, hbm],
-        out_shape=[jax.ShapeDtypeStruct(part.shape, part.dtype), gathered_shape(shard)],
-        scratch_shapes=[slots_for(part, count), sems, sems] + gather_scratch(),
+        in_specs=[vmem],
+        out_specs=vmem,
+        out_shape=jax.ShapeDtypeStruct(part.shape, part.dtype),
+        scratch_shapes=[slots_for(part, count), sems, sems],
         compiler_params=pltpu.CompilerParams(
             collective_id=call_id, has_side_effects=True, vmem_limit_bytes=VMEM_GRANT
         ),
-    )(part, shard)
+    )(part)
 
 
 def sum_kernel(part, own_rows, total, all_rows, slots, send_sem, recv_sem, *line_sems):
@@ -2056,6 +2045,7 @@
     tokens_rows = tokens.reshape(rows, width)
     ct_low = cotangent.reshape(rows, width)
     swap_now = swaps_in_kernels(width)
+    out_first = gathered_rows(outproj[: inner // 2])
     ffn_pack = gathered_rows(
         jnp.concatenate([gateup[0], gateup[1], jnp.transpose(downproj)], 1)
     )
@@ -2078,7 +2068,7 @@
     columns = selproj.shape[1]
     select_width = -(-columns // LANE) * LANE
     select_weights = jnp.pad(selproj, ((0, 0), (0, select_width - columns)))
-    select_cols, out_first = run_select(0, matmul(scan_in, select_weights), outproj[: inner // 2])
+    select_cols = run_select(0, matmul(scan_in, select_weights))
 
     def columns_of(swapped, array):
         if not swapped:

time: 474 us -> 471 us (level)
  Pallas kernels: 385 us -> 377 us
    pallas_call x1, Pallas kernels: 47.5 us -> 70.9 us  [mixer_out(): pl.pallas_call(functools.partial(mixer_out_kernel, len(arrays)), in_specs...]
    pallas_call x1, Pallas kernels: 76.2 us -> 55.5 us  [run_head(): pl.pallas_call(head_kernel, in_specs=[vmem] * 2 + [hbm] * 2, out_specs=[v...]
    pallas_call x1, Pallas kernels: 28.9 us -> 17.5 us  [run_select(): pl.pallas_call(select_kernel, in_specs=[vmem], out_specs=vmem, out_shape=...]
    all_gather x2 -> x3, waiting for transfers between devices: 8.01 us -> 12.7 us  [gathered_rows(): return lax.all_gather(rows, PLANE, axis=0, tiled=True)]
    unnamed x71 -> x69, local copies, waits for them, and re-layouts: 16.1 us -> 16.3 us
  transfers between devices with their start and end apart: 3 -> 4, of which waited for: 2 -> 3; matrix products, arithmetic and copies ran while one was open for 8% -> 9% of each run, Pallas kernels for 62% -> 60%
where the time goes in v16:
time: 471 us; the launch traced here: 470 us
  Pallas kernels  377 us (80%)
  local copies, waits for them, and re-layouts  31.8 us (7%)
  other arithmetic  23.6 us (5%)
  waiting for transfers between devices  15.4 us (3%)
  between operations  14.2 us (3%)
  matrix products  6.86 us (1%)
    pallas_call x1, Pallas kernels, run_tail(): pl.pallas_call(functools.partial(tail_kernel, swaps), in_specs=[vmem] * 1...  75.8 us
    pallas_call x1, Pallas kernels, mixer_out(): pl.pallas_call(functools.partial(mixer_out_kernel, len(arrays)), in_specs...  70.9 us
    pallas_call x1, Pallas kernels, run_head(): pl.pallas_call(head_kernel, in_specs=[vmem] * 2 + [hbm] * 2, out_specs=[v...  55.5 us
    pallas_call x1, Pallas kernels, ffn_back(): pl.pallas_call(functools.partial(ffn_back_kernel, len(arrays)), in_specs=...  54.1 us
    pallas_call x1, Pallas kernels, scan_backward_pair(): pl.pallas_call(functools.partial(backward_pair_kernel, len(arrays), n_sta...  35 us
    pallas_call x1, Pallas kernels, scan_forward_pair(): pl.pallas_call(functools.partial(forward_pair_kernel, n_state, tiles, gro...  33.3 us
    pallas_call x1, Pallas kernels, run_ffn(): pl.pallas_call(functools.partial(ffn_kernel, swaps), in_specs=[vmem, vmem...  19.4 us
    pallas_call x1, Pallas kernels, run_select(): pl.pallas_call(select_kernel, in_specs=[vmem], out_specs=vmem, out_shape=...  17.5 us
  transfers between devices with their start and end apart: 4, of which 3 were waited for; matrix products, arithmetic and copies ran while one was open for 9% of the time, Pallas kernels for 60%

profile of v16, /device:TPU:0, one launch (start us, length us, event | category | flops | bytes accessed | tf_op | source)
XLA Modules:
  0.0 470.2 jit_solution(7112644241776289374)
XLA Ops:
  7.3 2.0 fusion.22
  9.3 1.5 copy.32
  11.0 1.8 pad_maximum_fusion
  16.4 55.5 %shard_map.262 = (bf16[256,1024]{1,0:T(8,128)(2,1)}, f32[256,1024]{1,0:T(8,128)}, bf16[32,1024]{1,0:T(8,128)(2,1)}, bf16[2048,1024]{1,0:T(8,128)(2,1)}, bf16[2048,1024]{1,0:T(8,128)(2,1)}) custom-call(bf16[256,2048]{1,0:T(8,128)(2,1)} %bitcast.88, bf16[1,2048]{1,0:T(2,128)(2,1)} %reshape.110.gain.gain_row, bf16[256,1024]{1,0:T(8,128)(2,1)} %get-tuple-element.110.in_conv, ...), custom_call_target="tpu_custom_call" | custom-call | tf_op jit(solution)/shard_map/pallas_call | solution.py:1986
  75.1 1.8 fusion.20
  77.9 17.5 %shard_map.263 = f32[256,256]{1,0:T(8,128)} custom-call(f32[256,256]{1,0:T(8,128)} %fusion.10.part), custom_call_target="tpu_custom_call" | custom-call | tf_op jit(solution)/shard_map/pallas_call | solution.py:662
  97.9 3.0 compare_select_fusion
  100.9 33.3 %shard_map.264 = (f32[256,16,8,128]{3,2,1,0:T(8,128)}, f32[256,1024]{1,0:T(8,128)}, bf16[4096,256]{1,0:T(8,128)(2,1)}) custom-call(f32[256,1024]{1,0:T(8,128)} %get-tuple-element.124.step_ref, f32[256,1024]{1,0:T(8,128)} %get-tuple-element.97.input_ref, f32[4096]{0:T(1024)} %reshape.114.brow_ref, f32[4096]{0:T(1024)} %reshape.115.crow_ref, ...), custom_call_target="tpu_custom_call" | custom-call | tf_op jit(solution)/shard_map/pallas_call | solution.py:1095
  134.5 2.7 multiply_convert_fusion.2.gated
  137.1 1.3 multiply_convert_fusion.refs_0_
  138.4 70.9 %shard_map.265 = (bf16[256,2048]{1,0:T(8,128)(2,1)}, f32[64,2048]{1,0:T(8,128)}, bf16[2048,1024]{1,0:T(8,128)(2,1)}, bf16[2048,256]{1,0:T(8,128)(2,1)}) custom-call(bf16[256,1024]{1,0:T(8,128)(2,1)} %multiply_convert_fusion.2.gated, bf16[4096,256]{1,0:T(8,128)(2,1)} %all-gather.4.cloned.1.call-done.out_first, bf16[4096,256]{1,0:T(8,128)(2,1)} %get-tuple-element.57.out_last, ...), custom_call_target="tpu_custom_call" | custom-call | tf_op jit(solution)/shard_map/pallas_call | solution.py:755
  209.4 3.7 all-gather.6.cloned.1.call-done.weights
  213.1 19.4 %shard_map.266 = (bf16[256,6144]{1,0:T(8,128)(2,1)}, bf16[2048,256]{1,0:T(8,128)(2,1)}) custom-call(bf16[256,2048]{1,0:T(8,128)(2,1)} %get-tuple-element.58.normed.refs_0_, bf16[256,2048]{1,0:T(8,128)(2,1)} %bitcast.93, bf16[2048,6144]{1,0:T(8,128)(2,1)} %all-gather.6.cloned.1.call-done.weights), custom_call_target="tpu_custom_call" | custom-call | tf_op jit(solution)/shard_map/pallas_call | solution.py:831
  232.5 1.5 slice.147.step_low
  235.4 54.1 %shard_map.267 = (bf16[256,2048]{1,0:T(8,128)(2,1)}, f32[64,2048]{1,0:T(8,128)}, f32[1,2048]{1,0:T(1,128)}, f32[256,1024]{1,0:T(8,128)}, bf16[256,2048]{1,0:T(8,128)(2,1)}, /*index=5*/bf16[2048,256]{1,0:T(8,128)(2,1)}) custom-call(bf16[256,6144]{1,0:T(8,128)(2,1)} %get-tuple-element.59.made, bf16[256,2048]{1,0:T(8,128)(2,1)} %bitcast.94, ...), custom_call_target="tpu_custom_call" | custom-call | tf_op jit(solution)/shard_map/pallas_call | solution.py:941
  289.5 3.9 multiply_reduce_fusion.1
  293.4 35.0 %shard_map.268 = (f32[256,1024]{1,0:T(8,128)}, f32[256,1024]{1,0:T(8,128)}, f32[16,8,128]{2,1,0:T(8,128)}, f32[256,32,128]{2,1,0:T(8,128)}, bf16[64,1024]{1,0:T(8,128)(2,1)}, /*index=5*/bf16[64,1024]{1,0:T(8,128)(2,1)}) custom-call(f32[256,1024]{1,0:T(8,128)} %get-tuple-element.124.step_ref, f32[256,1024]{1,0:T(8,128)} %get-tuple-element.97.input_ref, ...), custom_call_target="tpu_custom_call" | custom-call | tf_op jit(solution)/shard_map/pallas_call | solution.py:1304
  328.4 3.4 reduce_sum.82
  331.8 2.2 fusion.17
  335.1 15.2 %shard_map.269 = (bf16[256,256]{1,0:T(8,128)(2,1)}, bf16[256,1024]{1,0:T(8,128)(2,1)}) custom-call(bf16[256,256]{1,0:T(8,128)(2,1)} %maximum_maximum_fusion.part, bf16[64,1024]{1,0:T(8,128)(2,1)} %get-tuple-element.67.own_rows), custom_call_target="tpu_custom_call" | custom-call | tf_op jit(solution)/shard_map/pallas_call | solution.py:693
  350.3 2.5 multiply_reduce_fusion.5
  353.4 1.4 collective-permute-start
  357.3 2.7 collective-permute-done
  360.9 9.0 %all-gather.8.cloned.1.call-done.ffn_all = bf16[2048,6144]{1,0:T(8,128)(2,1)} async-done(((bf16[256,6144]{1,0:T(8,128)(2,1)}), bf16[2048,6144]{1,0:T(8,128)(2,1)}) %all-gather.8.cloned.1.call-update) | async-done | bytes 25165840 | tf_op jit(solution)/shard_map/all_gather | solution.py:366
  369.9 75.8 %shard_map.270 = (bf16[256,2048]{1,0:T(8,128)(2,1)}, bf16[256,2048]{1,0:T(8,128)(2,1)}, f32[32,1024]{1,0:T(8,128)}, f32[128,1024]{1,0:T(8,128)}, f32[160,1024]{1...) custom-call(bf16[256,1024]{1,0:T(8,128)(2,1)} %bitcast.95, ...), custom_call_target="tpu_custom_call" | custom-call | tf_op jit(solution)/shard_map/pallas_call | solution.py:1835
  445.8 1.5 fusion.24
  447.3 1.4 slice.111
  448.6 1.5 slice_bitcast_fusion.4
  451.6 2.5 copy.51
  455.0 1.3 copy.53
  459.3 2.1 copy.57
  462.4 1.3 copy.58
  (105 shorter events, 23.3 us)
Async XLA Ops:
  7.2 90.7 %copy-start = (bf16[128,1024]{1,0:T(8,128)(2,1)S(1)}, bf16[128,1024]{1,0:T(8,128)(2,1)}, u32[]{:S(2)}) copy-start(bf16[128,1024]{1,0:T(8,128)(2,1)} %param.21) | copy-start | bytes 786436
  7.2 3.6 copy-start.7
  7.2 131.2 %all-gather.4.cloned.1.call-start = ((), (), s32[]{:S(2)}) async-start(), calls=%async_computation | async-start | bytes 2359296 | tf_op jit(solution)/shard_map/all_gather | solution.py:366
  9.3 203.8 %all-gather.6.cloned.1.call-start = ((), (), s32[]{:S(2)}) async-start(), calls=%async_computation.1 | async-start | bytes 28311552 | tf_op jit(solution)/shard_map/all_gather | solution.py:366
  12.8 0.7 copy-start.23
  12.8 1.3 copy-start.25
  12.8 1.3 copy-start.26
  12.8 1.3 copy-start.27
  12.8 1.3 copy-start.24
  12.8 1.9 copy-start.17
  12.8 2.6 copy-start.11
  12.8 357.1 %all-gather.8.cloned.1.call-start = ((), (), s32[]{:S(2)}) async-start(), calls=%async_computation.2 | async-start | bytes 28311552 | tf_op jit(solution)/shard_map/all_gather | solution.py:366
  16.4 57.5 %copy-start.22 = (bf16[4,1024]{1,0:T(4,128)(2,1)S(1)}, bf16[4,1024]{1,0:T(4,128)(2,1)}, u32[]{:S(2)}) copy-start(bf16[4,1024]{1,0:T(4,128)(2,1)} %param.18) | copy-start | bytes 24580
  75.1 1.8 copy-start.16
  76.8 212.7 %copy-start.2 = (bf16[256,1024]{1,0:T(8,128)(2,1)}, bf16[256,1024]{1,0:T(8,128)(2,1)S(1)}, u32[]{:S(2)}) copy-start(bf16[256,1024]{1,0:T(8,128)(2,1)S(1)} %get-tuple-element.98.scan_in) | copy-start | bytes 1572868
  97.9 36.3 %copy-start.1 = (bf16[2,128,2048]{2,1,0:T(8,128)(2,1)S(1)}, bf16[2,128,2048]{2,1,0:T(8,128)(2,1)}, u32[]{:S(2)}) copy-start(bf16[2,128,2048]{2,1,0:T(8,128)(2,1)} %param.15) | copy-start | bytes 3145732
  235.4 54.1 %copy-start.5 = (f32[256,1024]{1,0:T(8,128)S(1)}, f32[256,1024]{1,0:T(8,128)}, u32[]{:S(2)}) copy-start(f32[256,1024]{1,0:T(8,128)} %get-tuple-element.56) | copy-start | bytes 3145732
  328.4 3.5 copy-start.10
  331.8 2.5 copy-start.28
  331.8 18.4 %copy-start.4 = (f32[256,1024]{1,0:T(8,128)S(1)}, f32[256,1024]{1,0:T(8,128)}, u32[]{:S(2)}) copy-start(f32[256,1024]{1,0:T(8,128)} %get-tuple-element.96.ograd_ref) | copy-start | bytes 3145732
  334.0 18.8 %copy-start.3 = (bf16[256,1024]{1,0:T(8,128)(2,1)}, bf16[256,1024]{1,0:T(8,128)(2,1)S(1)}, u32[]{:S(2)}) copy-start(bf16[256,1024]{1,0:T(8,128)(2,1)S(1)} %get-tuple-element.101.pre_low) | copy-start | bytes 1572868
  350.3 2.5 copy-start.21
  353.4 2.0 copy-start.18
  353.4 2.0 copy-start.19
  353.4 6.6 %collective-permute-start = (f32[2,3,1024]{2,1,0:T(4,128)S(1)}, f32[2,3,1024]{2,1,0:T(4,128)S(1)}, u32[]{:S(2)}, u32[]{:S(2)}) collective-permute-start(f32[2,3,1024]{2,1,0:T(4,128)S(1)} %pad_add_fusion.1), channel_id=1, source_target_pairs={{4,0},{5,1},{6,2},{7,3},{12,8},{13,9},{14,10},{15,11},{20,16},{21,... | collective-permute-start | bytes 73736 | tf_op jit(solution)/shard_map/ppermute | solution.py:23
  445.8 8.3 %copy-start.13 = (bf16[256,2048]{1,0:T(8,128)(2,1)S(1)}, bf16[256,2048]{1,0:T(8,128)(2,1)}, u32[]{:S(2)}) copy-start(bf16[256,2048]{1,0:T(8,128)(2,1)} %get-tuple-element.82) | copy-start | bytes 3145732
  451.6 3.4 copy-start.9
  455.0 1.5 copy-start.14
  455.0 2.4 copy-start.15
  455.0 3.1 copy-start.12
  456.6 2.7 copy-start.6
  459.3 3.1 copy-start.8
  (1 other events, 0.6 us)
Sparse Core Ops, SparseCore 0:
  9.9 39.1 all-gather.3
  51.6 161.4 all-gather.5
  232.6 137.2 all-gather.7

commit v17 on v16

--- a/solution.py
+++ b/solution.py
@@ -715,15 +715,15 @@
     gather_send, gather_recv, local_sem, *refs = refs[7:]
     group = Group(("tp",), None, None)
     gather = PlaneGather(gated, gated_all, gather_send, gather_recv)
-    half = gated.shape[1] // 2
-    share = out_first.shape[1]
+    inner, share = gated.shape[1], out_first.shape[1]
+    first = out_first.shape[0] * share // part.shape[1]
+    last = inner - first
     greet([(("tp",), group.others), (PLANE, gather.others)])
     gather.begin(local_sem)
-    for at in range(out_first.shape[0] // half):
-        rows = slice(at * half, (at + 1) * half)
+    for at in range(out_first.shape[0] // first):
         part[:, at * share : (at + 1) * share] = (
-            matmul(gated[:, :half], out_first[rows, :])
-            + matmul(gated[:, half:], out_last[rows, :])
+            matmul(gated[:, :first], out_first[at * first : (at + 1) * first, :])
+            + matmul(gated[:, first:], out_last[at * last : (at + 1) * last, :])
         ).astype(part.dtype)
     firsts = [line.begin(j) for j in range(line.blocks)]
     if n_swaps:
@@ -913,17 +913,18 @@
     middle_grad[...] = grad
     group.own(middle_low)[...] = grad.astype(middle_low.dtype)
     spread.run()
-    half = gated_grad.shape[1] // 2
-    share = out_first.shape[1]
-    for side, shards in enumerate((out_first, out_last)):
+    share, at_column = out_first.shape[1], 0
+    for shards in (out_first, out_last):
+        depth = shards.shape[0] * share // middle_low.shape[1]
         total = None
-        for at in range(shards.shape[0] // half):
+        for at in range(shards.shape[0] // depth):
             one = matmul_nt(
                 middle_low[:, at * share : (at + 1) * share],
-                shards[at * half : (at + 1) * half, :],
+                shards[at * depth : (at + 1) * depth, :],
             )
             total = one if total is None else total + one
-        gated_grad[:, side * half : (side + 1) * half] = total
+        gated_grad[:, at_column : at_column + depth] = total
+        at_column += depth
     if n_swaps:
         swap.end()
 
@@ -934,7 +935,7 @@
     hbm = pl.BlockSpec(memory_space=pltpu.HBM)
     rows, width = ct.shape
     hidden = made.shape[1] // 3
-    inner = 2 * out_first.shape[0] // group_size(PLANE)
+    inner = (out_first.shape[0] + out_last.shape[0]) // group_size(PLANE)
     low, full = jnp.bfloat16, jnp.float32
     part = jax.ShapeDtypeStruct((rows, width), low)
     dma = pltpu.SemaphoreType.DMA
@@ -2045,7 +2046,7 @@
     tokens_rows = tokens.reshape(rows, width)
     ct_low = cotangent.reshape(rows, width)
     swap_now = swaps_in_kernels(width)
-    out_first = gathered_rows(outproj[: inner // 2])
+    out_first = gathered_rows(outproj[: inner // 4])
     ffn_pack = gathered_rows(
         jnp.concatenate([gateup[0], gateup[1], jnp.transpose(downproj)], 1)
     )
@@ -2090,7 +2091,7 @@
             c_rows,
             rate,
             seqs,
-            outproj[inner // 2 :],
+            outproj[inner // 4 :],
         )
     else:
         span_decay = jnp.exp(
@@ -2099,7 +2100,7 @@
         ends = scan_ends(step_size, scan_float, b_rows, rate, seqs, False)
         start = from_earlier(ends, span_decay, 1)
         prior, scan_out = scan_forward(start, step_size, scan_float, b_rows, c_rows, rate, seqs)
-        out_last = gathered_rows(outproj[inner // 2 :])
+        out_last = gathered_rows(outproj[inner // 4 :])
     mixer_core = scan_out + skip_weight[None] * scan_float
     gate_sig = jax.nn.silu(gate_mix)
     gated = (mixer_core * gate_sig).astype(low)

time: 471 us -> 474 us (level)
  Pallas kernels: 377 us -> 382 us
    pallas_call x1, Pallas kernels: 33.3 us -> 45 us  [scan_forward_pair(): pl.pallas_call(functools.partial(forward_pair_kernel, n_state, tiles, gro...]
    pallas_call x1, Pallas kernels: 70.9 us -> 65.2 us  [mixer_out(): pl.pallas_call(functools.partial(mixer_out_kernel, len(arrays)), in_specs...]
    unnamed x69 -> x71, local copies, waits for them, and re-layouts: 16.3 us -> 16.3 us
  transfers between devices with their start and end apart: 4 -> 4, of which waited for: 3 -> 2; matrix products, arithmetic and copies ran while one was open for 9% -> 9% of each run, Pallas kernels for 60% -> 61%
where the time goes in v17:
time: 474 us; the launch traced here: 473 us
  Pallas kernels  382 us (81%)
  local copies, waits for them, and re-layouts  32.3 us (7%)
  other arithmetic  23.6 us (5%)
  between operations  14.2 us (3%)
  waiting for transfers between devices  12 us (3%)
  matrix products  6.82 us (1%)
    pallas_call x1, Pallas kernels, run_tail(): pl.pallas_call(functools.partial(tail_kernel, swaps), in_specs=[vmem] * 1...  75.8 us
    pallas_call x1, Pallas kernels, mixer_out(): pl.pallas_call(functools.partial(mixer_out_kernel, len(arrays)), in_specs...  65.2 us
    pallas_call x1, Pallas kernels, run_head(): pl.pallas_call(head_kernel, in_specs=[vmem] * 2 + [hbm] * 2, out_specs=[v...  55.1 us
    pallas_call x1, Pallas kernels, ffn_back(): pl.pallas_call(functools.partial(ffn_back_kernel, len(arrays)), in_specs=...  54.2 us
    pallas_call x1, Pallas kernels, scan_forward_pair(): pl.pallas_call(functools.partial(forward_pair_kernel, n_state, tiles, gro...  45 us
    pallas_call x1, Pallas kernels, scan_backward_pair(): pl.pallas_call(functools.partial(backward_pair_kernel, len(arrays), n_sta...  32.5 us
    pallas_call x1, Pallas kernels, run_ffn(): pl.pallas_call(functools.partial(ffn_kernel, swaps), in_specs=[vmem, vmem...  20.2 us
    pallas_call x1, Pallas kernels, run_select(): pl.pallas_call(select_kernel, in_specs=[vmem], out_specs=vmem, out_shape=...  17.8 us
  transfers between devices with their start and end apart: 4, of which 2 were waited for; matrix products, arithmetic and copies ran while one was open for 9% of the time, Pallas kernels for 61%

profile of v17, /device:TPU:0, one launch (start us, length us, event | category | flops | bytes accessed | tf_op | source)
XLA Modules:
  0.0 472.5 jit_solution(1467582902501413000)
XLA Ops:
  7.3 1.7 slice.105
  9.0 1.5 copy.32
  10.7 1.8 pad_maximum_fusion
  16.9 55.1 %shard_map.262 = (bf16[256,1024]{1,0:T(8,128)(2,1)}, f32[256,1024]{1,0:T(8,128)}, bf16[32,1024]{1,0:T(8,128)(2,1)}, bf16[2048,1024]{1,0:T(8,128)(2,1)}, bf16[2048,1024]{1,0:T(8,128)(2,1)}) custom-call(bf16[256,2048]{1,0:T(8,128)(2,1)} %bitcast.88, bf16[1,2048]{1,0:T(2,128)(2,1)} %reshape.110.gain.gain_row, bf16[256,1024]{1,0:T(8,128)(2,1)} %get-tuple-element.110.in_conv, ...), custom_call_target="tpu_custom_call" | custom-call | tf_op jit(solution)/shard_map/pallas_call | solution.py:1987
  72.8 1.2 maximum_convert_fusion
  75.1 1.8 fusion.20
  77.9 17.8 %shard_map.263 = f32[256,256]{1,0:T(8,128)} custom-call(f32[256,256]{1,0:T(8,128)} %fusion.10.part), custom_call_target="tpu_custom_call" | custom-call | tf_op jit(solution)/shard_map/pallas_call | solution.py:662
  98.2 3.0 compare_select_fusion
  101.3 45.0 %shard_map.264 = (f32[256,16,8,128]{3,2,1,0:T(8,128)}, f32[256,1024]{1,0:T(8,128)}, bf16[6144,256]{1,0:T(8,128)(2,1)}) custom-call(f32[256,1024]{1,0:T(8,128)} %get-tuple-element.122.step_ref, f32[256,1024]{1,0:T(8,128)} %get-tuple-element.97.input_ref, f32[4096]{0:T(1024)} %reshape.114.brow_ref, f32[4096]{0:T(1024)} %reshape.115.crow_ref, ...), custom_call_target="tpu_custom_call" | custom-call | tf_op jit(solution)/shard_map/pallas_call | solution.py:1096
  146.5 2.7 multiply_convert_fusion.2.gated
  149.2 1.3 multiply_convert_fusion.refs_0_
  150.5 65.2 %shard_map.265 = (bf16[256,2048]{1,0:T(8,128)(2,1)}, f32[64,2048]{1,0:T(8,128)}, bf16[2048,1024]{1,0:T(8,128)(2,1)}, bf16[2048,256]{1,0:T(8,128)(2,1)}) custom-call(bf16[256,1024]{1,0:T(8,128)(2,1)} %multiply_convert_fusion.2.gated, bf16[2048,256]{1,0:T(8,128)(2,1)} %all-gather.4.cloned.1.call-done.out_first, bf16[6144,256]{1,0:T(8,128)(2,1)} %get-tuple-element.57.out_last, ...), custom_call_target="tpu_custom_call" | custom-call | tf_op jit(solution)/shard_map/pallas_call | solution.py:755
  215.7 20.2 %shard_map.266 = (bf16[256,6144]{1,0:T(8,128)(2,1)}, bf16[2048,256]{1,0:T(8,128)(2,1)}) custom-call(bf16[256,2048]{1,0:T(8,128)(2,1)} %get-tuple-element.58.normed.refs_0_, bf16[256,2048]{1,0:T(8,128)(2,1)} %bitcast.93, bf16[2048,6144]{1,0:T(8,128)(2,1)} %all-gather.6.cloned.1.call-done.weights), custom_call_target="tpu_custom_call" | custom-call | tf_op jit(solution)/shard_map/pallas_call | solution.py:831
  236.0 1.5 slice.147.step_low
  238.9 54.2 %shard_map.267 = (bf16[256,2048]{1,0:T(8,128)(2,1)}, f32[64,2048]{1,0:T(8,128)}, f32[1,2048]{1,0:T(1,128)}, f32[256,1024]{1,0:T(8,128)}, bf16[256,2048]{1,0:T(8,128)(2,1)}, /*index=5*/bf16[2048,256]{1,0:T(8,128)(2,1)}) custom-call(bf16[256,6144]{1,0:T(8,128)(2,1)} %get-tuple-element.59.made, bf16[256,2048]{1,0:T(8,128)(2,1)} %bitcast.94, ...), custom_call_target="tpu_custom_call" | custom-call | tf_op jit(solution)/shard_map/pallas_call | solution.py:942
  293.1 3.9 multiply_reduce_fusion.1
  297.0 32.5 %shard_map.268 = (f32[256,1024]{1,0:T(8,128)}, f32[256,1024]{1,0:T(8,128)}, f32[16,8,128]{2,1,0:T(8,128)}, f32[256,32,128]{2,1,0:T(8,128)}, bf16[64,1024]{1,0:T(8,128)(2,1)}, /*index=5*/bf16[64,1024]{1,0:T(8,128)(2,1)}) custom-call(f32[256,1024]{1,0:T(8,128)} %get-tuple-element.122.step_ref, f32[256,1024]{1,0:T(8,128)} %get-tuple-element.97.input_ref, ...), custom_call_target="tpu_custom_call" | custom-call | tf_op jit(solution)/shard_map/pallas_call | solution.py:1305
  329.5 3.4 reduce_sum.82
  333.0 2.2 fusion.17
  336.2 16.2 %shard_map.269 = (bf16[256,256]{1,0:T(8,128)(2,1)}, bf16[256,1024]{1,0:T(8,128)(2,1)}) custom-call(bf16[256,256]{1,0:T(8,128)(2,1)} %maximum_maximum_fusion.part, bf16[64,1024]{1,0:T(8,128)(2,1)} %get-tuple-element.67.own_rows), custom_call_target="tpu_custom_call" | custom-call | tf_op jit(solution)/shard_map/pallas_call | solution.py:693
  352.4 2.5 multiply_reduce_fusion.5
  355.5 1.4 collective-permute-start
  359.4 2.7 collective-permute-done
  363.0 9.2 %all-gather.8.cloned.1.call-done.ffn_all = bf16[2048,6144]{1,0:T(8,128)(2,1)} async-done(((bf16[256,6144]{1,0:T(8,128)(2,1)}), bf16[2048,6144]{1,0:T(8,128)(2,1)}) %all-gather.8.cloned.1.call-update) | async-done | bytes 25165840 | tf_op jit(solution)/shard_map/all_gather | solution.py:366
  372.2 75.8 %shard_map.270 = (bf16[256,2048]{1,0:T(8,128)(2,1)}, bf16[256,2048]{1,0:T(8,128)(2,1)}, f32[32,1024]{1,0:T(8,128)}, f32[128,1024]{1,0:T(8,128)}, f32[160,1024]{1...) custom-call(bf16[256,1024]{1,0:T(8,128)(2,1)} %bitcast.95, ...), custom_call_target="tpu_custom_call" | custom-call | tf_op jit(solution)/shard_map/pallas_call | solution.py:1836
  448.1 1.5 fusion.23
  449.5 1.4 slice.111
  450.9 1.5 slice_bitcast_fusion.4
  453.9 2.5 copy.51
  457.3 1.3 copy.53
  461.6 2.1 copy.57
  464.7 1.3 copy.58
  (108 shorter events, 22.9 us)
Async XLA Ops:
  7.2 91.1 %copy-start = (bf16[128,1024]{1,0:T(8,128)(2,1)S(1)}, bf16[128,1024]{1,0:T(8,128)(2,1)}, u32[]{:S(2)}) copy-start(bf16[128,1024]{1,0:T(8,128)(2,1)} %param.21) | copy-start | bytes 786436
  7.2 3.3 copy-start.7
  7.2 143.3 %all-gather.4.cloned.1.call-start = ((), (), s32[]{:S(2)}) async-start(), calls=%async_computation | async-start | bytes 1179648 | tf_op jit(solution)/shard_map/all_gather | solution.py:366
  9.0 206.7 %all-gather.6.cloned.1.call-start = ((), (), s32[]{:S(2)}) async-start(), calls=%async_computation.1 | async-start | bytes 28311552 | tf_op jit(solution)/shard_map/all_gather | solution.py:366
  12.5 1.3 copy-start.15
  12.5 2.1 copy-start.26
  12.5 2.1 copy-start.27
  12.5 2.1 copy-start.28
  12.5 2.1 copy-start.25
  12.5 2.7 copy-start.18
  12.5 3.3 copy-start.11
  12.6 359.6 %all-gather.8.cloned.1.call-start = ((), (), s32[]{:S(2)}) async-start(), calls=%async_computation.2 | async-start | bytes 28311552 | tf_op jit(solution)/shard_map/all_gather | solution.py:366
  16.9 57.1 %copy-start.23 = (bf16[4,1024]{1,0:T(4,128)(2,1)S(1)}, bf16[4,1024]{1,0:T(4,128)(2,1)}, u32[]{:S(2)}) copy-start(bf16[4,1024]{1,0:T(4,128)(2,1)} %param.18) | copy-start | bytes 24580
  75.1 1.8 copy-start.17
  76.9 216.2 %copy-start.2 = (bf16[256,1024]{1,0:T(8,128)(2,1)}, bf16[256,1024]{1,0:T(8,128)(2,1)S(1)}, u32[]{:S(2)}) copy-start(bf16[256,1024]{1,0:T(8,128)(2,1)S(1)} %get-tuple-element.98.scan_in) | copy-start | bytes 1572868
  98.2 48.0 %copy-start.1 = (bf16[2,128,2048]{2,1,0:T(8,128)(2,1)S(1)}, bf16[2,128,2048]{2,1,0:T(8,128)(2,1)}, u32[]{:S(2)}) copy-start(bf16[2,128,2048]{2,1,0:T(8,128)(2,1)} %param.15) | copy-start | bytes 3145732
  238.9 54.2 %copy-start.5 = (f32[256,1024]{1,0:T(8,128)S(1)}, f32[256,1024]{1,0:T(8,128)}, u32[]{:S(2)}) copy-start(f32[256,1024]{1,0:T(8,128)} %get-tuple-element.56) | copy-start | bytes 3145732
  329.5 3.5 copy-start.10
  333.0 2.5 copy-start.29
  333.0 19.4 %copy-start.4 = (f32[256,1024]{1,0:T(8,128)S(1)}, f32[256,1024]{1,0:T(8,128)}, u32[]{:S(2)}) copy-start(f32[256,1024]{1,0:T(8,128)} %get-tuple-element.96.ograd_ref) | copy-start | bytes 3145732
  335.2 19.7 %copy-start.3 = (bf16[256,1024]{1,0:T(8,128)(2,1)}, bf16[256,1024]{1,0:T(8,128)(2,1)S(1)}, u32[]{:S(2)}) copy-start(bf16[256,1024]{1,0:T(8,128)(2,1)S(1)} %get-tuple-element.101.pre_low) | copy-start | bytes 1572868
  352.4 2.5 copy-start.22
  355.5 2.0 copy-start.19
  355.5 2.0 copy-start.20
  355.5 6.6 %collective-permute-start = (f32[2,3,1024]{2,1,0:T(4,128)S(1)}, f32[2,3,1024]{2,1,0:T(4,128)S(1)}, u32[]{:S(2)}, u32[]{:S(2)}) collective-permute-start(f32[2,3,1024]{2,1,0:T(4,128)S(1)} %pad_add_fusion.1), channel_id=1, source_target_pairs={{4,0},{5,1},{6,2},{7,3},{12,8},{13,9},{14,10},{15,11},{20,16},{21,... | collective-permute-start | bytes 73736 | tf_op jit(solution)/shard_map/ppermute | solution.py:23
  448.0 8.3 %copy-start.13 = (bf16[256,2048]{1,0:T(8,128)(2,1)S(1)}, bf16[256,2048]{1,0:T(8,128)(2,1)}, u32[]{:S(2)}) copy-start(bf16[256,2048]{1,0:T(8,128)(2,1)} %get-tuple-element.82) | copy-start | bytes 3145732
  453.9 3.4 copy-start.9
  457.3 1.5 copy-start.14
  457.3 2.4 copy-start.16
  457.3 3.1 copy-start.12
  458.8 2.7 copy-start.6
  461.6 3.1 copy-start.8
  (2 other events, 1.3 us)
Sparse Core Ops, SparseCore 0:
  9.9 30.3 all-gather.3
  42.8 172.3 all-gather.5
  236.1 136.0 all-gather.7

commit v18 on v16

--- a/solution.py
+++ b/solution.py
@@ -773,15 +773,16 @@
     )(gated, out_first, out_last, tokens, gain, *arrays)
 
 
-def ffn_kernel(swaps, normed, ct, weights, made, *refs):
+def ffn_kernel(n_swaps, normed, ct, weights, *refs):
     hidden = weights.shape[1] // 3
-    if swaps:
-        *swapped, block_buf, block_sem, send_sem, recv_sem, local_sem = refs
-        swap = Swap([ct], swapped, send_sem, recv_sem, local_sem)
+    arrays, refs = refs[:n_swaps], refs[n_swaps:]
+    made, *refs = refs
+    swapped, refs = refs[:n_swaps], refs[n_swaps:]
+    block_buf, block_sem, *swap_sems = refs
+    if n_swaps:
+        swap = Swap(arrays, swapped, *swap_sems)
         greet([(PLANE, swap.plane.others)])
         swap.begin()
-    else:
-        block_buf, block_sem = refs
 
     def columns(j, which):
         return pl.ds(pl.multiple_of(which * hidden + j * WIDE, WIDE), WIDE)
@@ -819,18 +820,17 @@
         made[:, columns(j, 1)] = (act_grad * up * slope).astype(made.dtype)
         made[:, columns(j, 2)] = (act_grad * silu).astype(made.dtype)
 
-    if swaps:
+    if n_swaps:
         swap.end()
 
 
-def run_ffn(call_id, normed, ct, weights, swaps):
+def run_ffn(call_id, normed, ct, weights, arrays):
     rows, width = normed.shape
-    arrays = [ct] if swaps else []
     vmem = pl.BlockSpec(memory_space=pltpu.VMEM)
-    params = dict(collective_id=call_id, has_side_effects=True) if swaps else {}
+    params = dict(collective_id=call_id, has_side_effects=True) if arrays else {}
     return pl.pallas_call(
-        functools.partial(ffn_kernel, swaps),
-        in_specs=[vmem, vmem, pl.BlockSpec(memory_space=pltpu.HBM)],
+        functools.partial(ffn_kernel, len(arrays)),
+        in_specs=[vmem, vmem, pl.BlockSpec(memory_space=pltpu.HBM)] + [vmem] * len(arrays),
         out_specs=[vmem] + [pl.BlockSpec(memory_space=pltpu.HBM)] * len(arrays),
         out_shape=[jax.ShapeDtypeStruct((rows, weights.shape[1]), jnp.bfloat16)]
         + swap_shapes(arrays),
@@ -840,7 +840,7 @@
         ]
         + swap_scratch(arrays),
         compiler_params=pltpu.CompilerParams(vmem_limit_bytes=VMEM_GRANT, **params),
-    )(normed, ct, weights)
+    )(normed, ct, weights, *arrays)
 
 
 def ffn_back_kernel(
@@ -1767,9 +1767,9 @@
     if swaps:
         swap.begin()
     products(ffn_all, gu_middle, gu_end, flat(1), to_gateup, *wide)
-    tokens_spread.pass_on()
     gather.hand_over_last()
     small_total.hand_over()
+    tokens_spread.pass_on()
     gather.end()
     products(mix_all, 0, 2 * inner // WIDE, flat(0), side_by_side(grad_inproj, 0), *wide)
     small_total.end()
@@ -2103,18 +2103,19 @@
     mixer_core = scan_out + skip_weight[None] * scan_float
     gate_sig = jax.nn.silu(gate_mix)
     gated = (mixer_core * gate_sig).astype(low)
-    normed_two, middle, gated_all, *swapped = mixer_out(
+    normed_two, middle, gated_all = mixer_out(
         1,
         gated,
         out_first,
         out_last,
         tokens_rows,
         gain_ffn_row,
-        [normed_one] if swap_now else [],
+        [],
     )
-    normed_one_cols = columns_of(swapped, normed_one)
-    made, *swapped = run_ffn(8, normed_two, ct_low, ffn_pack, swap_now)
-    ct_cols = columns_of(swapped, ct_low)
+    to_swap = [ct_low, normed_one] if swap_now else []
+    made, *swapped = run_ffn(8, normed_two, ct_low, ffn_pack, to_swap)
+    ct_cols = columns_of(swapped[:1], ct_low)
+    normed_one_cols = columns_of(swapped[1:], normed_one)
     ffn_all = gathered_rows(made)
     middle_low, middle_grad, ffngain_part, gated_grad, ffn_part, *swapped = ffn_back(
         2,

time: 471 us -> 472 us (level)
  waiting for transfers between devices: 15.4 us -> 24.1 us
  Pallas kernels: 377 us -> 369 us
    pallas_call x1, Pallas kernels: 70.9 us -> 51 us  [mixer_out(): pl.pallas_call(functools.partial(mixer_out_kernel, len(arrays)), in_specs...]
    pallas_call x1, Pallas kernels: 19.4 us -> 31.5 us  [run_ffn(): pl.pallas_call(functools.partial(ffn_kernel, len(arrays)), in_specs=[vmem...]
    all_gather x3, waiting for transfers between devices: 12.7 us -> 21.4 us  [gathered_rows(): return lax.all_gather(rows, PLANE, axis=0, tiled=True)]
  transfers between devices with their start and end apart: 4 -> 4, of which waited for: 3 -> 3; matrix products, arithmetic and copies ran while one was open for 9% -> 9% of each run, Pallas kernels for 60% -> 56%
where the time goes in v18:
time: 472 us; the launch traced here: 471 us
  Pallas kernels  369 us (78%)
  local copies, waits for them, and re-layouts  31.8 us (7%)
  waiting for transfers between devices  24.1 us (5%)
  other arithmetic  23.6 us (5%)
  between operations  14.2 us (3%)
  matrix products  6.86 us (1%)
    pallas_call x1, Pallas kernels, run_tail(): pl.pallas_call(functools.partial(tail_kernel, swaps), in_specs=[vmem] * 1...  75.8 us
    pallas_call x1, Pallas kernels, run_head(): pl.pallas_call(head_kernel, in_specs=[vmem] * 2 + [hbm] * 2, out_specs=[v...  55.5 us
    pallas_call x1, Pallas kernels, ffn_back(): pl.pallas_call(functools.partial(ffn_back_kernel, len(arrays)), in_specs=...  54.1 us
    pallas_call x1, Pallas kernels, mixer_out(): pl.pallas_call(functools.partial(mixer_out_kernel, len(arrays)), in_specs...  51 us
    pallas_call x1, Pallas kernels, scan_backward_pair(): pl.pallas_call(functools.partial(backward_pair_kernel, len(arrays), n_sta...  35 us
    pallas_call x1, Pallas kernels, scan_forward_pair(): pl.pallas_call(functools.partial(forward_pair_kernel, n_state, tiles, gro...  33.3 us
    pallas_call x1, Pallas kernels, run_ffn(): pl.pallas_call(functools.partial(ffn_kernel, len(arrays)), in_specs=[vmem...  31.5 us
    all_gather x3, waiting for transfers between devices, gathered_rows(): return lax.all_gather(rows, PLANE, axis=0, tiled=True)  21.4 us
  transfers between devices with their start and end apart: 4, of which 3 were waited for; matrix products, arithmetic and copies ran while one was open for 9% of the time, Pallas kernels for 56%

profile of v18, /device:TPU:0, one launch (start us, length us, event | category | flops | bytes accessed | tf_op | source)
XLA Modules:
  0.0 471.0 jit_solution(5763485103428306726)
XLA Ops:
  7.3 2.0 fusion.22
  9.3 1.5 copy.32
  11.0 1.8 pad_maximum_fusion
  16.4 55.5 %shard_map.262 = (bf16[256,1024]{1,0:T(8,128)(2,1)}, f32[256,1024]{1,0:T(8,128)}, bf16[32,1024]{1,0:T(8,128)(2,1)}, bf16[2048,1024]{1,0:T(8,128)(2,1)}, bf16[2048,1024]{1,0:T(8,128)(2,1)}) custom-call(bf16[256,2048]{1,0:T(8,128)(2,1)} %bitcast.88, bf16[1,2048]{1,0:T(2,128)(2,1)} %reshape.110.gain.gain_row, bf16[256,1024]{1,0:T(8,128)(2,1)} %get-tuple-element.110.in_conv, ...), custom_call_target="tpu_custom_call" | custom-call | tf_op jit(solution)/shard_map/pallas_call | solution.py:1986
  75.1 1.8 fusion.20
  77.9 17.5 %shard_map.263 = f32[256,256]{1,0:T(8,128)} custom-call(f32[256,256]{1,0:T(8,128)} %fusion.10.part), custom_call_target="tpu_custom_call" | custom-call | tf_op jit(solution)/shard_map/pallas_call | solution.py:662
  97.9 3.0 compare_select_fusion
  100.9 33.3 %shard_map.264 = (f32[256,16,8,128]{3,2,1,0:T(8,128)}, f32[256,1024]{1,0:T(8,128)}, bf16[4096,256]{1,0:T(8,128)(2,1)}) custom-call(f32[256,1024]{1,0:T(8,128)} %get-tuple-element.124.step_ref, f32[256,1024]{1,0:T(8,128)} %get-tuple-element.97.input_ref, f32[4096]{0:T(1024)} %reshape.114.brow_ref, f32[4096]{0:T(1024)} %reshape.115.crow_ref, ...), custom_call_target="tpu_custom_call" | custom-call | tf_op jit(solution)/shard_map/pallas_call | solution.py:1095
  134.5 2.7 multiply_convert_fusion.2.gated
  137.1 1.3 multiply_convert_fusion.refs_1_
  138.4 51.0 %shard_map.265 = (bf16[256,2048]{1,0:T(8,128)(2,1)}, f32[64,2048]{1,0:T(8,128)}, bf16[2048,1024]{1,0:T(8,128)(2,1)}) custom-call(bf16[256,1024]{1,0:T(8,128)(2,1)} %multiply_convert_fusion.2.gated, bf16[4096,256]{1,0:T(8,128)(2,1)} %all-gather.4.cloned.1.call-done.out_first, bf16[4096,256]{1,0:T(8,128)(2,1)} %get-tuple-element.57.out_last, ...), custom_call_target="tpu_custom_call" | custom-call | tf_op jit(solution)/shard_map/pallas_call | solution.py:755
  189.4 12.4 %all-gather.6.cloned.1.call-done.weights = bf16[2048,6144]{1,0:T(8,128)(2,1)} async-done(((bf16[256,6144]{1,0:T(8,128)(2,1)}), bf16[2048,6144]{1,0:T(8,128)(2,1)}) %all-gather.6.cloned.1.call-update) | async-done | bytes 25165840 | tf_op jit(solution)/shard_map/all_gather | solution.py:366
  201.8 31.5 %shard_map.266 = (bf16[256,6144]{1,0:T(8,128)(2,1)}, bf16[2048,256]{1,0:T(8,128)(2,1)}, bf16[2048,256]{1,0:T(8,128)(2,1)}) custom-call(bf16[256,2048]{1,0:T(8,128)(2,1)} %get-tuple-element.58.normed.refs_0_, bf16[256,2048]{1,0:T(8,128)(2,1)} %bitcast.91, bf16[2048,6144]{1,0:T(8,128)(2,1)} %all-gather.6.cloned.1.call-done.weights, ...), custom_call_target="tpu_custom_call" | custom-call | tf_op jit(solution)/shard_map/pallas_call | solution.py:831
  233.3 1.5 slice.147.step_low
  236.2 54.1 %shard_map.267 = (bf16[256,2048]{1,0:T(8,128)(2,1)}, f32[64,2048]{1,0:T(8,128)}, f32[1,2048]{1,0:T(1,128)}, f32[256,1024]{1,0:T(8,128)}, bf16[256,2048]{1,0:T(8,128)(2,1)}, /*index=5*/bf16[2048,256]{1,0:T(8,128)(2,1)}) custom-call(bf16[256,6144]{1,0:T(8,128)(2,1)} %get-tuple-element.59.made, bf16[256,2048]{1,0:T(8,128)(2,1)} %bitcast.93, ...), custom_call_target="tpu_custom_call" | custom-call | tf_op jit(solution)/shard_map/pallas_call | solution.py:941
  290.3 3.9 multiply_reduce_fusion.1
  294.2 35.0 %shard_map.268 = (f32[256,1024]{1,0:T(8,128)}, f32[256,1024]{1,0:T(8,128)}, f32[16,8,128]{2,1,0:T(8,128)}, f32[256,32,128]{2,1,0:T(8,128)}, bf16[64,1024]{1,0:T(8,128)(2,1)}, /*index=5*/bf16[64,1024]{1,0:T(8,128)(2,1)}) custom-call(f32[256,1024]{1,0:T(8,128)} %get-tuple-element.124.step_ref, f32[256,1024]{1,0:T(8,128)} %get-tuple-element.97.input_ref, ...), custom_call_target="tpu_custom_call" | custom-call | tf_op jit(solution)/shard_map/pallas_call | solution.py:1304
  329.2 3.4 reduce_sum.82
  332.7 2.2 fusion.17
  335.9 15.2 %shard_map.269 = (bf16[256,256]{1,0:T(8,128)(2,1)}, bf16[256,1024]{1,0:T(8,128)(2,1)}) custom-call(bf16[256,256]{1,0:T(8,128)(2,1)} %maximum_maximum_fusion.part, bf16[64,1024]{1,0:T(8,128)(2,1)} %get-tuple-element.67.own_rows), custom_call_target="tpu_custom_call" | custom-call | tf_op jit(solution)/shard_map/pallas_call | solution.py:693
  351.1 2.5 multiply_reduce_fusion.5
  354.2 1.4 collective-permute-start
  358.1 2.7 collective-permute-done
  361.8 9.0 %all-gather.8.cloned.1.call-done.ffn_all = bf16[2048,6144]{1,0:T(8,128)(2,1)} async-done(((bf16[256,6144]{1,0:T(8,128)(2,1)}), bf16[2048,6144]{1,0:T(8,128)(2,1)}) %all-gather.8.cloned.1.call-update) | async-done | bytes 25165840 | tf_op jit(solution)/shard_map/all_gather | solution.py:366
  370.7 75.8 %shard_map.270 = (bf16[256,2048]{1,0:T(8,128)(2,1)}, bf16[256,2048]{1,0:T(8,128)(2,1)}, f32[32,1024]{1,0:T(8,128)}, f32[128,1024]{1,0:T(8,128)}, f32[160,1024]{1...) custom-call(bf16[256,1024]{1,0:T(8,128)(2,1)} %bitcast.96, ...), custom_call_target="tpu_custom_call" | custom-call | tf_op jit(solution)/shard_map/pallas_call | solution.py:1835
  446.6 1.5 fusion.24
  448.1 1.4 slice.111
  449.4 1.5 slice_bitcast_fusion.4
  452.4 2.5 copy.51
  455.8 1.3 copy.53
  460.1 2.1 copy.57
  463.2 1.3 copy.58
  (105 shorter events, 23.3 us)
Async XLA Ops:
  7.2 90.7 %copy-start = (bf16[128,1024]{1,0:T(8,128)(2,1)S(1)}, bf16[128,1024]{1,0:T(8,128)(2,1)}, u32[]{:S(2)}) copy-start(bf16[128,1024]{1,0:T(8,128)(2,1)} %param.21) | copy-start | bytes 786436
  7.2 3.6 copy-start.7
  7.2 131.2 %all-gather.4.cloned.1.call-start = ((), (), s32[]{:S(2)}) async-start(), calls=%async_computation | async-start | bytes 2359296 | tf_op jit(solution)/shard_map/all_gather | solution.py:366
  9.3 192.6 %all-gather.6.cloned.1.call-start = ((), (), s32[]{:S(2)}) async-start(), calls=%async_computation.1 | async-start | bytes 28311552 | tf_op jit(solution)/shard_map/all_gather | solution.py:366
  12.8 0.7 copy-start.23
  12.8 1.3 copy-start.25
  12.8 1.3 copy-start.26
  12.8 1.3 copy-start.27
  12.8 1.3 copy-start.24
  12.8 1.9 copy-start.17
  12.8 2.6 copy-start.11
  12.8 357.9 %all-gather.8.cloned.1.call-start = ((), (), s32[]{:S(2)}) async-start(), calls=%async_computation.2 | async-start | bytes 28311552 | tf_op jit(solution)/shard_map/all_gather | solution.py:366
  16.4 57.5 %copy-start.22 = (bf16[4,1024]{1,0:T(4,128)(2,1)S(1)}, bf16[4,1024]{1,0:T(4,128)(2,1)}, u32[]{:S(2)}) copy-start(bf16[4,1024]{1,0:T(4,128)(2,1)} %param.18) | copy-start | bytes 24580
  75.1 1.8 copy-start.16
  76.8 213.5 %copy-start.2 = (bf16[256,1024]{1,0:T(8,128)(2,1)}, bf16[256,1024]{1,0:T(8,128)(2,1)S(1)}, u32[]{:S(2)}) copy-start(bf16[256,1024]{1,0:T(8,128)(2,1)S(1)} %get-tuple-element.98.scan_in) | copy-start | bytes 1572868
  97.9 36.3 %copy-start.1 = (bf16[2,128,2048]{2,1,0:T(8,128)(2,1)S(1)}, bf16[2,128,2048]{2,1,0:T(8,128)(2,1)}, u32[]{:S(2)}) copy-start(bf16[2,128,2048]{2,1,0:T(8,128)(2,1)} %param.15) | copy-start | bytes 3145732
  236.2 54.1 %copy-start.5 = (f32[256,1024]{1,0:T(8,128)S(1)}, f32[256,1024]{1,0:T(8,128)}, u32[]{:S(2)}) copy-start(f32[256,1024]{1,0:T(8,128)} %get-tuple-element.56) | copy-start | bytes 3145732
  329.2 3.5 copy-start.10
  332.6 2.5 copy-start.28
  332.6 18.4 %copy-start.4 = (f32[256,1024]{1,0:T(8,128)S(1)}, f32[256,1024]{1,0:T(8,128)}, u32[]{:S(2)}) copy-start(f32[256,1024]{1,0:T(8,128)} %get-tuple-element.96.ograd_ref) | copy-start | bytes 3145732
  334.9 18.8 %copy-start.3 = (bf16[256,1024]{1,0:T(8,128)(2,1)}, bf16[256,1024]{1,0:T(8,128)(2,1)S(1)}, u32[]{:S(2)}) copy-start(bf16[256,1024]{1,0:T(8,128)(2,1)S(1)} %get-tuple-element.101.pre_low) | copy-start | bytes 1572868
  351.1 2.5 copy-start.21
  354.2 2.0 copy-start.18
  354.2 2.0 copy-start.19
  354.2 6.6 %collective-permute-start = (f32[2,3,1024]{2,1,0:T(4,128)S(1)}, f32[2,3,1024]{2,1,0:T(4,128)S(1)}, u32[]{:S(2)}, u32[]{:S(2)}) collective-permute-start(f32[2,3,1024]{2,1,0:T(4,128)S(1)} %pad_add_fusion.1), channel_id=1, source_target_pairs={{4,0},{5,1},{6,2},{7,3},{12,8},{13,9},{14,10},{15,11},{20,16},{21,... | collective-permute-start | bytes 73736 | tf_op jit(solution)/shard_map/ppermute | solution.py:23
  446.6 8.3 %copy-start.13 = (bf16[256,2048]{1,0:T(8,128)(2,1)S(1)}, bf16[256,2048]{1,0:T(8,128)(2,1)}, u32[]{:S(2)}) copy-start(bf16[256,2048]{1,0:T(8,128)(2,1)} %get-tuple-element.82) | copy-start | bytes 3145732
  452.4 3.4 copy-start.9
  455.8 1.5 copy-start.14
  455.8 2.4 copy-start.15
  455.8 3.1 copy-start.12
  457.4 2.7 copy-start.6
  460.1 3.1 copy-start.8
  (1 other events, 0.6 us)
Sparse Core Ops, SparseCore 0:
  9.9 39.1 all-gather.3
  51.6 150.2 all-gather.5
  233.4 137.2 all-gather.7

commit v19 on v16

--- a/solution.py
+++ b/solution.py
@@ -1767,9 +1767,9 @@
     if swaps:
         swap.begin()
     products(ffn_all, gu_middle, gu_end, flat(1), to_gateup, *wide)
-    tokens_spread.pass_on()
     gather.hand_over_last()
     small_total.hand_over()
+    tokens_spread.pass_on()
     gather.end()
     products(mix_all, 0, 2 * inner // WIDE, flat(0), side_by_side(grad_inproj, 0), *wide)
     small_total.end()

time: 471 us -> 471 us (level)
  no operation moved by 1% of the time
where the time goes in v19:
time: 471 us; the launch traced here: 470 us
  Pallas kernels  377 us (80%)
  local copies, waits for them, and re-layouts  31.8 us (7%)
  other arithmetic  23.6 us (5%)
  waiting for transfers between devices  15.4 us (3%)
  between operations  14.2 us (3%)
  matrix products  6.86 us (1%)
    pallas_call x1, Pallas kernels, run_tail(): pl.pallas_call(functools.partial(tail_kernel, swaps), in_specs=[vmem] * 1...  75.8 us
    pallas_call x1, Pallas kernels, mixer_out(): pl.pallas_call(functools.partial(mixer_out_kernel, len(arrays)), in_specs...  70.9 us
    pallas_call x1, Pallas kernels, run_head(): pl.pallas_call(head_kernel, in_specs=[vmem] * 2 + [hbm] * 2, out_specs=[v...  55.5 us
    pallas_call x1, Pallas kernels, ffn_back(): pl.pallas_call(functools.partial(ffn_back_kernel, len(arrays)), in_specs=...  54.1 us
    pallas_call x1, Pallas kernels, scan_backward_pair(): pl.pallas_call(functools.partial(backward_pair_kernel, len(arrays), n_sta...  35 us
    pallas_call x1, Pallas kernels, scan_forward_pair(): pl.pallas_call(functools.partial(forward_pair_kernel, n_state, tiles, gro...  33.3 us
    pallas_call x1, Pallas kernels, run_ffn(): pl.pallas_call(functools.partial(ffn_kernel, swaps), in_specs=[vmem, vmem...  19.4 us
    pallas_call x1, Pallas kernels, run_select(): pl.pallas_call(select_kernel, in_specs=[vmem], out_specs=vmem, out_shape=...  17.5 us
  transfers between devices with their start and end apart: 4, of which 3 were waited for; matrix products, arithmetic and copies ran while one was open for 9% of the time, Pallas kernels for 60%

profile of v19, /device:TPU:0, one launch (start us, length us, event | category | flops | bytes accessed | tf_op | source)
XLA Modules:
  0.0 470.2 jit_solution(9849087394684750273)
XLA Ops:
  7.3 2.0 fusion.22
  9.3 1.5 copy.32
  11.0 1.8 pad_maximum_fusion
  16.4 55.5 %shard_map.262 = (bf16[256,1024]{1,0:T(8,128)(2,1)}, f32[256,1024]{1,0:T(8,128)}, bf16[32,1024]{1,0:T(8,128)(2,1)}, bf16[2048,1024]{1,0:T(8,128)(2,1)}, bf16[2048,1024]{1,0:T(8,128)(2,1)}) custom-call(bf16[256,2048]{1,0:T(8,128)(2,1)} %bitcast.88, bf16[1,2048]{1,0:T(2,128)(2,1)} %reshape.110.gain.gain_row, bf16[256,1024]{1,0:T(8,128)(2,1)} %get-tuple-element.110.in_conv, ...), custom_call_target="tpu_custom_call" | custom-call | tf_op jit(solution)/shard_map/pallas_call | solution.py:1986
  75.1 1.8 fusion.20
  77.9 17.5 %shard_map.263 = f32[256,256]{1,0:T(8,128)} custom-call(f32[256,256]{1,0:T(8,128)} %fusion.10.part), custom_call_target="tpu_custom_call" | custom-call | tf_op jit(solution)/shard_map/pallas_call | solution.py:662
  97.9 3.0 compare_select_fusion
  100.9 33.3 %shard_map.264 = (f32[256,16,8,128]{3,2,1,0:T(8,128)}, f32[256,1024]{1,0:T(8,128)}, bf16[4096,256]{1,0:T(8,128)(2,1)}) custom-call(f32[256,1024]{1,0:T(8,128)} %get-tuple-element.124.step_ref, f32[256,1024]{1,0:T(8,128)} %get-tuple-element.97.input_ref, f32[4096]{0:T(1024)} %reshape.114.brow_ref, f32[4096]{0:T(1024)} %reshape.115.crow_ref, ...), custom_call_target="tpu_custom_call" | custom-call | tf_op jit(solution)/shard_map/pallas_call | solution.py:1095
  134.5 2.7 multiply_convert_fusion.2.gated
  137.1 1.3 multiply_convert_fusion.refs_0_
  138.4 70.9 %shard_map.265 = (bf16[256,2048]{1,0:T(8,128)(2,1)}, f32[64,2048]{1,0:T(8,128)}, bf16[2048,1024]{1,0:T(8,128)(2,1)}, bf16[2048,256]{1,0:T(8,128)(2,1)}) custom-call(bf16[256,1024]{1,0:T(8,128)(2,1)} %multiply_convert_fusion.2.gated, bf16[4096,256]{1,0:T(8,128)(2,1)} %all-gather.4.cloned.1.call-done.out_first, bf16[4096,256]{1,0:T(8,128)(2,1)} %get-tuple-element.57.out_last, ...), custom_call_target="tpu_custom_call" | custom-call | tf_op jit(solution)/shard_map/pallas_call | solution.py:755
  209.4 3.7 all-gather.6.cloned.1.call-done.weights
  213.1 19.4 %shard_map.266 = (bf16[256,6144]{1,0:T(8,128)(2,1)}, bf16[2048,256]{1,0:T(8,128)(2,1)}) custom-call(bf16[256,2048]{1,0:T(8,128)(2,1)} %get-tuple-element.58.normed.refs_0_, bf16[256,2048]{1,0:T(8,128)(2,1)} %bitcast.93, bf16[2048,6144]{1,0:T(8,128)(2,1)} %all-gather.6.cloned.1.call-done.weights), custom_call_target="tpu_custom_call" | custom-call | tf_op jit(solution)/shard_map/pallas_call | solution.py:831
  232.5 1.5 slice.147.step_low
  235.4 54.1 %shard_map.267 = (bf16[256,2048]{1,0:T(8,128)(2,1)}, f32[64,2048]{1,0:T(8,128)}, f32[1,2048]{1,0:T(1,128)}, f32[256,1024]{1,0:T(8,128)}, bf16[256,2048]{1,0:T(8,128)(2,1)}, /*index=5*/bf16[2048,256]{1,0:T(8,128)(2,1)}) custom-call(bf16[256,6144]{1,0:T(8,128)(2,1)} %get-tuple-element.59.made, bf16[256,2048]{1,0:T(8,128)(2,1)} %bitcast.94, ...), custom_call_target="tpu_custom_call" | custom-call | tf_op jit(solution)/shard_map/pallas_call | solution.py:941
  289.5 3.9 multiply_reduce_fusion.1
  293.4 35.0 %shard_map.268 = (f32[256,1024]{1,0:T(8,128)}, f32[256,1024]{1,0:T(8,128)}, f32[16,8,128]{2,1,0:T(8,128)}, f32[256,32,128]{2,1,0:T(8,128)}, bf16[64,1024]{1,0:T(8,128)(2,1)}, /*index=5*/bf16[64,1024]{1,0:T(8,128)(2,1)}) custom-call(f32[256,1024]{1,0:T(8,128)} %get-tuple-element.124.step_ref, f32[256,1024]{1,0:T(8,128)} %get-tuple-element.97.input_ref, ...), custom_call_target="tpu_custom_call" | custom-call | tf_op jit(solution)/shard_map/pallas_call | solution.py:1304
  328.4 3.4 reduce_sum.82
  331.8 2.2 fusion.17
  335.1 15.2 %shard_map.269 = (bf16[256,256]{1,0:T(8,128)(2,1)}, bf16[256,1024]{1,0:T(8,128)(2,1)}) custom-call(bf16[256,256]{1,0:T(8,128)(2,1)} %maximum_maximum_fusion.part, bf16[64,1024]{1,0:T(8,128)(2,1)} %get-tuple-element.67.own_rows), custom_call_target="tpu_custom_call" | custom-call | tf_op jit(solution)/shard_map/pallas_call | solution.py:693
  350.3 2.5 multiply_reduce_fusion.5
  353.4 1.4 collective-permute-start
  357.3 2.7 collective-permute-done
  360.9 9.0 %all-gather.8.cloned.1.call-done.ffn_all = bf16[2048,6144]{1,0:T(8,128)(2,1)} async-done(((bf16[256,6144]{1,0:T(8,128)(2,1)}), bf16[2048,6144]{1,0:T(8,128)(2,1)}) %all-gather.8.cloned.1.call-update) | async-done | bytes 25165840 | tf_op jit(solution)/shard_map/all_gather | solution.py:366
  369.9 75.8 %shard_map.270 = (bf16[256,2048]{1,0:T(8,128)(2,1)}, bf16[256,2048]{1,0:T(8,128)(2,1)}, f32[32,1024]{1,0:T(8,128)}, f32[128,1024]{1,0:T(8,128)}, f32[160,1024]{1...) custom-call(bf16[256,1024]{1,0:T(8,128)(2,1)} %bitcast.95, ...), custom_call_target="tpu_custom_call" | custom-call | tf_op jit(solution)/shard_map/pallas_call | solution.py:1835
  445.8 1.5 fusion.24
  447.3 1.4 slice.111
  448.6 1.5 slice_bitcast_fusion.4
  451.6 2.5 copy.51
  455.0 1.3 copy.53
  459.3 2.1 copy.57
  462.4 1.3 copy.58
  (105 shorter events, 23.3 us)
Async XLA Ops:
  7.2 90.7 %copy-start = (bf16[128,1024]{1,0:T(8,128)(2,1)S(1)}, bf16[128,1024]{1,0:T(8,128)(2,1)}, u32[]{:S(2)}) copy-start(bf16[128,1024]{1,0:T(8,128)(2,1)} %param.21) | copy-start | bytes 786436
  7.2 3.6 copy-start.7
  7.2 131.2 %all-gather.4.cloned.1.call-start = ((), (), s32[]{:S(2)}) async-start(), calls=%async_computation | async-start | bytes 2359296 | tf_op jit(solution)/shard_map/all_gather | solution.py:366
  9.3 203.8 %all-gather.6.cloned.1.call-start = ((), (), s32[]{:S(2)}) async-start(), calls=%async_computation.1 | async-start | bytes 28311552 | tf_op jit(solution)/shard_map/all_gather | solution.py:366
  12.8 0.7 copy-start.23
  12.8 1.3 copy-start.25
  12.8 1.3 copy-start.26
  12.8 1.3 copy-start.27
  12.8 1.3 copy-start.24
  12.8 1.9 copy-start.17
  12.8 2.6 copy-start.11
  12.8 357.1 %all-gather.8.cloned.1.call-start = ((), (), s32[]{:S(2)}) async-start(), calls=%async_computation.2 | async-start | bytes 28311552 | tf_op jit(solution)/shard_map/all_gather | solution.py:366
  16.4 57.5 %copy-start.22 = (bf16[4,1024]{1,0:T(4,128)(2,1)S(1)}, bf16[4,1024]{1,0:T(4,128)(2,1)}, u32[]{:S(2)}) copy-start(bf16[4,1024]{1,0:T(4,128)(2,1)} %param.18) | copy-start | bytes 24580
  75.1 1.8 copy-start.16
  76.8 212.7 %copy-start.2 = (bf16[256,1024]{1,0:T(8,128)(2,1)}, bf16[256,1024]{1,0:T(8,128)(2,1)S(1)}, u32[]{:S(2)}) copy-start(bf16[256,1024]{1,0:T(8,128)(2,1)S(1)} %get-tuple-element.98.scan_in) | copy-start | bytes 1572868
  97.9 36.3 %copy-start.1 = (bf16[2,128,2048]{2,1,0:T(8,128)(2,1)S(1)}, bf16[2,128,2048]{2,1,0:T(8,128)(2,1)}, u32[]{:S(2)}) copy-start(bf16[2,128,2048]{2,1,0:T(8,128)(2,1)} %param.15) | copy-start | bytes 3145732
  235.4 54.1 %copy-start.5 = (f32[256,1024]{1,0:T(8,128)S(1)}, f32[256,1024]{1,0:T(8,128)}, u32[]{:S(2)}) copy-start(f32[256,1024]{1,0:T(8,128)} %get-tuple-element.56) | copy-start | bytes 3145732
  328.4 3.5 copy-start.10
  331.8 2.5 copy-start.28
  331.8 18.4 %copy-start.4 = (f32[256,1024]{1,0:T(8,128)S(1)}, f32[256,1024]{1,0:T(8,128)}, u32[]{:S(2)}) copy-start(f32[256,1024]{1,0:T(8,128)} %get-tuple-element.96.ograd_ref) | copy-start | bytes 3145732
  334.0 18.8 %copy-start.3 = (bf16[256,1024]{1,0:T(8,128)(2,1)}, bf16[256,1024]{1,0:T(8,128)(2,1)S(1)}, u32[]{:S(2)}) copy-start(bf16[256,1024]{1,0:T(8,128)(2,1)S(1)} %get-tuple-element.101.pre_low) | copy-start | bytes 1572868
  350.3 2.5 copy-start.21
  353.4 2.0 copy-start.18
  353.4 2.0 copy-start.19
  353.4 6.6 %collective-permute-start = (f32[2,3,1024]{2,1,0:T(4,128)S(1)}, f32[2,3,1024]{2,1,0:T(4,128)S(1)}, u32[]{:S(2)}, u32[]{:S(2)}) collective-permute-start(f32[2,3,1024]{2,1,0:T(4,128)S(1)} %pad_add_fusion.1), channel_id=1, source_target_pairs={{4,0},{5,1},{6,2},{7,3},{12,8},{13,9},{14,10},{15,11},{20,16},{21,... | collective-permute-start | bytes 73736 | tf_op jit(solution)/shard_map/ppermute | solution.py:23
  445.8 8.3 %copy-start.13 = (bf16[256,2048]{1,0:T(8,128)(2,1)S(1)}, bf16[256,2048]{1,0:T(8,128)(2,1)}, u32[]{:S(2)}) copy-start(bf16[256,2048]{1,0:T(8,128)(2,1)} %get-tuple-element.82) | copy-start | bytes 3145732
  451.6 3.4 copy-start.9
  455.0 1.5 copy-start.14
  455.0 2.4 copy-start.15
  455.0 3.1 copy-start.12
  456.6 2.7 copy-start.6
  459.3 3.1 copy-start.8
  (1 other events, 0.6 us)
Sparse Core Ops, SparseCore 0:
  9.9 39.1 all-gather.3
  51.6 161.4 all-gather.5
  232.6 137.2 all-gather.7
